TPU v7x, 32 devices: a whole 2x2x4 slice. The times are simulated.
32 devices in a mesh: group: 2 (over y), expert: 2 (over core), tile: 8 (over z, x).
Axes of the slice: x: 2, y: 2, z: 4, core: 2. Of those that a mesh axis runs over, the one named last changes fastest.
Arguments:
- tokens: bfloat16 [64, 6144], P(('group', 'tile'), 'expert'), parts along dimension 0, may hold values from -6 to 6
- routes: int32 [64, 2], P(('group', 'tile')), parts along dimension 0, may hold values from 0 to 7, as said below
- gates: float32 [64, 2], P(('group', 'tile')), parts along dimension 0, may hold values from 0.2 to 1
- w_gate: bfloat16 [2, 6144, 16384], P('expert', None, 'tile'), may hold values from -0.078125 to 0.078125
- w_up: bfloat16 [2, 6144, 16384], P('expert', None, 'tile'), may hold values from -0.078125 to 0.078125
- w_down: bfloat16 [2, 6144, 16384], P('expert', 'tile'), may hold values from -0.046875 to 0.046875
Outputs:
- mixed_out: bfloat16 [64, 6144], P(('group', 'tile'), 'expert'), parts along dimension 0
There are 2 independent parts, one for each index of `group`. A program takes and returns all parts, laid end to end along the dimension named above; an argument that names none is the same for every part. Nothing has to cross between parts.
Inputs may be any that keep to these rules, and one draw needn't show every extreme that they name: `routes`: each row names two different experts. Over the 4 rows of one index of tile, each expert below 2 is named by at most 2 rows, and in every draw some expert below 2 is named by exactly 2 rows of every such block.
All inputs are finite; a program needn't handle non-finite values.
Results may differ from a plain program's by a relative error of at most 0.0095.
Values may be sent and summed in bfloat16 or wider, within the bound.
No kernel may reach another device: no remote copies, remote signals or barrier semaphores. Data moves between devices by JAX's collectives and lax.ppermute only.
A program may use at most 192 MiB of HBM per device.

v0:
```python
import jax
import jax.numpy as jnp
from jax import lax
from jax.sharding import PartitionSpec as P


def local(tokens, routes, gates, w_gate, w_up, w_down):
    experts = lax.axis_size("expert")
    tile_count = lax.axis_size("tile")
    own_expert = lax.axis_index("expert")
    half_width = tokens.shape[1]
    tok_rows = tokens.shape[0]
    slot_count = max(2, tok_rows // 2)
    window_ids = lax.broadcasted_iota(jnp.int32, (1, 1, experts), 2)
    is_named = routes[:, :, None] == window_ids
    chosen = jnp.any(is_named, axis=1)
    weight = jnp.sum(jnp.where(is_named, gates[:, :, None], jnp.float32(0.0)), axis=1)
    position = jnp.cumsum(chosen.astype(jnp.int32), axis=0) - 1
    slot_ids = lax.broadcasted_iota(jnp.int32, (1, slot_count, 1), 1)
    dispatch = jnp.logical_and(chosen.T[:, None, :], position.T[:, None, :] == slot_ids)
    placing = dispatch.astype(jnp.bfloat16)
    outgoing = jnp.einsum(
        "ecr,rd->ecd", placing, tokens, preferred_element_type=jnp.float32
    ).astype(jnp.bfloat16)
    slot_weight = jnp.einsum("ecr,re->ec", dispatch.astype(jnp.float32), weight)
    everything = lax.all_gather(outgoing[None], ("expert", "tile"), axis=0, tiled=True)
    picked = lax.dynamic_slice_in_dim(everything, own_expert, 1, 1)[:, 0]
    picked = picked.reshape(experts, tile_count, slot_count, half_width)
    gathered = jnp.transpose(picked, (1, 2, 0, 3)).reshape(
        tile_count * slot_count, experts * half_width
    )
    gate_proj = jnp.dot(gathered, w_gate[0], preferred_element_type=jnp.float32)
    up_proj = jnp.dot(gathered, w_up[0], preferred_element_type=jnp.float32)
    hidden = (jax.nn.silu(gate_proj) * up_proj).astype(jnp.bfloat16)
    columns = w_down[0]
    summed = lax.dot_general(
        columns,
        lax.all_gather(hidden, "tile", axis=1, tiled=True),
        (((1,), (1,)), ((), ())),
        preferred_element_type=jnp.float32,
    )
    homeward = lax.all_to_all(summed, "tile", split_axis=1, concat_axis=0, tiled=True)
    returned = lax.all_to_all(homeward, "expert", split_axis=0, concat_axis=1, tiled=True)
    contribution = (slot_weight.reshape(1, experts * slot_count) * returned).astype(jnp.bfloat16)
    flat_places = placing.reshape(experts * slot_count, tok_rows)
    return jnp.einsum(
        "st,ds->td", flat_places, contribution, preferred_element_type=jnp.float32
    ).astype(jnp.bfloat16)


def solution(mesh):
    in_specs = (
        P(("group", "tile"), "expert"),
        P(("group", "tile"), None),
        P(("group", "tile"), None),
        P("expert", None, "tile"),
        P("expert", None, "tile"),
        P("expert", "tile", None),
    )
    out_specs = P(("group", "tile"), "expert")
    return jax.shard_map(local, mesh=mesh, in_specs=in_specs, out_specs=out_specs, check_vma=False)
```

profile of v0, /device:TPU:0, one launch (start us, length us, event | category | flops | bytes accessed | tf_op | source)
XLA Modules:
  0.0 116.2 jit_solution(7326944887709235587)
XLA Ops:
  0.0 0.0 copy-start
  0.0 0.7 fusion.20
  0.7 0.1 copy.29
  0.9 0.1 copy.24
  1.0 0.0 copy-done
  1.0 0.1 convolution_convert_fusion
  1.1 36.6 %all-gather = bf16[32,2,3072]{2,1,0:T(2,128)(2,1)S(1)} all-gather(bf16[2,2,3072]{2,1,0:T(2,128)(2,1)S(1)} %convolution_convert_fusion), channel_id=2, replica_groups=mesh['group'=2,'expert'=2,'tile'=8] {'expert','tile'}, dimensions={0}, use_global_device_ids=true | all-gather | bytes 417792 | tf_op jit(solution)/shard_map/all_gather | solution.py:26
  37.7 0.1 constant_dynamic-slice_fusion
  37.9 0.2 copy.26
  38.2 9.9 %fusion.4 = f32[16,2048]{1,0:T(8,128)S(1)} fusion(bf16[16,6144]{1,0:T(8,128)(2,1)S(1)} %bitcast.57, bf16[1,6144,2048]{2,1,0:T(8,128)(2,1)} %param.9), kind=kOutput, calls=%fused_computation.4 | convolution fusion | flops 402653184 | bytes 25493504 | tf_op jit(solution)/shard_map/dot_general | solution.py:32
  48.1 0.0 copy-start.1
  48.1 10.0 %fusion.10 = bf16[16,2048]{1,0:T(8,128)(2,1)S(1)} fusion(bf16[16,6144]{1,0:T(8,128)(2,1)S(1)} %bitcast.58, bf16[1,6144,2048]{2,1,0:T(8,128)(2,1)} %param.10, f32[16,2048]{1,0:T(8,128)S(1)} %fusion.4), kind=kOutput, calls=%fused_computation.10 | convolution fusion | flops 402849792 | bytes 25559040 | tf_op jit(solution)/shard_map/dot_general | solution.py:33
  58.0 0.0 copy-start.2
  58.1 0.0 copy-start.3
  58.1 31.3 %all_gather.7 = bf16[16,16384]{1,0:T(8,128)(2,1)S(1)} all-gather(bf16[16,2048]{1,0:T(8,128)(2,1)S(1)} %fusion.10), channel_id=1, replica_groups=mesh['group'=2,'expert'=2,'tile'=8] {'tile'}, dimensions={1}, use_global_device_ids=true | all-gather | bytes 589824 | tf_op jit(solution)/shard_map/all_gather | solution.py:38
  89.3 11.5 %fusion.13 = f32[768,16]{0,1:T(8,128)S(1)} fusion(bf16[16,16384]{1,0:T(8,128)(2,1)S(1)} %all_gather.7, bf16[1,768,16384]{2,1,0:T(8,128)(2,1)} %param.11), kind=kOutput, calls=%fused_computation.11 | convolution fusion | flops 402653184 | bytes 25739264 | tf_op jit(solution)/shard_map/dot_general | solution.py:36
  100.8 0.7 all_to_all.22
  101.5 3.3 %all-to-all-start = ((f32[768,8,2]{0,2,1:T(2,128)}), f32[768,8,2]{0,2,1:T(2,128)S(1)}, u32[]{:S(2)}, u32[]{:S(2)}) async-start(f32[768,8,2]{0,2,1:T(2,128)} %all_to_all.22), calls=%async_computation | async-start | bytes 98304 | tf_op jit(solution)/shard_map/all_to_all | solution.py:42
  104.8 0.0 copy-done.2
  104.9 0.0 copy-done.3
  104.9 0.1 fusion.21
  105.0 6.6 %all-to-all-done = f32[768,8,2]{0,2,1:T(2,128)S(1)} async-done(((f32[768,8,2]{0,2,1:T(2,128)}), f32[768,8,2]{0,2,1:T(2,128)S(1)}, u32[]{:S(2)}, u32[]{:S(2)}) %all-to-all-start) | async-done | bytes 49184 | tf_op jit(solution)/shard_map/all_to_all | solution.py:42
  111.6 3.8 %all_to_all.29 = f32[2,3072,2]{1,2,0:T(2,128)S(1)} all-to-all(f32[2,3072,2]{1,2,0:T(2,128)S(1)} %bitcast.62), channel_id=1, replica_groups=mesh['group'=2,'expert'=2,'tile'=8] {'expert'}, dimensions={0} | all-to-all | bytes 98304 | tf_op jit(solution)/shard_map/all_to_all | solution.py:43
  115.3 0.8 fusion.6
  116.2 0.0 copy-done.1
  (7 shorter events, 0.1 us)
Async XLA Ops:
  0.0 1.0 copy-start
  48.1 68.1 %copy-start.1 = (bf16[4,3072]{1,0:T(4,128)(2,1)S(1)}, bf16[4,3072]{1,0:T(4,128)(2,1)}, u32[]{:S(2)}) copy-start(bf16[4,3072]{1,0:T(4,128)(2,1)} %param.6) | copy-start | bytes 73732
  58.0 46.8 %copy-start.2 = (s32[4,2]{0,1:T(2,128)S(1)}, s32[4,2]{0,1:T(2,128)}, u32[]{:S(2)}) copy-start(s32[4,2]{0,1:T(2,128)} %param.7) | copy-start | bytes 100
  58.1 46.8 %copy-start.3 = (f32[4,2]{0,1:T(2,128)S(1)}, f32[4,2]{0,1:T(2,128)}, u32[]{:S(2)}) copy-start(f32[4,2]{0,1:T(2,128)} %param.8) | copy-start | bytes 100
  101.5 10.1 %all-to-all-start = ((f32[768,8,2]{0,2,1:T(2,128)}), f32[768,8,2]{0,2,1:T(2,128)S(1)}, u32[]{:S(2)}, u32[]{:S(2)}) async-start(f32[768,8,2]{0,2,1:T(2,128)} %all_to_all.22), calls=%async_computation | async-start | bytes 98304 | tf_op jit(solution)/shard_map/all_to_all | solution.py:42
where the time goes:
time: 116 us
  blocking collectives  71.6 us (62%)
  matrix products  32.4 us (28%)
  waiting for transfers between devices  6.58 us (6%)
  starting transfers between devices  3.34 us (3%)
  local copies, waits for them, and re-layouts  1.31 us (1%)
    all_gather x1, blocking collectives, local(): lax.all_gather(outgoing[None], ('expert', 'tile'), axis=0, tiled=True)  36.6 us
    all_gather x1, blocking collectives, local(): lax.all_gather(hidden, 'tile', axis=1, tiled=True)  31.3 us
    dot_general x1, matrix products, local(): lax.dot_general(columns, lax.all_gather(hidden, 'tile', axis=1, tiled=Tru...  11.5 us
    dot_general x1, matrix products, local(): up_proj = jnp.dot(gathered, w_up[0], preferred_element_type=jnp.float32)  9.96 us
    dot_general x1, matrix products, local(): gate_proj = jnp.dot(gathered, w_gate[0], preferred_element_type=jnp.float32)  9.91 us
    all_to_all x1, waiting for transfers between devices, local(): lax.all_to_all(summed, 'tile', split_axis=1, concat_axis=0, tiled=True)  6.58 us
    all_to_all x1, blocking collectives, local(): lax.all_to_all(homeward, 'expert', split_axis=0, concat_axis=1, tiled=True)  3.76 us
    all_to_all x1, starting transfers between devices, local(): lax.all_to_all(summed, 'tile', split_axis=1, concat_axis=0, tiled=True)  3.34 us
  transfers between devices with their start and end apart: 1, of which 1 were waited for; matrix products, arithmetic and copies ran while one was open for 0% of the time, Pallas kernels for 0%

commit v1 on v0

v1 whole, which is shorter than its diff:
```python
import functools

import jax
import jax.numpy as jnp
from jax import lax
from jax.experimental import pallas as pl
from jax.experimental.pallas import tpu as pltpu
from jax.sharding import PartitionSpec as P

MIB = 1 << 20
SLOTS = 2
VMEM = pl.BlockSpec(memory_space=pltpu.VMEM)
SMEM = pl.BlockSpec(memory_space=pltpu.SMEM)
ANY = pl.BlockSpec(memory_space=pl.ANY)


def in_hbm(x):
    return pltpu.with_memory_space_constraint(x, pltpu.HBM)


def dispatch_kernel(tokens_ref, routes_ref, sends_ref, *, experts):
    tokens = tokens_ref[...].astype(jnp.float32)
    tiles = sends_ref.shape[0] // experts
    rows = tokens.shape[0]
    for e in range(experts):
        taken = jnp.int32(0)
        slots = [jnp.zeros((1, tokens.shape[1]), jnp.float32) for _ in range(SLOTS)]
        for r in range(rows):
            named = jnp.logical_or(routes_ref[r, 0] == e, routes_ref[r, 1] == e)
            for c in range(SLOTS):
                here = jnp.logical_and(named, taken == c).astype(jnp.float32)
                slots[c] = slots[c] + here * tokens[r:r + 1, :]
            taken = taken + named.astype(jnp.int32)
        block = jnp.concatenate(slots, axis=0).astype(jnp.bfloat16)
        for t in range(tiles):
            sends_ref[e * tiles + t] = block


def load_kernel(after_ref, hbm_ref, vmem_ref, sems):
    parts = sems.shape[0]
    rows = hbm_ref.shape[1] // parts
    copies = []
    for i in range(parts):
        part = pl.ds(i * rows, rows)
        copies.append(pltpu.make_async_copy(hbm_ref.at[0, part], vmem_ref.at[part], sems.at[i]))
        copies[-1].start()
    for copy in copies:
        copy.wait()


def load(w, after, name):
    parts = 6
    return pl.pallas_call(
        load_kernel,
        out_shape=pltpu.VMEM(w.shape[1:], w.dtype),
        in_specs=[ANY, ANY],
        out_specs=VMEM,
        scratch_shapes=[pltpu.SemaphoreType.DMA((parts,))],
        compiler_params=pltpu.CompilerParams(vmem_limit_bytes=MIB),
        cost_estimate=pl.CostEstimate(flops=0, bytes_accessed=2 * w.size * 2, transcendentals=0),
        name=name,
    )(after, in_hbm(w))


def hidden_kernel(rows_ref, w_gate_ref, w_up_hbm, hidden_ref, x_ref, ring, gate_ref, up_ref, sems):
    slots = hidden_ref.shape[0]
    half = rows_ref.shape[2]
    depth, chunk = ring.shape[0], ring.shape[1]
    steps = w_gate_ref.shape[0] // chunk

    def copy(i):
        return pltpu.make_async_copy(w_up_hbm.at[0, pl.ds(i * chunk, chunk)], ring.at[i % depth], sems.at[i % depth])

    for i in range(depth):
        copy(i).start()
    x_ref[...] = rows_ref[...].reshape(x_ref.shape)
    for i in range(steps):
        h, k = divmod(i * chunk, half)
        x = x_ref[h * slots:(h + 1) * slots, k:k + chunk]
        gate = jnp.dot(x, w_gate_ref[i * chunk:(i + 1) * chunk, :], preferred_element_type=jnp.float32)
        copy(i).wait()
        up = jnp.dot(x, ring[i % depth], preferred_element_type=jnp.float32)
        if i + depth < steps:
            copy(i + depth).start()
        gate_ref[...] = gate if i == 0 else gate_ref[...] + gate
        up_ref[...] = up if i == 0 else up_ref[...] + up
    gate = gate_ref[...]
    hidden_ref[...] = (gate / (1.0 + jnp.exp(-gate)) * up_ref[...]).astype(jnp.bfloat16)


def down_kernel(n, *refs):
    blocks, w_ref, sends_ref = refs[:n], refs[n], refs[n + 1]
    me = lax.axis_index("tile")
    tiles = blocks[0].shape[0] // SLOTS
    width = blocks[0].shape[1]
    total = jnp.zeros((blocks[0].shape[0], w_ref.shape[0]), jnp.float32)
    for k in range(n):
        columns = pl.ds(pl.multiple_of((me ^ k) * width, width), width)
        total += lax.dot_general(
            blocks[k][...], w_ref[:, columns], (((1,), (1,)), ((), ())),
            preferred_element_type=jnp.float32,
        )
    for t in range(tiles):
        for e in range(sends_ref.shape[0] // tiles):
            sends_ref[e * tiles + t] = total[t * SLOTS:(t + 1) * SLOTS, :]


def spread(x, experts):
    x = x.reshape(1, x.shape[0] // SLOTS, SLOTS, x.shape[1])
    return jnp.broadcast_to(x, (experts,) + x.shape[1:]).reshape(-1, SLOTS, x.shape[3])


def local(tokens, routes, gates, w_gate, w_up, w_down):
    experts = lax.axis_size("expert")
    tiles = lax.axis_size("tile")
    own = lax.axis_index("expert")
    half_width = tokens.shape[1]
    width = w_gate.shape[2]
    features = w_down.shape[1]
    slots = tiles * SLOTS
    direct = tiles <= 8

    sends = pl.pallas_call(
        functools.partial(dispatch_kernel, experts=experts),
        out_shape=jax.ShapeDtypeStruct((experts * tiles, SLOTS, half_width), jnp.bfloat16),
        in_specs=[VMEM, SMEM],
        out_specs=VMEM,
        compiler_params=pltpu.CompilerParams(vmem_limit_bytes=16 * MIB),
        name="dispatch",
    )(tokens, routes)
    gate_held = load(w_gate, sends, "load_gate")
    rows = lax.all_to_all(sends, ("expert", "tile"), split_axis=0, concat_axis=0, tiled=True)

    chunk = half_width // 4
    depth = 4
    hidden = pl.pallas_call(
        hidden_kernel,
        out_shape=jax.ShapeDtypeStruct((slots, width), jnp.bfloat16),
        in_specs=[VMEM, VMEM, ANY],
        out_specs=VMEM,
        scratch_shapes=[
            pltpu.VMEM((experts * slots, half_width), jnp.bfloat16),
            pltpu.VMEM((depth, chunk, width), jnp.bfloat16),
            pltpu.VMEM((slots, width), jnp.float32),
            pltpu.VMEM((slots, width), jnp.float32),
            pltpu.SemaphoreType.DMA((depth,)),
        ],
        compiler_params=pltpu.CompilerParams(vmem_limit_bytes=24 * MIB),
        name="hidden",
    )(rows, gate_held, in_hbm(w_up))

    if direct:
        down_held = load(w_down, hidden, "load_down")
        blocks = [hidden]
        for k in range(1, tiles):
            blocks.append(lax.ppermute(hidden, "tile", [(t, t ^ k) for t in range(tiles)]))
        sends = pl.pallas_call(
            functools.partial(down_kernel, tiles),
            out_shape=jax.ShapeDtypeStruct((experts * tiles, SLOTS, features), jnp.float32),
            in_specs=[VMEM] * (tiles + 1),
            out_specs=VMEM,
            compiler_params=pltpu.CompilerParams(vmem_limit_bytes=8 * MIB),
            name="down",
        )(*blocks, down_held)
    else:
        gathered = lax.all_gather(hidden, "tile", axis=1, tiled=True)
        sends = spread(lax.dot_general(
            gathered, w_down[0], (((1,), (1,)), ((), ())), preferred_element_type=jnp.float32
        ), experts)

    back = lax.all_to_all(sends, ("expert", "tile"), split_axis=0, concat_axis=0, tiled=True)
    back, routes, gates = lax.optimization_barrier((back, routes, gates))
    back = back.reshape(experts, tiles, SLOTS, features)
    back = lax.dynamic_slice_in_dim(back, own * (tiles // experts), tiles // experts, 1)
    back = jnp.transpose(back, (0, 2, 1, 3)).reshape(experts, SLOTS, half_width)

    window_ids = lax.broadcasted_iota(jnp.int32, (1, 1, experts), 2)
    is_named = routes[:, :, None] == window_ids
    chosen = jnp.any(is_named, axis=1)
    weight = jnp.sum(jnp.where(is_named, gates[:, :, None], jnp.float32(0.0)), axis=1)
    position = jnp.cumsum(chosen.astype(jnp.int32), axis=0) - 1
    mixed = jnp.zeros((tokens.shape[0], half_width), jnp.float32)
    for e in range(experts):
        for c in range(SLOTS):
            mask = jnp.logical_and(chosen[:, e:e + 1], position[:, e:e + 1] == c)
            contribution = (weight[:, e:e + 1] * back[e, c][None]).astype(jnp.bfloat16)
            mixed += jnp.where(mask, contribution, 0).astype(jnp.float32)
    return mixed.astype(jnp.bfloat16)


def solution(mesh):
    in_specs = (
        P(("group", "tile"), "expert"),
        P(("group", "tile"), None),
        P(("group", "tile"), None),
        P("expert", None, "tile"),
        P("expert", None, "tile"),
        P("expert", "tile", None),
    )
    out_specs = P(("group", "tile"), "expert")
    return jax.shard_map(local, mesh=mesh, in_specs=in_specs, out_specs=out_specs, check_vma=False)
```

time: 116 us -> 85.7 us (0.74)
  blocking collectives: 71.6 us -> 0 us
  Pallas kernels: 0 us -> 34.2 us
  matrix products: 32.4 us -> 0 us
  starting transfers between devices: 3.34 us -> 24.6 us
  local copies, waits for them, and re-layouts: 1.31 us -> 18.1 us
    all_gather x2 -> x0, blocking collectives: 67.9 us -> none  [the longest x1 36.6 us: local(): lax.all_gather(outgoing[None], ('expert', 'tile'), axis=0, tiled=True)]
    pallas_call x0 -> x5, Pallas kernels: none -> 34.2 us  [the longest x2 16.6 us: load(): pl.pallas_call(load_kernel, out_shape=pltpu.VMEM(w.shape[1:], w.dtype), i...]
    dot_general x6 -> x0, matrix products: 32.4 us -> none  [the longest x1 11.5 us: local(): lax.dot_general(columns, lax.all_gather(hidden, 'tile', axis=1, tiled=Tru...]
    unnamed x10 -> x12, local copies, waits for them, and re-layouts: 0.17 us -> 18.1 us
    ppermute x0 -> x7, starting transfers between devices: none -> 11.2 us  [local(): lax.ppermute(hidden, 'tile', [(t, t ^ k) for t in range(tiles)])]
    all_to_all x1 -> x2, starting transfers between devices: 3.34 us -> 13.4 us  [local(): lax.all_to_all(sends, ('expert', 'tile'), split_axis=0, concat_axis=0, ti...]
    all_to_all x1 -> x0, blocking collectives: 3.76 us -> none  [local(): lax.all_to_all(homeward, 'expert', split_axis=0, concat_axis=1, tiled=True)]
    all_to_all x1 -> x2, waiting for transfers between devices: 6.58 us -> 7.2 us  [local(): lax.all_to_all(sends, ('expert', 'tile'), split_axis=0, concat_axis=0, ti...]
  transfers between devices with their start and end apart: 1 -> 9, of which waited for: 1 -> 1; matrix products, arithmetic and copies ran while one was open for 0% -> 0% of each run, Pallas kernels for 0% -> 19%
where the time goes in v1:
time: 85.7 us; the launch traced here: 85.3 us
  Pallas kernels  34.2 us (40%)
  starting transfers between devices  24.6 us (29%)
  local copies, waits for them, and re-layouts  18.1 us (21%)
  waiting for transfers between devices  7.22 us (8%)
  other arithmetic  1.03 us (1%)
    unnamed x12, local copies, waits for them, and re-layouts  18.1 us
    pallas_call x2, Pallas kernels, load(): pl.pallas_call(load_kernel, out_shape=pltpu.VMEM(w.shape[1:], w.dtype), i...  16.6 us
    all_to_all x2, starting transfers between devices, local(): lax.all_to_all(sends, ('expert', 'tile'), split_axis=0, concat_axis=0, ti...  13.4 us
    ppermute x7, starting transfers between devices, local(): lax.ppermute(hidden, 'tile', [(t, t ^ k) for t in range(tiles)])  11.2 us
    pallas_call x1, Pallas kernels, local(): pl.pallas_call(hidden_kernel, out_shape=jax.ShapeDtypeStruct((slots, widt...  9.02 us
    pallas_call x1, Pallas kernels, local(): pl.pallas_call(functools.partial(down_kernel, tiles), out_shape=jax.Shape...  7.23 us
    all_to_all x2, waiting for transfers between devices, local(): lax.all_to_all(sends, ('expert', 'tile'), split_axis=0, concat_axis=0, ti...  7.2 us
  transfers between devices with their start and end apart: 9, of which 1 were waited for; matrix products, arithmetic and copies ran while one was open for 0% of the time, Pallas kernels for 19%

profile of v1, /device:TPU:0, one launch (start us, length us, event | category | flops | bytes accessed | tf_op | source)
XLA Modules:
  0.0 85.3 jit_solution(17120879463461081647)
XLA Ops:
  0.0 0.8 copy.10.routes_ref
  0.8 0.7 copy-done.2
  1.5 1.4 %dispatch.1.after_ref = bf16[16,2,3072]{2,1,0:T(2,128)(2,1)} custom-call(bf16[4,3072]{1,0:T(4,128)(2,1)S(1)} %copy-done.2, s32[4,2]{1,0:T(4,128)S(1)} %copy.10.routes_ref), custom_call_target="tpu_custom_call" | custom-call | tf_op jit(solution)/shard_map/dispatch/pallas_call | solution.py:123
  2.9 7.4 %all-to-all-start = ((bf16[16,2,3072]{2,1,0:T(2,128)(2,1)}), bf16[16,2,3072]{2,1,0:T(2,128)(2,1)S(1)}, u32[]{:S(2)}, u32[]{:S(2)}) async-start(bf16[16,2,3072]{2,1,0:T(2,128)(2,1)} %dispatch.1.after_ref), calls=%async_computation | async-start | bytes 393216 | tf_op jit(solution)/shard_map/all_to_all | solution.py:132
  10.2 8.3 %load_gate.1.w_gate_ref = bf16[6144,2048]{1,0:T(8,128)(2,1)S(1)} custom-call(bf16[16,2,3072]{2,1,0:T(2,128)(2,1)} %dispatch.1.after_ref, bf16[1,6144,2048]{2,1,0:T(8,128)(2,1)} %hbm_ref.2), custom_call_target="tpu_custom_call" | custom-call | bytes 50331648 | tf_op jit(solution)/shard_map/load_gate/pallas_call | solution.py:53
  18.5 8.3 %copy-done = bf16[6144,2048]{1,0:T(8,128)(2,1)} copy-done((bf16[6144,2048]{1,0:T(8,128)(2,1)}, bf16[6144,2048]{1,0:T(8,128)(2,1)S(1)}, u32[]{:S(2)}) %copy-start) | copy-done | bytes 25165848
  26.8 0.0 all-to-all-done.rows_ref
  26.8 8.2 %copy-done.1 = bf16[6144,2048]{1,0:T(8,128)(2,1)S(1)} copy-done((bf16[6144,2048]{1,0:T(8,128)(2,1)S(1)}, bf16[6144,2048]{1,0:T(8,128)(2,1)}, u32[]{:S(2)}) %copy-start.1) | copy-done | bytes 25165848
  35.0 9.0 %hidden.1.after_ref.refs_0_ = bf16[16,2048]{1,0:T(8,128)(2,1)S(1)} custom-call(bf16[16,2,3072]{2,1,0:T(2,128)(2,1)S(1)} %all-to-all-done.rows_ref, bf16[6144,2048]{1,0:T(8,128)(2,1)S(1)} %copy-done.1, bf16[1,6144,2048]{2,1,0:T(8,128)(2,1)} %w_up_hbm.1), custom_call_target="tpu_custom_call" | custom-call | tf_op jit(solution)/shard_map/hidden/pallas_call | solution.py:136
  44.0 2.0 %collective-permute-start = (bf16[16,2048]{1,0:T(8,128)(2,1)S(1)}, bf16[16,2048]{1,0:T(8,128)(2,1)S(1)}, u32[]{:S(2)}, u32[]{:S(2)}) collective-permute-start(bf16[16,2048]{1,0:T(8,128)(2,1)S(1)} %hidden.1.after_ref.refs_0_), channel_id=1, source_target_pairs={{0,1},{1,0},{2,3},{3,2},{4,5},{5,4},{6,7},{7,6},{8,9},{9,8},{10,11... | collective-permute-start | bytes 196616 | tf_op jit(solution)/shard_map/ppermute | solution.py:156
  46.0 1.5 %collective-permute-start.1 = (bf16[16,2048]{1,0:T(8,128)(2,1)S(1)}, bf16[16,2048]{1,0:T(8,128)(2,1)S(1)}, u32[]{:S(2)}, u32[]{:S(2)}) collective-permute-start(bf16[16,2048]{1,0:T(8,128)(2,1)S(1)} %hidden.1.after_ref.refs_0_), channel_id=1, source_target_pairs={{0,2},{1,3},{2,0},{3,1},{4,6},{5,7},{6,4},{7,5},{8,10},{9,11},{10,... | collective-permute-start | bytes 196616 | tf_op jit(solution)/shard_map/ppermute | solution.py:156
  47.5 0.1 collective-permute-start.2
  47.6 2.8 %collective-permute-start.3 = (bf16[16,2048]{1,0:T(8,128)(2,1)S(1)}, bf16[16,2048]{1,0:T(8,128)(2,1)S(1)}, u32[]{:S(2)}, u32[]{:S(2)}) collective-permute-start(bf16[16,2048]{1,0:T(8,128)(2,1)S(1)} %hidden.1.after_ref.refs_0_), channel_id=1, source_target_pairs={{0,4},{1,5},{2,6},{3,7},{4,0},{5,1},{6,2},{7,3},{8,12},{9,13},{10,... | collective-permute-start | bytes 196616 | tf_op jit(solution)/shard_map/ppermute | solution.py:156
  50.4 1.5 %collective-permute-start.4 = (bf16[16,2048]{1,0:T(8,128)(2,1)S(1)}, bf16[16,2048]{1,0:T(8,128)(2,1)S(1)}, u32[]{:S(2)}, u32[]{:S(2)}) collective-permute-start(bf16[16,2048]{1,0:T(8,128)(2,1)S(1)} %hidden.1.after_ref.refs_0_), channel_id=1, source_target_pairs={{0,5},{1,4},{2,7},{3,6},{4,1},{5,0},{6,3},{7,2},{8,13},{9,12},{10,... | collective-permute-start | bytes 196616 | tf_op jit(solution)/shard_map/ppermute | solution.py:156
  51.9 0.0 collective-permute-done.refs_1_
  51.9 3.3 %collective-permute-start.5 = (bf16[16,2048]{1,0:T(8,128)(2,1)S(1)}, bf16[16,2048]{1,0:T(8,128)(2,1)S(1)}, u32[]{:S(2)}, u32[]{:S(2)}) collective-permute-start(bf16[16,2048]{1,0:T(8,128)(2,1)S(1)} %hidden.1.after_ref.refs_0_), channel_id=1, source_target_pairs={{0,6},{1,7},{2,4},{3,5},{4,2},{5,3},{6,0},{7,1},{8,14},{9,15},{10,... | collective-permute-start | bytes 196616 | tf_op jit(solution)/shard_map/ppermute | solution.py:156
  55.1 0.0 collective-permute-done.1.refs_2_
  55.1 0.1 collective-permute-start.6
  55.2 8.3 %load_down.1.refs_8_ = bf16[768,16384]{1,0:T(8,128)(2,1)S(1)} custom-call(bf16[16,2048]{1,0:T(8,128)(2,1)S(1)} %hidden.1.after_ref.refs_0_, bf16[1,768,16384]{2,1,0:T(8,128)(2,1)} %hbm_ref.3), custom_call_target="tpu_custom_call" | custom-call | bytes 50331648 | tf_op jit(solution)/shard_map/load_down/pallas_call | solution.py:53
  63.5 0.0 copy-start.3
  63.6 0.0 copy-start.4
  63.6 0.0 collective-permute-done.2.refs_3_
  63.6 0.0 collective-permute-done.3.refs_4_
  63.6 0.0 collective-permute-done.4.refs_5_
  63.6 0.0 collective-permute-done.5.refs_6_
  63.6 0.0 collective-permute-done.6.refs_7_
  63.6 7.2 %down.1 = f32[16,2,768]{2,1,0:T(2,128)} custom-call(bf16[16,2048]{1,0:T(8,128)(2,1)S(1)} %hidden.1.after_ref.refs_0_, bf16[16,2048]{1,0:T(8,128)(2,1)S(1)} %collective-permute-done.refs_1_, bf16[16,2048]{1,0:T(8,128)(2,1)S(1)} %collective-permute-done.1.refs_2_, bf16[16,2048]{1,0:T(8,128)(2,1)S(1)} %collective-permute-done.2.refs_3_, ...), custom_call_target="tpu_custom_call" | custom-call | tf_op jit(solution)/shard_map/down/pallas_call | solution.py:157
  70.8 6.0 %all-to-all-start.1 = ((f32[16,2,768]{2,1,0:T(2,128)}), f32[16,2,768]{2,1,0:T(2,128)S(1)}, u32[]{:S(2)}, u32[]{:S(2)}) async-start(f32[16,2,768]{2,1,0:T(2,128)} %down.1), calls=%async_computation.1 | async-start | bytes 196608 | tf_op jit(solution)/shard_map/all_to_all | solution.py:171
  76.9 7.2 %all-to-all-done.1 = f32[16,2,768]{2,1,0:T(2,128)S(1)} async-done(((f32[16,2,768]{2,1,0:T(2,128)}), f32[16,2,768]{2,1,0:T(2,128)S(1)}, u32[]{:S(2)}, u32[]{:S(2)}) %all-to-all-start.1) | async-done | bytes 98336 | tf_op jit(solution)/shard_map/all_to_all | solution.py:171
  84.1 0.1 copy.12
  84.2 0.2 and_reduce_fusion.3
  84.6 0.7 add_convert_fusion
  (13 shorter events, 0.1 us)
Async XLA Ops:
  0.8 0.7 copy-start.2
  2.9 24.0 %all-to-all-start = ((bf16[16,2,3072]{2,1,0:T(2,128)(2,1)}), bf16[16,2,3072]{2,1,0:T(2,128)(2,1)S(1)}, u32[]{:S(2)}, u32[]{:S(2)}) async-start(bf16[16,2,3072]{2,1,0:T(2,128)(2,1)} %dispatch.1.after_ref), calls=%async_computation | async-start | bytes 393216 | tf_op jit(solution)/shard_map/all_to_all | solution.py:132
  18.5 8.3 %copy-start = (bf16[6144,2048]{1,0:T(8,128)(2,1)}, bf16[6144,2048]{1,0:T(8,128)(2,1)S(1)}, u32[]{:S(2)}) copy-start(bf16[6144,2048]{1,0:T(8,128)(2,1)S(1)} %load_gate.1.w_gate_ref) | copy-start | bytes 75497472
  26.8 8.2 %copy-start.1 = (bf16[6144,2048]{1,0:T(8,128)(2,1)S(1)}, bf16[6144,2048]{1,0:T(8,128)(2,1)}, u32[]{:S(2)}) copy-start(bf16[6144,2048]{1,0:T(8,128)(2,1)} %copy-done) | copy-start | bytes 75497472
  44.0 7.8 %collective-permute-start = (bf16[16,2048]{1,0:T(8,128)(2,1)S(1)}, bf16[16,2048]{1,0:T(8,128)(2,1)S(1)}, u32[]{:S(2)}, u32[]{:S(2)}) collective-permute-start(bf16[16,2048]{1,0:T(8,128)(2,1)S(1)} %hidden.1.after_ref.refs_0_), channel_id=1, source_target_pairs={{0,1},{1,0},{2,3},{3,2},{4,5},{5,4},{6,7},{7,6},{8,9},{9,8},{10,11... | collective-permute-start | bytes 196616 | tf_op jit(solution)/shard_map/ppermute | solution.py:156
  46.0 9.1 %collective-permute-start.1 = (bf16[16,2048]{1,0:T(8,128)(2,1)S(1)}, bf16[16,2048]{1,0:T(8,128)(2,1)S(1)}, u32[]{:S(2)}, u32[]{:S(2)}) collective-permute-start(bf16[16,2048]{1,0:T(8,128)(2,1)S(1)} %hidden.1.after_ref.refs_0_), channel_id=1, source_target_pairs={{0,2},{1,3},{2,0},{3,1},{4,6},{5,7},{6,4},{7,5},{8,10},{9,11},{10,... | collective-permute-start | bytes 196616 | tf_op jit(solution)/shard_map/ppermute | solution.py:156
  47.5 16.1 %collective-permute-start.2 = (bf16[16,2048]{1,0:T(8,128)(2,1)S(1)}, bf16[16,2048]{1,0:T(8,128)(2,1)S(1)}, u32[]{:S(2)}, u32[]{:S(2)}) collective-permute-start(bf16[16,2048]{1,0:T(8,128)(2,1)S(1)} %hidden.1.after_ref.refs_0_), channel_id=1, source_target_pairs={{0,3},{1,2},{2,1},{3,0},{4,7},{5,6},{6,5},{7,4},{8,11},{9,10},{10,... | collective-permute-start | bytes 196616 | tf_op jit(solution)/shard_map/ppermute | solution.py:156
  47.6 16.0 %collective-permute-start.3 = (bf16[16,2048]{1,0:T(8,128)(2,1)S(1)}, bf16[16,2048]{1,0:T(8,128)(2,1)S(1)}, u32[]{:S(2)}, u32[]{:S(2)}) collective-permute-start(bf16[16,2048]{1,0:T(8,128)(2,1)S(1)} %hidden.1.after_ref.refs_0_), channel_id=1, source_target_pairs={{0,4},{1,5},{2,6},{3,7},{4,0},{5,1},{6,2},{7,3},{8,12},{9,13},{10,... | collective-permute-start | bytes 196616 | tf_op jit(solution)/shard_map/ppermute | solution.py:156
  50.4 13.2 %collective-permute-start.4 = (bf16[16,2048]{1,0:T(8,128)(2,1)S(1)}, bf16[16,2048]{1,0:T(8,128)(2,1)S(1)}, u32[]{:S(2)}, u32[]{:S(2)}) collective-permute-start(bf16[16,2048]{1,0:T(8,128)(2,1)S(1)} %hidden.1.after_ref.refs_0_), channel_id=1, source_target_pairs={{0,5},{1,4},{2,7},{3,6},{4,1},{5,0},{6,3},{7,2},{8,13},{9,12},{10,... | collective-permute-start | bytes 196616 | tf_op jit(solution)/shard_map/ppermute | solution.py:156
  51.9 11.7 %collective-permute-start.5 = (bf16[16,2048]{1,0:T(8,128)(2,1)S(1)}, bf16[16,2048]{1,0:T(8,128)(2,1)S(1)}, u32[]{:S(2)}, u32[]{:S(2)}) collective-permute-start(bf16[16,2048]{1,0:T(8,128)(2,1)S(1)} %hidden.1.after_ref.refs_0_), channel_id=1, source_target_pairs={{0,6},{1,7},{2,4},{3,5},{4,2},{5,3},{6,0},{7,1},{8,14},{9,15},{10,... | collective-permute-start | bytes 196616 | tf_op jit(solution)/shard_map/ppermute | solution.py:156
  55.1 8.5 %collective-permute-start.6 = (bf16[16,2048]{1,0:T(8,128)(2,1)S(1)}, bf16[16,2048]{1,0:T(8,128)(2,1)S(1)}, u32[]{:S(2)}, u32[]{:S(2)}) collective-permute-start(bf16[16,2048]{1,0:T(8,128)(2,1)S(1)} %hidden.1.after_ref.refs_0_), channel_id=1, source_target_pairs={{0,7},{1,6},{2,5},{3,4},{4,3},{5,2},{6,1},{7,0},{8,15},{9,14},{10,... | collective-permute-start | bytes 196616 | tf_op jit(solution)/shard_map/ppermute | solution.py:156
  63.5 20.5 %copy-start.3 = (s32[4,2]{0,1:T(2,128)S(1)}, s32[4,2]{0,1:T(2,128)}, u32[]{:S(2)}) copy-start(s32[4,2]{0,1:T(2,128)} %param.7) | copy-start | bytes 100
  63.6 20.9 %copy-start.4 = (f32[4,2]{0,1:T(2,128)S(1)}, f32[4,2]{0,1:T(2,128)}, u32[]{:S(2)}) copy-start(f32[4,2]{0,1:T(2,128)} %param.8) | copy-start | bytes 100
  70.8 13.2 %all-to-all-start.1 = ((f32[16,2,768]{2,1,0:T(2,128)}), f32[16,2,768]{2,1,0:T(2,128)S(1)}, u32[]{:S(2)}, u32[]{:S(2)}) async-start(f32[16,2,768]{2,1,0:T(2,128)} %down.1), calls=%async_computation.1 | async-start | bytes 196608 | tf_op jit(solution)/shard_map/all_to_all | solution.py:171

commit v2 on v0

--- a/solution.py
+++ b/solution.py
@@ -1,10 +1,204 @@
+import functools
+
 import jax
 import jax.numpy as jnp
 from jax import lax
+from jax.experimental import pallas as pl
+from jax.experimental.pallas import tpu as pltpu
 from jax.sharding import PartitionSpec as P
 
-
-def local(tokens, routes, gates, w_gate, w_up, w_down):
+MIB = 1 << 20
+SLOTS = 2
+VMEM = pl.BlockSpec(memory_space=pltpu.VMEM)
+SMEM = pl.BlockSpec(memory_space=pltpu.SMEM)
+
+
+def load_kernel(after_ref, hbm_ref, vmem_ref, sems):
+    parts = sems.shape[0]
+    rows = hbm_ref.shape[1] // parts
+    copies = []
+    for i in range(parts):
+        part = pl.ds(i * rows, rows)
+        copies.append(pltpu.make_async_copy(hbm_ref.at[:, part], vmem_ref.at[:, part], sems.at[i]))
+        copies[-1].start()
+    for copy in copies:
+        copy.wait()
+
+
+def load(w, after, name):
+    parts = 6
+    return pl.pallas_call(
+        load_kernel,
+        out_shape=pltpu.VMEM(w.shape, w.dtype),
+        in_specs=[pl.BlockSpec(memory_space=pl.ANY)] * 2,
+        out_specs=VMEM,
+        scratch_shapes=[pltpu.SemaphoreType.DMA((parts,))],
+        compiler_params=pltpu.CompilerParams(vmem_limit_bytes=MIB),
+        cost_estimate=pl.CostEstimate(flops=0, bytes_accessed=2 * w.size * 2, transcendentals=0),
+        name=name,
+    )(after, pltpu.with_memory_space_constraint(w, pltpu.HBM))
+
+
+def call(kernel, name, out, in_specs, limit, seconds=0.0, scratch=()):
+    return pl.pallas_call(
+        kernel,
+        out_shape=out,
+        in_specs=in_specs,
+        out_specs=jax.tree.map(lambda _: VMEM, out),
+        scratch_shapes=scratch,
+        compiler_params=pltpu.CompilerParams(vmem_limit_bytes=limit),
+        cost_estimate=pl.CostEstimate(flops=int(seconds*1e15), bytes_accessed=0, transcendentals=0),
+        name=name,
+    )
+
+
+def slot_rows(routes_ref, e, rows):
+    taken = jnp.int32(0)
+    found = []
+    for r in range(rows):
+        named = jnp.logical_or(routes_ref[0, r] == e, routes_ref[1, r] == e)
+        found.append((named, taken))
+        taken = taken + named.astype(jnp.int32)
+    return found
+
+
+def dispatch_kernel(tokens_ref, routes_ref, sends_ref):
+    tokens = tokens_ref[...].astype(jnp.float32)
+    rows = tokens.shape[0]
+    blocks = []
+    for e in range(sends_ref.shape[0] // SLOTS):
+        found = slot_rows(routes_ref, e, rows)
+        for c in range(SLOTS):
+            row = jnp.zeros((1, tokens.shape[1]), jnp.float32)
+            for r, (named, slot) in enumerate(found):
+                here = jnp.logical_and(named, slot == c).astype(jnp.float32)
+                row = row + here * tokens[r:r + 1, :]
+            blocks.append(row)
+    sends_ref[...] = jnp.concatenate(blocks, axis=0).astype(jnp.bfloat16)
+
+
+def merge_kernel(*refs):
+    *blocks, own_ref, other_ref, own_f32, other_f32 = refs
+    me, mine = lax.axis_index("tile"), lax.axis_index("expert")
+    for k, block in enumerate(blocks):
+        rows = block[...].astype(jnp.float32)
+        first, second = rows[:SLOTS], rows[SLOTS:]
+        own_f32[me ^ k] = jnp.where(mine == 0, first, second)
+        other_f32[me ^ k] = jnp.where(mine == 0, second, first)
+    own_ref[...] = own_f32[...].reshape(own_ref.shape).astype(jnp.bfloat16)
+    other_ref[...] = other_f32[...].reshape(other_ref.shape).astype(jnp.bfloat16)
+
+
+def project_kernel(own_ref, other_ref, w_gate_ref, w_up_hbm, gate_ref, up_ref, ring, sems):
+    mine = lax.axis_index("expert")
+    half = own_ref.shape[1]
+    depth, chunk = ring.shape[0], ring.shape[1]
+    steps = 2 * half // chunk
+
+    def first_row(i):
+        part, k = divmod(i * chunk, half)
+        return pl.multiple_of((mine if part == 0 else 1 - mine) * half + k, chunk)
+
+    def copy(i):
+        return pltpu.make_async_copy(
+            w_up_hbm.at[0, pl.ds(first_row(i), chunk)], ring.at[i % depth], sems.at[i % depth])
+
+    for i in range(depth):
+        copy(i).start()
+    for i in range(steps):
+        part, k = divmod(i * chunk, half)
+        x = (own_ref if part == 0 else other_ref)[:, k:k + chunk]
+        gate = jnp.dot(x, w_gate_ref[0, pl.ds(first_row(i), chunk), :], preferred_element_type=jnp.float32)
+        copy(i).wait()
+        up = jnp.dot(x, ring[i % depth], preferred_element_type=jnp.float32)
+        if i + depth < steps:
+            copy(i + depth).start()
+        gate_ref[...] = gate if i == 0 else gate_ref[...] + gate
+        up_ref[...] = up if i == 0 else up_ref[...] + up
+
+
+def activate_kernel(gate_ref, up_ref, hidden_ref):
+    gate = gate_ref[...]
+    hidden_ref[...] = (gate / (1.0 + jnp.exp(-gate)) * up_ref[...]).astype(jnp.bfloat16)
+
+
+def down_kernel(n, *refs):
+    blocks, w_ref, sends_ref = refs[:n], refs[n], refs[n + 1]
+    me = lax.axis_index("tile")
+    width = blocks[0].shape[1]
+    total = jnp.zeros((w_ref.shape[1], blocks[0].shape[0]), jnp.float32)
+    for k in range(n):
+        columns = pl.ds(pl.multiple_of((me ^ k) * width, width), width)
+        total += lax.dot_general(
+            w_ref[0, :, columns], blocks[k][...], (((1,), (1,)), ((), ())),
+            preferred_element_type=jnp.float32,
+        )
+    total = total.T
+    for t in range(sends_ref.shape[0]):
+        sends_ref[t] = total[t * SLOTS:(t + 1) * SLOTS, :]
+
+
+def combine_kernel(own_ref, other_ref, routes_ref, gates_ref, out_ref):
+    mine = lax.axis_index("expert")
+    tiles, _, features = own_ref.shape
+    halves = tiles // 2
+    rows = out_ref.shape[0]
+    found = [slot_rows(routes_ref, e, rows) for e in range(2)]
+    weight = [[
+        jnp.where(routes_ref[0, r] == e, gates_ref[0, r], 0.0)
+        + jnp.where(routes_ref[1, r] == e, gates_ref[1, r], 0.0)
+        for r in range(rows)
+    ] for e in range(2)]
+    for i in range(halves):
+        own, other = own_ref[mine * halves + i], other_ref[mine * halves + i]
+        lines = []
+        for r in range(rows):
+            line = jnp.zeros((1, features), jnp.float32)
+            for e in range(2):
+                named, slot = found[e][r]
+                both = jnp.where(mine == e, own, other)
+                value = jnp.where(slot == 0, both[0:1], both[1:2])
+                value = (weight[e][r] * value).astype(jnp.bfloat16).astype(jnp.float32)
+                line = line + jnp.where(named, value, 0.0)
+            lines.append(line)
+        out_ref[:, i * features:(i + 1) * features] = jnp.concatenate(lines, axis=0).astype(jnp.bfloat16)
+
+
+def local_direct(tokens, routes, gates, w_gate, w_up, w_down):
+    tiles = lax.axis_size("tile")
+    rows, half_width = tokens.shape
+    width, features = w_gate.shape[2], w_down.shape[1]
+    slots = tiles * SLOTS
+    routes, gates = routes.T, gates.T
+
+    def to_tiles(x):
+        return [x] + [lax.ppermute(x, "tile", [(t, t ^ k) for t in range(tiles)]) for k in range(1, tiles)]
+
+    def to_core(x):
+        return lax.ppermute(x, "expert", [(0, 1), (1, 0)])
+
+    f32 = lambda *shape: jax.ShapeDtypeStruct(shape, jnp.float32)
+    bf16 = lambda *shape: jax.ShapeDtypeStruct(shape, jnp.bfloat16)
+    sends = call(dispatch_kernel, "dispatch", bf16(2 * SLOTS, half_width), [VMEM, SMEM], 16 * MIB, 0)(tokens, routes)
+    own, other = call(
+        merge_kernel, "merge", (bf16(slots, half_width),) * 2, [VMEM] * tiles, 16 * MIB, 0e-6,
+        [pltpu.VMEM((tiles, SLOTS, half_width), jnp.float32)] * 2,
+    )(*to_tiles(sends))
+    other = to_core(other)
+    chunk, depth = half_width // 4, 3
+    gate, up = call(
+        project_kernel, "project", (f32(slots, width),) * 2, [VMEM, VMEM, VMEM, pl.BlockSpec(memory_space=pl.ANY)], 20 * MIB, 0,
+        [pltpu.VMEM((depth, chunk, width), jnp.bfloat16), pltpu.SemaphoreType.DMA((depth,))],
+    )(own, other, load(w_gate, sends, "load_gate"), pltpu.with_memory_space_constraint(w_up, pltpu.HBM))
+    hidden = call(activate_kernel, "activate", bf16(slots, width), [VMEM, VMEM], 16 * MIB, 0)(gate, up)
+    result = call(functools.partial(down_kernel, tiles), "down", f32(tiles, SLOTS, features), [VMEM] * (tiles + 1), 16 * MIB, 0e-6)(
+        *to_tiles(hidden), load(w_down, hidden, "load_down"))
+    back = lax.all_to_all(result, "tile", split_axis=0, concat_axis=0, tiled=True)
+    return call(combine_kernel, "combine", bf16(rows, half_width), [VMEM, VMEM, SMEM, SMEM], 16 * MIB)(
+        back, to_core(back), routes, gates)
+
+
+def local_gathered(tokens, routes, gates, w_gate, w_up, w_down):
     experts = lax.axis_size("expert")
     tile_count = lax.axis_size("tile")
     own_expert = lax.axis_index("expert")
@@ -58,4 +252,5 @@
         P("expert", "tile", None),
     )
     out_specs = P(("group", "tile"), "expert")
+    local = local_direct if mesh.shape["tile"] <= 8 else local_gathered
     return jax.shard_map(local, mesh=mesh, in_specs=in_specs, out_specs=out_specs, check_vma=False)

time: 116 us -> 77.1 us (0.66)
  blocking collectives: 71.6 us -> 11.5 us
  Pallas kernels: 0 us -> 34.5 us
  matrix products: 32.4 us -> 0 us
  starting transfers between devices: 3.34 us -> 23.7 us
    all_gather x2 -> x0, blocking collectives: 67.9 us -> none  [the longest x1 36.6 us: local(): lax.all_gather(outgoing[None], ('expert', 'tile'), axis=0, tiled=True)]
    pallas_call x0 -> x8, Pallas kernels: none -> 34.5 us  [the longest x2 16.6 us: load(): pl.pallas_call(load_kernel, out_shape=pltpu.VMEM(w.shape, w.dtype), in_sp...]
    dot_general x6 -> x0, matrix products: 32.4 us -> none  [the longest x1 11.5 us: local(): lax.dot_general(columns, lax.all_gather(hidden, 'tile', axis=1, tiled=Tru...]
    ppermute x0 -> x16, starting transfers between devices: none -> 23.7 us  [the longest x14 23.6 us: to_tiles(): lax.ppermute(x, 'tile', [(t, t ^ k) for t in range(tiles)])]
    all_to_all x1, blocking collectives: 3.76 us -> 11.5 us  [local_direct(): lax.all_to_all(result, 'tile', split_axis=0, concat_axis=0, tiled=True)]
    all_to_all x1 -> x0, waiting for transfers between devices: 6.58 us -> none  [local(): lax.all_to_all(summed, 'tile', split_axis=1, concat_axis=0, tiled=True)]
    ppermute x0 -> x16, waiting for transfers between devices: none -> 5.6 us  [the longest x14 4.37 us: to_tiles(): lax.ppermute(x, 'tile', [(t, t ^ k) for t in range(tiles)])]
    all_to_all x1 -> x0, starting transfers between devices: 3.34 us -> none  [local(): lax.all_to_all(summed, 'tile', split_axis=1, concat_axis=0, tiled=True)]
  transfers between devices with their start and end apart: 1 -> 16, of which waited for: 1 -> 5; matrix products, arithmetic and copies ran while one was open for 0% -> 0% of each run, Pallas kernels for 0% -> 22%
where the time goes in v2:
time: 77.1 us; the launch traced here: 76.8 us
  Pallas kernels  34.5 us (45%)
  starting transfers between devices  23.7 us (31%)
  blocking collectives  11.5 us (15%)
  waiting for transfers between devices  5.6 us (7%)
  local copies, waits for them, and re-layouts  1.43 us (2%)
    ppermute x14, starting transfers between devices, to_tiles(): lax.ppermute(x, 'tile', [(t, t ^ k) for t in range(tiles)])  23.6 us
    pallas_call x2, Pallas kernels, load(): pl.pallas_call(load_kernel, out_shape=pltpu.VMEM(w.shape, w.dtype), in_sp...  16.6 us
    all_to_all x1, blocking collectives, local_direct(): lax.all_to_all(result, 'tile', split_axis=0, concat_axis=0, tiled=True)  11.5 us
    pallas_call x1, Pallas kernels, local_direct(): call(project_kernel, 'project', (f32(slots, width),) * 2, [VMEM, VMEM, VM...  9.05 us
    pallas_call x1, Pallas kernels, local_direct(): call(functools.partial(down_kernel, tiles), 'down', f32(tiles, SLOTS, fea...  6.66 us
    ppermute x14, waiting for transfers between devices, to_tiles(): lax.ppermute(x, 'tile', [(t, t ^ k) for t in range(tiles)])  4.37 us
  transfers between devices with their start and end apart: 16, of which 5 were waited for; matrix products, arithmetic and copies ran while one was open for 0% of the time, Pallas kernels for 22%

profile of v2, /device:TPU:0, one launch (start us, length us, event | category | flops | bytes accessed | tf_op | source)
XLA Modules:
  0.0 76.8 jit_solution(16218248486545065951)
XLA Ops:
  0.0 0.7 copy-done
  0.7 0.7 copy-done.1
  1.4 0.7 dispatch.1.refs_0_.after_ref
  2.1 6.0 %collective-permute-start.6 = (bf16[4,3072]{1,0:T(4,128)(2,1)S(1)}, bf16[4,3072]{1,0:T(4,128)(2,1)S(1)}, u32[]{:S(2)}, u32[]{:S(2)}) collective-permute-start(bf16[4,3072]{1,0:T(4,128)(2,1)S(1)} %dispatch.1.refs_0_.after_ref), channel_id=1, source_target_pairs={{0,7},{1,6},{2,5},{3,4},{4,3},{5,2},{6,1},{7,0},{8,15},{9,14},{10,... | collective-permute-start | bytes 73736 | tf_op jit(solution)/shard_map/ppermute | solution.py:175
  8.1 0.2 collective-permute-start.5
  8.3 0.8 collective-permute-start.4
  9.1 2.0 %collective-permute-start.3 = (bf16[4,3072]{1,0:T(4,128)(2,1)S(1)}, bf16[4,3072]{1,0:T(4,128)(2,1)S(1)}, u32[]{:S(2)}, u32[]{:S(2)}) collective-permute-start(bf16[4,3072]{1,0:T(4,128)(2,1)S(1)} %dispatch.1.refs_0_.after_ref), channel_id=1, source_target_pairs={{0,4},{1,5},{2,6},{3,7},{4,0},{5,1},{6,2},{7,3},{8,12},{9,13},{10,... | collective-permute-start | bytes 73736 | tf_op jit(solution)/shard_map/ppermute | solution.py:175
  11.1 2.3 %collective-permute-start.2 = (bf16[4,3072]{1,0:T(4,128)(2,1)S(1)}, bf16[4,3072]{1,0:T(4,128)(2,1)S(1)}, u32[]{:S(2)}, u32[]{:S(2)}) collective-permute-start(bf16[4,3072]{1,0:T(4,128)(2,1)S(1)} %dispatch.1.refs_0_.after_ref), channel_id=1, source_target_pairs={{0,3},{1,2},{2,1},{3,0},{4,7},{5,6},{6,5},{7,4},{8,11},{9,10},{10,... | collective-permute-start | bytes 73736 | tf_op jit(solution)/shard_map/ppermute | solution.py:175
  13.4 0.8 %collective-permute-start.1 = (bf16[4,3072]{1,0:T(4,128)(2,1)S(1)}, bf16[4,3072]{1,0:T(4,128)(2,1)S(1)}, u32[]{:S(2)}, u32[]{:S(2)}) collective-permute-start(bf16[4,3072]{1,0:T(4,128)(2,1)S(1)} %dispatch.1.refs_0_.after_ref), channel_id=1, source_target_pairs={{0,2},{1,3},{2,0},{3,1},{4,6},{5,7},{6,4},{7,5},{8,10},{9,11},{10,... | collective-permute-start | bytes 73736 | tf_op jit(solution)/shard_map/ppermute | solution.py:175
  14.2 0.4 collective-permute-start
  14.6 1.2 %collective-permute-done.2.refs_3_ = bf16[4,3072]{1,0:T(4,128)(2,1)S(1)} collective-permute-done((bf16[4,3072]{1,0:T(4,128)(2,1)S(1)}, bf16[4,3072]{1,0:T(4,128)(2,1)S(1)}, u32[]{:S(2)}, u32[]{:S(2)}) %collective-permute-start.2) | collective-permute-done | bytes 24608 | tf_op jit(solution)/shard_map/ppermute | solution.py:175
  15.9 1.4 %collective-permute-done.1.refs_2_ = bf16[4,3072]{1,0:T(4,128)(2,1)S(1)} collective-permute-done((bf16[4,3072]{1,0:T(4,128)(2,1)S(1)}, bf16[4,3072]{1,0:T(4,128)(2,1)S(1)}, u32[]{:S(2)}, u32[]{:S(2)}) %collective-permute-start.1) | collective-permute-done | bytes 24608 | tf_op jit(solution)/shard_map/ppermute | solution.py:175
  17.2 0.8 %collective-permute-done.refs_1_ = bf16[4,3072]{1,0:T(4,128)(2,1)S(1)} collective-permute-done((bf16[4,3072]{1,0:T(4,128)(2,1)S(1)}, bf16[4,3072]{1,0:T(4,128)(2,1)S(1)}, u32[]{:S(2)}, u32[]{:S(2)}) %collective-permute-start) | collective-permute-done | bytes 24608 | tf_op jit(solution)/shard_map/ppermute | solution.py:175
  18.0 0.1 merge.1
  18.2 0.1 collective-permute-start.7
  18.3 8.3 %load_gate.1.w_gate_ref = bf16[1,6144,2048]{2,1,0:T(8,128)(2,1)S(1)} custom-call(bf16[4,3072]{1,0:T(4,128)(2,1)S(1)} %dispatch.1.refs_0_.after_ref, bf16[1,6144,2048]{2,1,0:T(8,128)(2,1)} %hbm_ref.2), custom_call_target="tpu_custom_call" | custom-call | bytes 50331648 | tf_op jit(solution)/shard_map/load_gate/pallas_call | solution.py:30
  26.6 9.0 %project.1 = (f32[16,2048]{1,0:T(8,128)S(1)}, f32[16,2048]{1,0:T(8,128)S(1)}) custom-call(bf16[16,3072]{1,0:T(8,128)(2,1)S(1)} %get-tuple-element.9.own_ref, bf16[16,3072]{1,0:T(8,128)(2,1)S(1)} %collective-permute-done.7.other_ref, bf16[1,6144,2048]{2,1,0:T(8,128)(2,1)S(1)} %load_gate.1.w_gate_ref, bf16[1,6144,2048]{2,1,0:T(8,128)(2,1)} %w_up_hbm.1), custom_call_target="tpu_custom_call" | custom-call | tf_op jit(solution)/shard_map/project/pallas_call | solution.py:189
  35.7 3.6 %collective-permute-start.14 = (bf16[16,2048]{1,0:T(8,128)(2,1)S(1)}, bf16[16,2048]{1,0:T(8,128)(2,1)S(1)}, u32[]{:S(2)}, u32[]{:S(2)}) collective-permute-start(bf16[16,2048]{1,0:T(8,128)(2,1)S(1)} %activate.1.after_ref.refs_0_), channel_id=1, source_target_pairs={{0,7},{1,6},{2,5},{3,4},{4,3},{5,2},{6,1},{7,0},{8,15},{9,14},{10,... | collective-permute-start | bytes 196616 | tf_op jit(solution)/shard_map/ppermute | solution.py:175
  39.3 0.1 collective-permute-start.13
  39.4 1.5 %collective-permute-start.12 = (bf16[16,2048]{1,0:T(8,128)(2,1)S(1)}, bf16[16,2048]{1,0:T(8,128)(2,1)S(1)}, u32[]{:S(2)}, u32[]{:S(2)}) collective-permute-start(bf16[16,2048]{1,0:T(8,128)(2,1)S(1)} %activate.1.after_ref.refs_0_), channel_id=1, source_target_pairs={{0,5},{1,4},{2,7},{3,6},{4,1},{5,0},{6,3},{7,2},{8,13},{9,12},{10,... | collective-permute-start | bytes 196616 | tf_op jit(solution)/shard_map/ppermute | solution.py:175
  40.9 2.5 %collective-permute-start.11 = (bf16[16,2048]{1,0:T(8,128)(2,1)S(1)}, bf16[16,2048]{1,0:T(8,128)(2,1)S(1)}, u32[]{:S(2)}, u32[]{:S(2)}) collective-permute-start(bf16[16,2048]{1,0:T(8,128)(2,1)S(1)} %activate.1.after_ref.refs_0_), channel_id=1, source_target_pairs={{0,4},{1,5},{2,6},{3,7},{4,0},{5,1},{6,2},{7,3},{8,12},{9,13},{10,... | collective-permute-start | bytes 196616 | tf_op jit(solution)/shard_map/ppermute | solution.py:175
  43.4 1.2 %collective-permute-start.10 = (bf16[16,2048]{1,0:T(8,128)(2,1)S(1)}, bf16[16,2048]{1,0:T(8,128)(2,1)S(1)}, u32[]{:S(2)}, u32[]{:S(2)}) collective-permute-start(bf16[16,2048]{1,0:T(8,128)(2,1)S(1)} %activate.1.after_ref.refs_0_), channel_id=1, source_target_pairs={{0,3},{1,2},{2,1},{3,0},{4,7},{5,6},{6,5},{7,4},{8,11},{9,10},{10,... | collective-permute-start | bytes 196616 | tf_op jit(solution)/shard_map/ppermute | solution.py:175
  44.6 0.6 collective-permute-start.9
  45.3 0.9 %collective-permute-done.13.refs_6_ = bf16[16,2048]{1,0:T(8,128)(2,1)S(1)} collective-permute-done((bf16[16,2048]{1,0:T(8,128)(2,1)S(1)}, bf16[16,2048]{1,0:T(8,128)(2,1)S(1)}, u32[]{:S(2)}, u32[]{:S(2)}) %collective-permute-start.13) | collective-permute-done | bytes 65568 | tf_op jit(solution)/shard_map/ppermute | solution.py:175
  46.2 1.5 %collective-permute-start.8 = (bf16[16,2048]{1,0:T(8,128)(2,1)S(1)}, bf16[16,2048]{1,0:T(8,128)(2,1)S(1)}, u32[]{:S(2)}, u32[]{:S(2)}) collective-permute-start(bf16[16,2048]{1,0:T(8,128)(2,1)S(1)} %activate.1.after_ref.refs_0_), channel_id=1, source_target_pairs={{0,1},{1,0},{2,3},{3,2},{4,5},{5,4},{6,7},{7,6},{8,9},{9,8},{10,11... | collective-permute-start | bytes 196616 | tf_op jit(solution)/shard_map/ppermute | solution.py:175
  47.7 8.3 %load_down.1.refs_8_ = bf16[1,768,16384]{2,1,0:T(8,128)(2,1)S(1)} custom-call(bf16[16,2048]{1,0:T(8,128)(2,1)S(1)} %activate.1.after_ref.refs_0_, bf16[1,768,16384]{2,1,0:T(8,128)(2,1)} %hbm_ref.3), custom_call_target="tpu_custom_call" | custom-call | bytes 50331648 | tf_op jit(solution)/shard_map/load_down/pallas_call | solution.py:30
  56.0 0.0 copy-start.2
  56.0 0.0 copy-start.3
  56.1 6.7 %down.1 = f32[8,2,768]{2,1,0:T(2,128)S(1)} custom-call(bf16[16,2048]{1,0:T(8,128)(2,1)S(1)} %activate.1.after_ref.refs_0_, bf16[16,2048]{1,0:T(8,128)(2,1)S(1)} %collective-permute-done.8.refs_1_, bf16[16,2048]{1,0:T(8,128)(2,1)S(1)} %collective-permute-done.9.refs_2_, bf16[16,2048]{1,0:T(8,128)(2,1)S(1)} %collective-permute-done.10.refs_3_, ...), custom_call_target="tpu_custom_call" | custom-call | tf_op jit(solution)/shard_map/down/pallas_call | solution.py:194
  62.8 11.5 %all_to_all.5.own_ref = f32[8,2,768]{2,1,0:T(2,128)S(1)} all-to-all(f32[8,2,768]{2,1,0:T(2,128)S(1)} %down.1), channel_id=1, replica_groups=mesh['group'=2,'expert'=2,'tile'=8] {'tile'}, dimensions={0} | all-to-all | bytes 98304 | tf_op jit(solution)/shard_map/all_to_all | solution.py:196
  74.2 1.2 %collective-permute-done.15.other_ref = f32[8,2,768]{2,1,0:T(2,128)S(1)} collective-permute-done((f32[8,2,768]{2,1,0:T(2,128)S(1)}, f32[8,2,768]{2,1,0:T(2,128)S(1)}, u32[]{:S(2)}, u32[]{:S(2)}) %collective-permute-start.15) | collective-permute-done | bytes 49184 | tf_op jit(solution)/shard_map/ppermute | solution.py:178
  75.5 1.4 %combine.1 = bf16[4,3072]{1,0:T(4,128)(2,1)} custom-call(f32[8,2,768]{2,1,0:T(2,128)S(1)} %all_to_all.5.own_ref, f32[8,2,768]{2,1,0:T(2,128)S(1)} %collective-permute-done.15.other_ref, s32[2,4]{1,0:T(2,128)S(1)} %bitcast.3, f32[2,4]{1,0:T(2,128)S(1)} %bitcast.4), custom_call_target="tpu_custom_call" | custom-call | tf_op jit(solution)/shard_map/combine/pallas_call | solution.py:197
  (17 shorter events, 0.1 us)
Async XLA Ops:
  0.0 0.7 copy-start
  0.7 0.7 copy-start.1
  2.1 11.3 %collective-permute-start.6 = (bf16[4,3072]{1,0:T(4,128)(2,1)S(1)}, bf16[4,3072]{1,0:T(4,128)(2,1)S(1)}, u32[]{:S(2)}, u32[]{:S(2)}) collective-permute-start(bf16[4,3072]{1,0:T(4,128)(2,1)S(1)} %dispatch.1.refs_0_.after_ref), channel_id=1, source_target_pairs={{0,7},{1,6},{2,5},{3,4},{4,3},{5,2},{6,1},{7,0},{8,15},{9,14},{10,... | collective-permute-start | bytes 73736 | tf_op jit(solution)/shard_map/ppermute | solution.py:175
  8.1 6.1 %collective-permute-start.5 = (bf16[4,3072]{1,0:T(4,128)(2,1)S(1)}, bf16[4,3072]{1,0:T(4,128)(2,1)S(1)}, u32[]{:S(2)}, u32[]{:S(2)}) collective-permute-start(bf16[4,3072]{1,0:T(4,128)(2,1)S(1)} %dispatch.1.refs_0_.after_ref), channel_id=1, source_target_pairs={{0,6},{1,7},{2,4},{3,5},{4,2},{5,3},{6,0},{7,1},{8,14},{9,15},{10,... | collective-permute-start | bytes 73736 | tf_op jit(solution)/shard_map/ppermute | solution.py:175
  8.3 6.3 %collective-permute-start.4 = (bf16[4,3072]{1,0:T(4,128)(2,1)S(1)}, bf16[4,3072]{1,0:T(4,128)(2,1)S(1)}, u32[]{:S(2)}, u32[]{:S(2)}) collective-permute-start(bf16[4,3072]{1,0:T(4,128)(2,1)S(1)} %dispatch.1.refs_0_.after_ref), channel_id=1, source_target_pairs={{0,5},{1,4},{2,7},{3,6},{4,1},{5,0},{6,3},{7,2},{8,13},{9,12},{10,... | collective-permute-start | bytes 73736 | tf_op jit(solution)/shard_map/ppermute | solution.py:175
  9.1 5.5 %collective-permute-start.3 = (bf16[4,3072]{1,0:T(4,128)(2,1)S(1)}, bf16[4,3072]{1,0:T(4,128)(2,1)S(1)}, u32[]{:S(2)}, u32[]{:S(2)}) collective-permute-start(bf16[4,3072]{1,0:T(4,128)(2,1)S(1)} %dispatch.1.refs_0_.after_ref), channel_id=1, source_target_pairs={{0,4},{1,5},{2,6},{3,7},{4,0},{5,1},{6,2},{7,3},{8,12},{9,13},{10,... | collective-permute-start | bytes 73736 | tf_op jit(solution)/shard_map/ppermute | solution.py:175
  11.1 4.7 %collective-permute-start.2 = (bf16[4,3072]{1,0:T(4,128)(2,1)S(1)}, bf16[4,3072]{1,0:T(4,128)(2,1)S(1)}, u32[]{:S(2)}, u32[]{:S(2)}) collective-permute-start(bf16[4,3072]{1,0:T(4,128)(2,1)S(1)} %dispatch.1.refs_0_.after_ref), channel_id=1, source_target_pairs={{0,3},{1,2},{2,1},{3,0},{4,7},{5,6},{6,5},{7,4},{8,11},{9,10},{10,... | collective-permute-start | bytes 73736 | tf_op jit(solution)/shard_map/ppermute | solution.py:175
  13.4 3.8 %collective-permute-start.1 = (bf16[4,3072]{1,0:T(4,128)(2,1)S(1)}, bf16[4,3072]{1,0:T(4,128)(2,1)S(1)}, u32[]{:S(2)}, u32[]{:S(2)}) collective-permute-start(bf16[4,3072]{1,0:T(4,128)(2,1)S(1)} %dispatch.1.refs_0_.after_ref), channel_id=1, source_target_pairs={{0,2},{1,3},{2,0},{3,1},{4,6},{5,7},{6,4},{7,5},{8,10},{9,11},{10,... | collective-permute-start | bytes 73736 | tf_op jit(solution)/shard_map/ppermute | solution.py:175
  14.2 3.8 %collective-permute-start = (bf16[4,3072]{1,0:T(4,128)(2,1)S(1)}, bf16[4,3072]{1,0:T(4,128)(2,1)S(1)}, u32[]{:S(2)}, u32[]{:S(2)}) collective-permute-start(bf16[4,3072]{1,0:T(4,128)(2,1)S(1)} %dispatch.1.refs_0_.after_ref), channel_id=1, source_target_pairs={{0,1},{1,0},{2,3},{3,2},{4,5},{5,4},{6,7},{7,6},{8,9},{9,8},{10,11... | collective-permute-start | bytes 73736 | tf_op jit(solution)/shard_map/ppermute | solution.py:175
  18.2 8.4 %collective-permute-start.7 = (bf16[16,3072]{1,0:T(8,128)(2,1)S(1)}, bf16[16,3072]{1,0:T(8,128)(2,1)S(1)}, u32[]{:S(2)}, u32[]{:S(2)}) collective-permute-start(bf16[16,3072]{1,0:T(8,128)(2,1)S(1)} %get-tuple-element.10), channel_id=1, source_target_pairs={{0,8},{8,0},{1,9},{9,1},{2,10},{10,2},{3,11},{11,3},{4,12},{12,4},... | collective-permute-start | bytes 294920 | tf_op jit(solution)/shard_map/ppermute | solution.py:178
  35.7 9.0 %collective-permute-start.14 = (bf16[16,2048]{1,0:T(8,128)(2,1)S(1)}, bf16[16,2048]{1,0:T(8,128)(2,1)S(1)}, u32[]{:S(2)}, u32[]{:S(2)}) collective-permute-start(bf16[16,2048]{1,0:T(8,128)(2,1)S(1)} %activate.1.after_ref.refs_0_), channel_id=1, source_target_pairs={{0,7},{1,6},{2,5},{3,4},{4,3},{5,2},{6,1},{7,0},{8,15},{9,14},{10,... | collective-permute-start | bytes 196616 | tf_op jit(solution)/shard_map/ppermute | solution.py:175
  39.3 6.9 %collective-permute-start.13 = (bf16[16,2048]{1,0:T(8,128)(2,1)S(1)}, bf16[16,2048]{1,0:T(8,128)(2,1)S(1)}, u32[]{:S(2)}, u32[]{:S(2)}) collective-permute-start(bf16[16,2048]{1,0:T(8,128)(2,1)S(1)} %activate.1.after_ref.refs_0_), channel_id=1, source_target_pairs={{0,6},{1,7},{2,4},{3,5},{4,2},{5,3},{6,0},{7,1},{8,14},{9,15},{10,... | collective-permute-start | bytes 196616 | tf_op jit(solution)/shard_map/ppermute | solution.py:175
  39.4 16.6 %collective-permute-start.12 = (bf16[16,2048]{1,0:T(8,128)(2,1)S(1)}, bf16[16,2048]{1,0:T(8,128)(2,1)S(1)}, u32[]{:S(2)}, u32[]{:S(2)}) collective-permute-start(bf16[16,2048]{1,0:T(8,128)(2,1)S(1)} %activate.1.after_ref.refs_0_), channel_id=1, source_target_pairs={{0,5},{1,4},{2,7},{3,6},{4,1},{5,0},{6,3},{7,2},{8,13},{9,12},{10,... | collective-permute-start | bytes 196616 | tf_op jit(solution)/shard_map/ppermute | solution.py:175
  40.9 15.2 %collective-permute-start.11 = (bf16[16,2048]{1,0:T(8,128)(2,1)S(1)}, bf16[16,2048]{1,0:T(8,128)(2,1)S(1)}, u32[]{:S(2)}, u32[]{:S(2)}) collective-permute-start(bf16[16,2048]{1,0:T(8,128)(2,1)S(1)} %activate.1.after_ref.refs_0_), channel_id=1, source_target_pairs={{0,4},{1,5},{2,6},{3,7},{4,0},{5,1},{6,2},{7,3},{8,12},{9,13},{10,... | collective-permute-start | bytes 196616 | tf_op jit(solution)/shard_map/ppermute | solution.py:175
  43.4 12.7 %collective-permute-start.10 = (bf16[16,2048]{1,0:T(8,128)(2,1)S(1)}, bf16[16,2048]{1,0:T(8,128)(2,1)S(1)}, u32[]{:S(2)}, u32[]{:S(2)}) collective-permute-start(bf16[16,2048]{1,0:T(8,128)(2,1)S(1)} %activate.1.after_ref.refs_0_), channel_id=1, source_target_pairs={{0,3},{1,2},{2,1},{3,0},{4,7},{5,6},{6,5},{7,4},{8,11},{9,10},{10,... | collective-permute-start | bytes 196616 | tf_op jit(solution)/shard_map/ppermute | solution.py:175
  44.6 11.4 %collective-permute-start.9 = (bf16[16,2048]{1,0:T(8,128)(2,1)S(1)}, bf16[16,2048]{1,0:T(8,128)(2,1)S(1)}, u32[]{:S(2)}, u32[]{:S(2)}) collective-permute-start(bf16[16,2048]{1,0:T(8,128)(2,1)S(1)} %activate.1.after_ref.refs_0_), channel_id=1, source_target_pairs={{0,2},{1,3},{2,0},{3,1},{4,6},{5,7},{6,4},{7,5},{8,10},{9,11},{10,... | collective-permute-start | bytes 196616 | tf_op jit(solution)/shard_map/ppermute | solution.py:175
  46.2 9.9 %collective-permute-start.8 = (bf16[16,2048]{1,0:T(8,128)(2,1)S(1)}, bf16[16,2048]{1,0:T(8,128)(2,1)S(1)}, u32[]{:S(2)}, u32[]{:S(2)}) collective-permute-start(bf16[16,2048]{1,0:T(8,128)(2,1)S(1)} %activate.1.after_ref.refs_0_), channel_id=1, source_target_pairs={{0,1},{1,0},{2,3},{3,2},{4,5},{5,4},{6,7},{7,6},{8,9},{9,8},{10,11... | collective-permute-start | bytes 196616 | tf_op jit(solution)/shard_map/ppermute | solution.py:175
  56.0 19.4 %copy-start.2 = (s32[4,2]{0,1:T(2,128)S(1)}, s32[4,2]{0,1:T(2,128)}, u32[]{:S(2)}) copy-start(s32[4,2]{0,1:T(2,128)} %param.7) | copy-start | bytes 100
  56.0 19.4 %copy-start.3 = (f32[4,2]{0,1:T(2,128)S(1)}, f32[4,2]{0,1:T(2,128)}, u32[]{:S(2)}) copy-start(f32[4,2]{0,1:T(2,128)} %param.8) | copy-start | bytes 100
  74.2 1.2 %collective-permute-start.15 = (f32[8,2,768]{2,1,0:T(2,128)S(1)}, f32[8,2,768]{2,1,0:T(2,128)S(1)}, u32[]{:S(2)}, u32[]{:S(2)}) collective-permute-start(f32[8,2,768]{2,1,0:T(2,128)S(1)} %all_to_all.5.own_ref), channel_id=1, source_target_pairs={{0,8},{8,0},{1,9},{9,1},{2,10},{10,2},{3,11},{11,3},{4,12},{12,4},... | collective-permute-start | bytes 147464 | tf_op jit(solution)/shard_map/ppermute | solution.py:178

commit v3 on v2

--- a/solution.py
+++ b/solution.py
@@ -11,32 +11,15 @@
 SLOTS = 2
 VMEM = pl.BlockSpec(memory_space=pltpu.VMEM)
 SMEM = pl.BlockSpec(memory_space=pltpu.SMEM)
-
-
-def load_kernel(after_ref, hbm_ref, vmem_ref, sems):
-    parts = sems.shape[0]
-    rows = hbm_ref.shape[1] // parts
-    copies = []
-    for i in range(parts):
-        part = pl.ds(i * rows, rows)
-        copies.append(pltpu.make_async_copy(hbm_ref.at[:, part], vmem_ref.at[:, part], sems.at[i]))
-        copies[-1].start()
-    for copy in copies:
-        copy.wait()
-
-
-def load(w, after, name):
-    parts = 6
-    return pl.pallas_call(
-        load_kernel,
-        out_shape=pltpu.VMEM(w.shape, w.dtype),
-        in_specs=[pl.BlockSpec(memory_space=pl.ANY)] * 2,
-        out_specs=VMEM,
-        scratch_shapes=[pltpu.SemaphoreType.DMA((parts,))],
-        compiler_params=pltpu.CompilerParams(vmem_limit_bytes=MIB),
-        cost_estimate=pl.CostEstimate(flops=0, bytes_accessed=2 * w.size * 2, transcendentals=0),
-        name=name,
-    )(after, pltpu.with_memory_space_constraint(w, pltpu.HBM))
+ANY = pl.BlockSpec(memory_space=pl.ANY)
+
+
+def in_vmem(x):
+    return pltpu.with_memory_space_constraint(x, pltpu.VMEM)
+
+
+def in_hbm(x):
+    return pltpu.with_memory_space_constraint(x, pltpu.HBM)
 
 
 def call(kernel, name, out, in_specs, limit, seconds=0.0, scratch=()):
@@ -62,11 +45,19 @@
     return found
 
 
-def dispatch_kernel(tokens_ref, routes_ref, sends_ref):
+def dispatch_kernel(tokens_hbm, routes_hbm, sends_ref, tokens_ref, routes_ref, sems):
+    copies = [
+        pltpu.make_async_copy(routes_hbm, routes_ref, sems.at[0]),
+        pltpu.make_async_copy(tokens_hbm, tokens_ref, sems.at[1]),
+    ]
+    for copy in copies:
+        copy.start()
+    for copy in copies:
+        copy.wait()
     tokens = tokens_ref[...].astype(jnp.float32)
     rows = tokens.shape[0]
     blocks = []
-    for e in range(sends_ref.shape[0] // SLOTS):
+    for e in range(sends_ref.shape[1] // SLOTS):
         found = slot_rows(routes_ref, e, rows)
         for c in range(SLOTS):
             row = jnp.zeros((1, tokens.shape[1]), jnp.float32)
@@ -74,19 +65,21 @@
                 here = jnp.logical_and(named, slot == c).astype(jnp.float32)
                 row = row + here * tokens[r:r + 1, :]
             blocks.append(row)
-    sends_ref[...] = jnp.concatenate(blocks, axis=0).astype(jnp.bfloat16)
-
-
-def merge_kernel(*refs):
-    *blocks, own_ref, other_ref, own_f32, other_f32 = refs
-    me, mine = lax.axis_index("tile"), lax.axis_index("expert")
-    for k, block in enumerate(blocks):
-        rows = block[...].astype(jnp.float32)
-        first, second = rows[:SLOTS], rows[SLOTS:]
-        own_f32[me ^ k] = jnp.where(mine == 0, first, second)
-        other_f32[me ^ k] = jnp.where(mine == 0, second, first)
-    own_ref[...] = own_f32[...].reshape(own_ref.shape).astype(jnp.bfloat16)
-    other_ref[...] = other_f32[...].reshape(other_ref.shape).astype(jnp.bfloat16)
+    block = jnp.concatenate(blocks, axis=0).astype(jnp.bfloat16)
+    for t in range(sends_ref.shape[0]):
+        sends_ref[t] = block
+
+
+def merge_kernel(blocks_ref, own_ref, other_ref, first_f32, second_f32):
+    mine = lax.axis_index("expert")
+    for t in range(blocks_ref.shape[0]):
+        rows = blocks_ref[t].astype(jnp.float32)
+        first_f32[t] = rows[:SLOTS]
+        second_f32[t] = rows[SLOTS:]
+    first = first_f32[...].reshape(own_ref.shape).astype(jnp.bfloat16)
+    second = second_f32[...].reshape(own_ref.shape).astype(jnp.bfloat16)
+    own_ref[...] = jnp.where(mine == 0, first, second)
+    other_ref[...] = jnp.where(mine == 0, second, first)
 
 
 def project_kernel(own_ref, other_ref, w_gate_ref, w_up_hbm, gate_ref, up_ref, ring, sems):
@@ -123,19 +116,29 @@
 
 
 def down_kernel(n, *refs):
-    blocks, w_ref, sends_ref = refs[:n], refs[n], refs[n + 1]
+    blocks, w_ref, sends_ref, total_ref = refs[:n], refs[n], refs[n + 1], refs[n + 2]
     me = lax.axis_index("tile")
     width = blocks[0].shape[1]
-    total = jnp.zeros((w_ref.shape[1], blocks[0].shape[0]), jnp.float32)
-    for k in range(n):
-        columns = pl.ds(pl.multiple_of((me ^ k) * width, width), width)
-        total += lax.dot_general(
-            w_ref[0, :, columns], blocks[k][...], (((1,), (1,)), ((), ())),
-            preferred_element_type=jnp.float32,
-        )
-    total = total.T
+    slots = blocks[0].shape[0]
+    part = 128
+    contract = (((1,), (1,)), ((), ()))
+
+    def step(i, carry):
+        rows = [pl.ds(pl.multiple_of((2 * i + h) * part, part), part) for h in range(2)]
+        first = jnp.zeros((slots, part), jnp.float32)
+        second = jnp.zeros((part, slots), jnp.float32)
+        for k in range(n):
+            columns = pl.ds(pl.multiple_of((me ^ k) * width, width), width)
+            x = blocks[k][...]
+            first += lax.dot_general(x, w_ref[0, rows[0], columns], contract, preferred_element_type=jnp.float32)
+            second += lax.dot_general(w_ref[0, rows[1], columns], x, contract, preferred_element_type=jnp.float32)
+        total_ref[:, rows[0]] = first
+        total_ref[:, rows[1]] = second.T
+        return carry
+
+    lax.fori_loop(0, w_ref.shape[1] // (2 * part), step, 0)
     for t in range(sends_ref.shape[0]):
-        sends_ref[t] = total[t * SLOTS:(t + 1) * SLOTS, :]
+        sends_ref[t] = total_ref[t * SLOTS:(t + 1) * SLOTS, :]
 
 
 def combine_kernel(own_ref, other_ref, routes_ref, gates_ref, out_ref):
@@ -179,22 +182,28 @@
 
     f32 = lambda *shape: jax.ShapeDtypeStruct(shape, jnp.float32)
     bf16 = lambda *shape: jax.ShapeDtypeStruct(shape, jnp.bfloat16)
-    sends = call(dispatch_kernel, "dispatch", bf16(2 * SLOTS, half_width), [VMEM, SMEM], 16 * MIB, 0)(tokens, routes)
+    sends = call(
+        dispatch_kernel, "dispatch", bf16(tiles, 2 * SLOTS, half_width), [ANY, ANY], 4 * MIB, 300e-6,
+        [pltpu.VMEM((rows, half_width), jnp.bfloat16), pltpu.SMEM((2, rows), jnp.int32), pltpu.SemaphoreType.DMA((2,))],
+    )(in_hbm(tokens), in_hbm(routes))
+    blocks = lax.all_to_all(sends, "tile", split_axis=0, concat_axis=0, tiled=True)
     own, other = call(
-        merge_kernel, "merge", (bf16(slots, half_width),) * 2, [VMEM] * tiles, 16 * MIB, 0e-6,
+        merge_kernel, "merge", (bf16(slots, half_width),) * 2, [VMEM], 4 * MIB, 0e-6,
         [pltpu.VMEM((tiles, SLOTS, half_width), jnp.float32)] * 2,
-    )(*to_tiles(sends))
+    )(blocks)
     other = to_core(other)
     chunk, depth = half_width // 4, 3
     gate, up = call(
-        project_kernel, "project", (f32(slots, width),) * 2, [VMEM, VMEM, VMEM, pl.BlockSpec(memory_space=pl.ANY)], 20 * MIB, 0,
+        project_kernel, "project", (f32(slots, width),) * 2, [VMEM, VMEM, VMEM, ANY], 20 * MIB, 0,
         [pltpu.VMEM((depth, chunk, width), jnp.bfloat16), pltpu.SemaphoreType.DMA((depth,))],
-    )(own, other, load(w_gate, sends, "load_gate"), pltpu.with_memory_space_constraint(w_up, pltpu.HBM))
-    hidden = call(activate_kernel, "activate", bf16(slots, width), [VMEM, VMEM], 16 * MIB, 0)(gate, up)
-    result = call(functools.partial(down_kernel, tiles), "down", f32(tiles, SLOTS, features), [VMEM] * (tiles + 1), 16 * MIB, 0e-6)(
-        *to_tiles(hidden), load(w_down, hidden, "load_down"))
+    )(own, other, in_vmem(w_gate), in_hbm(w_up))
+    hidden = call(activate_kernel, "activate", bf16(slots, width), [VMEM, VMEM], 4 * MIB, 200e-6)(gate, up)
+    result = call(
+        functools.partial(down_kernel, tiles), "down", f32(tiles, SLOTS, features), [VMEM] * (tiles + 1), 8 * MIB, 0,
+        [pltpu.VMEM((slots, features), jnp.float32)],
+    )(*to_tiles(hidden), in_vmem(w_down))
     back = lax.all_to_all(result, "tile", split_axis=0, concat_axis=0, tiled=True)
-    return call(combine_kernel, "combine", bf16(rows, half_width), [VMEM, VMEM, SMEM, SMEM], 16 * MIB)(
+    return call(combine_kernel, "combine", bf16(rows, half_width), [VMEM, VMEM, SMEM, SMEM], 4 * MIB)(
         back, to_core(back), routes, gates)
 
 

time: 77.1 us -> 61.7 us (0.80)
  Pallas kernels: 34.5 us -> 18.5 us
  blocking collectives: 11.5 us -> 24.7 us
  starting transfers between devices: 23.7 us -> 11.2 us
  local copies, waits for them, and re-layouts: 1.43 us -> 0.02 us
  waiting for transfers between devices: 5.6 us -> 6.98 us
    pallas_call x5 -> x3, Pallas kernels: 17.4 us -> 1.15 us  [the longest x1 1.01 us: local_direct(): call(dispatch_kernel, 'dispatch', bf16(tiles, 2 * SLOTS, half_width), [AN...]
    all_to_all x0 -> x1, blocking collectives: none -> 15.3 us  [local_direct(): lax.all_to_all(sends, 'tile', split_axis=0, concat_axis=0, tiled=True)]
    ppermute x14 -> x7, starting transfers between devices: 23.6 us -> 11.1 us  [to_tiles(): lax.ppermute(x, 'tile', [(t, t ^ k) for t in range(tiles)])]
    all_to_all x1, blocking collectives: 11.5 us -> 9.43 us  [local_direct(): lax.all_to_all(result, 'tile', split_axis=0, concat_axis=0, tiled=True)]
    unnamed x8, local copies, waits for them, and re-layouts: 1.43 us -> 0.02 us
    ppermute x2, waiting for transfers between devices: 1.23 us -> 2.52 us  [to_core(): return lax.ppermute(x, 'expert', [(0, 1), (1, 0)])]
    ppermute x14 -> x7, waiting for transfers between devices: 4.37 us -> 4.46 us  [to_tiles(): lax.ppermute(x, 'tile', [(t, t ^ k) for t in range(tiles)])]
  transfers between devices with their start and end apart: 16 -> 9, of which waited for: 5 -> 7; matrix products, arithmetic and copies ran while one was open for 0% -> 0% of each run, Pallas kernels for 22% -> 0%
where the time goes in v3:
time: 61.7 us; the launch traced here: 61.5 us
  blocking collectives  24.7 us (40%)
  Pallas kernels  18.5 us (30%)
  starting transfers between devices  11.2 us (18%)
  waiting for transfers between devices  6.98 us (11%)
    all_to_all x1, blocking collectives, local_direct(): lax.all_to_all(sends, 'tile', split_axis=0, concat_axis=0, tiled=True)  15.3 us
    ppermute x7, starting transfers between devices, to_tiles(): lax.ppermute(x, 'tile', [(t, t ^ k) for t in range(tiles)])  11.1 us
    all_to_all x1, blocking collectives, local_direct(): lax.all_to_all(result, 'tile', split_axis=0, concat_axis=0, tiled=True)  9.43 us
    pallas_call x1, Pallas kernels, local_direct(): call(project_kernel, 'project', (f32(slots, width),) * 2, [VMEM, VMEM, VM...  9.04 us
    pallas_call x1, Pallas kernels, local_direct(): call(functools.partial(down_kernel, tiles), 'down', f32(tiles, SLOTS, fea...  6.96 us
    ppermute x7, waiting for transfers between devices, to_tiles(): lax.ppermute(x, 'tile', [(t, t ^ k) for t in range(tiles)])  4.46 us
    ppermute x2, waiting for transfers between devices, to_core(): return lax.ppermute(x, 'expert', [(0, 1), (1, 0)])  2.52 us
    pallas_call x1, Pallas kernels, local_direct(): call(combine_kernel, 'combine', bf16(rows, half_width), [VMEM, VMEM, SMEM...  1.38 us
  transfers between devices with their start and end apart: 9, of which 7 were waited for; matrix products, arithmetic and copies ran while one was open for 0% of the time, Pallas kernels for 0%

profile of v3, /device:TPU:0, one launch (start us, length us, event | category | flops | bytes accessed | tf_op | source)
XLA Modules:
  0.0 61.5 jit_solution(4401834649101338437)
XLA Ops:
  0.0 1.0 %dispatch.1 = bf16[8,4,3072]{2,1,0:T(4,128)(2,1)S(1)} custom-call(bf16[4,3072]{1,0:T(4,128)(2,1)} %tokens_hbm.1, s32[2,4]{1,0:T(2,128)} %bitcast.2), custom_call_target="tpu_custom_call" | custom-call | flops 299999985664 | tf_op jit(solution)/shard_map/dispatch/pallas_call | solution.py:185
  1.0 15.3 %all_to_all.10.blocks_ref = bf16[8,4,3072]{2,1,0:T(4,128)(2,1)S(1)} all-to-all(bf16[8,4,3072]{2,1,0:T(4,128)(2,1)S(1)} %dispatch.1), channel_id=1, replica_groups=mesh['group'=2,'expert'=2,'tile'=8] {'tile'}, dimensions={0} | all-to-all | bytes 393216 | tf_op jit(solution)/shard_map/all_to_all | solution.py:189
  16.3 0.1 merge.1
  16.4 0.1 collective-permute-start
  16.5 1.3 %collective-permute-done.other_ref = bf16[16,3072]{1,0:T(8,128)(2,1)S(1)} collective-permute-done((bf16[16,3072]{1,0:T(8,128)(2,1)S(1)}, bf16[16,3072]{1,0:T(8,128)(2,1)S(1)}, u32[]{:S(2)}, u32[]{:S(2)}) %collective-permute-start) | collective-permute-done | bytes 98336 | tf_op jit(solution)/shard_map/ppermute | solution.py:181
  17.7 0.0 copy-done
  17.7 9.0 %project.1 = (f32[16,2048]{1,0:T(8,128)S(1)}, f32[16,2048]{1,0:T(8,128)S(1)}) custom-call(bf16[16,3072]{1,0:T(8,128)(2,1)S(1)} %get-tuple-element.9.own_ref, bf16[16,3072]{1,0:T(8,128)(2,1)S(1)} %collective-permute-done.other_ref, bf16[1,6144,2048]{2,1,0:T(8,128)(2,1)S(1)} %copy-done, bf16[1,6144,2048]{2,1,0:T(8,128)(2,1)} %w_up_hbm.1), custom_call_target="tpu_custom_call" | custom-call | tf_op jit(solution)/shard_map/project/pallas_call | solution.py:196
  26.8 0.0 copy-start.1
  26.9 0.0 copy-start.2
  26.9 0.0 copy-start.3
  26.9 1.9 %collective-permute-start.7 = (bf16[16,2048]{1,0:T(8,128)(2,1)S(1)}, bf16[16,2048]{1,0:T(8,128)(2,1)S(1)}, u32[]{:S(2)}, u32[]{:S(2)}) collective-permute-start(bf16[16,2048]{1,0:T(8,128)(2,1)S(1)} %activate.1.refs_0_), channel_id=1, source_target_pairs={{0,7},{1,6},{2,5},{3,4},{4,3},{5,2},{6,1},{7,0},{8,15},{9,14},{10,... | collective-permute-start | bytes 196616 | tf_op jit(solution)/shard_map/ppermute | solution.py:178
  28.8 2.5 %collective-permute-start.6 = (bf16[16,2048]{1,0:T(8,128)(2,1)S(1)}, bf16[16,2048]{1,0:T(8,128)(2,1)S(1)}, u32[]{:S(2)}, u32[]{:S(2)}) collective-permute-start(bf16[16,2048]{1,0:T(8,128)(2,1)S(1)} %activate.1.refs_0_), channel_id=1, source_target_pairs={{0,6},{1,7},{2,4},{3,5},{4,2},{5,3},{6,0},{7,1},{8,14},{9,15},{10,... | collective-permute-start | bytes 196616 | tf_op jit(solution)/shard_map/ppermute | solution.py:178
  31.3 0.0 collective-permute-start.5
  31.3 3.3 %collective-permute-start.4 = (bf16[16,2048]{1,0:T(8,128)(2,1)S(1)}, bf16[16,2048]{1,0:T(8,128)(2,1)S(1)}, u32[]{:S(2)}, u32[]{:S(2)}) collective-permute-start(bf16[16,2048]{1,0:T(8,128)(2,1)S(1)} %activate.1.refs_0_), channel_id=1, source_target_pairs={{0,4},{1,5},{2,6},{3,7},{4,0},{5,1},{6,2},{7,3},{8,12},{9,13},{10,... | collective-permute-start | bytes 196616 | tf_op jit(solution)/shard_map/ppermute | solution.py:178
  34.6 0.0 collective-permute-start.3
  34.6 0.1 collective-permute-done.7.refs_7_
  34.7 2.5 %collective-permute-start.2 = (bf16[16,2048]{1,0:T(8,128)(2,1)S(1)}, bf16[16,2048]{1,0:T(8,128)(2,1)S(1)}, u32[]{:S(2)}, u32[]{:S(2)}) collective-permute-start(bf16[16,2048]{1,0:T(8,128)(2,1)S(1)} %activate.1.refs_0_), channel_id=1, source_target_pairs={{0,2},{1,3},{2,0},{3,1},{4,6},{5,7},{6,4},{7,5},{8,10},{9,11},{10,... | collective-permute-start | bytes 196616 | tf_op jit(solution)/shard_map/ppermute | solution.py:178
  37.1 0.0 collective-permute-done.6.refs_6_
  37.1 1.0 %collective-permute-start.1 = (bf16[16,2048]{1,0:T(8,128)(2,1)S(1)}, bf16[16,2048]{1,0:T(8,128)(2,1)S(1)}, u32[]{:S(2)}, u32[]{:S(2)}) collective-permute-start(bf16[16,2048]{1,0:T(8,128)(2,1)S(1)} %activate.1.refs_0_), channel_id=1, source_target_pairs={{0,1},{1,0},{2,3},{3,2},{4,5},{5,4},{6,7},{7,6},{8,9},{9,8},{10,11... | collective-permute-start | bytes 196616 | tf_op jit(solution)/shard_map/ppermute | solution.py:178
  38.1 2.7 %collective-permute-done.5.refs_5_ = bf16[16,2048]{1,0:T(8,128)(2,1)S(1)} collective-permute-done((bf16[16,2048]{1,0:T(8,128)(2,1)S(1)}, bf16[16,2048]{1,0:T(8,128)(2,1)S(1)}, u32[]{:S(2)}, u32[]{:S(2)}) %collective-permute-start.5) | collective-permute-done | bytes 65568 | tf_op jit(solution)/shard_map/ppermute | solution.py:178
  40.8 0.5 collective-permute-done.4.refs_4_
  41.3 0.7 %collective-permute-done.3.refs_3_ = bf16[16,2048]{1,0:T(8,128)(2,1)S(1)} collective-permute-done((bf16[16,2048]{1,0:T(8,128)(2,1)S(1)}, bf16[16,2048]{1,0:T(8,128)(2,1)S(1)}, u32[]{:S(2)}, u32[]{:S(2)}) %collective-permute-start.3) | collective-permute-done | bytes 65568 | tf_op jit(solution)/shard_map/ppermute | solution.py:178
  42.0 0.4 collective-permute-done.2.refs_2_
  42.5 0.0 collective-permute-done.1.refs_1_
  42.5 0.0 copy-done.1
  42.5 7.0 %down.1 = f32[8,2,768]{2,1,0:T(2,128)S(1)} custom-call(bf16[16,2048]{1,0:T(8,128)(2,1)S(1)} %activate.1.refs_0_, bf16[16,2048]{1,0:T(8,128)(2,1)S(1)} %collective-permute-done.1.refs_1_, bf16[16,2048]{1,0:T(8,128)(2,1)S(1)} %collective-permute-done.2.refs_2_, bf16[16,2048]{1,0:T(8,128)(2,1)S(1)} %collective-permute-done.3.refs_3_, ...), custom_call_target="tpu_custom_call" | custom-call | tf_op jit(solution)/shard_map/down/pallas_call | solution.py:201
  49.4 9.4 %all_to_all.11.own_ref = f32[8,2,768]{2,1,0:T(2,128)S(1)} all-to-all(f32[8,2,768]{2,1,0:T(2,128)S(1)} %down.1), channel_id=1, replica_groups=mesh['group'=2,'expert'=2,'tile'=8] {'tile'}, dimensions={0} | all-to-all | bytes 98304 | tf_op jit(solution)/shard_map/all_to_all | solution.py:205
  58.9 0.0 collective-permute-start.8
  58.9 1.2 %collective-permute-done.8.other_ref = f32[8,2,768]{2,1,0:T(2,128)S(1)} collective-permute-done((f32[8,2,768]{2,1,0:T(2,128)S(1)}, f32[8,2,768]{2,1,0:T(2,128)S(1)}, u32[]{:S(2)}, u32[]{:S(2)}) %collective-permute-start.8) | collective-permute-done | bytes 49184 | tf_op jit(solution)/shard_map/ppermute | solution.py:181
  60.1 0.0 copy-done.2
  60.1 0.0 copy-done.3
  60.1 1.4 %combine.1 = bf16[4,3072]{1,0:T(4,128)(2,1)} custom-call(f32[8,2,768]{2,1,0:T(2,128)S(1)} %all_to_all.11.own_ref, f32[8,2,768]{2,1,0:T(2,128)S(1)} %collective-permute-done.8.other_ref, s32[2,4]{1,0:T(2,128)S(1)} %bitcast.3, f32[2,4]{1,0:T(2,128)S(1)} %bitcast.4), custom_call_target="tpu_custom_call" | custom-call | tf_op jit(solution)/shard_map/combine/pallas_call | solution.py:206
  (2 shorter events, 0.1 us)
Async XLA Ops:
  0.0 17.7 %copy-start = (bf16[1,6144,2048]{2,1,0:T(8,128)(2,1)S(1)}, bf16[1,6144,2048]{2,1,0:T(8,128)(2,1)}, u32[]{:S(2)}) copy-start(bf16[1,6144,2048]{2,1,0:T(8,128)(2,1)} %w_gate_ref.1) | copy-start | bytes 75497472
  16.4 1.4 %collective-permute-start = (bf16[16,3072]{1,0:T(8,128)(2,1)S(1)}, bf16[16,3072]{1,0:T(8,128)(2,1)S(1)}, u32[]{:S(2)}, u32[]{:S(2)}) collective-permute-start(bf16[16,3072]{1,0:T(8,128)(2,1)S(1)} %get-tuple-element.10), channel_id=1, source_target_pairs={{0,8},{8,0},{1,9},{9,1},{2,10},{10,2},{3,11},{11,3},{4,12},{12,4},... | collective-permute-start | bytes 294920 | tf_op jit(solution)/shard_map/ppermute | solution.py:181
  26.8 15.7 %copy-start.1 = (bf16[1,768,16384]{2,1,0:T(8,128)(2,1)S(1)}, bf16[1,768,16384]{2,1,0:T(8,128)(2,1)}, u32[]{:S(2)}) copy-start(bf16[1,768,16384]{2,1,0:T(8,128)(2,1)} %refs_8_.1) | copy-start | bytes 75497472
  26.9 33.2 %copy-start.2 = (s32[4,2]{0,1:T(2,128)S(1)}, s32[4,2]{0,1:T(2,128)}, u32[]{:S(2)}) copy-start(s32[4,2]{0,1:T(2,128)} %param.7) | copy-start | bytes 100
  26.9 33.2 %copy-start.3 = (f32[4,2]{0,1:T(2,128)S(1)}, f32[4,2]{0,1:T(2,128)}, u32[]{:S(2)}) copy-start(f32[4,2]{0,1:T(2,128)} %param.8) | copy-start | bytes 100
  26.9 7.8 %collective-permute-start.7 = (bf16[16,2048]{1,0:T(8,128)(2,1)S(1)}, bf16[16,2048]{1,0:T(8,128)(2,1)S(1)}, u32[]{:S(2)}, u32[]{:S(2)}) collective-permute-start(bf16[16,2048]{1,0:T(8,128)(2,1)S(1)} %activate.1.refs_0_), channel_id=1, source_target_pairs={{0,7},{1,6},{2,5},{3,4},{4,3},{5,2},{6,1},{7,0},{8,15},{9,14},{10,... | collective-permute-start | bytes 196616 | tf_op jit(solution)/shard_map/ppermute | solution.py:178
  28.8 8.3 %collective-permute-start.6 = (bf16[16,2048]{1,0:T(8,128)(2,1)S(1)}, bf16[16,2048]{1,0:T(8,128)(2,1)S(1)}, u32[]{:S(2)}, u32[]{:S(2)}) collective-permute-start(bf16[16,2048]{1,0:T(8,128)(2,1)S(1)} %activate.1.refs_0_), channel_id=1, source_target_pairs={{0,6},{1,7},{2,4},{3,5},{4,2},{5,3},{6,0},{7,1},{8,14},{9,15},{10,... | collective-permute-start | bytes 196616 | tf_op jit(solution)/shard_map/ppermute | solution.py:178
  31.3 9.5 %collective-permute-start.5 = (bf16[16,2048]{1,0:T(8,128)(2,1)S(1)}, bf16[16,2048]{1,0:T(8,128)(2,1)S(1)}, u32[]{:S(2)}, u32[]{:S(2)}) collective-permute-start(bf16[16,2048]{1,0:T(8,128)(2,1)S(1)} %activate.1.refs_0_), channel_id=1, source_target_pairs={{0,5},{1,4},{2,7},{3,6},{4,1},{5,0},{6,3},{7,2},{8,13},{9,12},{10,... | collective-permute-start | bytes 196616 | tf_op jit(solution)/shard_map/ppermute | solution.py:178
  31.3 10.0 %collective-permute-start.4 = (bf16[16,2048]{1,0:T(8,128)(2,1)S(1)}, bf16[16,2048]{1,0:T(8,128)(2,1)S(1)}, u32[]{:S(2)}, u32[]{:S(2)}) collective-permute-start(bf16[16,2048]{1,0:T(8,128)(2,1)S(1)} %activate.1.refs_0_), channel_id=1, source_target_pairs={{0,4},{1,5},{2,6},{3,7},{4,0},{5,1},{6,2},{7,3},{8,12},{9,13},{10,... | collective-permute-start | bytes 196616 | tf_op jit(solution)/shard_map/ppermute | solution.py:178
  34.6 7.4 %collective-permute-start.3 = (bf16[16,2048]{1,0:T(8,128)(2,1)S(1)}, bf16[16,2048]{1,0:T(8,128)(2,1)S(1)}, u32[]{:S(2)}, u32[]{:S(2)}) collective-permute-start(bf16[16,2048]{1,0:T(8,128)(2,1)S(1)} %activate.1.refs_0_), channel_id=1, source_target_pairs={{0,3},{1,2},{2,1},{3,0},{4,7},{5,6},{6,5},{7,4},{8,11},{9,10},{10,... | collective-permute-start | bytes 196616 | tf_op jit(solution)/shard_map/ppermute | solution.py:178
  34.7 7.8 %collective-permute-start.2 = (bf16[16,2048]{1,0:T(8,128)(2,1)S(1)}, bf16[16,2048]{1,0:T(8,128)(2,1)S(1)}, u32[]{:S(2)}, u32[]{:S(2)}) collective-permute-start(bf16[16,2048]{1,0:T(8,128)(2,1)S(1)} %activate.1.refs_0_), channel_id=1, source_target_pairs={{0,2},{1,3},{2,0},{3,1},{4,6},{5,7},{6,4},{7,5},{8,10},{9,11},{10,... | collective-permute-start | bytes 196616 | tf_op jit(solution)/shard_map/ppermute | solution.py:178
  37.1 5.3 %collective-permute-start.1 = (bf16[16,2048]{1,0:T(8,128)(2,1)S(1)}, bf16[16,2048]{1,0:T(8,128)(2,1)S(1)}, u32[]{:S(2)}, u32[]{:S(2)}) collective-permute-start(bf16[16,2048]{1,0:T(8,128)(2,1)S(1)} %activate.1.refs_0_), channel_id=1, source_target_pairs={{0,1},{1,0},{2,3},{3,2},{4,5},{5,4},{6,7},{7,6},{8,9},{9,8},{10,11... | collective-permute-start | bytes 196616 | tf_op jit(solution)/shard_map/ppermute | solution.py:178
  58.9 1.2 %collective-permute-start.8 = (f32[8,2,768]{2,1,0:T(2,128)S(1)}, f32[8,2,768]{2,1,0:T(2,128)S(1)}, u32[]{:S(2)}, u32[]{:S(2)}) collective-permute-start(f32[8,2,768]{2,1,0:T(2,128)S(1)} %all_to_all.11.own_ref), channel_id=1, source_target_pairs={{0,8},{8,0},{1,9},{9,1},{2,10},{10,2},{3,11},{11,3},{4,12},{12,4},... | collective-permute-start | bytes 147464 | tf_op jit(solution)/shard_map/ppermute | solution.py:181

commit v4 on v0

--- a/solution.py
+++ b/solution.py
@@ -1,10 +1,220 @@
+import functools
+
 import jax
 import jax.numpy as jnp
 from jax import lax
+from jax.experimental import pallas as pl
+from jax.experimental.pallas import tpu as pltpu
 from jax.sharding import PartitionSpec as P
 
-
-def local(tokens, routes, gates, w_gate, w_up, w_down):
+MIB = 1 << 20
+SLOTS = 2
+VMEM = pl.BlockSpec(memory_space=pltpu.VMEM)
+ANY = pl.BlockSpec(memory_space=pl.ANY)
+
+
+def in_vmem(x):
+    return pltpu.with_memory_space_constraint(x, pltpu.VMEM)
+
+
+def in_hbm(x):
+    return pltpu.with_memory_space_constraint(x, pltpu.HBM)
+
+
+def call(kernel, name, out, in_specs, limit, seconds=0.0, scratch=()):
+    return pl.pallas_call(
+        kernel,
+        out_shape=out,
+        in_specs=in_specs,
+        out_specs=jax.tree.map(lambda _: VMEM, out),
+        scratch_shapes=scratch,
+        compiler_params=pltpu.CompilerParams(vmem_limit_bytes=limit),
+        cost_estimate=pl.CostEstimate(flops=int(seconds*1e15), bytes_accessed=0, transcendentals=0),
+        name=name,
+    )
+
+
+def slot_rows(routes_ref, e, rows):
+    taken = jnp.int32(0)
+    found = []
+    for r in range(rows):
+        named = jnp.logical_or(routes_ref[0, r] == e, routes_ref[1, r] == e)
+        found.append((named, taken))
+        taken = taken + named.astype(jnp.int32)
+    return found
+
+
+def dispatch_kernel(tokens_hbm, routes_hbm, gates_hbm, sends_ref, table_ref, tokens_ref, routes_ref, gates_ref, sems):
+    copies = [
+        pltpu.make_async_copy(routes_hbm, routes_ref, sems.at[0]),
+        pltpu.make_async_copy(gates_hbm, gates_ref, sems.at[1]),
+        pltpu.make_async_copy(tokens_hbm, tokens_ref, sems.at[2]),
+    ]
+    for copy in copies:
+        copy.start()
+    for copy in copies:
+        copy.wait()
+    tokens = tokens_ref[...].astype(jnp.float32)
+    rows = tokens.shape[0]
+    tiles = sends_ref.shape[0] // 2
+    for e in range(2):
+        found = slot_rows(routes_ref, e, rows)
+        base = e * (1 + SLOTS)
+        line = (1, table_ref.shape[2])
+        for r in range(rows):
+            weight = jnp.where(routes_ref[0, r] == e, gates_ref[0, r], 0.0)
+            weight = weight + jnp.where(routes_ref[1, r] == e, gates_ref[1, r], 0.0)
+            table_ref[base, r:r + 1, :] = jnp.full(line, weight, jnp.float32)
+        slots = []
+        for c in range(SLOTS):
+            row = jnp.zeros((1, tokens.shape[1]), jnp.float32)
+            for r, (named, slot) in enumerate(found):
+                here = jnp.logical_and(named, slot == c).astype(jnp.float32)
+                row = row + here * tokens[r:r + 1, :]
+                table_ref[base + 1 + c, r:r + 1, :] = jnp.full(line, here, jnp.float32)
+            slots.append(row)
+        block = jnp.concatenate(slots, axis=0).astype(jnp.bfloat16)
+        for t in range(tiles):
+            sends_ref[e * tiles + t] = block
+
+
+def merge_kernel(blocks_ref, rows_ref):
+    rows_ref[...] = blocks_ref[...].reshape(rows_ref.shape)
+
+
+def project(rows_ref, w_ref, columns):
+    slots, half = rows_ref.shape[0] // 2, rows_ref.shape[1]
+    total = jnp.dot(rows_ref[:slots, :], w_ref[0, :half, columns], preferred_element_type=jnp.float32)
+    return total + jnp.dot(rows_ref[slots:, :], w_ref[0, half:, columns], preferred_element_type=jnp.float32)
+
+
+def over_columns(width, body):
+    tile = 256
+
+    def step(i, carry):
+        body(pl.ds(pl.multiple_of(i * tile, tile), tile))
+        return carry
+
+    lax.fori_loop(0, width // tile, step, 0)
+
+
+def gate_kernel(rows_ref, w_ref, out_ref):
+    def body(columns):
+        out_ref[:, columns] = project(rows_ref, w_ref, columns)
+
+    over_columns(out_ref.shape[1], body)
+
+
+def hidden_kernel(rows_ref, w_ref, gate_ref, hidden_ref):
+    def body(columns):
+        up = project(rows_ref, w_ref, columns)
+        gate = gate_ref[:, columns]
+        hidden_ref[:, columns] = (gate / (1.0 + jnp.exp(-gate)) * up).astype(jnp.bfloat16)
+
+    over_columns(hidden_ref.shape[1], body)
+
+
+def down_kernel(steps, order, first, last, *refs):
+    n = len(steps)
+    blocks, w_ref, rest = refs[:n], refs[n], refs[n + 1:]
+    out_ref = rest[-1]
+    me = lax.axis_index("tile")
+    slots, width = blocks[0].shape
+    part = 256
+    starts = []
+    for step in steps:
+        tile = jnp.int32(0)
+        for i, t in enumerate(order):
+            tile = jnp.where(me == t, order[(i + step) % len(order)], tile)
+        starts.append(pl.multiple_of(tile * width, width))
+    for i in range(w_ref.shape[1] // part):
+        rows = slice(i * part, (i + 1) * part)
+        total = None if first else rest[0][rows, :]
+        for block, start in zip(blocks, starts):
+            term = lax.dot_general(
+                w_ref[0, rows, pl.ds(start, width)], block[...], (((1,), (1,)), ((), ())),
+                preferred_element_type=jnp.float32,
+            )
+            total = term if total is None else total + term
+        if not last:
+            out_ref[rows, :] = total
+        else:
+            total = total.T
+            for t in range(out_ref.shape[0]):
+                out_ref[t, :, rows] = total[t * SLOTS:(t + 1) * SLOTS, :]
+
+
+def combine_kernel(own_ref, other_ref, table_ref, out_ref):
+    mine = lax.axis_index("expert")
+    halves, features = own_ref.shape[0] // 2, own_ref.shape[2]
+    weight = [table_ref[e * (1 + SLOTS)][:, :1] for e in range(2)]
+    inside = [[table_ref[e * (1 + SLOTS) + 1 + c][:, :1] for c in range(SLOTS)] for e in range(2)]
+    for i in range(halves):
+        own, other = own_ref[mine * halves + i], other_ref[mine * halves + i]
+        mixed = jnp.zeros((out_ref.shape[0], features), jnp.float32)
+        for e in range(2):
+            both = jnp.where(mine == e, own, other)
+            for c in range(SLOTS):
+                value = (weight[e] * both[c:c + 1]).astype(jnp.bfloat16).astype(jnp.float32)
+                mixed = mixed + jnp.where(inside[e][c] != 0.0, value, 0.0)
+        out_ref[:, i * features:(i + 1) * features] = mixed.astype(jnp.bfloat16)
+
+
+def local_direct(tokens, routes, gates, w_gate, w_up, w_down):
+    tiles = lax.axis_size("tile")
+    rows, half_width = tokens.shape
+    width, features = w_gate.shape[2], w_down.shape[1]
+    slots = tiles * SLOTS
+    routes, gates = routes.T, gates.T
+
+    def to_core(x):
+        return lax.ppermute(x, "expert", [(0, 1), (1, 0)])
+
+    f32 = lambda *shape: jax.ShapeDtypeStruct(shape, jnp.float32)
+    bf16 = lambda *shape: jax.ShapeDtypeStruct(shape, jnp.bfloat16)
+    sends, table = call(
+        dispatch_kernel, "dispatch",
+        (bf16(2 * tiles, SLOTS, half_width), f32(2 * (1 + SLOTS), rows, 128)), [ANY] * 3, 4 * MIB, 600e-6,
+        [
+            pltpu.VMEM((rows, half_width), jnp.bfloat16),
+            pltpu.SMEM((2, rows), jnp.int32),
+            pltpu.SMEM((2, rows), jnp.float32),
+            pltpu.SemaphoreType.DMA((3,)),
+        ],
+    )(in_hbm(tokens), in_hbm(routes), in_hbm(gates))
+    blocks = lax.all_to_all(sends, ("expert", "tile"), split_axis=0, concat_axis=0, tiled=True)
+    x = call(merge_kernel, "merge", bf16(2 * slots, half_width), [VMEM], 4 * MIB, 0e-6)(blocks)
+    gate = call(gate_kernel, "gate", f32(slots, width), [VMEM] * 2, 4 * MIB, 0e-6)(x, in_vmem(w_gate))
+    hidden = call(hidden_kernel, "hidden", bf16(slots, width), [VMEM] * 3, 4 * MIB, 200e-6)(x, in_vmem(w_up), gate)
+    order = list(range(0, tiles, 2)) + list(range(tiles - 1, 0, -2))
+    ahead = [(t, order[(i + 1) % tiles]) for i, t in enumerate(order)]
+    back = [(t, order[i - 1]) for i, t in enumerate(order)]
+
+    def down(total, steps, blocks):
+        first, last = total is None, -(tiles // 2) in steps
+        out = f32(tiles, SLOTS, features) if last else f32(features, slots)
+        return call(
+            functools.partial(down_kernel, steps, order, first, last), "down", out,
+            [VMEM] * (len(blocks) + 2 - first), 8 * MIB, 0e-6,
+        )(*blocks, in_vmem(w_down), *(() if first else (total,)))
+
+    below, above = hidden, hidden
+    total, steps, blocks = None, [0], [hidden]
+    for i in range(1, tiles // 2 + 1):
+        below = lax.ppermute(below, "tile", ahead)
+        if 2 * i < tiles:
+            above = lax.ppermute(above, "tile", back)
+        if i >= 3:
+            total, steps, blocks = down(total, steps, blocks), [], []
+        steps, blocks = steps + [-i], blocks + [below]
+        if 2 * i < tiles:
+            steps, blocks = steps + [i], blocks + [above]
+    result = down(total, steps, blocks)
+    back = lax.all_to_all(result, "tile", split_axis=0, concat_axis=0, tiled=True)
+    return call(combine_kernel, "combine", bf16(rows, half_width), [VMEM] * 3, 4 * MIB)(back, to_core(back), table)
+
+
+def local_gathered(tokens, routes, gates, w_gate, w_up, w_down):
     experts = lax.axis_size("expert")
     tile_count = lax.axis_size("tile")
     own_expert = lax.axis_index("expert")
@@ -58,4 +268,5 @@
         P("expert", "tile", None),
     )
     out_specs = P(("group", "tile"), "expert")
+    local = local_direct if mesh.shape["tile"] <= 8 else local_gathered
     return jax.shard_map(local, mesh=mesh, in_specs=in_specs, out_specs=out_specs, check_vma=False)

time: 116 us -> 59 us (0.51)
  blocking collectives: 71.6 us -> 26.2 us
  matrix products: 32.4 us -> 0 us
  Pallas kernels: 0 us -> 17.5 us
  starting transfers between devices: 3.34 us -> 6.18 us
  waiting for transfers between devices: 6.58 us -> 8.82 us
  local copies, waits for them, and re-layouts: 1.31 us -> 0.01 us
    all_gather x2 -> x0, blocking collectives: 67.9 us -> none  [the longest x1 36.6 us: local(): lax.all_gather(outgoing[None], ('expert', 'tile'), axis=0, tiled=True)]
    dot_general x6 -> x0, matrix products: 32.4 us -> none  [the longest x1 11.5 us: local(): lax.dot_general(columns, lax.all_gather(hidden, 'tile', axis=1, tiled=Tru...]
    all_to_all x1 -> x2, blocking collectives: 3.76 us -> 26.2 us  [the longest x1 16.4 us: local_direct(): lax.all_to_all(sends, ('expert', 'tile'), split_axis=0, concat_axis=0, ti...]
    pallas_call x0 -> x8, Pallas kernels: none -> 17.5 us  [the longest x3 6.96 us: down(): call(functools.partial(down_kernel, steps, order, first, last), 'down', o...]
    ppermute x0 -> x8, waiting for transfers between devices: none -> 8.82 us  [the longest x4 7.26 us: local_direct(): below = lax.ppermute(below, 'tile', ahead)]
    all_to_all x1 -> x0, waiting for transfers between devices: 6.58 us -> none  [local(): lax.all_to_all(summed, 'tile', split_axis=1, concat_axis=0, tiled=True)]
    ppermute x0 -> x8, starting transfers between devices: none -> 6.18 us  [the longest x3 4 us: local_direct(): above = lax.ppermute(above, 'tile', back)]
    all_to_all x1 -> x0, starting transfers between devices: 3.34 us -> none  [local(): lax.all_to_all(summed, 'tile', split_axis=1, concat_axis=0, tiled=True)]
  transfers between devices with their start and end apart: 1 -> 8, of which waited for: 1 -> 5; matrix products, arithmetic and copies ran while one was open for 0% -> 0% of each run, Pallas kernels for 0% -> 10%
where the time goes in v4:
time: 59 us; the launch traced here: 58.8 us
  blocking collectives  26.2 us (44%)
  Pallas kernels  17.5 us (30%)
  waiting for transfers between devices  8.82 us (15%)
  starting transfers between devices  6.18 us (10%)
    all_to_all x1, blocking collectives, local_direct(): lax.all_to_all(sends, ('expert', 'tile'), split_axis=0, concat_axis=0, ti...  16.4 us
    all_to_all x1, blocking collectives, local_direct(): lax.all_to_all(result, 'tile', split_axis=0, concat_axis=0, tiled=True)  9.8 us
    ppermute x4, waiting for transfers between devices, local_direct(): below = lax.ppermute(below, 'tile', ahead)  7.26 us
    pallas_call x3, Pallas kernels, down(): call(functools.partial(down_kernel, steps, order, first, last), 'down', o...  6.96 us
    pallas_call x1, Pallas kernels, local_direct(): call(hidden_kernel, 'hidden', bf16(slots, width), [VMEM] * 3, 4 * MIB, 0....  4.44 us
    pallas_call x1, Pallas kernels, local_direct(): call(gate_kernel, 'gate', f32(slots, width), [VMEM] * 2, 4 * MIB, 0.0)  4.27 us
    ppermute x3, starting transfers between devices, local_direct(): above = lax.ppermute(above, 'tile', back)  4 us
    ppermute x4, starting transfers between devices, local_direct(): below = lax.ppermute(below, 'tile', ahead)  2.17 us
  transfers between devices with their start and end apart: 8, of which 5 were waited for; matrix products, arithmetic and copies ran while one was open for 0% of the time, Pallas kernels for 10%

profile of v4, /device:TPU:0, one launch (start us, length us, event | category | flops | bytes accessed | tf_op | source)
XLA Modules:
  0.0 58.8 jit_solution(16024851703630197735)
XLA Ops:
  0.0 0.0 copy-start.1
  0.0 1.0 %dispatch.1 = (bf16[16,2,3072]{2,1,0:T(2,128)(2,1)S(1)}, f32[6,4,128]{2,1,0:T(4,128)S(1)}) custom-call(bf16[4,3072]{1,0:T(4,128)(2,1)} %tokens_hbm.1, s32[2,4]{1,0:T(2,128)} %bitcast.2, f32[2,4]{1,0:T(2,128)} %bitcast.3), custom_call_target="tpu_custom_call" | custom-call | flops 599999971328 | tf_op jit(solution)/shard_map/dispatch/pallas_call | solution.py:175
  1.0 0.0 copy-start.2
  1.0 16.4 %all_to_all.10.blocks_ref = bf16[16,2,3072]{2,1,0:T(2,128)(2,1)S(1)} all-to-all(bf16[16,2,3072]{2,1,0:T(2,128)(2,1)S(1)} %get-tuple-element.7), channel_id=1, replica_groups=mesh['group'=2,'expert'=2,'tile'=8] {'expert','tile'}, dimensions={0} | all-to-all | bytes 393216 | tf_op jit(solution)/shard_map/all_to_all | solution.py:185
  17.5 0.0 copy-done.1
  17.5 4.3 %gate.1.gate_ref = f32[16,2048]{1,0:T(8,128)S(1)} custom-call(bf16[32,3072]{1,0:T(8,128)(2,1)S(1)} %merge.1.rows_ref, bf16[1,6144,2048]{2,1,0:T(8,128)(2,1)S(1)} %copy-done.1), custom_call_target="tpu_custom_call" | custom-call | tf_op jit(solution)/shard_map/gate/pallas_call | solution.py:187
  21.8 0.0 copy-done.2
  21.8 0.0 copy-start
  21.8 4.4 %hidden.1.refs_0_ = bf16[16,2048]{1,0:T(8,128)(2,1)S(1)} custom-call(bf16[32,3072]{1,0:T(8,128)(2,1)S(1)} %merge.1.rows_ref, bf16[1,6144,2048]{2,1,0:T(8,128)(2,1)S(1)} %copy-done.2, f32[16,2048]{1,0:T(8,128)S(1)} %gate.1.gate_ref), custom_call_target="tpu_custom_call" | custom-call | flops 199999995904 | tf_op jit(solution)/shard_map/hidden/pallas_call | solution.py:188
  26.2 0.7 %collective-permute-start = (bf16[16,2048]{1,0:T(8,128)(2,1)S(1)}, bf16[16,2048]{1,0:T(8,128)(2,1)S(1)}, u32[]{:S(2)}, u32[]{:S(2)}) collective-permute-start(bf16[16,2048]{1,0:T(8,128)(2,1)S(1)} %hidden.1.refs_0_), channel_id=1, source_target_pairs={{0,2},{2,4},{4,6},{6,7},{7,5},{5,3},{3,1},{1,0},{8,10},{10,12},{12... | collective-permute-start | bytes 196616 | tf_op jit(solution)/shard_map/ppermute | solution.py:204
  26.9 1.3 %collective-permute-start.4 = (bf16[16,2048]{1,0:T(8,128)(2,1)S(1)}, bf16[16,2048]{1,0:T(8,128)(2,1)S(1)}, u32[]{:S(2)}, u32[]{:S(2)}) collective-permute-start(bf16[16,2048]{1,0:T(8,128)(2,1)S(1)} %hidden.1.refs_0_), channel_id=1, source_target_pairs={{0,1},{2,0},{4,2},{6,4},{7,6},{5,7},{3,5},{1,3},{8,9},{10,8},{12,1... | collective-permute-start | bytes 196616 | tf_op jit(solution)/shard_map/ppermute | solution.py:206
  28.3 2.2 %collective-permute-done.refs_1_ = bf16[16,2048]{1,0:T(8,128)(2,1)S(1)} collective-permute-done((bf16[16,2048]{1,0:T(8,128)(2,1)S(1)}, bf16[16,2048]{1,0:T(8,128)(2,1)S(1)}, u32[]{:S(2)}, u32[]{:S(2)}) %collective-permute-start) | collective-permute-done | bytes 65568 | tf_op jit(solution)/shard_map/ppermute | solution.py:204
  30.5 0.7 %collective-permute-start.1 = (bf16[16,2048]{1,0:T(8,128)(2,1)S(1)}, bf16[16,2048]{1,0:T(8,128)(2,1)S(1)}, u32[]{:S(2)}, u32[]{:S(2)}) collective-permute-start(bf16[16,2048]{1,0:T(8,128)(2,1)S(1)} %collective-permute-done.refs_1_), channel_id=1, source_target_pairs={{0,2},{2,4},{4,6},{6,7},{7,5},{5,3},{3,1},{1,0},{8,10},{10,12},{12... | collective-permute-start | bytes 196616 | tf_op jit(solution)/shard_map/ppermute | solution.py:204
  31.2 0.0 collective-permute-done.4.refs_2_
  31.2 1.3 %collective-permute-start.5 = (bf16[16,2048]{1,0:T(8,128)(2,1)S(1)}, bf16[16,2048]{1,0:T(8,128)(2,1)S(1)}, u32[]{:S(2)}, u32[]{:S(2)}) collective-permute-start(bf16[16,2048]{1,0:T(8,128)(2,1)S(1)} %collective-permute-done.4.refs_2_), channel_id=1, source_target_pairs={{0,1},{2,0},{4,2},{6,4},{7,6},{5,7},{3,5},{1,3},{8,9},{10,8},{12,1... | collective-permute-start | bytes 196616 | tf_op jit(solution)/shard_map/ppermute | solution.py:206
  32.5 2.6 %collective-permute-done.1.refs_3_ = bf16[16,2048]{1,0:T(8,128)(2,1)S(1)} collective-permute-done((bf16[16,2048]{1,0:T(8,128)(2,1)S(1)}, bf16[16,2048]{1,0:T(8,128)(2,1)S(1)}, u32[]{:S(2)}, u32[]{:S(2)}) %collective-permute-start.1) | collective-permute-done | bytes 65568 | tf_op jit(solution)/shard_map/ppermute | solution.py:204
  35.1 0.4 collective-permute-start.2
  35.5 0.3 collective-permute-done.5.refs_4_
  35.8 1.3 %collective-permute-start.6 = (bf16[16,2048]{1,0:T(8,128)(2,1)S(1)}, bf16[16,2048]{1,0:T(8,128)(2,1)S(1)}, u32[]{:S(2)}, u32[]{:S(2)}) collective-permute-start(bf16[16,2048]{1,0:T(8,128)(2,1)S(1)} %collective-permute-done.5.refs_4_), channel_id=1, source_target_pairs={{0,1},{2,0},{4,2},{6,4},{7,6},{5,7},{3,5},{1,3},{8,9},{10,8},{12,1... | collective-permute-start | bytes 196616 | tf_op jit(solution)/shard_map/ppermute | solution.py:206
  37.2 2.4 %collective-permute-done.2.refs_0_ = bf16[16,2048]{1,0:T(8,128)(2,1)S(1)} collective-permute-done((bf16[16,2048]{1,0:T(8,128)(2,1)S(1)}, bf16[16,2048]{1,0:T(8,128)(2,1)S(1)}, u32[]{:S(2)}, u32[]{:S(2)}) %collective-permute-start.2) | collective-permute-done | bytes 65568 | tf_op jit(solution)/shard_map/ppermute | solution.py:204
  39.6 0.4 collective-permute-start.3
  40.0 0.0 copy-done
  40.0 4.2 %down.3.refs_3_ = f32[768,16]{1,0:T(8,128)S(1)} custom-call(bf16[16,2048]{1,0:T(8,128)(2,1)S(1)} %hidden.1.refs_0_, bf16[16,2048]{1,0:T(8,128)(2,1)S(1)} %collective-permute-done.refs_1_, bf16[16,2048]{1,0:T(8,128)(2,1)S(1)} %collective-permute-done.4.refs_2_, bf16[16,2048]{1,0:T(8,128)(2,1)S(1)} %collective-permute-done.1.refs_3_, ...), custom_call_target="tpu_custom_call" | custom-call | tf_op jit(solution)/shard_map/down/pallas_call | solution.py:196
  44.2 0.0 collective-permute-done.6.refs_1_
  44.2 1.8 %down.4.refs_2_ = f32[768,16]{1,0:T(8,128)S(1)} custom-call(bf16[16,2048]{1,0:T(8,128)(2,1)S(1)} %collective-permute-done.2.refs_0_, bf16[16,2048]{1,0:T(8,128)(2,1)S(1)} %collective-permute-done.6.refs_1_, bf16[1,768,16384]{2,1,0:T(8,128)(2,1)S(1)} %copy-done, f32[768,16]{1,0:T(8,128)S(1)} %down.3.refs_3_), custom_call_target="tpu_custom_call" | custom-call | tf_op jit(solution)/shard_map/down/pallas_call | solution.py:196
  46.0 0.0 collective-permute-done.3.refs_0_
  46.0 1.0 %down.5 = f32[8,2,768]{2,1,0:T(2,128)S(1)} custom-call(bf16[16,2048]{1,0:T(8,128)(2,1)S(1)} %collective-permute-done.3.refs_0_, bf16[1,768,16384]{2,1,0:T(8,128)(2,1)S(1)} %copy-done, f32[768,16]{1,0:T(8,128)S(1)} %down.4.refs_2_), custom_call_target="tpu_custom_call" | custom-call | tf_op jit(solution)/shard_map/down/pallas_call | solution.py:196
  47.0 9.8 %all_to_all.11.own_ref = f32[8,2,768]{2,1,0:T(2,128)S(1)} all-to-all(f32[8,2,768]{2,1,0:T(2,128)S(1)} %down.5), channel_id=1, replica_groups=mesh['group'=2,'expert'=2,'tile'=8] {'tile'}, dimensions={0} | all-to-all | bytes 98304 | tf_op jit(solution)/shard_map/all_to_all | solution.py:213
  56.8 0.0 collective-permute-start.7
  56.8 1.2 %collective-permute-done.7.other_ref = f32[8,2,768]{2,1,0:T(2,128)S(1)} collective-permute-done((f32[8,2,768]{2,1,0:T(2,128)S(1)}, f32[8,2,768]{2,1,0:T(2,128)S(1)}, u32[]{:S(2)}, u32[]{:S(2)}) %collective-permute-start.7) | collective-permute-done | bytes 49184 | tf_op jit(solution)/shard_map/ppermute | solution.py:171
  58.0 0.7 %combine.1 = bf16[4,3072]{1,0:T(4,128)(2,1)} custom-call(f32[8,2,768]{2,1,0:T(2,128)S(1)} %all_to_all.11.own_ref, f32[8,2,768]{2,1,0:T(2,128)S(1)} %collective-permute-done.7.other_ref, f32[6,4,128]{2,1,0:T(4,128)S(1)} %get-tuple-element.8.table_ref), custom_call_target="tpu_custom_call" | custom-call | tf_op jit(solution)/shard_map/combine/pallas_call | solution.py:214
  (1 shorter events, 0.0 us)
Async XLA Ops:
  0.0 17.5 %copy-start.1 = (bf16[1,6144,2048]{2,1,0:T(8,128)(2,1)S(1)}, bf16[1,6144,2048]{2,1,0:T(8,128)(2,1)}, u32[]{:S(2)}) copy-start(bf16[1,6144,2048]{2,1,0:T(8,128)(2,1)} %w_ref.2) | copy-start | bytes 75497472
  1.0 20.8 %copy-start.2 = (bf16[1,6144,2048]{2,1,0:T(8,128)(2,1)S(1)}, bf16[1,6144,2048]{2,1,0:T(8,128)(2,1)}, u32[]{:S(2)}) copy-start(bf16[1,6144,2048]{2,1,0:T(8,128)(2,1)} %w_ref.3) | copy-start | bytes 75497472
  21.8 18.2 %copy-start = (bf16[1,768,16384]{2,1,0:T(8,128)(2,1)S(1)}, bf16[1,768,16384]{2,1,0:T(8,128)(2,1)}, u32[]{:S(2)}) copy-start(bf16[1,768,16384]{2,1,0:T(8,128)(2,1)} %refs_1_.1) | copy-start | bytes 75497472
  26.2 4.3 %collective-permute-start = (bf16[16,2048]{1,0:T(8,128)(2,1)S(1)}, bf16[16,2048]{1,0:T(8,128)(2,1)S(1)}, u32[]{:S(2)}, u32[]{:S(2)}) collective-permute-start(bf16[16,2048]{1,0:T(8,128)(2,1)S(1)} %hidden.1.refs_0_), channel_id=1, source_target_pairs={{0,2},{2,4},{4,6},{6,7},{7,5},{5,3},{3,1},{1,0},{8,10},{10,12},{12... | collective-permute-start | bytes 196616 | tf_op jit(solution)/shard_map/ppermute | solution.py:204
  26.9 4.3 %collective-permute-start.4 = (bf16[16,2048]{1,0:T(8,128)(2,1)S(1)}, bf16[16,2048]{1,0:T(8,128)(2,1)S(1)}, u32[]{:S(2)}, u32[]{:S(2)}) collective-permute-start(bf16[16,2048]{1,0:T(8,128)(2,1)S(1)} %hidden.1.refs_0_), channel_id=1, source_target_pairs={{0,1},{2,0},{4,2},{6,4},{7,6},{5,7},{3,5},{1,3},{8,9},{10,8},{12,1... | collective-permute-start | bytes 196616 | tf_op jit(solution)/shard_map/ppermute | solution.py:206
  30.5 4.6 %collective-permute-start.1 = (bf16[16,2048]{1,0:T(8,128)(2,1)S(1)}, bf16[16,2048]{1,0:T(8,128)(2,1)S(1)}, u32[]{:S(2)}, u32[]{:S(2)}) collective-permute-start(bf16[16,2048]{1,0:T(8,128)(2,1)S(1)} %collective-permute-done.refs_1_), channel_id=1, source_target_pairs={{0,2},{2,4},{4,6},{6,7},{7,5},{5,3},{3,1},{1,0},{8,10},{10,12},{12... | collective-permute-start | bytes 196616 | tf_op jit(solution)/shard_map/ppermute | solution.py:204
  31.2 4.6 %collective-permute-start.5 = (bf16[16,2048]{1,0:T(8,128)(2,1)S(1)}, bf16[16,2048]{1,0:T(8,128)(2,1)S(1)}, u32[]{:S(2)}, u32[]{:S(2)}) collective-permute-start(bf16[16,2048]{1,0:T(8,128)(2,1)S(1)} %collective-permute-done.4.refs_2_), channel_id=1, source_target_pairs={{0,1},{2,0},{4,2},{6,4},{7,6},{5,7},{3,5},{1,3},{8,9},{10,8},{12,1... | collective-permute-start | bytes 196616 | tf_op jit(solution)/shard_map/ppermute | solution.py:206
  35.1 4.4 %collective-permute-start.2 = (bf16[16,2048]{1,0:T(8,128)(2,1)S(1)}, bf16[16,2048]{1,0:T(8,128)(2,1)S(1)}, u32[]{:S(2)}, u32[]{:S(2)}) collective-permute-start(bf16[16,2048]{1,0:T(8,128)(2,1)S(1)} %collective-permute-done.1.refs_3_), channel_id=1, source_target_pairs={{0,2},{2,4},{4,6},{6,7},{7,5},{5,3},{3,1},{1,0},{8,10},{10,12},{12... | collective-permute-start | bytes 196616 | tf_op jit(solution)/shard_map/ppermute | solution.py:204
  35.8 8.4 %collective-permute-start.6 = (bf16[16,2048]{1,0:T(8,128)(2,1)S(1)}, bf16[16,2048]{1,0:T(8,128)(2,1)S(1)}, u32[]{:S(2)}, u32[]{:S(2)}) collective-permute-start(bf16[16,2048]{1,0:T(8,128)(2,1)S(1)} %collective-permute-done.5.refs_4_), channel_id=1, source_target_pairs={{0,1},{2,0},{4,2},{6,4},{7,6},{5,7},{3,5},{1,3},{8,9},{10,8},{12,1... | collective-permute-start | bytes 196616 | tf_op jit(solution)/shard_map/ppermute | solution.py:206
  39.6 6.4 %collective-permute-start.3 = (bf16[16,2048]{1,0:T(8,128)(2,1)S(1)}, bf16[16,2048]{1,0:T(8,128)(2,1)S(1)}, u32[]{:S(2)}, u32[]{:S(2)}) collective-permute-start(bf16[16,2048]{1,0:T(8,128)(2,1)S(1)} %collective-permute-done.2.refs_0_), channel_id=1, source_target_pairs={{0,2},{2,4},{4,6},{6,7},{7,5},{5,3},{3,1},{1,0},{8,10},{10,12},{12... | collective-permute-start | bytes 196616 | tf_op jit(solution)/shard_map/ppermute | solution.py:204
  56.8 1.2 %collective-permute-start.7 = (f32[8,2,768]{2,1,0:T(2,128)S(1)}, f32[8,2,768]{2,1,0:T(2,128)S(1)}, u32[]{:S(2)}, u32[]{:S(2)}) collective-permute-start(f32[8,2,768]{2,1,0:T(2,128)S(1)} %all_to_all.11.own_ref), channel_id=1, source_target_pairs={{0,8},{8,0},{1,9},{9,1},{2,10},{10,2},{3,11},{11,3},{4,12},{12,4},... | collective-permute-start | bytes 147464 | tf_op jit(solution)/shard_map/ppermute | solution.py:171

commit v5 on v4

--- a/solution.py
+++ b/solution.py
@@ -120,6 +120,7 @@
     out_ref = rest[-1]
     me = lax.axis_index("tile")
     slots, width = blocks[0].shape
+    high = me // (len(order) // 2)
     part = 256
     starts = []
     for step in steps:
@@ -140,20 +141,43 @@
             out_ref[rows, :] = total
         else:
             total = total.T
-            for t in range(out_ref.shape[0]):
-                out_ref[t, :, rows] = total[t * SLOTS:(t + 1) * SLOTS, :]
-
-
-def combine_kernel(own_ref, other_ref, table_ref, out_ref):
-    mine = lax.axis_index("expert")
-    halves, features = own_ref.shape[0] // 2, own_ref.shape[2]
+            keep_ref, send_ref = rest[-2:]
+            for t in range(keep_ref.shape[0]):
+                low_rows = total[t * SLOTS:(t + 1) * SLOTS, :]
+                high_rows = total[slots // 2 + t * SLOTS:slots // 2 + (t + 1) * SLOTS, :]
+                keep_ref[t, :, rows] = jnp.where(high == 0, low_rows, high_rows)
+                send_ref[t, :, rows] = jnp.where(high == 0, high_rows, low_rows)
+
+
+def core_kernel(kept_ref, got_ref, keep_ref, send_ref):
+    swap = lax.axis_index("tile") // 4 != lax.axis_index("expert")
+    kept, got = kept_ref[...], got_ref[...]
+    keep_ref[...] = jnp.where(swap, got, kept)
+    send_ref[...] = jnp.where(swap, kept, got)
+
+
+def split_kernel(bit, kept_ref, got_ref, keep_ref, send_ref):
+    mine = (lax.axis_index("tile") // bit) % 2
+    for i, ref in enumerate((kept_ref, got_ref)):
+        n = ref.shape[0] // 2
+        for j in range(n):
+            low, high = ref[j], ref[n + j]
+            keep_ref[j, i] = jnp.where(mine == 0, low, high)
+            send_ref[j, i] = jnp.where(mine == 0, high, low)
+
+
+def combine_kernel(kept_ref, got_ref, table_ref, out_ref):
+    me, mine = lax.axis_index("tile"), lax.axis_index("expert")
+    features = kept_ref.shape[-1]
     weight = [table_ref[e * (1 + SLOTS)][:, :1] for e in range(2)]
     inside = [[table_ref[e * (1 + SLOTS) + 1 + c][:, :1] for c in range(SLOTS)] for e in range(2)]
-    for i in range(halves):
-        own, other = own_ref[mine * halves + i], other_ref[mine * halves + i]
+    for i in range(4):
+        far = (me // 2) % 2 ^ i // 2
+        kept, got = kept_ref[0, far], got_ref[0, far]
+        parts = jnp.where(me % 2 == i % 2, kept, got)
         mixed = jnp.zeros((out_ref.shape[0], features), jnp.float32)
         for e in range(2):
-            both = jnp.where(mine == e, own, other)
+            both = jnp.where(mine == e, parts[0], parts[1])
             for c in range(SLOTS):
                 value = (weight[e] * both[c:c + 1]).astype(jnp.bfloat16).astype(jnp.float32)
                 mixed = mixed + jnp.where(inside[e][c] != 0.0, value, 0.0)
@@ -166,6 +190,9 @@
     width, features = w_gate.shape[2], w_down.shape[1]
     slots = tiles * SLOTS
     routes, gates = routes.T, gates.T
+
+    def swap(x, bit):
+        return lax.ppermute(x, "tile", [(t, t ^ bit) for t in range(tiles)])
 
     def to_core(x):
         return lax.ppermute(x, "expert", [(0, 1), (1, 0)])
@@ -188,11 +215,11 @@
     hidden = call(hidden_kernel, "hidden", bf16(slots, width), [VMEM] * 3, 4 * MIB, 200e-6)(x, in_vmem(w_up), gate)
     order = list(range(0, tiles, 2)) + list(range(tiles - 1, 0, -2))
     ahead = [(t, order[(i + 1) % tiles]) for i, t in enumerate(order)]
-    back = [(t, order[i - 1]) for i, t in enumerate(order)]
+    behind = [(t, order[i - 1]) for i, t in enumerate(order)]
 
     def down(total, steps, blocks):
         first, last = total is None, -(tiles // 2) in steps
-        out = f32(tiles, SLOTS, features) if last else f32(features, slots)
+        out = (f32(tiles // 2, SLOTS, features),) * 2 if last else f32(features, slots)
         return call(
             functools.partial(down_kernel, steps, order, first, last), "down", out,
             [VMEM] * (len(blocks) + 2 - first), 8 * MIB, 0e-6,
@@ -203,15 +230,26 @@
     for i in range(1, tiles // 2 + 1):
         below = lax.ppermute(below, "tile", ahead)
         if 2 * i < tiles:
-            above = lax.ppermute(above, "tile", back)
-        if i >= 3:
+            above = lax.ppermute(above, "tile", behind)
+        if i >= 2:
             total, steps, blocks = down(total, steps, blocks), [], []
+            total, below, above = lax.optimization_barrier((total, below, above))
         steps, blocks = steps + [-i], blocks + [below]
         if 2 * i < tiles:
             steps, blocks = steps + [i], blocks + [above]
     result = down(total, steps, blocks)
-    back = lax.all_to_all(result, "tile", split_axis=0, concat_axis=0, tiled=True)
-    return call(combine_kernel, "combine", bf16(rows, half_width), [VMEM] * 3, 4 * MIB)(back, to_core(back), table)
+    keep, send = result
+    keep, send = call(core_kernel, "core", (f32(*keep.shape),) * 2, [VMEM] * 2, 4 * MIB)(keep, swap(send, 4))
+    got = to_core(send)
+    keep, send = call(
+        functools.partial(split_kernel, 2), "split", (f32(2, 2, SLOTS, features),) * 2, [VMEM] * 2, 4 * MIB
+    )(keep, got)
+    got = swap(send, 2)
+    keep, send = call(
+        functools.partial(split_kernel, 1), "split", (f32(1, 2, 2, SLOTS, features),) * 2, [VMEM] * 2, 4 * MIB
+    )(keep, got)
+    got = swap(send, 1)
+    return call(combine_kernel, "combine", bf16(rows, half_width), [VMEM] * 3, 4 * MIB)(keep, got, table)
 
 
 def local_gathered(tokens, routes, gates, w_gate, w_up, w_down):
@@ -268,5 +306,5 @@
         P("expert", "tile", None),
     )
     out_specs = P(("group", "tile"), "expert")
-    local = local_direct if mesh.shape["tile"] <= 8 else local_gathered
+    local = local_direct if mesh.shape["tile"] == 8 else local_gathered
     return jax.shard_map(local, mesh=mesh, in_specs=in_specs, out_specs=out_specs, check_vma=False)

time: 59 us -> 61.4 us (1.041)
  blocking collectives: 26.2 us -> 16.4 us
  waiting for transfers between devices: 8.82 us -> 18.1 us
  starting transfers between devices: 6.18 us -> 8.99 us
    ppermute x3 -> x6, waiting for transfers between devices: 0.33 us -> 14.1 us  [the longest x3 10.3 us: swap(): return lax.ppermute(x, 'tile', [(t, t ^ bit) for t in range(tiles)])]
    all_to_all x1 -> x0, blocking collectives: 9.8 us -> none  [local_direct(): lax.all_to_all(result, 'tile', split_axis=0, concat_axis=0, tiled=True)]
    ppermute x4, waiting for transfers between devices: 7.26 us -> 2.82 us  [local_direct(): below = lax.ppermute(below, 'tile', ahead)]
    ppermute x4, starting transfers between devices: 2.17 us -> 5.26 us  [local_direct(): below = lax.ppermute(below, 'tile', ahead)]
    ppermute x3 -> x6, starting transfers between devices: 4 us -> 3.66 us  [the longest x3 2.22 us: swap(): return lax.ppermute(x, 'tile', [(t, t ^ bit) for t in range(tiles)])]
    pallas_call x3 -> x4, Pallas kernels: 6.96 us -> 7.07 us  [down(): call(functools.partial(down_kernel, steps, order, first, last), 'down', o...]
  transfers between devices with their start and end apart: 8 -> 11, of which waited for: 5 -> 9; matrix products, arithmetic and copies ran while one was open for 0% -> 0% of each run, Pallas kernels for 10% -> 10%
where the time goes in v5:
time: 61.4 us; the launch traced here: 61.2 us
  waiting for transfers between devices  18.1 us (29%)
  Pallas kernels  17.6 us (29%)
  blocking collectives  16.4 us (27%)
  starting transfers between devices  8.99 us (15%)
    all_to_all x1, blocking collectives, local_direct(): lax.all_to_all(sends, ('expert', 'tile'), split_axis=0, concat_axis=0, ti...  16.4 us
    ppermute x3, waiting for transfers between devices, swap(): return lax.ppermute(x, 'tile', [(t, t ^ bit) for t in range(tiles)])  10.3 us
    pallas_call x4, Pallas kernels, down(): call(functools.partial(down_kernel, steps, order, first, last), 'down', o...  7.07 us
    ppermute x4, starting transfers between devices, local_direct(): below = lax.ppermute(below, 'tile', ahead)  5.26 us
    pallas_call x1, Pallas kernels, local_direct(): call(hidden_kernel, 'hidden', bf16(slots, width), [VMEM] * 3, 4 * MIB, 0....  4.44 us
    pallas_call x1, Pallas kernels, local_direct(): call(gate_kernel, 'gate', f32(slots, width), [VMEM] * 2, 4 * MIB, 0.0)  4.27 us
    ppermute x3, waiting for transfers between devices, local_direct(): above = lax.ppermute(above, 'tile', behind)  3.74 us
    ppermute x4, waiting for transfers between devices, local_direct(): below = lax.ppermute(below, 'tile', ahead)  2.82 us
  transfers between devices with their start and end apart: 11, of which 9 were waited for; matrix products, arithmetic and copies ran while one was open for 0% of the time, Pallas kernels for 10%

profile of v5, /device:TPU:0, one launch (start us, length us, event | category | flops | bytes accessed | tf_op | source)
XLA Modules:
  0.0 61.2 jit_solution(2603351851828223632)
XLA Ops:
  0.0 1.0 %dispatch.1 = (bf16[16,2,3072]{2,1,0:T(2,128)(2,1)S(1)}, f32[6,4,128]{2,1,0:T(4,128)S(1)}) custom-call(bf16[4,3072]{1,0:T(4,128)(2,1)} %tokens_hbm.1, s32[2,4]{1,0:T(2,128)} %bitcast.2, f32[2,4]{1,0:T(2,128)} %bitcast.3), custom_call_target="tpu_custom_call" | custom-call | flops 599999971328 | tf_op jit(solution)/shard_map/dispatch/pallas_call | solution.py:202
  1.0 0.0 copy-start.2
  1.0 16.4 %all_to_all.5.blocks_ref = bf16[16,2,3072]{2,1,0:T(2,128)(2,1)S(1)} all-to-all(bf16[16,2,3072]{2,1,0:T(2,128)(2,1)S(1)} %get-tuple-element.23), channel_id=1, replica_groups=mesh['group'=2,'expert'=2,'tile'=8] {'expert','tile'}, dimensions={0} | all-to-all | bytes 393216 | tf_op jit(solution)/shard_map/all_to_all | solution.py:212
  17.5 0.0 copy-done.1
  17.5 4.3 %gate.1.gate_ref = f32[16,2048]{1,0:T(8,128)S(1)} custom-call(bf16[32,3072]{1,0:T(8,128)(2,1)S(1)} %merge.1.rows_ref, bf16[1,6144,2048]{2,1,0:T(8,128)(2,1)S(1)} %copy-done.1), custom_call_target="tpu_custom_call" | custom-call | tf_op jit(solution)/shard_map/gate/pallas_call | solution.py:214
  21.8 4.4 %hidden.1.refs_0_ = bf16[16,2048]{1,0:T(8,128)(2,1)S(1)} custom-call(bf16[32,3072]{1,0:T(8,128)(2,1)S(1)} %merge.1.rows_ref, bf16[1,6144,2048]{2,1,0:T(8,128)(2,1)S(1)} %copy-done.2, f32[16,2048]{1,0:T(8,128)S(1)} %gate.1.gate_ref), custom_call_target="tpu_custom_call" | custom-call | flops 199999995904 | tf_op jit(solution)/shard_map/hidden/pallas_call | solution.py:215
  26.2 0.6 collective-permute-start.1
  26.8 1.5 %collective-permute-start = (bf16[16,2048]{1,0:T(8,128)(2,1)S(1)}, bf16[16,2048]{1,0:T(8,128)(2,1)S(1)}, u32[]{:S(2)}, u32[]{:S(2)}) collective-permute-start(bf16[16,2048]{1,0:T(8,128)(2,1)S(1)} %hidden.1.refs_0_), channel_id=1, source_target_pairs={{0,2},{2,4},{4,6},{6,7},{7,5},{5,3},{3,1},{1,0},{8,10},{10,12},{12... | collective-permute-start | bytes 196616 | tf_op jit(solution)/shard_map/ppermute | solution.py:231
  28.3 2.2 %collective-permute-done.1.refs_2_ = bf16[16,2048]{1,0:T(8,128)(2,1)S(1)} collective-permute-done((bf16[16,2048]{1,0:T(8,128)(2,1)S(1)}, bf16[16,2048]{1,0:T(8,128)(2,1)S(1)}, u32[]{:S(2)}, u32[]{:S(2)}) %collective-permute-start.1) | collective-permute-done | bytes 65568 | tf_op jit(solution)/shard_map/ppermute | solution.py:233
  30.5 0.6 collective-permute-start.3
  31.1 0.0 collective-permute-done.refs_1_
  31.1 1.5 %collective-permute-start.2 = (bf16[16,2048]{1,0:T(8,128)(2,1)S(1)}, bf16[16,2048]{1,0:T(8,128)(2,1)S(1)}, u32[]{:S(2)}, u32[]{:S(2)}) collective-permute-start(bf16[16,2048]{1,0:T(8,128)(2,1)S(1)} %collective-permute-done.refs_1_), channel_id=1, source_target_pairs={{0,2},{2,4},{4,6},{6,7},{7,5},{5,3},{3,1},{1,0},{8,10},{10,12},{12... | collective-permute-start | bytes 196616 | tf_op jit(solution)/shard_map/ppermute | solution.py:231
  32.5 2.6 %down.4.refs_3_ = f32[768,16]{1,0:T(8,128)S(1)} custom-call(bf16[16,2048]{1,0:T(8,128)(2,1)S(1)} %hidden.1.refs_0_, bf16[16,2048]{1,0:T(8,128)(2,1)S(1)} %collective-permute-done.refs_1_, bf16[16,2048]{1,0:T(8,128)(2,1)S(1)} %collective-permute-done.1.refs_2_, bf16[1,768,16384]{2,1,0:T(8,128)(2,1)S(1)} %copy-done), custom_call_target="tpu_custom_call" | custom-call | tf_op jit(solution)/shard_map/down/pallas_call | solution.py:223
  35.1 0.2 collective-permute-done.2.refs_0_
  35.3 1.7 %collective-permute-start.4 = (bf16[16,2048]{1,0:T(8,128)(2,1)S(1)}, bf16[16,2048]{1,0:T(8,128)(2,1)S(1)}, u32[]{:S(2)}, u32[]{:S(2)}) collective-permute-start(bf16[16,2048]{1,0:T(8,128)(2,1)S(1)} %collective-permute-done.2.refs_0_), channel_id=1, source_target_pairs={{0,2},{2,4},{4,6},{6,7},{7,5},{5,3},{3,1},{1,0},{8,10},{10,12},{12... | collective-permute-start | bytes 196616 | tf_op jit(solution)/shard_map/ppermute | solution.py:231
  37.1 0.3 collective-permute-start.5
  37.4 1.8 %down.5.refs_3_ = f32[768,16]{1,0:T(8,128)S(1)} custom-call(bf16[16,2048]{1,0:T(8,128)(2,1)S(1)} %collective-permute-done.2.refs_0_, bf16[16,2048]{1,0:T(8,128)(2,1)S(1)} %collective-permute-done.3.refs_1_, bf16[1,768,16384]{2,1,0:T(8,128)(2,1)S(1)} %copy-done, f32[768,16]{1,0:T(8,128)S(1)} %down.4.refs_3_), custom_call_target="tpu_custom_call" | custom-call | tf_op jit(solution)/shard_map/down/pallas_call | solution.py:223
  39.1 0.7 %collective-permute-done.4.refs_0_ = bf16[16,2048]{1,0:T(8,128)(2,1)S(1)} collective-permute-done((bf16[16,2048]{1,0:T(8,128)(2,1)S(1)}, bf16[16,2048]{1,0:T(8,128)(2,1)S(1)}, u32[]{:S(2)}, u32[]{:S(2)}) %collective-permute-start.4) | collective-permute-done | bytes 65568 | tf_op jit(solution)/shard_map/ppermute | solution.py:231
  39.8 1.5 %collective-permute-done.5.refs_1_ = bf16[16,2048]{1,0:T(8,128)(2,1)S(1)} collective-permute-done((bf16[16,2048]{1,0:T(8,128)(2,1)S(1)}, bf16[16,2048]{1,0:T(8,128)(2,1)S(1)}, u32[]{:S(2)}, u32[]{:S(2)}) %collective-permute-start.5) | collective-permute-done | bytes 65568 | tf_op jit(solution)/shard_map/ppermute | solution.py:233
  41.3 0.6 collective-permute-start.6
  41.9 1.8 %down.6.refs_2_ = f32[768,16]{1,0:T(8,128)S(1)} custom-call(bf16[16,2048]{1,0:T(8,128)(2,1)S(1)} %collective-permute-done.4.refs_0_, bf16[16,2048]{1,0:T(8,128)(2,1)S(1)} %collective-permute-done.5.refs_1_, bf16[1,768,16384]{2,1,0:T(8,128)(2,1)S(1)} %copy-done, f32[768,16]{1,0:T(8,128)S(1)} %down.5.refs_3_), custom_call_target="tpu_custom_call" | custom-call | tf_op jit(solution)/shard_map/down/pallas_call | solution.py:223
  43.7 1.9 %collective-permute-done.6.refs_0_ = bf16[16,2048]{1,0:T(8,128)(2,1)S(1)} collective-permute-done((bf16[16,2048]{1,0:T(8,128)(2,1)S(1)}, bf16[16,2048]{1,0:T(8,128)(2,1)S(1)}, u32[]{:S(2)}, u32[]{:S(2)}) %collective-permute-start.6) | collective-permute-done | bytes 65568 | tf_op jit(solution)/shard_map/ppermute | solution.py:231
  45.6 1.0 %down.7 = (f32[4,2,768]{2,1,0:T(2,128)S(1)}, f32[4,2,768]{2,1,0:T(2,128)S(1)}) custom-call(bf16[16,2048]{1,0:T(8,128)(2,1)S(1)} %collective-permute-done.6.refs_0_, bf16[1,768,16384]{2,1,0:T(8,128)(2,1)S(1)} %copy-done, f32[768,16]{1,0:T(8,128)S(1)} %down.6.refs_2_), custom_call_target="tpu_custom_call" | custom-call | tf_op jit(solution)/shard_map/down/pallas_call | solution.py:223
  46.6 0.9 %collective-permute-start.7 = (f32[4,2,768]{2,1,0:T(2,128)S(1)}, f32[4,2,768]{2,1,0:T(2,128)S(1)}, u32[]{:S(2)}, u32[]{:S(2)}) collective-permute-start(f32[4,2,768]{2,1,0:T(2,128)S(1)} %get-tuple-element.33), channel_id=1, source_target_pairs={{0,4},{1,5},{2,6},{3,7},{4,0},{5,1},{6,2},{7,3},{8,12},{9,13},{10,... | collective-permute-start | bytes 73736 | tf_op jit(solution)/shard_map/ppermute | solution.py:195
  47.5 3.8 %collective-permute-done.7.got_ref = f32[4,2,768]{2,1,0:T(2,128)S(1)} collective-permute-done((f32[4,2,768]{2,1,0:T(2,128)S(1)}, f32[4,2,768]{2,1,0:T(2,128)S(1)}, u32[]{:S(2)}, u32[]{:S(2)}) %collective-permute-start.7) | collective-permute-done | bytes 24608 | tf_op jit(solution)/shard_map/ppermute | solution.py:195
  51.4 0.1 collective-permute-start.8
  51.5 1.2 %collective-permute-done.8.got_ref = f32[4,2,768]{2,1,0:T(2,128)S(1)} collective-permute-done((f32[4,2,768]{2,1,0:T(2,128)S(1)}, f32[4,2,768]{2,1,0:T(2,128)S(1)}, u32[]{:S(2)}, u32[]{:S(2)}) %collective-permute-start.8) | collective-permute-done | bytes 24608 | tf_op jit(solution)/shard_map/ppermute | solution.py:198
  52.6 0.9 %collective-permute-start.9 = (f32[2,2,2,768]{3,2,1,0:T(2,128)S(1)}, f32[2,2,2,768]{3,2,1,0:T(2,128)S(1)}, u32[]{:S(2)}, u32[]{:S(2)}) collective-permute-start(f32[2,2,2,768]{3,2,1,0:T(2,128)S(1)} %get-tuple-element.37), channel_id=1, source_target_pairs={{0,2},{1,3},{2,0},{3,1},{4,6},{5,7},{6,4},{7,5},{8,10},{9,11},{10,... | collective-permute-start | bytes 73736 | tf_op jit(solution)/shard_map/ppermute | solution.py:195
  53.6 3.0 %collective-permute-done.9.got_ref = f32[2,2,2,768]{3,2,1,0:T(2,128)S(1)} collective-permute-done((f32[2,2,2,768]{3,2,1,0:T(2,128)S(1)}, f32[2,2,2,768]{3,2,1,0:T(2,128)S(1)}, u32[]{:S(2)}, u32[]{:S(2)}) %collective-permute-start.9) | collective-permute-done | bytes 24608 | tf_op jit(solution)/shard_map/ppermute | solution.py:195
  56.6 0.4 collective-permute-start.10
  56.9 3.5 %collective-permute-done.10.got_ref = f32[1,2,2,2,768]{4,3,2,1,0:T(2,128)S(1)} collective-permute-done((f32[1,2,2,2,768]{4,3,2,1,0:T(2,128)S(1)}, f32[1,2,2,2,768]{4,3,2,1,0:T(2,128)S(1)}, u32[]{:S(2)}, u32[]{:S(2)}) %collective-permute-start.10) | collective-permute-done | bytes 24608 | tf_op jit(solution)/shard_map/ppermute | solution.py:195
  60.4 0.7 %combine.1 = bf16[4,3072]{1,0:T(4,128)(2,1)} custom-call(f32[1,2,2,2,768]{4,3,2,1,0:T(2,128)S(1)} %get-tuple-element.38.kept_ref, f32[1,2,2,2,768]{4,3,2,1,0:T(2,128)S(1)} %collective-permute-done.10.got_ref, f32[6,4,128]{2,1,0:T(4,128)S(1)} %get-tuple-element.40.table_ref), custom_call_target="tpu_custom_call" | custom-call | tf_op jit(solution)/shard_map/combine/pallas_call | solution.py:252
  (9 shorter events, 0.1 us)
Async XLA Ops:
  0.0 17.5 %copy-start.1 = (bf16[1,6144,2048]{2,1,0:T(8,128)(2,1)S(1)}, bf16[1,6144,2048]{2,1,0:T(8,128)(2,1)}, u32[]{:S(2)}) copy-start(bf16[1,6144,2048]{2,1,0:T(8,128)(2,1)} %w_ref.2) | copy-start | bytes 75497472
  1.0 20.8 %copy-start.2 = (bf16[1,6144,2048]{2,1,0:T(8,128)(2,1)S(1)}, bf16[1,6144,2048]{2,1,0:T(8,128)(2,1)}, u32[]{:S(2)}) copy-start(bf16[1,6144,2048]{2,1,0:T(8,128)(2,1)} %w_ref.3) | copy-start | bytes 75497472
  21.8 10.8 %copy-start = (bf16[1,768,16384]{2,1,0:T(8,128)(2,1)S(1)}, bf16[1,768,16384]{2,1,0:T(8,128)(2,1)}, u32[]{:S(2)}) copy-start(bf16[1,768,16384]{2,1,0:T(8,128)(2,1)} %refs_1_.1) | copy-start | bytes 75497472
  26.2 4.3 %collective-permute-start.1 = (bf16[16,2048]{1,0:T(8,128)(2,1)S(1)}, bf16[16,2048]{1,0:T(8,128)(2,1)S(1)}, u32[]{:S(2)}, u32[]{:S(2)}) collective-permute-start(bf16[16,2048]{1,0:T(8,128)(2,1)S(1)} %hidden.1.refs_0_), channel_id=1, source_target_pairs={{0,1},{2,0},{4,2},{6,4},{7,6},{5,7},{3,5},{1,3},{8,9},{10,8},{12,1... | collective-permute-start | bytes 196616 | tf_op jit(solution)/shard_map/ppermute | solution.py:233
  26.8 4.3 %collective-permute-start = (bf16[16,2048]{1,0:T(8,128)(2,1)S(1)}, bf16[16,2048]{1,0:T(8,128)(2,1)S(1)}, u32[]{:S(2)}, u32[]{:S(2)}) collective-permute-start(bf16[16,2048]{1,0:T(8,128)(2,1)S(1)} %hidden.1.refs_0_), channel_id=1, source_target_pairs={{0,2},{2,4},{4,6},{6,7},{7,5},{5,3},{3,1},{1,0},{8,10},{10,12},{12... | collective-permute-start | bytes 196616 | tf_op jit(solution)/shard_map/ppermute | solution.py:231
  30.5 4.6 %collective-permute-start.3 = (bf16[16,2048]{1,0:T(8,128)(2,1)S(1)}, bf16[16,2048]{1,0:T(8,128)(2,1)S(1)}, u32[]{:S(2)}, u32[]{:S(2)}) collective-permute-start(bf16[16,2048]{1,0:T(8,128)(2,1)S(1)} %collective-permute-done.1.refs_2_), channel_id=1, source_target_pairs={{0,1},{2,0},{4,2},{6,4},{7,6},{5,7},{3,5},{1,3},{8,9},{10,8},{12,1... | collective-permute-start | bytes 196616 | tf_op jit(solution)/shard_map/ppermute | solution.py:233
  31.1 4.3 %collective-permute-start.2 = (bf16[16,2048]{1,0:T(8,128)(2,1)S(1)}, bf16[16,2048]{1,0:T(8,128)(2,1)S(1)}, u32[]{:S(2)}, u32[]{:S(2)}) collective-permute-start(bf16[16,2048]{1,0:T(8,128)(2,1)S(1)} %collective-permute-done.refs_1_), channel_id=1, source_target_pairs={{0,2},{2,4},{4,6},{6,7},{7,5},{5,3},{3,1},{1,0},{8,10},{10,12},{12... | collective-permute-start | bytes 196616 | tf_op jit(solution)/shard_map/ppermute | solution.py:231
  35.3 4.5 %collective-permute-start.4 = (bf16[16,2048]{1,0:T(8,128)(2,1)S(1)}, bf16[16,2048]{1,0:T(8,128)(2,1)S(1)}, u32[]{:S(2)}, u32[]{:S(2)}) collective-permute-start(bf16[16,2048]{1,0:T(8,128)(2,1)S(1)} %collective-permute-done.2.refs_0_), channel_id=1, source_target_pairs={{0,2},{2,4},{4,6},{6,7},{7,5},{5,3},{3,1},{1,0},{8,10},{10,12},{12... | collective-permute-start | bytes 196616 | tf_op jit(solution)/shard_map/ppermute | solution.py:231
  37.1 4.3 %collective-permute-start.5 = (bf16[16,2048]{1,0:T(8,128)(2,1)S(1)}, bf16[16,2048]{1,0:T(8,128)(2,1)S(1)}, u32[]{:S(2)}, u32[]{:S(2)}) collective-permute-start(bf16[16,2048]{1,0:T(8,128)(2,1)S(1)} %collective-permute-done.3.refs_1_), channel_id=1, source_target_pairs={{0,1},{2,0},{4,2},{6,4},{7,6},{5,7},{3,5},{1,3},{8,9},{10,8},{12,1... | collective-permute-start | bytes 196616 | tf_op jit(solution)/shard_map/ppermute | solution.py:233
  41.3 4.3 %collective-permute-start.6 = (bf16[16,2048]{1,0:T(8,128)(2,1)S(1)}, bf16[16,2048]{1,0:T(8,128)(2,1)S(1)}, u32[]{:S(2)}, u32[]{:S(2)}) collective-permute-start(bf16[16,2048]{1,0:T(8,128)(2,1)S(1)} %collective-permute-done.4.refs_0_), channel_id=1, source_target_pairs={{0,2},{2,4},{4,6},{6,7},{7,5},{5,3},{3,1},{1,0},{8,10},{10,12},{12... | collective-permute-start | bytes 196616 | tf_op jit(solution)/shard_map/ppermute | solution.py:231
  46.6 4.8 %collective-permute-start.7 = (f32[4,2,768]{2,1,0:T(2,128)S(1)}, f32[4,2,768]{2,1,0:T(2,128)S(1)}, u32[]{:S(2)}, u32[]{:S(2)}) collective-permute-start(f32[4,2,768]{2,1,0:T(2,128)S(1)} %get-tuple-element.33), channel_id=1, source_target_pairs={{0,4},{1,5},{2,6},{3,7},{4,0},{5,1},{6,2},{7,3},{8,12},{9,13},{10,... | collective-permute-start | bytes 73736 | tf_op jit(solution)/shard_map/ppermute | solution.py:195
  51.4 1.3 %collective-permute-start.8 = (f32[4,2,768]{2,1,0:T(2,128)S(1)}, f32[4,2,768]{2,1,0:T(2,128)S(1)}, u32[]{:S(2)}, u32[]{:S(2)}) collective-permute-start(f32[4,2,768]{2,1,0:T(2,128)S(1)} %get-tuple-element.35), channel_id=1, source_target_pairs={{0,8},{8,0},{1,9},{9,1},{2,10},{10,2},{3,11},{11,3},{4,12},{12,4},... | collective-permute-start | bytes 73736 | tf_op jit(solution)/shard_map/ppermute | solution.py:198
  52.6 3.9 %collective-permute-start.9 = (f32[2,2,2,768]{3,2,1,0:T(2,128)S(1)}, f32[2,2,2,768]{3,2,1,0:T(2,128)S(1)}, u32[]{:S(2)}, u32[]{:S(2)}) collective-permute-start(f32[2,2,2,768]{3,2,1,0:T(2,128)S(1)} %get-tuple-element.37), channel_id=1, source_target_pairs={{0,2},{1,3},{2,0},{3,1},{4,6},{5,7},{6,4},{7,5},{8,10},{9,11},{10,... | collective-permute-start | bytes 73736 | tf_op jit(solution)/shard_map/ppermute | solution.py:195
  56.6 3.9 %collective-permute-start.10 = (f32[1,2,2,2,768]{4,3,2,1,0:T(2,128)S(1)}, f32[1,2,2,2,768]{4,3,2,1,0:T(2,128)S(1)}, u32[]{:S(2)}, u32[]{:S(2)}) collective-permute-start(f32[1,2,2,2,768]{4,3,2,1,0:T(2,128)S(1)} %get-tuple-element.39), channel_id=1, source_target_pairs={{0,1},{1,0},{2,3},{3,2},{4,5},{5,4},{6,7},{7,6},{8,9},{9,8},{10,11... | collective-permute-start | bytes 73736 | tf_op jit(solution)/shard_map/ppermute | solution.py:195

commit v6 on v4

--- a/solution.py
+++ b/solution.py
@@ -95,7 +95,7 @@
         body(pl.ds(pl.multiple_of(i * tile, tile), tile))
         return carry
 
-    lax.fori_loop(0, width // tile, step, 0)
+    lax.fori_loop(0, width // tile, step, 0, unroll=4)
 
 
 def gate_kernel(rows_ref, w_ref, out_ref):
@@ -188,7 +188,7 @@
     hidden = call(hidden_kernel, "hidden", bf16(slots, width), [VMEM] * 3, 4 * MIB, 200e-6)(x, in_vmem(w_up), gate)
     order = list(range(0, tiles, 2)) + list(range(tiles - 1, 0, -2))
     ahead = [(t, order[(i + 1) % tiles]) for i, t in enumerate(order)]
-    back = [(t, order[i - 1]) for i, t in enumerate(order)]
+    behind = [(t, order[i - 1]) for i, t in enumerate(order)]
 
     def down(total, steps, blocks):
         first, last = total is None, -(tiles // 2) in steps
@@ -203,9 +203,10 @@
     for i in range(1, tiles // 2 + 1):
         below = lax.ppermute(below, "tile", ahead)
         if 2 * i < tiles:
-            above = lax.ppermute(above, "tile", back)
-        if i >= 3:
+            above = lax.ppermute(above, "tile", behind)
+        if i >= 2:
             total, steps, blocks = down(total, steps, blocks), [], []
+            total, below, above = lax.optimization_barrier((total, below, above))
         steps, blocks = steps + [-i], blocks + [below]
         if 2 * i < tiles:
             steps, blocks = steps + [i], blocks + [above]
@@ -268,5 +269,5 @@
         P("expert", "tile", None),
     )
     out_specs = P(("group", "tile"), "expert")
-    local = local_direct if mesh.shape["tile"] <= 8 else local_gathered
+    local = local_direct if mesh.shape["tile"] == 8 else local_gathered
     return jax.shard_map(local, mesh=mesh, in_specs=in_specs, out_specs=out_specs, check_vma=False)

time: 59 us -> 56.3 us (0.954)
  Pallas kernels: 17.5 us -> 15.9 us
  waiting for transfers between devices: 8.82 us -> 7.81 us
  blocking collectives: 26.2 us -> 25.6 us
    ppermute x4, waiting for transfers between devices: 7.26 us -> 2.84 us  [local_direct(): below = lax.ppermute(below, 'tile', ahead)]
    ppermute x3, waiting for transfers between devices: 0.33 us -> 3.74 us  [local_direct(): above = lax.ppermute(above, 'tile', behind)]
    ppermute x4, starting transfers between devices: 2.17 us -> 5.3 us  [local_direct(): below = lax.ppermute(below, 'tile', ahead)]
    ppermute x3, starting transfers between devices: 4 us -> 1.4 us  [local_direct(): above = lax.ppermute(above, 'tile', behind)]
    pallas_call x1, Pallas kernels: 4.44 us -> 3.53 us  [local_direct(): call(hidden_kernel, 'hidden', bf16(slots, width), [VMEM] * 3, 4 * MIB, 0....]
    pallas_call x1, Pallas kernels: 4.27 us -> 3.52 us  [local_direct(): call(gate_kernel, 'gate', f32(slots, width), [VMEM] * 2, 4 * MIB, 0.0)]
    all_to_all x1, blocking collectives: 9.8 us -> 9.17 us  [local_direct(): lax.all_to_all(result, 'tile', split_axis=0, concat_axis=0, tiled=True)]
    pallas_call x3 -> x4, Pallas kernels: 6.96 us -> 7.07 us  [down(): call(functools.partial(down_kernel, steps, order, first, last), 'down', o...]
  transfers between devices with their start and end apart: 8 -> 8, of which waited for: 5 -> 6; matrix products, arithmetic and copies ran while one was open for 0% -> 0% of each run, Pallas kernels for 10% -> 11%
where the time goes in v6:
time: 56.3 us; the launch traced here: 56.1 us
  blocking collectives  25.6 us (45%)
  Pallas kernels  15.9 us (28%)
  waiting for transfers between devices  7.81 us (14%)
  starting transfers between devices  6.7 us (12%)
    all_to_all x1, blocking collectives, local_direct(): lax.all_to_all(sends, ('expert', 'tile'), split_axis=0, concat_axis=0, ti...  16.4 us
    all_to_all x1, blocking collectives, local_direct(): lax.all_to_all(result, 'tile', split_axis=0, concat_axis=0, tiled=True)  9.17 us
    pallas_call x4, Pallas kernels, down(): call(functools.partial(down_kernel, steps, order, first, last), 'down', o...  7.07 us
    ppermute x4, starting transfers between devices, local_direct(): below = lax.ppermute(below, 'tile', ahead)  5.3 us
    ppermute x3, waiting for transfers between devices, local_direct(): above = lax.ppermute(above, 'tile', behind)  3.74 us
    pallas_call x1, Pallas kernels, local_direct(): call(hidden_kernel, 'hidden', bf16(slots, width), [VMEM] * 3, 4 * MIB, 0....  3.53 us
    pallas_call x1, Pallas kernels, local_direct(): call(gate_kernel, 'gate', f32(slots, width), [VMEM] * 2, 4 * MIB, 0.0)  3.52 us
    ppermute x4, waiting for transfers between devices, local_direct(): below = lax.ppermute(below, 'tile', ahead)  2.84 us
  transfers between devices with their start and end apart: 8, of which 6 were waited for; matrix products, arithmetic and copies ran while one was open for 0% of the time, Pallas kernels for 11%

profile of v6, /device:TPU:0, one launch (start us, length us, event | category | flops | bytes accessed | tf_op | source)
XLA Modules:
  0.0 56.1 jit_solution(800074259134658094)
XLA Ops:
  0.0 0.0 copy-start.1
  0.0 1.0 %dispatch.1 = (bf16[16,2,3072]{2,1,0:T(2,128)(2,1)S(1)}, f32[6,4,128]{2,1,0:T(4,128)S(1)}) custom-call(bf16[4,3072]{1,0:T(4,128)(2,1)} %tokens_hbm.1, s32[2,4]{1,0:T(2,128)} %bitcast.2, f32[2,4]{1,0:T(2,128)} %bitcast.3), custom_call_target="tpu_custom_call" | custom-call | flops 599999971328 | tf_op jit(solution)/shard_map/dispatch/pallas_call | solution.py:175
  1.0 0.0 copy-start.2
  1.0 16.4 %all_to_all.10.blocks_ref = bf16[16,2,3072]{2,1,0:T(2,128)(2,1)S(1)} all-to-all(bf16[16,2,3072]{2,1,0:T(2,128)(2,1)S(1)} %get-tuple-element.15), channel_id=1, replica_groups=mesh['group'=2,'expert'=2,'tile'=8] {'expert','tile'}, dimensions={0} | all-to-all | bytes 393216 | tf_op jit(solution)/shard_map/all_to_all | solution.py:185
  17.5 0.0 copy-done.1
  17.5 3.5 %gate.1.gate_ref = f32[16,2048]{1,0:T(8,128)S(1)} custom-call(bf16[32,3072]{1,0:T(8,128)(2,1)S(1)} %merge.1.rows_ref, bf16[1,6144,2048]{2,1,0:T(8,128)(2,1)S(1)} %copy-done.1), custom_call_target="tpu_custom_call" | custom-call | tf_op jit(solution)/shard_map/gate/pallas_call | solution.py:187
  21.0 0.0 copy-done.2
  21.0 0.0 copy-start
  21.0 3.5 %hidden.1.refs_0_ = bf16[16,2048]{1,0:T(8,128)(2,1)S(1)} custom-call(bf16[32,3072]{1,0:T(8,128)(2,1)S(1)} %merge.1.rows_ref, bf16[1,6144,2048]{2,1,0:T(8,128)(2,1)S(1)} %copy-done.2, f32[16,2048]{1,0:T(8,128)S(1)} %gate.1.gate_ref), custom_call_target="tpu_custom_call" | custom-call | flops 199999995904 | tf_op jit(solution)/shard_map/hidden/pallas_call | solution.py:188
  24.6 0.6 %collective-permute-start.1 = (bf16[16,2048]{1,0:T(8,128)(2,1)S(1)}, bf16[16,2048]{1,0:T(8,128)(2,1)S(1)}, u32[]{:S(2)}, u32[]{:S(2)}) collective-permute-start(bf16[16,2048]{1,0:T(8,128)(2,1)S(1)} %hidden.1.refs_0_), channel_id=1, source_target_pairs={{0,1},{2,0},{4,2},{6,4},{7,6},{5,7},{3,5},{1,3},{8,9},{10,8},{12,1... | collective-permute-start | bytes 196616 | tf_op jit(solution)/shard_map/ppermute | solution.py:206
  25.1 1.5 %collective-permute-start = (bf16[16,2048]{1,0:T(8,128)(2,1)S(1)}, bf16[16,2048]{1,0:T(8,128)(2,1)S(1)}, u32[]{:S(2)}, u32[]{:S(2)}) collective-permute-start(bf16[16,2048]{1,0:T(8,128)(2,1)S(1)} %hidden.1.refs_0_), channel_id=1, source_target_pairs={{0,2},{2,4},{4,6},{6,7},{7,5},{5,3},{3,1},{1,0},{8,10},{10,12},{12... | collective-permute-start | bytes 196616 | tf_op jit(solution)/shard_map/ppermute | solution.py:204
  26.6 2.2 %collective-permute-done.1.refs_2_ = bf16[16,2048]{1,0:T(8,128)(2,1)S(1)} collective-permute-done((bf16[16,2048]{1,0:T(8,128)(2,1)S(1)}, bf16[16,2048]{1,0:T(8,128)(2,1)S(1)}, u32[]{:S(2)}, u32[]{:S(2)}) %collective-permute-start.1) | collective-permute-done | bytes 65568 | tf_op jit(solution)/shard_map/ppermute | solution.py:206
  28.8 0.6 %collective-permute-start.3 = (bf16[16,2048]{1,0:T(8,128)(2,1)S(1)}, bf16[16,2048]{1,0:T(8,128)(2,1)S(1)}, u32[]{:S(2)}, u32[]{:S(2)}) collective-permute-start(bf16[16,2048]{1,0:T(8,128)(2,1)S(1)} %collective-permute-done.1.refs_2_), channel_id=1, source_target_pairs={{0,1},{2,0},{4,2},{6,4},{7,6},{5,7},{3,5},{1,3},{8,9},{10,8},{12,1... | collective-permute-start | bytes 196616 | tf_op jit(solution)/shard_map/ppermute | solution.py:206
  29.4 0.0 collective-permute-done.refs_1_
  29.4 1.5 %collective-permute-start.2 = (bf16[16,2048]{1,0:T(8,128)(2,1)S(1)}, bf16[16,2048]{1,0:T(8,128)(2,1)S(1)}, u32[]{:S(2)}, u32[]{:S(2)}) collective-permute-start(bf16[16,2048]{1,0:T(8,128)(2,1)S(1)} %collective-permute-done.refs_1_), channel_id=1, source_target_pairs={{0,2},{2,4},{4,6},{6,7},{7,5},{5,3},{3,1},{1,0},{8,10},{10,12},{12... | collective-permute-start | bytes 196616 | tf_op jit(solution)/shard_map/ppermute | solution.py:204
  30.9 0.0 copy-done
  30.9 2.6 %down.4.refs_3_ = f32[768,16]{1,0:T(8,128)S(1)} custom-call(bf16[16,2048]{1,0:T(8,128)(2,1)S(1)} %hidden.1.refs_0_, bf16[16,2048]{1,0:T(8,128)(2,1)S(1)} %collective-permute-done.refs_1_, bf16[16,2048]{1,0:T(8,128)(2,1)S(1)} %collective-permute-done.1.refs_2_, bf16[1,768,16384]{2,1,0:T(8,128)(2,1)S(1)} %copy-done), custom_call_target="tpu_custom_call" | custom-call | tf_op jit(solution)/shard_map/down/pallas_call | solution.py:196
  33.4 0.0 collective-permute-done.3.refs_1_
  33.5 0.2 collective-permute-done.2.refs_0_
  33.7 1.8 %collective-permute-start.4 = (bf16[16,2048]{1,0:T(8,128)(2,1)S(1)}, bf16[16,2048]{1,0:T(8,128)(2,1)S(1)}, u32[]{:S(2)}, u32[]{:S(2)}) collective-permute-start(bf16[16,2048]{1,0:T(8,128)(2,1)S(1)} %collective-permute-done.2.refs_0_), channel_id=1, source_target_pairs={{0,2},{2,4},{4,6},{6,7},{7,5},{5,3},{3,1},{1,0},{8,10},{10,12},{12... | collective-permute-start | bytes 196616 | tf_op jit(solution)/shard_map/ppermute | solution.py:204
  35.4 0.3 collective-permute-start.5
  35.7 1.8 %down.5.refs_3_ = f32[768,16]{1,0:T(8,128)S(1)} custom-call(bf16[16,2048]{1,0:T(8,128)(2,1)S(1)} %collective-permute-done.2.refs_0_, bf16[16,2048]{1,0:T(8,128)(2,1)S(1)} %collective-permute-done.3.refs_1_, bf16[1,768,16384]{2,1,0:T(8,128)(2,1)S(1)} %copy-done, f32[768,16]{1,0:T(8,128)S(1)} %down.4.refs_3_), custom_call_target="tpu_custom_call" | custom-call | tf_op jit(solution)/shard_map/down/pallas_call | solution.py:196
  37.5 0.7 %collective-permute-done.4.refs_0_ = bf16[16,2048]{1,0:T(8,128)(2,1)S(1)} collective-permute-done((bf16[16,2048]{1,0:T(8,128)(2,1)S(1)}, bf16[16,2048]{1,0:T(8,128)(2,1)S(1)}, u32[]{:S(2)}, u32[]{:S(2)}) %collective-permute-start.4) | collective-permute-done | bytes 65568 | tf_op jit(solution)/shard_map/ppermute | solution.py:204
  38.2 1.5 %collective-permute-done.5.refs_1_ = bf16[16,2048]{1,0:T(8,128)(2,1)S(1)} collective-permute-done((bf16[16,2048]{1,0:T(8,128)(2,1)S(1)}, bf16[16,2048]{1,0:T(8,128)(2,1)S(1)}, u32[]{:S(2)}, u32[]{:S(2)}) %collective-permute-start.5) | collective-permute-done | bytes 65568 | tf_op jit(solution)/shard_map/ppermute | solution.py:206
  39.7 0.6 %collective-permute-start.6 = (bf16[16,2048]{1,0:T(8,128)(2,1)S(1)}, bf16[16,2048]{1,0:T(8,128)(2,1)S(1)}, u32[]{:S(2)}, u32[]{:S(2)}) collective-permute-start(bf16[16,2048]{1,0:T(8,128)(2,1)S(1)} %collective-permute-done.4.refs_0_), channel_id=1, source_target_pairs={{0,2},{2,4},{4,6},{6,7},{7,5},{5,3},{3,1},{1,0},{8,10},{10,12},{12... | collective-permute-start | bytes 196616 | tf_op jit(solution)/shard_map/ppermute | solution.py:204
  40.3 1.8 %down.6.refs_2_ = f32[768,16]{1,0:T(8,128)S(1)} custom-call(bf16[16,2048]{1,0:T(8,128)(2,1)S(1)} %collective-permute-done.4.refs_0_, bf16[16,2048]{1,0:T(8,128)(2,1)S(1)} %collective-permute-done.5.refs_1_, bf16[1,768,16384]{2,1,0:T(8,128)(2,1)S(1)} %copy-done, f32[768,16]{1,0:T(8,128)S(1)} %down.5.refs_3_), custom_call_target="tpu_custom_call" | custom-call | tf_op jit(solution)/shard_map/down/pallas_call | solution.py:196
  42.1 1.9 %collective-permute-done.6.refs_0_ = bf16[16,2048]{1,0:T(8,128)(2,1)S(1)} collective-permute-done((bf16[16,2048]{1,0:T(8,128)(2,1)S(1)}, bf16[16,2048]{1,0:T(8,128)(2,1)S(1)}, u32[]{:S(2)}, u32[]{:S(2)}) %collective-permute-start.6) | collective-permute-done | bytes 65568 | tf_op jit(solution)/shard_map/ppermute | solution.py:204
  44.0 1.0 %down.7 = f32[8,2,768]{2,1,0:T(2,128)S(1)} custom-call(bf16[16,2048]{1,0:T(8,128)(2,1)S(1)} %collective-permute-done.6.refs_0_, bf16[1,768,16384]{2,1,0:T(8,128)(2,1)S(1)} %copy-done, f32[768,16]{1,0:T(8,128)S(1)} %down.6.refs_2_), custom_call_target="tpu_custom_call" | custom-call | tf_op jit(solution)/shard_map/down/pallas_call | solution.py:196
  45.0 9.2 %all_to_all.11.own_ref = f32[8,2,768]{2,1,0:T(2,128)S(1)} all-to-all(f32[8,2,768]{2,1,0:T(2,128)S(1)} %down.7), channel_id=1, replica_groups=mesh['group'=2,'expert'=2,'tile'=8] {'tile'}, dimensions={0} | all-to-all | bytes 98304 | tf_op jit(solution)/shard_map/all_to_all | solution.py:214
  54.1 0.0 collective-permute-start.7
  54.1 1.2 %collective-permute-done.7.other_ref = f32[8,2,768]{2,1,0:T(2,128)S(1)} collective-permute-done((f32[8,2,768]{2,1,0:T(2,128)S(1)}, f32[8,2,768]{2,1,0:T(2,128)S(1)}, u32[]{:S(2)}, u32[]{:S(2)}) %collective-permute-start.7) | collective-permute-done | bytes 49184 | tf_op jit(solution)/shard_map/ppermute | solution.py:171
  55.4 0.7 %combine.1 = bf16[4,3072]{1,0:T(4,128)(2,1)} custom-call(f32[8,2,768]{2,1,0:T(2,128)S(1)} %all_to_all.11.own_ref, f32[8,2,768]{2,1,0:T(2,128)S(1)} %collective-permute-done.7.other_ref, f32[6,4,128]{2,1,0:T(4,128)S(1)} %get-tuple-element.24.table_ref), custom_call_target="tpu_custom_call" | custom-call | tf_op jit(solution)/shard_map/combine/pallas_call | solution.py:215
  (1 shorter events, 0.0 us)
Async XLA Ops:
  0.0 17.5 %copy-start.1 = (bf16[1,6144,2048]{2,1,0:T(8,128)(2,1)S(1)}, bf16[1,6144,2048]{2,1,0:T(8,128)(2,1)}, u32[]{:S(2)}) copy-start(bf16[1,6144,2048]{2,1,0:T(8,128)(2,1)} %w_ref.2) | copy-start | bytes 75497472
  1.0 20.0 %copy-start.2 = (bf16[1,6144,2048]{2,1,0:T(8,128)(2,1)S(1)}, bf16[1,6144,2048]{2,1,0:T(8,128)(2,1)}, u32[]{:S(2)}) copy-start(bf16[1,6144,2048]{2,1,0:T(8,128)(2,1)} %w_ref.3) | copy-start | bytes 75497472
  21.0 9.8 %copy-start = (bf16[1,768,16384]{2,1,0:T(8,128)(2,1)S(1)}, bf16[1,768,16384]{2,1,0:T(8,128)(2,1)}, u32[]{:S(2)}) copy-start(bf16[1,768,16384]{2,1,0:T(8,128)(2,1)} %refs_1_.1) | copy-start | bytes 75497472
  24.6 4.3 %collective-permute-start.1 = (bf16[16,2048]{1,0:T(8,128)(2,1)S(1)}, bf16[16,2048]{1,0:T(8,128)(2,1)S(1)}, u32[]{:S(2)}, u32[]{:S(2)}) collective-permute-start(bf16[16,2048]{1,0:T(8,128)(2,1)S(1)} %hidden.1.refs_0_), channel_id=1, source_target_pairs={{0,1},{2,0},{4,2},{6,4},{7,6},{5,7},{3,5},{1,3},{8,9},{10,8},{12,1... | collective-permute-start | bytes 196616 | tf_op jit(solution)/shard_map/ppermute | solution.py:206
  25.1 4.3 %collective-permute-start = (bf16[16,2048]{1,0:T(8,128)(2,1)S(1)}, bf16[16,2048]{1,0:T(8,128)(2,1)S(1)}, u32[]{:S(2)}, u32[]{:S(2)}) collective-permute-start(bf16[16,2048]{1,0:T(8,128)(2,1)S(1)} %hidden.1.refs_0_), channel_id=1, source_target_pairs={{0,2},{2,4},{4,6},{6,7},{7,5},{5,3},{3,1},{1,0},{8,10},{10,12},{12... | collective-permute-start | bytes 196616 | tf_op jit(solution)/shard_map/ppermute | solution.py:204
  28.8 4.6 %collective-permute-start.3 = (bf16[16,2048]{1,0:T(8,128)(2,1)S(1)}, bf16[16,2048]{1,0:T(8,128)(2,1)S(1)}, u32[]{:S(2)}, u32[]{:S(2)}) collective-permute-start(bf16[16,2048]{1,0:T(8,128)(2,1)S(1)} %collective-permute-done.1.refs_2_), channel_id=1, source_target_pairs={{0,1},{2,0},{4,2},{6,4},{7,6},{5,7},{3,5},{1,3},{8,9},{10,8},{12,1... | collective-permute-start | bytes 196616 | tf_op jit(solution)/shard_map/ppermute | solution.py:206
  29.4 4.3 %collective-permute-start.2 = (bf16[16,2048]{1,0:T(8,128)(2,1)S(1)}, bf16[16,2048]{1,0:T(8,128)(2,1)S(1)}, u32[]{:S(2)}, u32[]{:S(2)}) collective-permute-start(bf16[16,2048]{1,0:T(8,128)(2,1)S(1)} %collective-permute-done.refs_1_), channel_id=1, source_target_pairs={{0,2},{2,4},{4,6},{6,7},{7,5},{5,3},{3,1},{1,0},{8,10},{10,12},{12... | collective-permute-start | bytes 196616 | tf_op jit(solution)/shard_map/ppermute | solution.py:204
  33.7 4.5 %collective-permute-start.4 = (bf16[16,2048]{1,0:T(8,128)(2,1)S(1)}, bf16[16,2048]{1,0:T(8,128)(2,1)S(1)}, u32[]{:S(2)}, u32[]{:S(2)}) collective-permute-start(bf16[16,2048]{1,0:T(8,128)(2,1)S(1)} %collective-permute-done.2.refs_0_), channel_id=1, source_target_pairs={{0,2},{2,4},{4,6},{6,7},{7,5},{5,3},{3,1},{1,0},{8,10},{10,12},{12... | collective-permute-start | bytes 196616 | tf_op jit(solution)/shard_map/ppermute | solution.py:204
  35.4 4.3 %collective-permute-start.5 = (bf16[16,2048]{1,0:T(8,128)(2,1)S(1)}, bf16[16,2048]{1,0:T(8,128)(2,1)S(1)}, u32[]{:S(2)}, u32[]{:S(2)}) collective-permute-start(bf16[16,2048]{1,0:T(8,128)(2,1)S(1)} %collective-permute-done.3.refs_1_), channel_id=1, source_target_pairs={{0,1},{2,0},{4,2},{6,4},{7,6},{5,7},{3,5},{1,3},{8,9},{10,8},{12,1... | collective-permute-start | bytes 196616 | tf_op jit(solution)/shard_map/ppermute | solution.py:206
  39.7 4.3 %collective-permute-start.6 = (bf16[16,2048]{1,0:T(8,128)(2,1)S(1)}, bf16[16,2048]{1,0:T(8,128)(2,1)S(1)}, u32[]{:S(2)}, u32[]{:S(2)}) collective-permute-start(bf16[16,2048]{1,0:T(8,128)(2,1)S(1)} %collective-permute-done.4.refs_0_), channel_id=1, source_target_pairs={{0,2},{2,4},{4,6},{6,7},{7,5},{5,3},{3,1},{1,0},{8,10},{10,12},{12... | collective-permute-start | bytes 196616 | tf_op jit(solution)/shard_map/ppermute | solution.py:204
  54.1 1.2 %collective-permute-start.7 = (f32[8,2,768]{2,1,0:T(2,128)S(1)}, f32[8,2,768]{2,1,0:T(2,128)S(1)}, u32[]{:S(2)}, u32[]{:S(2)}) collective-permute-start(f32[8,2,768]{2,1,0:T(2,128)S(1)} %all_to_all.11.own_ref), channel_id=1, source_target_pairs={{0,8},{8,0},{1,9},{9,1},{2,10},{10,2},{3,11},{11,3},{4,12},{12,4},... | collective-permute-start | bytes 147464 | tf_op jit(solution)/shard_map/ppermute | solution.py:171

commit v7 on v6

--- a/solution.py
+++ b/solution.py
@@ -95,7 +95,7 @@
         body(pl.ds(pl.multiple_of(i * tile, tile), tile))
         return carry
 
-    lax.fori_loop(0, width // tile, step, 0, unroll=4)
+    lax.fori_loop(0, width // tile, step, 0, unroll=8)
 
 
 def gate_kernel(rows_ref, w_ref, out_ref):
@@ -114,19 +114,14 @@
     over_columns(hidden_ref.shape[1], body)
 
 
-def down_kernel(steps, order, first, last, *refs):
+def down_kernel(steps, first, last, *refs):
     n = len(steps)
     blocks, w_ref, rest = refs[:n], refs[n], refs[n + 1:]
     out_ref = rest[-1]
     me = lax.axis_index("tile")
     slots, width = blocks[0].shape
     part = 256
-    starts = []
-    for step in steps:
-        tile = jnp.int32(0)
-        for i, t in enumerate(order):
-            tile = jnp.where(me == t, order[(i + step) % len(order)], tile)
-        starts.append(pl.multiple_of(tile * width, width))
+    starts = [pl.multiple_of((me ^ step) * width, width) for step in steps]
     for i in range(w_ref.shape[1] // part):
         rows = slice(i * part, (i + 1) * part)
         total = None if first else rest[0][rows, :]
@@ -186,31 +181,22 @@
     x = call(merge_kernel, "merge", bf16(2 * slots, half_width), [VMEM], 4 * MIB, 0e-6)(blocks)
     gate = call(gate_kernel, "gate", f32(slots, width), [VMEM] * 2, 4 * MIB, 0e-6)(x, in_vmem(w_gate))
     hidden = call(hidden_kernel, "hidden", bf16(slots, width), [VMEM] * 3, 4 * MIB, 200e-6)(x, in_vmem(w_up), gate)
-    order = list(range(0, tiles, 2)) + list(range(tiles - 1, 0, -2))
-    ahead = [(t, order[(i + 1) % tiles]) for i, t in enumerate(order)]
-    behind = [(t, order[i - 1]) for i, t in enumerate(order)]
-
-    def down(total, steps, blocks):
-        first, last = total is None, -(tiles // 2) in steps
+    def down(total, steps, blocks, last):
+        first = total is None
         out = f32(tiles, SLOTS, features) if last else f32(features, slots)
         return call(
-            functools.partial(down_kernel, steps, order, first, last), "down", out,
+            functools.partial(down_kernel, steps, first, last), "down", out,
             [VMEM] * (len(blocks) + 2 - first), 8 * MIB, 0e-6,
         )(*blocks, in_vmem(w_down), *(() if first else (total,)))
 
-    below, above = hidden, hidden
-    total, steps, blocks = None, [0], [hidden]
-    for i in range(1, tiles // 2 + 1):
-        below = lax.ppermute(below, "tile", ahead)
-        if 2 * i < tiles:
-            above = lax.ppermute(above, "tile", behind)
-        if i >= 2:
-            total, steps, blocks = down(total, steps, blocks), [], []
-            total, below, above = lax.optimization_barrier((total, below, above))
-        steps, blocks = steps + [-i], blocks + [below]
-        if 2 * i < tiles:
-            steps, blocks = steps + [i], blocks + [above]
-    result = down(total, steps, blocks)
+    far_first = range(tiles - 1, 0, -1)
+    blocks = [(0, hidden)] + [
+        (k, lax.ppermute(hidden, "tile", [(t, t ^ k) for t in range(tiles)])) for k in far_first]
+    total = None
+    for first, last in ((0, 4), (4, 6), (6, 8)):
+        part = blocks[first:last]
+        total = down(total, [k for k, _ in part], [block for _, block in part], last == tiles)
+    result = total
     back = lax.all_to_all(result, "tile", split_axis=0, concat_axis=0, tiled=True)
     return call(combine_kernel, "combine", bf16(rows, half_width), [VMEM] * 3, 4 * MIB)(back, to_core(back), table)
 

time: 56.3 us -> 56.8 us (level)
  starting transfers between devices: 6.7 us -> 11.1 us
  waiting for transfers between devices: 7.81 us -> 3.82 us
  blocking collectives: 25.6 us -> 26.2 us
    ppermute x7, starting transfers between devices: 6.7 us -> 11.1 us  [local_direct(): lax.ppermute(hidden, 'tile', [(t, t ^ k) for t in range(tiles)])]
    ppermute x7, waiting for transfers between devices: 6.58 us -> 2.59 us  [local_direct(): lax.ppermute(hidden, 'tile', [(t, t ^ k) for t in range(tiles)])]
    pallas_call x4 -> x3, Pallas kernels: 7.07 us -> 6.95 us  [down(): call(functools.partial(down_kernel, steps, first, last), 'down', out, [VM...]
  transfers between devices with their start and end apart: 8 -> 8, of which waited for: 6 -> 3; matrix products, arithmetic and copies ran while one was open for 0% -> 0% of each run, Pallas kernels for 11% -> 9%
where the time goes in v7:
time: 56.8 us; the launch traced here: 56.6 us
  blocking collectives  26.2 us (46%)
  Pallas kernels  15.5 us (27%)
  starting transfers between devices  11.1 us (20%)
  waiting for transfers between devices  3.82 us (7%)
    all_to_all x1, blocking collectives, local_direct(): lax.all_to_all(sends, ('expert', 'tile'), split_axis=0, concat_axis=0, ti...  16.4 us
    ppermute x7, starting transfers between devices, local_direct(): lax.ppermute(hidden, 'tile', [(t, t ^ k) for t in range(tiles)])  11.1 us
    all_to_all x1, blocking collectives, local_direct(): lax.all_to_all(result, 'tile', split_axis=0, concat_axis=0, tiled=True)  9.73 us
    pallas_call x3, Pallas kernels, down(): call(functools.partial(down_kernel, steps, first, last), 'down', out, [VM...  6.95 us
    pallas_call x1, Pallas kernels, local_direct(): call(hidden_kernel, 'hidden', bf16(slots, width), [VMEM] * 3, 4 * MIB, 0....  3.37 us
    pallas_call x1, Pallas kernels, local_direct(): call(gate_kernel, 'gate', f32(slots, width), [VMEM] * 2, 4 * MIB, 0.0)  3.34 us
    ppermute x7, waiting for transfers between devices, local_direct(): lax.ppermute(hidden, 'tile', [(t, t ^ k) for t in range(tiles)])  2.59 us
    ppermute x1, waiting for transfers between devices, to_core(): return lax.ppermute(x, 'expert', [(0, 1), (1, 0)])  1.23 us
  transfers between devices with their start and end apart: 8, of which 3 were waited for; matrix products, arithmetic and copies ran while one was open for 0% of the time, Pallas kernels for 9%

profile of v7, /device:TPU:0, one launch (start us, length us, event | category | flops | bytes accessed | tf_op | source)
XLA Modules:
  0.0 56.6 jit_solution(13819585282693800113)
XLA Ops:
  0.0 0.0 copy-start.1
  0.0 1.0 %dispatch.1 = (bf16[16,2,3072]{2,1,0:T(2,128)(2,1)S(1)}, f32[6,4,128]{2,1,0:T(4,128)S(1)}) custom-call(bf16[4,3072]{1,0:T(4,128)(2,1)} %tokens_hbm.1, s32[2,4]{1,0:T(2,128)} %bitcast.2, f32[2,4]{1,0:T(2,128)} %bitcast.3), custom_call_target="tpu_custom_call" | custom-call | flops 599999971328 | tf_op jit(solution)/shard_map/dispatch/pallas_call | solution.py:170
  1.0 0.0 copy-start.2
  1.0 16.4 %all_to_all.10.blocks_ref = bf16[16,2,3072]{2,1,0:T(2,128)(2,1)S(1)} all-to-all(bf16[16,2,3072]{2,1,0:T(2,128)(2,1)S(1)} %get-tuple-element.7), channel_id=1, replica_groups=mesh['group'=2,'expert'=2,'tile'=8] {'expert','tile'}, dimensions={0} | all-to-all | bytes 393216 | tf_op jit(solution)/shard_map/all_to_all | solution.py:180
  17.5 0.0 copy-done.1
  17.5 3.3 %gate.1.gate_ref = f32[16,2048]{1,0:T(8,128)S(1)} custom-call(bf16[32,3072]{1,0:T(8,128)(2,1)S(1)} %merge.1.rows_ref, bf16[1,6144,2048]{2,1,0:T(8,128)(2,1)S(1)} %copy-done.1), custom_call_target="tpu_custom_call" | custom-call | tf_op jit(solution)/shard_map/gate/pallas_call | solution.py:182
  20.9 0.0 copy-done.2
  20.9 0.0 copy-start
  20.9 3.4 %hidden.1.refs_0_ = bf16[16,2048]{1,0:T(8,128)(2,1)S(1)} custom-call(bf16[32,3072]{1,0:T(8,128)(2,1)S(1)} %merge.1.rows_ref, bf16[1,6144,2048]{2,1,0:T(8,128)(2,1)S(1)} %copy-done.2, f32[16,2048]{1,0:T(8,128)S(1)} %gate.1.gate_ref), custom_call_target="tpu_custom_call" | custom-call | flops 199999995904 | tf_op jit(solution)/shard_map/hidden/pallas_call | solution.py:183
  24.2 1.0 %collective-permute-start.4 = (bf16[16,2048]{1,0:T(8,128)(2,1)S(1)}, bf16[16,2048]{1,0:T(8,128)(2,1)S(1)}, u32[]{:S(2)}, u32[]{:S(2)}) collective-permute-start(bf16[16,2048]{1,0:T(8,128)(2,1)S(1)} %hidden.1.refs_0_), channel_id=1, source_target_pairs={{0,7},{1,6},{2,5},{3,4},{4,3},{5,2},{6,1},{7,0},{8,15},{9,14},{10,... | collective-permute-start | bytes 196616 | tf_op jit(solution)/shard_map/ppermute | solution.py:194
  25.2 2.8 %collective-permute-start.5 = (bf16[16,2048]{1,0:T(8,128)(2,1)S(1)}, bf16[16,2048]{1,0:T(8,128)(2,1)S(1)}, u32[]{:S(2)}, u32[]{:S(2)}) collective-permute-start(bf16[16,2048]{1,0:T(8,128)(2,1)S(1)} %hidden.1.refs_0_), channel_id=1, source_target_pairs={{0,6},{1,7},{2,4},{3,5},{4,2},{5,3},{6,0},{7,1},{8,14},{9,15},{10,... | collective-permute-start | bytes 196616 | tf_op jit(solution)/shard_map/ppermute | solution.py:194
  28.1 0.0 collective-permute-start.6
  28.1 3.8 %collective-permute-start.2 = (bf16[16,2048]{1,0:T(8,128)(2,1)S(1)}, bf16[16,2048]{1,0:T(8,128)(2,1)S(1)}, u32[]{:S(2)}, u32[]{:S(2)}) collective-permute-start(bf16[16,2048]{1,0:T(8,128)(2,1)S(1)} %hidden.1.refs_0_), channel_id=1, source_target_pairs={{0,4},{1,5},{2,6},{3,7},{4,0},{5,1},{6,2},{7,3},{8,12},{9,13},{10,... | collective-permute-start | bytes 196616 | tf_op jit(solution)/shard_map/ppermute | solution.py:194
  31.9 0.0 collective-permute-start.3
  31.9 0.1 collective-permute-done.4.refs_1_
  31.9 2.0 %collective-permute-start = (bf16[16,2048]{1,0:T(8,128)(2,1)S(1)}, bf16[16,2048]{1,0:T(8,128)(2,1)S(1)}, u32[]{:S(2)}, u32[]{:S(2)}) collective-permute-start(bf16[16,2048]{1,0:T(8,128)(2,1)S(1)} %hidden.1.refs_0_), channel_id=1, source_target_pairs={{0,2},{1,3},{2,0},{3,1},{4,6},{5,7},{6,4},{7,5},{8,10},{9,11},{10,... | collective-permute-start | bytes 196616 | tf_op jit(solution)/shard_map/ppermute | solution.py:194
  33.9 0.0 collective-permute-done.5.refs_2_
  33.9 1.5 %collective-permute-start.1 = (bf16[16,2048]{1,0:T(8,128)(2,1)S(1)}, bf16[16,2048]{1,0:T(8,128)(2,1)S(1)}, u32[]{:S(2)}, u32[]{:S(2)}) collective-permute-start(bf16[16,2048]{1,0:T(8,128)(2,1)S(1)} %hidden.1.refs_0_), channel_id=1, source_target_pairs={{0,1},{1,0},{2,3},{3,2},{4,5},{5,4},{6,7},{7,6},{8,9},{9,8},{10,11... | collective-permute-start | bytes 196616 | tf_op jit(solution)/shard_map/ppermute | solution.py:194
  35.4 2.5 %collective-permute-done.6.refs_3_ = bf16[16,2048]{1,0:T(8,128)(2,1)S(1)} collective-permute-done((bf16[16,2048]{1,0:T(8,128)(2,1)S(1)}, bf16[16,2048]{1,0:T(8,128)(2,1)S(1)}, u32[]{:S(2)}, u32[]{:S(2)}) %collective-permute-start.6) | collective-permute-done | bytes 65568 | tf_op jit(solution)/shard_map/ppermute | solution.py:194
  37.9 0.0 copy-done
  37.9 3.4 %down.3.refs_3_ = f32[768,16]{1,0:T(8,128)S(1)} custom-call(bf16[16,2048]{1,0:T(8,128)(2,1)S(1)} %hidden.1.refs_0_, bf16[16,2048]{1,0:T(8,128)(2,1)S(1)} %collective-permute-done.4.refs_1_, bf16[16,2048]{1,0:T(8,128)(2,1)S(1)} %collective-permute-done.5.refs_2_, bf16[16,2048]{1,0:T(8,128)(2,1)S(1)} %collective-permute-done.6.refs_3_, ...), custom_call_target="tpu_custom_call" | custom-call | tf_op jit(solution)/shard_map/down/pallas_call | solution.py:187
  41.3 0.0 collective-permute-done.2.refs_0_
  41.3 0.0 collective-permute-done.3.refs_1_
  41.3 1.8 %down.4.refs_3_ = f32[768,16]{1,0:T(8,128)S(1)} custom-call(bf16[16,2048]{1,0:T(8,128)(2,1)S(1)} %collective-permute-done.2.refs_0_, bf16[16,2048]{1,0:T(8,128)(2,1)S(1)} %collective-permute-done.3.refs_1_, bf16[1,768,16384]{2,1,0:T(8,128)(2,1)S(1)} %copy-done, f32[768,16]{1,0:T(8,128)S(1)} %down.3.refs_3_), custom_call_target="tpu_custom_call" | custom-call | tf_op jit(solution)/shard_map/down/pallas_call | solution.py:187
  43.1 0.0 collective-permute-done.refs_0_
  43.1 0.0 collective-permute-done.1.refs_1_
  43.1 1.8 %down.5 = f32[8,2,768]{2,1,0:T(2,128)S(1)} custom-call(bf16[16,2048]{1,0:T(8,128)(2,1)S(1)} %collective-permute-done.refs_0_, bf16[16,2048]{1,0:T(8,128)(2,1)S(1)} %collective-permute-done.1.refs_1_, bf16[1,768,16384]{2,1,0:T(8,128)(2,1)S(1)} %copy-done, f32[768,16]{1,0:T(8,128)S(1)} %down.4.refs_3_), custom_call_target="tpu_custom_call" | custom-call | tf_op jit(solution)/shard_map/down/pallas_call | solution.py:187
  44.9 9.7 %all_to_all.11.own_ref = f32[8,2,768]{2,1,0:T(2,128)S(1)} all-to-all(f32[8,2,768]{2,1,0:T(2,128)S(1)} %down.5), channel_id=1, replica_groups=mesh['group'=2,'expert'=2,'tile'=8] {'tile'}, dimensions={0} | all-to-all | bytes 98304 | tf_op jit(solution)/shard_map/all_to_all | solution.py:200
  54.6 0.0 collective-permute-start.7
  54.6 1.2 %collective-permute-done.7.other_ref = f32[8,2,768]{2,1,0:T(2,128)S(1)} collective-permute-done((f32[8,2,768]{2,1,0:T(2,128)S(1)}, f32[8,2,768]{2,1,0:T(2,128)S(1)}, u32[]{:S(2)}, u32[]{:S(2)}) %collective-permute-start.7) | collective-permute-done | bytes 49184 | tf_op jit(solution)/shard_map/ppermute | solution.py:166
  55.9 0.7 %combine.1 = bf16[4,3072]{1,0:T(4,128)(2,1)} custom-call(f32[8,2,768]{2,1,0:T(2,128)S(1)} %all_to_all.11.own_ref, f32[8,2,768]{2,1,0:T(2,128)S(1)} %collective-permute-done.7.other_ref, f32[6,4,128]{2,1,0:T(4,128)S(1)} %get-tuple-element.8.table_ref), custom_call_target="tpu_custom_call" | custom-call | tf_op jit(solution)/shard_map/combine/pallas_call | solution.py:201
  (1 shorter events, 0.0 us)
Async XLA Ops:
  0.0 17.5 %copy-start.1 = (bf16[1,6144,2048]{2,1,0:T(8,128)(2,1)S(1)}, bf16[1,6144,2048]{2,1,0:T(8,128)(2,1)}, u32[]{:S(2)}) copy-start(bf16[1,6144,2048]{2,1,0:T(8,128)(2,1)} %w_ref.2) | copy-start | bytes 75497472
  1.0 19.8 %copy-start.2 = (bf16[1,6144,2048]{2,1,0:T(8,128)(2,1)S(1)}, bf16[1,6144,2048]{2,1,0:T(8,128)(2,1)}, u32[]{:S(2)}) copy-start(bf16[1,6144,2048]{2,1,0:T(8,128)(2,1)} %w_ref.3) | copy-start | bytes 75497472
  20.9 17.0 %copy-start = (bf16[1,768,16384]{2,1,0:T(8,128)(2,1)S(1)}, bf16[1,768,16384]{2,1,0:T(8,128)(2,1)}, u32[]{:S(2)}) copy-start(bf16[1,768,16384]{2,1,0:T(8,128)(2,1)} %refs_2_.3) | copy-start | bytes 75497472
  24.2 7.7 %collective-permute-start.4 = (bf16[16,2048]{1,0:T(8,128)(2,1)S(1)}, bf16[16,2048]{1,0:T(8,128)(2,1)S(1)}, u32[]{:S(2)}, u32[]{:S(2)}) collective-permute-start(bf16[16,2048]{1,0:T(8,128)(2,1)S(1)} %hidden.1.refs_0_), channel_id=1, source_target_pairs={{0,7},{1,6},{2,5},{3,4},{4,3},{5,2},{6,1},{7,0},{8,15},{9,14},{10,... | collective-permute-start | bytes 196616 | tf_op jit(solution)/shard_map/ppermute | solution.py:194
  25.2 8.7 %collective-permute-start.5 = (bf16[16,2048]{1,0:T(8,128)(2,1)S(1)}, bf16[16,2048]{1,0:T(8,128)(2,1)S(1)}, u32[]{:S(2)}, u32[]{:S(2)}) collective-permute-start(bf16[16,2048]{1,0:T(8,128)(2,1)S(1)} %hidden.1.refs_0_), channel_id=1, source_target_pairs={{0,6},{1,7},{2,4},{3,5},{4,2},{5,3},{6,0},{7,1},{8,14},{9,15},{10,... | collective-permute-start | bytes 196616 | tf_op jit(solution)/shard_map/ppermute | solution.py:194
  28.1 9.8 %collective-permute-start.6 = (bf16[16,2048]{1,0:T(8,128)(2,1)S(1)}, bf16[16,2048]{1,0:T(8,128)(2,1)S(1)}, u32[]{:S(2)}, u32[]{:S(2)}) collective-permute-start(bf16[16,2048]{1,0:T(8,128)(2,1)S(1)} %hidden.1.refs_0_), channel_id=1, source_target_pairs={{0,5},{1,4},{2,7},{3,6},{4,1},{5,0},{6,3},{7,2},{8,13},{9,12},{10,... | collective-permute-start | bytes 196616 | tf_op jit(solution)/shard_map/ppermute | solution.py:194
  28.1 13.2 %collective-permute-start.2 = (bf16[16,2048]{1,0:T(8,128)(2,1)S(1)}, bf16[16,2048]{1,0:T(8,128)(2,1)S(1)}, u32[]{:S(2)}, u32[]{:S(2)}) collective-permute-start(bf16[16,2048]{1,0:T(8,128)(2,1)S(1)} %hidden.1.refs_0_), channel_id=1, source_target_pairs={{0,4},{1,5},{2,6},{3,7},{4,0},{5,1},{6,2},{7,3},{8,12},{9,13},{10,... | collective-permute-start | bytes 196616 | tf_op jit(solution)/shard_map/ppermute | solution.py:194
  31.9 9.4 %collective-permute-start.3 = (bf16[16,2048]{1,0:T(8,128)(2,1)S(1)}, bf16[16,2048]{1,0:T(8,128)(2,1)S(1)}, u32[]{:S(2)}, u32[]{:S(2)}) collective-permute-start(bf16[16,2048]{1,0:T(8,128)(2,1)S(1)} %hidden.1.refs_0_), channel_id=1, source_target_pairs={{0,3},{1,2},{2,1},{3,0},{4,7},{5,6},{6,5},{7,4},{8,11},{9,10},{10,... | collective-permute-start | bytes 196616 | tf_op jit(solution)/shard_map/ppermute | solution.py:194
  31.9 11.1 %collective-permute-start = (bf16[16,2048]{1,0:T(8,128)(2,1)S(1)}, bf16[16,2048]{1,0:T(8,128)(2,1)S(1)}, u32[]{:S(2)}, u32[]{:S(2)}) collective-permute-start(bf16[16,2048]{1,0:T(8,128)(2,1)S(1)} %hidden.1.refs_0_), channel_id=1, source_target_pairs={{0,2},{1,3},{2,0},{3,1},{4,6},{5,7},{6,4},{7,5},{8,10},{9,11},{10,... | collective-permute-start | bytes 196616 | tf_op jit(solution)/shard_map/ppermute | solution.py:194
  33.9 9.2 %collective-permute-start.1 = (bf16[16,2048]{1,0:T(8,128)(2,1)S(1)}, bf16[16,2048]{1,0:T(8,128)(2,1)S(1)}, u32[]{:S(2)}, u32[]{:S(2)}) collective-permute-start(bf16[16,2048]{1,0:T(8,128)(2,1)S(1)} %hidden.1.refs_0_), channel_id=1, source_target_pairs={{0,1},{1,0},{2,3},{3,2},{4,5},{5,4},{6,7},{7,6},{8,9},{9,8},{10,11... | collective-permute-start | bytes 196616 | tf_op jit(solution)/shard_map/ppermute | solution.py:194
  54.6 1.2 %collective-permute-start.7 = (f32[8,2,768]{2,1,0:T(2,128)S(1)}, f32[8,2,768]{2,1,0:T(2,128)S(1)}, u32[]{:S(2)}, u32[]{:S(2)}) collective-permute-start(f32[8,2,768]{2,1,0:T(2,128)S(1)} %all_to_all.11.own_ref), channel_id=1, source_target_pairs={{0,8},{8,0},{1,9},{9,1},{2,10},{10,2},{3,11},{11,3},{4,12},{12,4},... | collective-permute-start | bytes 147464 | tf_op jit(solution)/shard_map/ppermute | solution.py:166

commit v8 on v7

--- a/solution.py
+++ b/solution.py
@@ -114,9 +114,16 @@
     over_columns(hidden_ref.shape[1], body)
 
 
-def down_kernel(steps, first, last, *refs):
-    n = len(steps)
-    blocks, w_ref, rest = refs[:n], refs[n], refs[n + 1:]
+def join_kernel(*refs):
+    *blocks, _, out_ref = refs
+    for i, block in enumerate(blocks):
+        out_ref[i] = block[...]
+
+
+def down_kernel(held, steps, first, last, *refs):
+    blocks, w_ref, rest = refs[:held], refs[held], refs[held + 1:]
+    if len(blocks) < len(steps):
+        blocks = [blocks[0].at[i] for i in range(len(steps))]
     out_ref = rest[-1]
     me = lax.axis_index("tile")
     slots, width = blocks[0].shape
@@ -162,6 +169,9 @@
     slots = tiles * SLOTS
     routes, gates = routes.T, gates.T
 
+    def swap(x, bit):
+        return lax.ppermute(x, "tile", [(t, t ^ bit) for t in range(tiles)])
+
     def to_core(x):
         return lax.ppermute(x, "expert", [(0, 1), (1, 0)])
 
@@ -181,22 +191,22 @@
     x = call(merge_kernel, "merge", bf16(2 * slots, half_width), [VMEM], 4 * MIB, 0e-6)(blocks)
     gate = call(gate_kernel, "gate", f32(slots, width), [VMEM] * 2, 4 * MIB, 0e-6)(x, in_vmem(w_gate))
     hidden = call(hidden_kernel, "hidden", bf16(slots, width), [VMEM] * 3, 4 * MIB, 200e-6)(x, in_vmem(w_up), gate)
+
     def down(total, steps, blocks, last):
         first = total is None
         out = f32(tiles, SLOTS, features) if last else f32(features, slots)
         return call(
-            functools.partial(down_kernel, steps, first, last), "down", out,
+            functools.partial(down_kernel, len(blocks), steps, first, last), "down", out,
             [VMEM] * (len(blocks) + 2 - first), 8 * MIB, 0e-6,
         )(*blocks, in_vmem(w_down), *(() if first else (total,)))
 
-    far_first = range(tiles - 1, 0, -1)
-    blocks = [(0, hidden)] + [
-        (k, lax.ppermute(hidden, "tile", [(t, t ^ k) for t in range(tiles)])) for k in far_first]
-    total = None
-    for first, last in ((0, 4), (4, 6), (6, 8)):
-        part = blocks[first:last]
-        total = down(total, [k for k, _ in part], [block for _, block in part], last == tiles)
-    result = total
+    near = [swap(hidden, k) for k in (6, 4, 2)]
+    beside = swap(hidden, 1)
+    column = call(join_kernel, "join", bf16(3, slots, width), [VMEM] * 4, 4 * MIB)(*near, beside)
+    other_column = swap(column, 1)
+    total = down(None, [0, 1], [hidden, beside], False)
+    total = down(total, [6, 4, 2], [column], False)
+    result = down(total, [7, 5, 3], [other_column], True)
     back = lax.all_to_all(result, "tile", split_axis=0, concat_axis=0, tiled=True)
     return call(combine_kernel, "combine", bf16(rows, half_width), [VMEM] * 3, 4 * MIB)(back, to_core(back), table)
 

time: 56.8 us -> 54.7 us (0.963)
  starting transfers between devices: 11.1 us -> 6.23 us
  waiting for transfers between devices: 3.82 us -> 6.46 us
    ppermute x7 -> x5, starting transfers between devices: 11.1 us -> 6.22 us  [swap(): return lax.ppermute(x, 'tile', [(t, t ^ bit) for t in range(tiles)])]
    ppermute x7 -> x5, waiting for transfers between devices: 2.59 us -> 5.23 us  [swap(): return lax.ppermute(x, 'tile', [(t, t ^ bit) for t in range(tiles)])]
    pallas_call x3 -> x4, Pallas kernels: 6.95 us -> 6.96 us  [the longest x3 6.95 us: down(): call(functools.partial(down_kernel, len(blocks), steps, first, last), 'do...]
  transfers between devices with their start and end apart: 8 -> 6, of which waited for: 3 -> 4; matrix products, arithmetic and copies ran while one was open for 0% -> 0% of each run, Pallas kernels for 9% -> 8%
where the time goes in v8:
time: 54.7 us; the launch traced here: 54.5 us
  blocking collectives  26.3 us (48%)
  Pallas kernels  15.5 us (28%)
  waiting for transfers between devices  6.46 us (12%)
  starting transfers between devices  6.23 us (11%)
    all_to_all x1, blocking collectives, local_direct(): lax.all_to_all(sends, ('expert', 'tile'), split_axis=0, concat_axis=0, ti...  16.4 us
    all_to_all x1, blocking collectives, local_direct(): lax.all_to_all(result, 'tile', split_axis=0, concat_axis=0, tiled=True)  9.86 us
    pallas_call x3, Pallas kernels, down(): call(functools.partial(down_kernel, len(blocks), steps, first, last), 'do...  6.95 us
    ppermute x5, starting transfers between devices, swap(): return lax.ppermute(x, 'tile', [(t, t ^ bit) for t in range(tiles)])  6.22 us
    ppermute x5, waiting for transfers between devices, swap(): return lax.ppermute(x, 'tile', [(t, t ^ bit) for t in range(tiles)])  5.23 us
    pallas_call x1, Pallas kernels, local_direct(): call(hidden_kernel, 'hidden', bf16(slots, width), [VMEM] * 3, 4 * MIB, 0....  3.37 us
    pallas_call x1, Pallas kernels, local_direct(): call(gate_kernel, 'gate', f32(slots, width), [VMEM] * 2, 4 * MIB, 0.0)  3.34 us
    ppermute x1, waiting for transfers between devices, to_core(): return lax.ppermute(x, 'expert', [(0, 1), (1, 0)])  1.23 us
  transfers between devices with their start and end apart: 6, of which 4 were waited for; matrix products, arithmetic and copies ran while one was open for 0% of the time, Pallas kernels for 8%

profile of v8, /device:TPU:0, one launch (start us, length us, event | category | flops | bytes accessed | tf_op | source)
XLA Modules:
  0.0 54.5 jit_solution(7837215067532964322)
XLA Ops:
  0.0 0.0 copy-start.1
  0.0 1.0 %dispatch.1 = (bf16[16,2,3072]{2,1,0:T(2,128)(2,1)S(1)}, f32[6,4,128]{2,1,0:T(4,128)S(1)}) custom-call(bf16[4,3072]{1,0:T(4,128)(2,1)} %tokens_hbm.1, s32[2,4]{1,0:T(2,128)} %bitcast.2, f32[2,4]{1,0:T(2,128)} %bitcast.3), custom_call_target="tpu_custom_call" | custom-call | flops 599999971328 | tf_op jit(solution)/shard_map/dispatch/pallas_call | solution.py:180
  1.0 0.0 copy-start.2
  1.0 16.4 %all_to_all.10.blocks_ref = bf16[16,2,3072]{2,1,0:T(2,128)(2,1)S(1)} all-to-all(bf16[16,2,3072]{2,1,0:T(2,128)(2,1)S(1)} %get-tuple-element.7), channel_id=1, replica_groups=mesh['group'=2,'expert'=2,'tile'=8] {'expert','tile'}, dimensions={0} | all-to-all | bytes 393216 | tf_op jit(solution)/shard_map/all_to_all | solution.py:190
  17.5 0.0 copy-done.1
  17.5 3.3 %gate.1.gate_ref = f32[16,2048]{1,0:T(8,128)S(1)} custom-call(bf16[32,3072]{1,0:T(8,128)(2,1)S(1)} %merge.1.rows_ref, bf16[1,6144,2048]{2,1,0:T(8,128)(2,1)S(1)} %copy-done.1), custom_call_target="tpu_custom_call" | custom-call | tf_op jit(solution)/shard_map/gate/pallas_call | solution.py:192
  20.9 0.0 copy-done.2
  20.9 0.0 copy-start
  20.9 3.4 %hidden.1.refs_0_ = bf16[16,2048]{1,0:T(8,128)(2,1)S(1)} custom-call(bf16[32,3072]{1,0:T(8,128)(2,1)S(1)} %merge.1.rows_ref, bf16[1,6144,2048]{2,1,0:T(8,128)(2,1)S(1)} %copy-done.2, f32[16,2048]{1,0:T(8,128)S(1)} %gate.1.gate_ref), custom_call_target="tpu_custom_call" | custom-call | flops 199999995904 | tf_op jit(solution)/shard_map/hidden/pallas_call | solution.py:193
  24.2 0.6 %collective-permute-start.3 = (bf16[16,2048]{1,0:T(8,128)(2,1)S(1)}, bf16[16,2048]{1,0:T(8,128)(2,1)S(1)}, u32[]{:S(2)}, u32[]{:S(2)}) collective-permute-start(bf16[16,2048]{1,0:T(8,128)(2,1)S(1)} %hidden.1.refs_0_), channel_id=1, source_target_pairs={{0,1},{1,0},{2,3},{3,2},{4,5},{5,4},{6,7},{7,6},{8,9},{9,8},{10,11... | collective-permute-start | bytes 196616 | tf_op jit(solution)/shard_map/ppermute | solution.py:173
  24.8 1.0 %collective-permute-start = (bf16[16,2048]{1,0:T(8,128)(2,1)S(1)}, bf16[16,2048]{1,0:T(8,128)(2,1)S(1)}, u32[]{:S(2)}, u32[]{:S(2)}) collective-permute-start(bf16[16,2048]{1,0:T(8,128)(2,1)S(1)} %hidden.1.refs_0_), channel_id=1, source_target_pairs={{0,6},{1,7},{2,4},{3,5},{4,2},{5,3},{6,0},{7,1},{8,14},{9,15},{10,... | collective-permute-start | bytes 196616 | tf_op jit(solution)/shard_map/ppermute | solution.py:173
  25.8 1.2 %collective-permute-start.1 = (bf16[16,2048]{1,0:T(8,128)(2,1)S(1)}, bf16[16,2048]{1,0:T(8,128)(2,1)S(1)}, u32[]{:S(2)}, u32[]{:S(2)}) collective-permute-start(bf16[16,2048]{1,0:T(8,128)(2,1)S(1)} %hidden.1.refs_0_), channel_id=1, source_target_pairs={{0,4},{1,5},{2,6},{3,7},{4,0},{5,1},{6,2},{7,3},{8,12},{9,13},{10,... | collective-permute-start | bytes 196616 | tf_op jit(solution)/shard_map/ppermute | solution.py:173
  27.0 2.2 %collective-permute-start.2 = (bf16[16,2048]{1,0:T(8,128)(2,1)S(1)}, bf16[16,2048]{1,0:T(8,128)(2,1)S(1)}, u32[]{:S(2)}, u32[]{:S(2)}) collective-permute-start(bf16[16,2048]{1,0:T(8,128)(2,1)S(1)} %hidden.1.refs_0_), channel_id=1, source_target_pairs={{0,2},{1,3},{2,0},{3,1},{4,6},{5,7},{6,4},{7,5},{8,10},{9,11},{10,... | collective-permute-start | bytes 196616 | tf_op jit(solution)/shard_map/ppermute | solution.py:173
  29.2 0.0 collective-permute-done.3.refs_3_.refs_1_
  29.2 2.4 %collective-permute-done.refs_0_ = bf16[16,2048]{1,0:T(8,128)(2,1)S(1)} collective-permute-done((bf16[16,2048]{1,0:T(8,128)(2,1)S(1)}, bf16[16,2048]{1,0:T(8,128)(2,1)S(1)}, u32[]{:S(2)}, u32[]{:S(2)}) %collective-permute-start) | collective-permute-done | bytes 65568 | tf_op jit(solution)/shard_map/ppermute | solution.py:173
  31.6 1.8 %collective-permute-done.1.refs_1_ = bf16[16,2048]{1,0:T(8,128)(2,1)S(1)} collective-permute-done((bf16[16,2048]{1,0:T(8,128)(2,1)S(1)}, bf16[16,2048]{1,0:T(8,128)(2,1)S(1)}, u32[]{:S(2)}, u32[]{:S(2)}) %collective-permute-start.1) | collective-permute-done | bytes 65568 | tf_op jit(solution)/shard_map/ppermute | solution.py:173
  33.4 0.0 collective-permute-done.2.refs_2_
  33.4 1.3 %collective-permute-start.4 = (bf16[3,16,2048]{2,1,0:T(8,128)(2,1)S(1)}, bf16[3,16,2048]{2,1,0:T(8,128)(2,1)S(1)}, u32[]{:S(2)}, u32[]{:S(2)}) collective-permute-start(bf16[3,16,2048]{2,1,0:T(8,128)(2,1)S(1)} %join.1.refs_0_), channel_id=1, source_target_pairs={{0,1},{1,0},{2,3},{3,2},{4,5},{5,4},{6,7},{7,6},{8,9},{9,8},{10,11... | collective-permute-start | bytes 589832 | tf_op jit(solution)/shard_map/ppermute | solution.py:173
  34.7 0.0 copy-done
  34.7 1.8 %down.3.refs_2_ = f32[768,16]{1,0:T(8,128)S(1)} custom-call(bf16[16,2048]{1,0:T(8,128)(2,1)S(1)} %hidden.1.refs_0_, bf16[16,2048]{1,0:T(8,128)(2,1)S(1)} %collective-permute-done.3.refs_3_.refs_1_, bf16[1,768,16384]{2,1,0:T(8,128)(2,1)S(1)} %copy-done), custom_call_target="tpu_custom_call" | custom-call | tf_op jit(solution)/shard_map/down/pallas_call | solution.py:198
  36.5 2.6 %down.4.refs_2_ = f32[768,16]{1,0:T(8,128)S(1)} custom-call(bf16[3,16,2048]{2,1,0:T(8,128)(2,1)S(1)} %join.1.refs_0_, bf16[1,768,16384]{2,1,0:T(8,128)(2,1)S(1)} %copy-done, f32[768,16]{1,0:T(8,128)S(1)} %down.3.refs_2_), custom_call_target="tpu_custom_call" | custom-call | tf_op jit(solution)/shard_map/down/pallas_call | solution.py:198
  39.0 1.0 %collective-permute-done.4.refs_0_ = bf16[3,16,2048]{2,1,0:T(8,128)(2,1)S(1)} collective-permute-done((bf16[3,16,2048]{2,1,0:T(8,128)(2,1)S(1)}, bf16[3,16,2048]{2,1,0:T(8,128)(2,1)S(1)}, u32[]{:S(2)}, u32[]{:S(2)}) %collective-permute-start.4) | collective-permute-done | bytes 196640 | tf_op jit(solution)/shard_map/ppermute | solution.py:173
  40.0 2.6 %down.5 = f32[8,2,768]{2,1,0:T(2,128)S(1)} custom-call(bf16[3,16,2048]{2,1,0:T(8,128)(2,1)S(1)} %collective-permute-done.4.refs_0_, bf16[1,768,16384]{2,1,0:T(8,128)(2,1)S(1)} %copy-done, f32[768,16]{1,0:T(8,128)S(1)} %down.4.refs_2_), custom_call_target="tpu_custom_call" | custom-call | tf_op jit(solution)/shard_map/down/pallas_call | solution.py:198
  42.7 9.9 %all_to_all.11.own_ref = f32[8,2,768]{2,1,0:T(2,128)S(1)} all-to-all(f32[8,2,768]{2,1,0:T(2,128)S(1)} %down.5), channel_id=1, replica_groups=mesh['group'=2,'expert'=2,'tile'=8] {'tile'}, dimensions={0} | all-to-all | bytes 98304 | tf_op jit(solution)/shard_map/all_to_all | solution.py:210
  52.5 0.0 collective-permute-start.5
  52.5 1.2 %collective-permute-done.5.other_ref = f32[8,2,768]{2,1,0:T(2,128)S(1)} collective-permute-done((f32[8,2,768]{2,1,0:T(2,128)S(1)}, f32[8,2,768]{2,1,0:T(2,128)S(1)}, u32[]{:S(2)}, u32[]{:S(2)}) %collective-permute-start.5) | collective-permute-done | bytes 49184 | tf_op jit(solution)/shard_map/ppermute | solution.py:176
  53.8 0.7 %combine.1 = bf16[4,3072]{1,0:T(4,128)(2,1)} custom-call(f32[8,2,768]{2,1,0:T(2,128)S(1)} %all_to_all.11.own_ref, f32[8,2,768]{2,1,0:T(2,128)S(1)} %collective-permute-done.5.other_ref, f32[6,4,128]{2,1,0:T(4,128)S(1)} %get-tuple-element.8.table_ref), custom_call_target="tpu_custom_call" | custom-call | tf_op jit(solution)/shard_map/combine/pallas_call | solution.py:211
  (2 shorter events, 0.0 us)
Async XLA Ops:
  0.0 17.5 %copy-start.1 = (bf16[1,6144,2048]{2,1,0:T(8,128)(2,1)S(1)}, bf16[1,6144,2048]{2,1,0:T(8,128)(2,1)}, u32[]{:S(2)}) copy-start(bf16[1,6144,2048]{2,1,0:T(8,128)(2,1)} %w_ref.2) | copy-start | bytes 75497472
  1.0 19.8 %copy-start.2 = (bf16[1,6144,2048]{2,1,0:T(8,128)(2,1)S(1)}, bf16[1,6144,2048]{2,1,0:T(8,128)(2,1)}, u32[]{:S(2)}) copy-start(bf16[1,6144,2048]{2,1,0:T(8,128)(2,1)} %w_ref.3) | copy-start | bytes 75497472
  20.9 13.8 %copy-start = (bf16[1,768,16384]{2,1,0:T(8,128)(2,1)S(1)}, bf16[1,768,16384]{2,1,0:T(8,128)(2,1)}, u32[]{:S(2)}) copy-start(bf16[1,768,16384]{2,1,0:T(8,128)(2,1)} %refs_1_.3) | copy-start | bytes 75497472
  24.2 5.0 %collective-permute-start.3 = (bf16[16,2048]{1,0:T(8,128)(2,1)S(1)}, bf16[16,2048]{1,0:T(8,128)(2,1)S(1)}, u32[]{:S(2)}, u32[]{:S(2)}) collective-permute-start(bf16[16,2048]{1,0:T(8,128)(2,1)S(1)} %hidden.1.refs_0_), channel_id=1, source_target_pairs={{0,1},{1,0},{2,3},{3,2},{4,5},{5,4},{6,7},{7,6},{8,9},{9,8},{10,11... | collective-permute-start | bytes 196616 | tf_op jit(solution)/shard_map/ppermute | solution.py:173
  24.8 6.8 %collective-permute-start = (bf16[16,2048]{1,0:T(8,128)(2,1)S(1)}, bf16[16,2048]{1,0:T(8,128)(2,1)S(1)}, u32[]{:S(2)}, u32[]{:S(2)}) collective-permute-start(bf16[16,2048]{1,0:T(8,128)(2,1)S(1)} %hidden.1.refs_0_), channel_id=1, source_target_pairs={{0,6},{1,7},{2,4},{3,5},{4,2},{5,3},{6,0},{7,1},{8,14},{9,15},{10,... | collective-permute-start | bytes 196616 | tf_op jit(solution)/shard_map/ppermute | solution.py:173
  25.8 7.6 %collective-permute-start.1 = (bf16[16,2048]{1,0:T(8,128)(2,1)S(1)}, bf16[16,2048]{1,0:T(8,128)(2,1)S(1)}, u32[]{:S(2)}, u32[]{:S(2)}) collective-permute-start(bf16[16,2048]{1,0:T(8,128)(2,1)S(1)} %hidden.1.refs_0_), channel_id=1, source_target_pairs={{0,4},{1,5},{2,6},{3,7},{4,0},{5,1},{6,2},{7,3},{8,12},{9,13},{10,... | collective-permute-start | bytes 196616 | tf_op jit(solution)/shard_map/ppermute | solution.py:173
  27.0 6.5 %collective-permute-start.2 = (bf16[16,2048]{1,0:T(8,128)(2,1)S(1)}, bf16[16,2048]{1,0:T(8,128)(2,1)S(1)}, u32[]{:S(2)}, u32[]{:S(2)}) collective-permute-start(bf16[16,2048]{1,0:T(8,128)(2,1)S(1)} %hidden.1.refs_0_), channel_id=1, source_target_pairs={{0,2},{1,3},{2,0},{3,1},{4,6},{5,7},{6,4},{7,5},{8,10},{9,11},{10,... | collective-permute-start | bytes 196616 | tf_op jit(solution)/shard_map/ppermute | solution.py:173
  33.4 6.6 %collective-permute-start.4 = (bf16[3,16,2048]{2,1,0:T(8,128)(2,1)S(1)}, bf16[3,16,2048]{2,1,0:T(8,128)(2,1)S(1)}, u32[]{:S(2)}, u32[]{:S(2)}) collective-permute-start(bf16[3,16,2048]{2,1,0:T(8,128)(2,1)S(1)} %join.1.refs_0_), channel_id=1, source_target_pairs={{0,1},{1,0},{2,3},{3,2},{4,5},{5,4},{6,7},{7,6},{8,9},{9,8},{10,11... | collective-permute-start | bytes 589832 | tf_op jit(solution)/shard_map/ppermute | solution.py:173
  52.5 1.2 %collective-permute-start.5 = (f32[8,2,768]{2,1,0:T(2,128)S(1)}, f32[8,2,768]{2,1,0:T(2,128)S(1)}, u32[]{:S(2)}, u32[]{:S(2)}) collective-permute-start(f32[8,2,768]{2,1,0:T(2,128)S(1)} %all_to_all.11.own_ref), channel_id=1, source_target_pairs={{0,8},{8,0},{1,9},{9,1},{2,10},{10,2},{3,11},{11,3},{4,12},{12,4},... | collective-permute-start | bytes 147464 | tf_op jit(solution)/shard_map/ppermute | solution.py:176

commit v9 on v7

--- a/solution.py
+++ b/solution.py
@@ -162,6 +162,9 @@
     slots = tiles * SLOTS
     routes, gates = routes.T, gates.T
 
+    def swap(x, bit):
+        return lax.ppermute(x, "tile", [(t, t ^ bit) for t in range(tiles)])
+
     def to_core(x):
         return lax.ppermute(x, "expert", [(0, 1), (1, 0)])
 
@@ -181,6 +184,7 @@
     x = call(merge_kernel, "merge", bf16(2 * slots, half_width), [VMEM], 4 * MIB, 0e-6)(blocks)
     gate = call(gate_kernel, "gate", f32(slots, width), [VMEM] * 2, 4 * MIB, 0e-6)(x, in_vmem(w_gate))
     hidden = call(hidden_kernel, "hidden", bf16(slots, width), [VMEM] * 3, 4 * MIB, 200e-6)(x, in_vmem(w_up), gate)
+
     def down(total, steps, blocks, last):
         first = total is None
         out = f32(tiles, SLOTS, features) if last else f32(features, slots)
@@ -189,14 +193,14 @@
             [VMEM] * (len(blocks) + 2 - first), 8 * MIB, 0e-6,
         )(*blocks, in_vmem(w_down), *(() if first else (total,)))
 
-    far_first = range(tiles - 1, 0, -1)
-    blocks = [(0, hidden)] + [
-        (k, lax.ppermute(hidden, "tile", [(t, t ^ k) for t in range(tiles)])) for k in far_first]
-    total = None
-    for first, last in ((0, 4), (4, 6), (6, 8)):
-        part = blocks[first:last]
-        total = down(total, [k for k, _ in part], [block for _, block in part], last == tiles)
-    result = total
+    beside = swap(hidden, 1)
+    column = [swap(hidden, k) for k in (6, 4, 2)]
+    total = down(None, [0, 1], [hidden, beside], False)
+    total, first = lax.optimization_barrier((total, column[0]))
+    column = [first] + column[1:]
+    other_column = [swap(block, 1) for block in column]
+    total = down(total, [6, 4, 2], column, False)
+    result = down(total, [7, 5, 3], other_column, True)
     back = lax.all_to_all(result, "tile", split_axis=0, concat_axis=0, tiled=True)
     return call(combine_kernel, "combine", bf16(rows, half_width), [VMEM] * 3, 4 * MIB)(back, to_core(back), table)
 

time: 56.8 us -> 53.4 us (0.940)
  starting transfers between devices: 11.1 us -> 8.4 us
  waiting for transfers between devices: 3.82 us -> 3.12 us
    ppermute x7, starting transfers between devices: 11.1 us -> 8.4 us  [swap(): return lax.ppermute(x, 'tile', [(t, t ^ bit) for t in range(tiles)])]
    ppermute x7, waiting for transfers between devices: 2.59 us -> 1.9 us  [swap(): return lax.ppermute(x, 'tile', [(t, t ^ bit) for t in range(tiles)])]
  transfers between devices with their start and end apart: 8 -> 8, of which waited for: 3 -> 4; matrix products, arithmetic and copies ran while one was open for 0% -> 0% of each run, Pallas kernels for 9% -> 8%
where the time goes in v9:
time: 53.4 us; the launch traced here: 53.2 us
  blocking collectives  26.1 us (49%)
  Pallas kernels  15.4 us (29%)
  starting transfers between devices  8.4 us (16%)
  waiting for transfers between devices  3.12 us (6%)
    all_to_all x1, blocking collectives, local_direct(): lax.all_to_all(sends, ('expert', 'tile'), split_axis=0, concat_axis=0, ti...  16.4 us
    all_to_all x1, blocking collectives, local_direct(): lax.all_to_all(result, 'tile', split_axis=0, concat_axis=0, tiled=True)  9.7 us
    ppermute x7, starting transfers between devices, swap(): return lax.ppermute(x, 'tile', [(t, t ^ bit) for t in range(tiles)])  8.4 us
    pallas_call x3, Pallas kernels, down(): call(functools.partial(down_kernel, steps, first, last), 'down', out, [VM...  6.94 us
    pallas_call x1, Pallas kernels, local_direct(): call(hidden_kernel, 'hidden', bf16(slots, width), [VMEM] * 3, 4 * MIB, 0....  3.37 us
    pallas_call x1, Pallas kernels, local_direct(): call(gate_kernel, 'gate', f32(slots, width), [VMEM] * 2, 4 * MIB, 0.0)  3.34 us
    ppermute x7, waiting for transfers between devices, swap(): return lax.ppermute(x, 'tile', [(t, t ^ bit) for t in range(tiles)])  1.9 us
    ppermute x1, waiting for transfers between devices, to_core(): return lax.ppermute(x, 'expert', [(0, 1), (1, 0)])  1.23 us
  transfers between devices with their start and end apart: 8, of which 4 were waited for; matrix products, arithmetic and copies ran while one was open for 0% of the time, Pallas kernels for 8%

profile of v9, /device:TPU:0, one launch (start us, length us, event | category | flops | bytes accessed | tf_op | source)
XLA Modules:
  0.0 53.2 jit_solution(11294502663379174873)
XLA Ops:
  0.0 0.0 copy-start.1
  0.0 1.0 %dispatch.1 = (bf16[16,2,3072]{2,1,0:T(2,128)(2,1)S(1)}, f32[6,4,128]{2,1,0:T(4,128)S(1)}) custom-call(bf16[4,3072]{1,0:T(4,128)(2,1)} %tokens_hbm.1, s32[2,4]{1,0:T(2,128)} %bitcast.2, f32[2,4]{1,0:T(2,128)} %bitcast.3), custom_call_target="tpu_custom_call" | custom-call | flops 599999971328 | tf_op jit(solution)/shard_map/dispatch/pallas_call | solution.py:173
  1.0 0.0 copy-start.2
  1.0 16.4 %all_to_all.10.blocks_ref = bf16[16,2,3072]{2,1,0:T(2,128)(2,1)S(1)} all-to-all(bf16[16,2,3072]{2,1,0:T(2,128)(2,1)S(1)} %get-tuple-element.9), channel_id=1, replica_groups=mesh['group'=2,'expert'=2,'tile'=8] {'expert','tile'}, dimensions={0} | all-to-all | bytes 393216 | tf_op jit(solution)/shard_map/all_to_all | solution.py:183
  17.5 0.0 copy-done.1
  17.5 3.3 %gate.1.gate_ref = f32[16,2048]{1,0:T(8,128)S(1)} custom-call(bf16[32,3072]{1,0:T(8,128)(2,1)S(1)} %merge.1.rows_ref, bf16[1,6144,2048]{2,1,0:T(8,128)(2,1)S(1)} %copy-done.1), custom_call_target="tpu_custom_call" | custom-call | tf_op jit(solution)/shard_map/gate/pallas_call | solution.py:185
  20.9 0.0 copy-done.2
  20.9 0.0 copy-start
  20.9 3.4 %hidden.1.refs_0_ = bf16[16,2048]{1,0:T(8,128)(2,1)S(1)} custom-call(bf16[32,3072]{1,0:T(8,128)(2,1)S(1)} %merge.1.rows_ref, bf16[1,6144,2048]{2,1,0:T(8,128)(2,1)S(1)} %copy-done.2, f32[16,2048]{1,0:T(8,128)S(1)} %gate.1.gate_ref), custom_call_target="tpu_custom_call" | custom-call | flops 199999995904 | tf_op jit(solution)/shard_map/hidden/pallas_call | solution.py:186
  24.2 0.6 %collective-permute-start = (bf16[16,2048]{1,0:T(8,128)(2,1)S(1)}, bf16[16,2048]{1,0:T(8,128)(2,1)S(1)}, u32[]{:S(2)}, u32[]{:S(2)}) collective-permute-start(bf16[16,2048]{1,0:T(8,128)(2,1)S(1)} %hidden.1.refs_0_), channel_id=1, source_target_pairs={{0,1},{1,0},{2,3},{3,2},{4,5},{5,4},{6,7},{7,6},{8,9},{9,8},{10,11... | collective-permute-start | bytes 196616 | tf_op jit(solution)/shard_map/ppermute | solution.py:166
  24.8 1.0 %collective-permute-start.1 = (bf16[16,2048]{1,0:T(8,128)(2,1)S(1)}, bf16[16,2048]{1,0:T(8,128)(2,1)S(1)}, u32[]{:S(2)}, u32[]{:S(2)}) collective-permute-start(bf16[16,2048]{1,0:T(8,128)(2,1)S(1)} %hidden.1.refs_0_), channel_id=1, source_target_pairs={{0,6},{1,7},{2,4},{3,5},{4,2},{5,3},{6,0},{7,1},{8,14},{9,15},{10,... | collective-permute-start | bytes 196616 | tf_op jit(solution)/shard_map/ppermute | solution.py:166
  25.8 1.2 %collective-permute-start.3 = (bf16[16,2048]{1,0:T(8,128)(2,1)S(1)}, bf16[16,2048]{1,0:T(8,128)(2,1)S(1)}, u32[]{:S(2)}, u32[]{:S(2)}) collective-permute-start(bf16[16,2048]{1,0:T(8,128)(2,1)S(1)} %hidden.1.refs_0_), channel_id=1, source_target_pairs={{0,4},{1,5},{2,6},{3,7},{4,0},{5,1},{6,2},{7,3},{8,12},{9,13},{10,... | collective-permute-start | bytes 196616 | tf_op jit(solution)/shard_map/ppermute | solution.py:166
  27.0 2.2 %collective-permute-start.5 = (bf16[16,2048]{1,0:T(8,128)(2,1)S(1)}, bf16[16,2048]{1,0:T(8,128)(2,1)S(1)}, u32[]{:S(2)}, u32[]{:S(2)}) collective-permute-start(bf16[16,2048]{1,0:T(8,128)(2,1)S(1)} %hidden.1.refs_0_), channel_id=1, source_target_pairs={{0,2},{1,3},{2,0},{3,1},{4,6},{5,7},{6,4},{7,5},{8,10},{9,11},{10,... | collective-permute-start | bytes 196616 | tf_op jit(solution)/shard_map/ppermute | solution.py:166
  29.2 0.0 collective-permute-done.refs_1_
  29.2 0.0 copy-done
  29.2 1.8 %down.3.refs_4_ = f32[768,16]{1,0:T(8,128)S(1)} custom-call(bf16[16,2048]{1,0:T(8,128)(2,1)S(1)} %hidden.1.refs_0_, bf16[16,2048]{1,0:T(8,128)(2,1)S(1)} %collective-permute-done.refs_1_, bf16[1,768,16384]{2,1,0:T(8,128)(2,1)S(1)} %copy-done), custom_call_target="tpu_custom_call" | custom-call | tf_op jit(solution)/shard_map/down/pallas_call | solution.py:191
  31.0 0.6 %collective-permute-done.1.refs_0_ = bf16[16,2048]{1,0:T(8,128)(2,1)S(1)} collective-permute-done((bf16[16,2048]{1,0:T(8,128)(2,1)S(1)}, bf16[16,2048]{1,0:T(8,128)(2,1)S(1)}, u32[]{:S(2)}, u32[]{:S(2)}) %collective-permute-start.1) | collective-permute-done | bytes 65568 | tf_op jit(solution)/shard_map/ppermute | solution.py:166
  31.6 1.4 %collective-permute-start.2 = (bf16[16,2048]{1,0:T(8,128)(2,1)S(1)}, bf16[16,2048]{1,0:T(8,128)(2,1)S(1)}, u32[]{:S(2)}, u32[]{:S(2)}) collective-permute-start(bf16[16,2048]{1,0:T(8,128)(2,1)S(1)} %collective-permute-done.1.refs_0_), channel_id=1, source_target_pairs={{0,1},{1,0},{2,3},{3,2},{4,5},{5,4},{6,7},{7,6},{8,9},{9,8},{10,11... | collective-permute-start | bytes 196616 | tf_op jit(solution)/shard_map/ppermute | solution.py:166
  33.0 0.4 collective-permute-done.3.refs_1_
  33.4 1.2 %collective-permute-start.4 = (bf16[16,2048]{1,0:T(8,128)(2,1)S(1)}, bf16[16,2048]{1,0:T(8,128)(2,1)S(1)}, u32[]{:S(2)}, u32[]{:S(2)}) collective-permute-start(bf16[16,2048]{1,0:T(8,128)(2,1)S(1)} %collective-permute-done.3.refs_1_), channel_id=1, source_target_pairs={{0,1},{1,0},{2,3},{3,2},{4,5},{5,4},{6,7},{7,6},{8,9},{9,8},{10,11... | collective-permute-start | bytes 196616 | tf_op jit(solution)/shard_map/ppermute | solution.py:166
  34.6 0.0 collective-permute-done.5.refs_2_
  34.6 0.8 %collective-permute-start.6 = (bf16[16,2048]{1,0:T(8,128)(2,1)S(1)}, bf16[16,2048]{1,0:T(8,128)(2,1)S(1)}, u32[]{:S(2)}, u32[]{:S(2)}) collective-permute-start(bf16[16,2048]{1,0:T(8,128)(2,1)S(1)} %collective-permute-done.5.refs_2_), channel_id=1, source_target_pairs={{0,1},{1,0},{2,3},{3,2},{4,5},{5,4},{6,7},{7,6},{8,9},{9,8},{10,11... | collective-permute-start | bytes 196616 | tf_op jit(solution)/shard_map/ppermute | solution.py:166
  35.5 2.6 %down.4.refs_4_ = f32[768,16]{1,0:T(8,128)S(1)} custom-call(bf16[16,2048]{1,0:T(8,128)(2,1)S(1)} %collective-permute-done.1.refs_0_, bf16[16,2048]{1,0:T(8,128)(2,1)S(1)} %collective-permute-done.3.refs_1_, bf16[16,2048]{1,0:T(8,128)(2,1)S(1)} %collective-permute-done.5.refs_2_, bf16[1,768,16384]{2,1,0:T(8,128)(2,1)S(1)} %copy-done, f32[768,16]{1,0:T(8,128)S(1)} %down.3.refs_4_), custom_call_target="tpu_custom_call" | custom-call | tf_op jit(solution)/shard_map/down/pallas_call | solution.py:191
  38.0 0.0 collective-permute-done.2.refs_0_
  38.0 0.0 collective-permute-done.4.refs_1_
  38.1 0.8 %collective-permute-done.6.refs_2_ = bf16[16,2048]{1,0:T(8,128)(2,1)S(1)} collective-permute-done((bf16[16,2048]{1,0:T(8,128)(2,1)S(1)}, bf16[16,2048]{1,0:T(8,128)(2,1)S(1)}, u32[]{:S(2)}, u32[]{:S(2)}) %collective-permute-start.6) | collective-permute-done | bytes 65568 | tf_op jit(solution)/shard_map/ppermute | solution.py:166
  38.9 2.6 %down.5 = f32[8,2,768]{2,1,0:T(2,128)S(1)} custom-call(bf16[16,2048]{1,0:T(8,128)(2,1)S(1)} %collective-permute-done.2.refs_0_, bf16[16,2048]{1,0:T(8,128)(2,1)S(1)} %collective-permute-done.4.refs_1_, bf16[16,2048]{1,0:T(8,128)(2,1)S(1)} %collective-permute-done.6.refs_2_, bf16[1,768,16384]{2,1,0:T(8,128)(2,1)S(1)} %copy-done, f32[768,16]{1,0:T(8,128)S(1)} %down.4.refs_4_), custom_call_target="tpu_custom_call" | custom-call | tf_op jit(solution)/shard_map/down/pallas_call | solution.py:191
  41.5 9.7 %all_to_all.11.own_ref = f32[8,2,768]{2,1,0:T(2,128)S(1)} all-to-all(f32[8,2,768]{2,1,0:T(2,128)S(1)} %down.5), channel_id=1, replica_groups=mesh['group'=2,'expert'=2,'tile'=8] {'tile'}, dimensions={0} | all-to-all | bytes 98304 | tf_op jit(solution)/shard_map/all_to_all | solution.py:204
  51.2 0.0 collective-permute-start.7
  51.2 1.2 %collective-permute-done.7.other_ref = f32[8,2,768]{2,1,0:T(2,128)S(1)} collective-permute-done((f32[8,2,768]{2,1,0:T(2,128)S(1)}, f32[8,2,768]{2,1,0:T(2,128)S(1)}, u32[]{:S(2)}, u32[]{:S(2)}) %collective-permute-start.7) | collective-permute-done | bytes 49184 | tf_op jit(solution)/shard_map/ppermute | solution.py:169
  52.4 0.7 %combine.1 = bf16[4,3072]{1,0:T(4,128)(2,1)} custom-call(f32[8,2,768]{2,1,0:T(2,128)S(1)} %all_to_all.11.own_ref, f32[8,2,768]{2,1,0:T(2,128)S(1)} %collective-permute-done.7.other_ref, f32[6,4,128]{2,1,0:T(4,128)S(1)} %get-tuple-element.12.table_ref), custom_call_target="tpu_custom_call" | custom-call | tf_op jit(solution)/shard_map/combine/pallas_call | solution.py:205
  (1 shorter events, 0.0 us)
Async XLA Ops:
  0.0 17.5 %copy-start.1 = (bf16[1,6144,2048]{2,1,0:T(8,128)(2,1)S(1)}, bf16[1,6144,2048]{2,1,0:T(8,128)(2,1)}, u32[]{:S(2)}) copy-start(bf16[1,6144,2048]{2,1,0:T(8,128)(2,1)} %w_ref.2) | copy-start | bytes 75497472
  1.0 19.8 %copy-start.2 = (bf16[1,6144,2048]{2,1,0:T(8,128)(2,1)S(1)}, bf16[1,6144,2048]{2,1,0:T(8,128)(2,1)}, u32[]{:S(2)}) copy-start(bf16[1,6144,2048]{2,1,0:T(8,128)(2,1)} %w_ref.3) | copy-start | bytes 75497472
  20.9 8.3 %copy-start = (bf16[1,768,16384]{2,1,0:T(8,128)(2,1)S(1)}, bf16[1,768,16384]{2,1,0:T(8,128)(2,1)}, u32[]{:S(2)}) copy-start(bf16[1,768,16384]{2,1,0:T(8,128)(2,1)} %refs_3_.3) | copy-start | bytes 75497472
  24.2 5.0 %collective-permute-start = (bf16[16,2048]{1,0:T(8,128)(2,1)S(1)}, bf16[16,2048]{1,0:T(8,128)(2,1)S(1)}, u32[]{:S(2)}, u32[]{:S(2)}) collective-permute-start(bf16[16,2048]{1,0:T(8,128)(2,1)S(1)} %hidden.1.refs_0_), channel_id=1, source_target_pairs={{0,1},{1,0},{2,3},{3,2},{4,5},{5,4},{6,7},{7,6},{8,9},{9,8},{10,11... | collective-permute-start | bytes 196616 | tf_op jit(solution)/shard_map/ppermute | solution.py:166
  24.8 6.8 %collective-permute-start.1 = (bf16[16,2048]{1,0:T(8,128)(2,1)S(1)}, bf16[16,2048]{1,0:T(8,128)(2,1)S(1)}, u32[]{:S(2)}, u32[]{:S(2)}) collective-permute-start(bf16[16,2048]{1,0:T(8,128)(2,1)S(1)} %hidden.1.refs_0_), channel_id=1, source_target_pairs={{0,6},{1,7},{2,4},{3,5},{4,2},{5,3},{6,0},{7,1},{8,14},{9,15},{10,... | collective-permute-start | bytes 196616 | tf_op jit(solution)/shard_map/ppermute | solution.py:166
  25.8 7.6 %collective-permute-start.3 = (bf16[16,2048]{1,0:T(8,128)(2,1)S(1)}, bf16[16,2048]{1,0:T(8,128)(2,1)S(1)}, u32[]{:S(2)}, u32[]{:S(2)}) collective-permute-start(bf16[16,2048]{1,0:T(8,128)(2,1)S(1)} %hidden.1.refs_0_), channel_id=1, source_target_pairs={{0,4},{1,5},{2,6},{3,7},{4,0},{5,1},{6,2},{7,3},{8,12},{9,13},{10,... | collective-permute-start | bytes 196616 | tf_op jit(solution)/shard_map/ppermute | solution.py:166
  27.0 7.7 %collective-permute-start.5 = (bf16[16,2048]{1,0:T(8,128)(2,1)S(1)}, bf16[16,2048]{1,0:T(8,128)(2,1)S(1)}, u32[]{:S(2)}, u32[]{:S(2)}) collective-permute-start(bf16[16,2048]{1,0:T(8,128)(2,1)S(1)} %hidden.1.refs_0_), channel_id=1, source_target_pairs={{0,2},{1,3},{2,0},{3,1},{4,6},{5,7},{6,4},{7,5},{8,10},{9,11},{10,... | collective-permute-start | bytes 196616 | tf_op jit(solution)/shard_map/ppermute | solution.py:166
  31.6 6.5 %collective-permute-start.2 = (bf16[16,2048]{1,0:T(8,128)(2,1)S(1)}, bf16[16,2048]{1,0:T(8,128)(2,1)S(1)}, u32[]{:S(2)}, u32[]{:S(2)}) collective-permute-start(bf16[16,2048]{1,0:T(8,128)(2,1)S(1)} %collective-permute-done.1.refs_0_), channel_id=1, source_target_pairs={{0,1},{1,0},{2,3},{3,2},{4,5},{5,4},{6,7},{7,6},{8,9},{9,8},{10,11... | collective-permute-start | bytes 196616 | tf_op jit(solution)/shard_map/ppermute | solution.py:166
  33.4 4.6 %collective-permute-start.4 = (bf16[16,2048]{1,0:T(8,128)(2,1)S(1)}, bf16[16,2048]{1,0:T(8,128)(2,1)S(1)}, u32[]{:S(2)}, u32[]{:S(2)}) collective-permute-start(bf16[16,2048]{1,0:T(8,128)(2,1)S(1)} %collective-permute-done.3.refs_1_), channel_id=1, source_target_pairs={{0,1},{1,0},{2,3},{3,2},{4,5},{5,4},{6,7},{7,6},{8,9},{9,8},{10,11... | collective-permute-start | bytes 196616 | tf_op jit(solution)/shard_map/ppermute | solution.py:166
  34.6 4.3 %collective-permute-start.6 = (bf16[16,2048]{1,0:T(8,128)(2,1)S(1)}, bf16[16,2048]{1,0:T(8,128)(2,1)S(1)}, u32[]{:S(2)}, u32[]{:S(2)}) collective-permute-start(bf16[16,2048]{1,0:T(8,128)(2,1)S(1)} %collective-permute-done.5.refs_2_), channel_id=1, source_target_pairs={{0,1},{1,0},{2,3},{3,2},{4,5},{5,4},{6,7},{7,6},{8,9},{9,8},{10,11... | collective-permute-start | bytes 196616 | tf_op jit(solution)/shard_map/ppermute | solution.py:166
  51.2 1.2 %collective-permute-start.7 = (f32[8,2,768]{2,1,0:T(2,128)S(1)}, f32[8,2,768]{2,1,0:T(2,128)S(1)}, u32[]{:S(2)}, u32[]{:S(2)}) collective-permute-start(f32[8,2,768]{2,1,0:T(2,128)S(1)} %all_to_all.11.own_ref), channel_id=1, source_target_pairs={{0,8},{8,0},{1,9},{9,1},{2,10},{10,2},{3,11},{11,3},{4,12},{12,4},... | collective-permute-start | bytes 147464 | tf_op jit(solution)/shard_map/ppermute | solution.py:169

commit v10 on v9

--- a/solution.py
+++ b/solution.py
@@ -120,23 +120,18 @@
     out_ref = rest[-1]
     me = lax.axis_index("tile")
     slots, width = blocks[0].shape
-    part = 256
-    starts = [pl.multiple_of((me ^ step) * width, width) for step in steps]
-    for i in range(w_ref.shape[1] // part):
-        rows = slice(i * part, (i + 1) * part)
-        total = None if first else rest[0][rows, :]
-        for block, start in zip(blocks, starts):
-            term = lax.dot_general(
-                w_ref[0, rows, pl.ds(start, width)], block[...], (((1,), (1,)), ((), ())),
-                preferred_element_type=jnp.float32,
-            )
-            total = term if total is None else total + term
-        if not last:
-            out_ref[rows, :] = total
-        else:
-            total = total.T
-            for t in range(out_ref.shape[0]):
-                out_ref[t, :, rows] = total[t * SLOTS:(t + 1) * SLOTS, :]
+    total = None if first else rest[0][...]
+    for step, block in zip(steps, blocks):
+        columns = pl.ds(pl.multiple_of((me ^ step) * width, width), width)
+        term = lax.dot_general(
+            w_ref[0, :, columns], block[...], (((1,), (1,)), ((), ())), preferred_element_type=jnp.float32)
+        total = term if total is None else total + term
+    if not last:
+        out_ref[...] = total
+    else:
+        total = total.T
+        for t in range(out_ref.shape[0]):
+            out_ref[t] = total[t * SLOTS:(t + 1) * SLOTS, :]
 
 
 def combine_kernel(own_ref, other_ref, table_ref, out_ref):
@@ -190,17 +185,19 @@
         out = f32(tiles, SLOTS, features) if last else f32(features, slots)
         return call(
             functools.partial(down_kernel, steps, first, last), "down", out,
-            [VMEM] * (len(blocks) + 2 - first), 8 * MIB, 0e-6,
+            [VMEM] * (len(blocks) + 2 - first), 10 * MIB, 0e-6,
         )(*blocks, in_vmem(w_down), *(() if first else (total,)))
 
+    column = [swap(hidden, k) for k in (6, 4, 2)]
     beside = swap(hidden, 1)
-    column = [swap(hidden, k) for k in (6, 4, 2)]
-    total = down(None, [0, 1], [hidden, beside], False)
-    total, first = lax.optimization_barrier((total, column[0]))
-    column = [first] + column[1:]
+    total = down(None, [0], [hidden], False)
+    total = down(total, [1], [beside], False)
+    total, column[0] = lax.optimization_barrier((total, column[0]))
     other_column = [swap(block, 1) for block in column]
-    total = down(total, [6, 4, 2], column, False)
-    result = down(total, [7, 5, 3], other_column, True)
+    total = down(total, [6, 4], column[:2], False)
+    total = down(total, [2], column[2:], False)
+    total = down(total, [7, 5], other_column[:2], False)
+    result = down(total, [3], other_column[2:], True)
     back = lax.all_to_all(result, "tile", split_axis=0, concat_axis=0, tiled=True)
     return call(combine_kernel, "combine", bf16(rows, half_width), [VMEM] * 3, 4 * MIB)(back, to_core(back), table)
 

time: 53.4 us -> 53.1 us (level)
  waiting for transfers between devices: 3.12 us -> 2.13 us
    ppermute x7, waiting for transfers between devices: 1.9 us -> 0.91 us  [swap(): return lax.ppermute(x, 'tile', [(t, t ^ bit) for t in range(tiles)])]
    pallas_call x3 -> x6, Pallas kernels: 6.94 us -> 7.4 us  [down(): call(functools.partial(down_kernel, steps, first, last), 'down', out, [VM...]
  transfers between devices with their start and end apart: 8 -> 8, of which waited for: 4 -> 3; matrix products, arithmetic and copies ran while one was open for 0% -> 0% of each run, Pallas kernels for 8% -> 12%
where the time goes in v10:
time: 53.1 us; the launch traced here: 52.9 us
  blocking collectives  26.4 us (50%)
  Pallas kernels  15.9 us (30%)
  starting transfers between devices  8.4 us (16%)
  waiting for transfers between devices  2.13 us (4%)
    all_to_all x1, blocking collectives, local_direct(): lax.all_to_all(sends, ('expert', 'tile'), split_axis=0, concat_axis=0, ti...  16.4 us
    all_to_all x1, blocking collectives, local_direct(): lax.all_to_all(result, 'tile', split_axis=0, concat_axis=0, tiled=True)  9.93 us
    ppermute x7, starting transfers between devices, swap(): return lax.ppermute(x, 'tile', [(t, t ^ bit) for t in range(tiles)])  8.4 us
    pallas_call x6, Pallas kernels, down(): call(functools.partial(down_kernel, steps, first, last), 'down', out, [VM...  7.4 us
    pallas_call x1, Pallas kernels, local_direct(): call(hidden_kernel, 'hidden', bf16(slots, width), [VMEM] * 3, 4 * MIB, 0....  3.37 us
    pallas_call x1, Pallas kernels, local_direct(): call(gate_kernel, 'gate', f32(slots, width), [VMEM] * 2, 4 * MIB, 0.0)  3.34 us
    ppermute x1, waiting for transfers between devices, to_core(): return lax.ppermute(x, 'expert', [(0, 1), (1, 0)])  1.23 us
  transfers between devices with their start and end apart: 8, of which 3 were waited for; matrix products, arithmetic and copies ran while one was open for 0% of the time, Pallas kernels for 12%

profile of v10, /device:TPU:0, one launch (start us, length us, event | category | flops | bytes accessed | tf_op | source)
XLA Modules:
  0.0 52.9 jit_solution(8843259041799485969)
XLA Ops:
  0.0 1.0 %dispatch.1 = (bf16[16,2,3072]{2,1,0:T(2,128)(2,1)S(1)}, f32[6,4,128]{2,1,0:T(4,128)S(1)}) custom-call(bf16[4,3072]{1,0:T(4,128)(2,1)} %tokens_hbm.1, s32[2,4]{1,0:T(2,128)} %bitcast.2, f32[2,4]{1,0:T(2,128)} %bitcast.3), custom_call_target="tpu_custom_call" | custom-call | flops 599999971328 | tf_op jit(solution)/shard_map/dispatch/pallas_call | solution.py:168
  1.0 0.0 copy-start.2
  1.0 16.4 %all_to_all.10.blocks_ref = bf16[16,2,3072]{2,1,0:T(2,128)(2,1)S(1)} all-to-all(bf16[16,2,3072]{2,1,0:T(2,128)(2,1)S(1)} %get-tuple-element.9), channel_id=1, replica_groups=mesh['group'=2,'expert'=2,'tile'=8] {'expert','tile'}, dimensions={0} | all-to-all | bytes 393216 | tf_op jit(solution)/shard_map/all_to_all | solution.py:178
  17.5 0.0 copy-done.1
  17.5 3.3 %gate.1.gate_ref = f32[16,2048]{1,0:T(8,128)S(1)} custom-call(bf16[32,3072]{1,0:T(8,128)(2,1)S(1)} %merge.1.rows_ref, bf16[1,6144,2048]{2,1,0:T(8,128)(2,1)S(1)} %copy-done.1), custom_call_target="tpu_custom_call" | custom-call | tf_op jit(solution)/shard_map/gate/pallas_call | solution.py:180
  20.9 0.0 copy-done.2
  20.9 3.4 %hidden.1.refs_0_ = bf16[16,2048]{1,0:T(8,128)(2,1)S(1)} custom-call(bf16[32,3072]{1,0:T(8,128)(2,1)S(1)} %merge.1.rows_ref, bf16[1,6144,2048]{2,1,0:T(8,128)(2,1)S(1)} %copy-done.2, f32[16,2048]{1,0:T(8,128)S(1)} %gate.1.gate_ref), custom_call_target="tpu_custom_call" | custom-call | flops 199999995904 | tf_op jit(solution)/shard_map/hidden/pallas_call | solution.py:181
  24.2 0.6 %collective-permute-start.2 = (bf16[16,2048]{1,0:T(8,128)(2,1)S(1)}, bf16[16,2048]{1,0:T(8,128)(2,1)S(1)}, u32[]{:S(2)}, u32[]{:S(2)}) collective-permute-start(bf16[16,2048]{1,0:T(8,128)(2,1)S(1)} %hidden.1.refs_0_), channel_id=1, source_target_pairs={{0,1},{1,0},{2,3},{3,2},{4,5},{5,4},{6,7},{7,6},{8,9},{9,8},{10,11... | collective-permute-start | bytes 196616 | tf_op jit(solution)/shard_map/ppermute | solution.py:161
  24.8 1.0 %collective-permute-start.3 = (bf16[16,2048]{1,0:T(8,128)(2,1)S(1)}, bf16[16,2048]{1,0:T(8,128)(2,1)S(1)}, u32[]{:S(2)}, u32[]{:S(2)}) collective-permute-start(bf16[16,2048]{1,0:T(8,128)(2,1)S(1)} %hidden.1.refs_0_), channel_id=1, source_target_pairs={{0,6},{1,7},{2,4},{3,5},{4,2},{5,3},{6,0},{7,1},{8,14},{9,15},{10,... | collective-permute-start | bytes 196616 | tf_op jit(solution)/shard_map/ppermute | solution.py:161
  25.8 1.2 %collective-permute-start.5 = (bf16[16,2048]{1,0:T(8,128)(2,1)S(1)}, bf16[16,2048]{1,0:T(8,128)(2,1)S(1)}, u32[]{:S(2)}, u32[]{:S(2)}) collective-permute-start(bf16[16,2048]{1,0:T(8,128)(2,1)S(1)} %hidden.1.refs_0_), channel_id=1, source_target_pairs={{0,4},{1,5},{2,6},{3,7},{4,0},{5,1},{6,2},{7,3},{8,12},{9,13},{10,... | collective-permute-start | bytes 196616 | tf_op jit(solution)/shard_map/ppermute | solution.py:161
  27.0 2.2 %collective-permute-start = (bf16[16,2048]{1,0:T(8,128)(2,1)S(1)}, bf16[16,2048]{1,0:T(8,128)(2,1)S(1)}, u32[]{:S(2)}, u32[]{:S(2)}) collective-permute-start(bf16[16,2048]{1,0:T(8,128)(2,1)S(1)} %hidden.1.refs_0_), channel_id=1, source_target_pairs={{0,2},{1,3},{2,0},{3,1},{4,6},{5,7},{6,4},{7,5},{8,10},{9,11},{10,... | collective-permute-start | bytes 196616 | tf_op jit(solution)/shard_map/ppermute | solution.py:161
  29.2 0.0 copy-done
  29.2 1.0 %down.6.refs_2_ = f32[768,16]{1,0:T(8,128)S(1)} custom-call(bf16[16,2048]{1,0:T(8,128)(2,1)S(1)} %hidden.1.refs_0_, bf16[1,768,16384]{2,1,0:T(8,128)(2,1)S(1)} %copy-done), custom_call_target="tpu_custom_call" | custom-call | tf_op jit(solution)/shard_map/down/pallas_call | solution.py:186
  30.2 0.0 collective-permute-done.2.refs_0_
  30.2 1.0 %down.7.refs_3_ = f32[768,16]{1,0:T(8,128)S(1)} custom-call(bf16[16,2048]{1,0:T(8,128)(2,1)S(1)} %collective-permute-done.2.refs_0_, bf16[1,768,16384]{2,1,0:T(8,128)(2,1)S(1)} %copy-done, f32[768,16]{1,0:T(8,128)S(1)} %down.6.refs_2_), custom_call_target="tpu_custom_call" | custom-call | tf_op jit(solution)/shard_map/down/pallas_call | solution.py:186
  31.1 0.5 collective-permute-done.3.refs_0_
  31.6 1.4 %collective-permute-start.4 = (bf16[16,2048]{1,0:T(8,128)(2,1)S(1)}, bf16[16,2048]{1,0:T(8,128)(2,1)S(1)}, u32[]{:S(2)}, u32[]{:S(2)}) collective-permute-start(bf16[16,2048]{1,0:T(8,128)(2,1)S(1)} %collective-permute-done.3.refs_0_), channel_id=1, source_target_pairs={{0,1},{1,0},{2,3},{3,2},{4,5},{5,4},{6,7},{7,6},{8,9},{9,8},{10,11... | collective-permute-start | bytes 196616 | tf_op jit(solution)/shard_map/ppermute | solution.py:161
  33.0 0.4 collective-permute-done.5.refs_1_
  33.4 1.2 %collective-permute-start.6 = (bf16[16,2048]{1,0:T(8,128)(2,1)S(1)}, bf16[16,2048]{1,0:T(8,128)(2,1)S(1)}, u32[]{:S(2)}, u32[]{:S(2)}) collective-permute-start(bf16[16,2048]{1,0:T(8,128)(2,1)S(1)} %collective-permute-done.5.refs_1_), channel_id=1, source_target_pairs={{0,1},{1,0},{2,3},{3,2},{4,5},{5,4},{6,7},{7,6},{8,9},{9,8},{10,11... | collective-permute-start | bytes 196616 | tf_op jit(solution)/shard_map/ppermute | solution.py:161
  34.6 0.0 collective-permute-done.refs_0_
  34.6 0.8 %collective-permute-start.1 = (bf16[16,2048]{1,0:T(8,128)(2,1)S(1)}, bf16[16,2048]{1,0:T(8,128)(2,1)S(1)}, u32[]{:S(2)}, u32[]{:S(2)}) collective-permute-start(bf16[16,2048]{1,0:T(8,128)(2,1)S(1)} %collective-permute-done.refs_0_), channel_id=1, source_target_pairs={{0,1},{1,0},{2,3},{3,2},{4,5},{5,4},{6,7},{7,6},{8,9},{9,8},{10,11... | collective-permute-start | bytes 196616 | tf_op jit(solution)/shard_map/ppermute | solution.py:161
  35.5 1.8 %down.8.refs_2_ = f32[768,16]{1,0:T(8,128)S(1)} custom-call(bf16[16,2048]{1,0:T(8,128)(2,1)S(1)} %collective-permute-done.3.refs_0_, bf16[16,2048]{1,0:T(8,128)(2,1)S(1)} %collective-permute-done.5.refs_1_, bf16[1,768,16384]{2,1,0:T(8,128)(2,1)S(1)} %copy-done, f32[768,16]{1,0:T(8,128)S(1)} %down.7.refs_3_), custom_call_target="tpu_custom_call" | custom-call | tf_op jit(solution)/shard_map/down/pallas_call | solution.py:186
  37.2 1.0 %down.9.refs_3_ = f32[768,16]{1,0:T(8,128)S(1)} custom-call(bf16[16,2048]{1,0:T(8,128)(2,1)S(1)} %collective-permute-done.refs_0_, bf16[1,768,16384]{2,1,0:T(8,128)(2,1)S(1)} %copy-done, f32[768,16]{1,0:T(8,128)S(1)} %down.8.refs_2_), custom_call_target="tpu_custom_call" | custom-call | tf_op jit(solution)/shard_map/down/pallas_call | solution.py:186
  38.2 0.0 collective-permute-done.4.refs_0_
  38.2 0.0 collective-permute-done.6.refs_1_
  38.2 1.8 %down.10.refs_2_ = f32[768,16]{1,0:T(8,128)S(1)} custom-call(bf16[16,2048]{1,0:T(8,128)(2,1)S(1)} %collective-permute-done.4.refs_0_, bf16[16,2048]{1,0:T(8,128)(2,1)S(1)} %collective-permute-done.6.refs_1_, bf16[1,768,16384]{2,1,0:T(8,128)(2,1)S(1)} %copy-done, f32[768,16]{1,0:T(8,128)S(1)} %down.9.refs_3_), custom_call_target="tpu_custom_call" | custom-call | tf_op jit(solution)/shard_map/down/pallas_call | solution.py:186
  40.0 0.0 collective-permute-done.1.refs_0_
  40.0 1.0 %down.11 = f32[8,2,768]{2,1,0:T(2,128)S(1)} custom-call(bf16[16,2048]{1,0:T(8,128)(2,1)S(1)} %collective-permute-done.1.refs_0_, bf16[1,768,16384]{2,1,0:T(8,128)(2,1)S(1)} %copy-done, f32[768,16]{1,0:T(8,128)S(1)} %down.10.refs_2_), custom_call_target="tpu_custom_call" | custom-call | tf_op jit(solution)/shard_map/down/pallas_call | solution.py:186
  41.0 9.9 %all_to_all.11.own_ref = f32[8,2,768]{2,1,0:T(2,128)S(1)} all-to-all(f32[8,2,768]{2,1,0:T(2,128)S(1)} %down.11), channel_id=1, replica_groups=mesh['group'=2,'expert'=2,'tile'=8] {'tile'}, dimensions={0} | all-to-all | bytes 98304 | tf_op jit(solution)/shard_map/all_to_all | solution.py:201
  50.9 0.0 collective-permute-start.7
  50.9 1.2 %collective-permute-done.7.other_ref = f32[8,2,768]{2,1,0:T(2,128)S(1)} collective-permute-done((f32[8,2,768]{2,1,0:T(2,128)S(1)}, f32[8,2,768]{2,1,0:T(2,128)S(1)}, u32[]{:S(2)}, u32[]{:S(2)}) %collective-permute-start.7) | collective-permute-done | bytes 49184 | tf_op jit(solution)/shard_map/ppermute | solution.py:164
  52.2 0.7 %combine.1 = bf16[4,3072]{1,0:T(4,128)(2,1)} custom-call(f32[8,2,768]{2,1,0:T(2,128)S(1)} %all_to_all.11.own_ref, f32[8,2,768]{2,1,0:T(2,128)S(1)} %collective-permute-done.7.other_ref, f32[6,4,128]{2,1,0:T(4,128)S(1)} %get-tuple-element.12.table_ref), custom_call_target="tpu_custom_call" | custom-call | tf_op jit(solution)/shard_map/combine/pallas_call | solution.py:202
  (3 shorter events, 0.0 us)
Async XLA Ops:
  0.0 17.5 %copy-start.1 = (bf16[1,6144,2048]{2,1,0:T(8,128)(2,1)S(1)}, bf16[1,6144,2048]{2,1,0:T(8,128)(2,1)}, u32[]{:S(2)}) copy-start(bf16[1,6144,2048]{2,1,0:T(8,128)(2,1)} %w_ref.2) | copy-start | bytes 75497472
  1.0 19.8 %copy-start.2 = (bf16[1,6144,2048]{2,1,0:T(8,128)(2,1)S(1)}, bf16[1,6144,2048]{2,1,0:T(8,128)(2,1)}, u32[]{:S(2)}) copy-start(bf16[1,6144,2048]{2,1,0:T(8,128)(2,1)} %w_ref.3) | copy-start | bytes 75497472
  20.9 8.3 %copy-start = (bf16[1,768,16384]{2,1,0:T(8,128)(2,1)S(1)}, bf16[1,768,16384]{2,1,0:T(8,128)(2,1)}, u32[]{:S(2)}) copy-start(bf16[1,768,16384]{2,1,0:T(8,128)(2,1)} %refs_1_.7) | copy-start | bytes 75497472
  24.2 5.9 %collective-permute-start.2 = (bf16[16,2048]{1,0:T(8,128)(2,1)S(1)}, bf16[16,2048]{1,0:T(8,128)(2,1)S(1)}, u32[]{:S(2)}, u32[]{:S(2)}) collective-permute-start(bf16[16,2048]{1,0:T(8,128)(2,1)S(1)} %hidden.1.refs_0_), channel_id=1, source_target_pairs={{0,1},{1,0},{2,3},{3,2},{4,5},{5,4},{6,7},{7,6},{8,9},{9,8},{10,11... | collective-permute-start | bytes 196616 | tf_op jit(solution)/shard_map/ppermute | solution.py:161
  24.8 6.8 %collective-permute-start.3 = (bf16[16,2048]{1,0:T(8,128)(2,1)S(1)}, bf16[16,2048]{1,0:T(8,128)(2,1)S(1)}, u32[]{:S(2)}, u32[]{:S(2)}) collective-permute-start(bf16[16,2048]{1,0:T(8,128)(2,1)S(1)} %hidden.1.refs_0_), channel_id=1, source_target_pairs={{0,6},{1,7},{2,4},{3,5},{4,2},{5,3},{6,0},{7,1},{8,14},{9,15},{10,... | collective-permute-start | bytes 196616 | tf_op jit(solution)/shard_map/ppermute | solution.py:161
  25.8 7.6 %collective-permute-start.5 = (bf16[16,2048]{1,0:T(8,128)(2,1)S(1)}, bf16[16,2048]{1,0:T(8,128)(2,1)S(1)}, u32[]{:S(2)}, u32[]{:S(2)}) collective-permute-start(bf16[16,2048]{1,0:T(8,128)(2,1)S(1)} %hidden.1.refs_0_), channel_id=1, source_target_pairs={{0,4},{1,5},{2,6},{3,7},{4,0},{5,1},{6,2},{7,3},{8,12},{9,13},{10,... | collective-permute-start | bytes 196616 | tf_op jit(solution)/shard_map/ppermute | solution.py:161
  27.0 7.7 %collective-permute-start = (bf16[16,2048]{1,0:T(8,128)(2,1)S(1)}, bf16[16,2048]{1,0:T(8,128)(2,1)S(1)}, u32[]{:S(2)}, u32[]{:S(2)}) collective-permute-start(bf16[16,2048]{1,0:T(8,128)(2,1)S(1)} %hidden.1.refs_0_), channel_id=1, source_target_pairs={{0,2},{1,3},{2,0},{3,1},{4,6},{5,7},{6,4},{7,5},{8,10},{9,11},{10,... | collective-permute-start | bytes 196616 | tf_op jit(solution)/shard_map/ppermute | solution.py:161
  31.6 6.6 %collective-permute-start.4 = (bf16[16,2048]{1,0:T(8,128)(2,1)S(1)}, bf16[16,2048]{1,0:T(8,128)(2,1)S(1)}, u32[]{:S(2)}, u32[]{:S(2)}) collective-permute-start(bf16[16,2048]{1,0:T(8,128)(2,1)S(1)} %collective-permute-done.3.refs_0_), channel_id=1, source_target_pairs={{0,1},{1,0},{2,3},{3,2},{4,5},{5,4},{6,7},{7,6},{8,9},{9,8},{10,11... | collective-permute-start | bytes 196616 | tf_op jit(solution)/shard_map/ppermute | solution.py:161
  33.4 4.8 %collective-permute-start.6 = (bf16[16,2048]{1,0:T(8,128)(2,1)S(1)}, bf16[16,2048]{1,0:T(8,128)(2,1)S(1)}, u32[]{:S(2)}, u32[]{:S(2)}) collective-permute-start(bf16[16,2048]{1,0:T(8,128)(2,1)S(1)} %collective-permute-done.5.refs_1_), channel_id=1, source_target_pairs={{0,1},{1,0},{2,3},{3,2},{4,5},{5,4},{6,7},{7,6},{8,9},{9,8},{10,11... | collective-permute-start | bytes 196616 | tf_op jit(solution)/shard_map/ppermute | solution.py:161
  34.6 5.4 %collective-permute-start.1 = (bf16[16,2048]{1,0:T(8,128)(2,1)S(1)}, bf16[16,2048]{1,0:T(8,128)(2,1)S(1)}, u32[]{:S(2)}, u32[]{:S(2)}) collective-permute-start(bf16[16,2048]{1,0:T(8,128)(2,1)S(1)} %collective-permute-done.refs_0_), channel_id=1, source_target_pairs={{0,1},{1,0},{2,3},{3,2},{4,5},{5,4},{6,7},{7,6},{8,9},{9,8},{10,11... | collective-permute-start | bytes 196616 | tf_op jit(solution)/shard_map/ppermute | solution.py:161
  50.9 1.2 %collective-permute-start.7 = (f32[8,2,768]{2,1,0:T(2,128)S(1)}, f32[8,2,768]{2,1,0:T(2,128)S(1)}, u32[]{:S(2)}, u32[]{:S(2)}) collective-permute-start(f32[8,2,768]{2,1,0:T(2,128)S(1)} %all_to_all.11.own_ref), channel_id=1, source_target_pairs={{0,8},{8,0},{1,9},{9,1},{2,10},{10,2},{3,11},{11,3},{4,12},{12,4},... | collective-permute-start | bytes 147464 | tf_op jit(solution)/shard_map/ppermute | solution.py:164

commit v11 on v10

--- a/solution.py
+++ b/solution.py
@@ -130,17 +130,27 @@
         out_ref[...] = total
     else:
         total = total.T
-        for t in range(out_ref.shape[0]):
-            out_ref[t] = total[t * SLOTS:(t + 1) * SLOTS, :]
-
-
-def combine_kernel(own_ref, other_ref, table_ref, out_ref):
-    mine = lax.axis_index("expert")
-    halves, features = own_ref.shape[0] // 2, own_ref.shape[2]
+        for t in range(2 * out_ref.shape[0]):
+            out_ref[t // 2, t % 2] = total[t * SLOTS:(t + 1) * SLOTS, :]
+
+
+def split_kernel(blocks_ref, *out_refs):
+    x, core = lax.axis_index("tile") % 2, lax.axis_index("expert")
+    for i, out_ref in enumerate(out_refs):
+        to_x, to_core = x ^ (i % 2), core ^ (i // 2)
+        for z in range(out_ref.shape[0]):
+            out_ref[z] = blocks_ref[to_core * out_ref.shape[0] + z, to_x]
+
+
+def combine_kernel(own_ref, own_x_ref, other_ref, other_x_ref, table_ref, out_ref):
+    x, mine = lax.axis_index("tile") % 2, lax.axis_index("expert")
+    features = own_ref.shape[2]
     weight = [table_ref[e * (1 + SLOTS)][:, :1] for e in range(2)]
     inside = [[table_ref[e * (1 + SLOTS) + 1 + c][:, :1] for c in range(SLOTS)] for e in range(2)]
-    for i in range(halves):
-        own, other = own_ref[mine * halves + i], other_ref[mine * halves + i]
+    for i in range(2 * own_ref.shape[0]):
+        z, at = i // 2, i % 2
+        own = jnp.where(x == at, own_ref[z], own_x_ref[z])
+        other = jnp.where(x == at, other_ref[z], other_x_ref[z])
         mixed = jnp.zeros((out_ref.shape[0], features), jnp.float32)
         for e in range(2):
             both = jnp.where(mine == e, own, other)
@@ -182,7 +192,7 @@
 
     def down(total, steps, blocks, last):
         first = total is None
-        out = f32(tiles, SLOTS, features) if last else f32(features, slots)
+        out = f32(tiles // 2, 2, SLOTS, features) if last else f32(features, slots)
         return call(
             functools.partial(down_kernel, steps, first, last), "down", out,
             [VMEM] * (len(blocks) + 2 - first), 10 * MIB, 0e-6,
@@ -198,8 +208,14 @@
     total = down(total, [2], column[2:], False)
     total = down(total, [7, 5], other_column[:2], False)
     result = down(total, [3], other_column[2:], True)
-    back = lax.all_to_all(result, "tile", split_axis=0, concat_axis=0, tiled=True)
-    return call(combine_kernel, "combine", bf16(rows, half_width), [VMEM] * 3, 4 * MIB)(back, to_core(back), table)
+    columns = [list(range(x, tiles, 2)) for x in range(2)]
+    back = lax.all_to_all(result, "tile", split_axis=0, concat_axis=0, axis_index_groups=columns, tiled=True)
+    quarter = f32(tiles // 4, SLOTS, features)
+    own, to_x, to_other, to_both = call(split_kernel, "split", (quarter,) * 4, [VMEM], 4 * MIB)(back)
+    pairs = [(e * tiles + t, (1 - e) * tiles + (t ^ 1)) for e in range(2) for t in range(tiles)]
+    both = lax.ppermute(to_both, ("expert", "tile"), pairs)
+    return call(combine_kernel, "combine", bf16(rows, half_width), [VMEM] * 5, 4 * MIB)(
+        own, swap(to_x, 1), to_core(to_other), both, table)
 
 
 def local_gathered(tokens, routes, gates, w_gate, w_up, w_down):

time: 53.1 us -> 54.5 us (1.026)
  starting transfers between devices: 8.4 us -> 10.5 us
  blocking collectives: 26.4 us -> 24.6 us
  waiting for transfers between devices: 2.13 us -> 3.08 us
    all_to_all x1, blocking collectives: 9.93 us -> 8.2 us  [local_direct(): lax.all_to_all(result, 'tile', split_axis=0, concat_axis=0, axis_index_gr...]
    ppermute x7 -> x8, waiting for transfers between devices: 0.91 us -> 2.46 us  [swap(): return lax.ppermute(x, 'tile', [(t, t ^ bit) for t in range(tiles)])]
    ppermute x1, waiting for transfers between devices: 1.23 us -> 0.01 us  [to_core(): return lax.ppermute(x, 'expert', [(0, 1), (1, 0)])]
    ppermute x7 -> x8, starting transfers between devices: 8.4 us -> 9.59 us  [swap(): return lax.ppermute(x, 'tile', [(t, t ^ bit) for t in range(tiles)])]
    ppermute x0 -> x1, starting transfers between devices: none -> 0.94 us  [local_direct(): both = lax.ppermute(to_both, ('expert', 'tile'), pairs)]
    ppermute x0 -> x1, waiting for transfers between devices: none -> 0.62 us  [local_direct(): both = lax.ppermute(to_both, ('expert', 'tile'), pairs)]
  transfers between devices with their start and end apart: 8 -> 10, of which waited for: 3 -> 4; matrix products, arithmetic and copies ran while one was open for 0% -> 0% of each run, Pallas kernels for 12% -> 12%
where the time goes in v11:
time: 54.5 us; the launch traced here: 54.3 us
  blocking collectives  24.6 us (45%)
  Pallas kernels  15.9 us (29%)
  starting transfers between devices  10.5 us (19%)
  waiting for transfers between devices  3.08 us (6%)
    all_to_all x1, blocking collectives, local_direct(): lax.all_to_all(sends, ('expert', 'tile'), split_axis=0, concat_axis=0, ti...  16.4 us
    ppermute x8, starting transfers between devices, swap(): return lax.ppermute(x, 'tile', [(t, t ^ bit) for t in range(tiles)])  9.59 us
    all_to_all x1, blocking collectives, local_direct(): lax.all_to_all(result, 'tile', split_axis=0, concat_axis=0, axis_index_gr...  8.2 us
    pallas_call x6, Pallas kernels, down(): call(functools.partial(down_kernel, steps, first, last), 'down', out, [VM...  7.4 us
    pallas_call x1, Pallas kernels, local_direct(): call(hidden_kernel, 'hidden', bf16(slots, width), [VMEM] * 3, 4 * MIB, 0....  3.37 us
    pallas_call x1, Pallas kernels, local_direct(): call(gate_kernel, 'gate', f32(slots, width), [VMEM] * 2, 4 * MIB, 0.0)  3.34 us
    ppermute x8, waiting for transfers between devices, swap(): return lax.ppermute(x, 'tile', [(t, t ^ bit) for t in range(tiles)])  2.46 us
  transfers between devices with their start and end apart: 10, of which 4 were waited for; matrix products, arithmetic and copies ran while one was open for 0% of the time, Pallas kernels for 12%

profile of v11, /device:TPU:0, one launch (start us, length us, event | category | flops | bytes accessed | tf_op | source)
XLA Modules:
  0.0 54.3 jit_solution(4723211117860873060)
XLA Ops:
  0.0 1.0 %dispatch.1 = (bf16[16,2,3072]{2,1,0:T(2,128)(2,1)S(1)}, f32[6,4,128]{2,1,0:T(4,128)S(1)}) custom-call(bf16[4,3072]{1,0:T(4,128)(2,1)} %tokens_hbm.1, s32[2,4]{1,0:T(2,128)} %bitcast.2, f32[2,4]{1,0:T(2,128)} %bitcast.3), custom_call_target="tpu_custom_call" | custom-call | flops 599999971328 | tf_op jit(solution)/shard_map/dispatch/pallas_call | solution.py:178
  1.0 0.0 copy-start.2
  1.0 16.4 %all_to_all.10.blocks_ref = bf16[16,2,3072]{2,1,0:T(2,128)(2,1)S(1)} all-to-all(bf16[16,2,3072]{2,1,0:T(2,128)(2,1)S(1)} %get-tuple-element.13), channel_id=1, replica_groups=mesh['group'=2,'expert'=2,'tile'=8] {'expert','tile'}, dimensions={0} | all-to-all | bytes 393216 | tf_op jit(solution)/shard_map/all_to_all | solution.py:188
  17.5 0.0 copy-done.1
  17.5 3.3 %gate.1.gate_ref = f32[16,2048]{1,0:T(8,128)S(1)} custom-call(bf16[32,3072]{1,0:T(8,128)(2,1)S(1)} %merge.1.rows_ref, bf16[1,6144,2048]{2,1,0:T(8,128)(2,1)S(1)} %copy-done.1), custom_call_target="tpu_custom_call" | custom-call | tf_op jit(solution)/shard_map/gate/pallas_call | solution.py:190
  20.9 3.4 %hidden.1.refs_0_ = bf16[16,2048]{1,0:T(8,128)(2,1)S(1)} custom-call(bf16[32,3072]{1,0:T(8,128)(2,1)S(1)} %merge.1.rows_ref, bf16[1,6144,2048]{2,1,0:T(8,128)(2,1)S(1)} %copy-done.2, f32[16,2048]{1,0:T(8,128)S(1)} %gate.1.gate_ref), custom_call_target="tpu_custom_call" | custom-call | flops 199999995904 | tf_op jit(solution)/shard_map/hidden/pallas_call | solution.py:191
  24.2 0.6 %collective-permute-start.2 = (bf16[16,2048]{1,0:T(8,128)(2,1)S(1)}, bf16[16,2048]{1,0:T(8,128)(2,1)S(1)}, u32[]{:S(2)}, u32[]{:S(2)}) collective-permute-start(bf16[16,2048]{1,0:T(8,128)(2,1)S(1)} %hidden.1.refs_0_), channel_id=1, source_target_pairs={{0,1},{1,0},{2,3},{3,2},{4,5},{5,4},{6,7},{7,6},{8,9},{9,8},{10,11... | collective-permute-start | bytes 196616 | tf_op jit(solution)/shard_map/ppermute | solution.py:171
  24.8 1.0 %collective-permute-start.3 = (bf16[16,2048]{1,0:T(8,128)(2,1)S(1)}, bf16[16,2048]{1,0:T(8,128)(2,1)S(1)}, u32[]{:S(2)}, u32[]{:S(2)}) collective-permute-start(bf16[16,2048]{1,0:T(8,128)(2,1)S(1)} %hidden.1.refs_0_), channel_id=1, source_target_pairs={{0,6},{1,7},{2,4},{3,5},{4,2},{5,3},{6,0},{7,1},{8,14},{9,15},{10,... | collective-permute-start | bytes 196616 | tf_op jit(solution)/shard_map/ppermute | solution.py:171
  25.8 1.2 %collective-permute-start.5 = (bf16[16,2048]{1,0:T(8,128)(2,1)S(1)}, bf16[16,2048]{1,0:T(8,128)(2,1)S(1)}, u32[]{:S(2)}, u32[]{:S(2)}) collective-permute-start(bf16[16,2048]{1,0:T(8,128)(2,1)S(1)} %hidden.1.refs_0_), channel_id=1, source_target_pairs={{0,4},{1,5},{2,6},{3,7},{4,0},{5,1},{6,2},{7,3},{8,12},{9,13},{10,... | collective-permute-start | bytes 196616 | tf_op jit(solution)/shard_map/ppermute | solution.py:171
  27.0 2.2 %collective-permute-start = (bf16[16,2048]{1,0:T(8,128)(2,1)S(1)}, bf16[16,2048]{1,0:T(8,128)(2,1)S(1)}, u32[]{:S(2)}, u32[]{:S(2)}) collective-permute-start(bf16[16,2048]{1,0:T(8,128)(2,1)S(1)} %hidden.1.refs_0_), channel_id=1, source_target_pairs={{0,2},{1,3},{2,0},{3,1},{4,6},{5,7},{6,4},{7,5},{8,10},{9,11},{10,... | collective-permute-start | bytes 196616 | tf_op jit(solution)/shard_map/ppermute | solution.py:171
  29.2 1.0 %down.6.refs_2_ = f32[768,16]{1,0:T(8,128)S(1)} custom-call(bf16[16,2048]{1,0:T(8,128)(2,1)S(1)} %hidden.1.refs_0_, bf16[1,768,16384]{2,1,0:T(8,128)(2,1)S(1)} %copy-done), custom_call_target="tpu_custom_call" | custom-call | tf_op jit(solution)/shard_map/down/pallas_call | solution.py:196
  30.2 0.0 collective-permute-done.2.refs_0_
  30.2 1.0 %down.7.refs_3_ = f32[768,16]{1,0:T(8,128)S(1)} custom-call(bf16[16,2048]{1,0:T(8,128)(2,1)S(1)} %collective-permute-done.2.refs_0_, bf16[1,768,16384]{2,1,0:T(8,128)(2,1)S(1)} %copy-done, f32[768,16]{1,0:T(8,128)S(1)} %down.6.refs_2_), custom_call_target="tpu_custom_call" | custom-call | tf_op jit(solution)/shard_map/down/pallas_call | solution.py:196
  31.1 0.5 collective-permute-done.3.refs_0_
  31.6 1.4 %collective-permute-start.4 = (bf16[16,2048]{1,0:T(8,128)(2,1)S(1)}, bf16[16,2048]{1,0:T(8,128)(2,1)S(1)}, u32[]{:S(2)}, u32[]{:S(2)}) collective-permute-start(bf16[16,2048]{1,0:T(8,128)(2,1)S(1)} %collective-permute-done.3.refs_0_), channel_id=1, source_target_pairs={{0,1},{1,0},{2,3},{3,2},{4,5},{5,4},{6,7},{7,6},{8,9},{9,8},{10,11... | collective-permute-start | bytes 196616 | tf_op jit(solution)/shard_map/ppermute | solution.py:171
  33.0 0.4 collective-permute-done.5.refs_1_
  33.4 1.2 %collective-permute-start.6 = (bf16[16,2048]{1,0:T(8,128)(2,1)S(1)}, bf16[16,2048]{1,0:T(8,128)(2,1)S(1)}, u32[]{:S(2)}, u32[]{:S(2)}) collective-permute-start(bf16[16,2048]{1,0:T(8,128)(2,1)S(1)} %collective-permute-done.5.refs_1_), channel_id=1, source_target_pairs={{0,1},{1,0},{2,3},{3,2},{4,5},{5,4},{6,7},{7,6},{8,9},{9,8},{10,11... | collective-permute-start | bytes 196616 | tf_op jit(solution)/shard_map/ppermute | solution.py:171
  34.6 0.0 collective-permute-done.refs_0_
  34.6 0.8 %collective-permute-start.1 = (bf16[16,2048]{1,0:T(8,128)(2,1)S(1)}, bf16[16,2048]{1,0:T(8,128)(2,1)S(1)}, u32[]{:S(2)}, u32[]{:S(2)}) collective-permute-start(bf16[16,2048]{1,0:T(8,128)(2,1)S(1)} %collective-permute-done.refs_0_), channel_id=1, source_target_pairs={{0,1},{1,0},{2,3},{3,2},{4,5},{5,4},{6,7},{7,6},{8,9},{9,8},{10,11... | collective-permute-start | bytes 196616 | tf_op jit(solution)/shard_map/ppermute | solution.py:171
  35.5 1.8 %down.8.refs_2_ = f32[768,16]{1,0:T(8,128)S(1)} custom-call(bf16[16,2048]{1,0:T(8,128)(2,1)S(1)} %collective-permute-done.3.refs_0_, bf16[16,2048]{1,0:T(8,128)(2,1)S(1)} %collective-permute-done.5.refs_1_, bf16[1,768,16384]{2,1,0:T(8,128)(2,1)S(1)} %copy-done, f32[768,16]{1,0:T(8,128)S(1)} %down.7.refs_3_), custom_call_target="tpu_custom_call" | custom-call | tf_op jit(solution)/shard_map/down/pallas_call | solution.py:196
  37.2 1.0 %down.9.refs_3_ = f32[768,16]{1,0:T(8,128)S(1)} custom-call(bf16[16,2048]{1,0:T(8,128)(2,1)S(1)} %collective-permute-done.refs_0_, bf16[1,768,16384]{2,1,0:T(8,128)(2,1)S(1)} %copy-done, f32[768,16]{1,0:T(8,128)S(1)} %down.8.refs_2_), custom_call_target="tpu_custom_call" | custom-call | tf_op jit(solution)/shard_map/down/pallas_call | solution.py:196
  38.2 0.0 collective-permute-done.6.refs_1_
  38.2 1.8 %down.10.refs_2_ = f32[768,16]{1,0:T(8,128)S(1)} custom-call(bf16[16,2048]{1,0:T(8,128)(2,1)S(1)} %collective-permute-done.4.refs_0_, bf16[16,2048]{1,0:T(8,128)(2,1)S(1)} %collective-permute-done.6.refs_1_, bf16[1,768,16384]{2,1,0:T(8,128)(2,1)S(1)} %copy-done, f32[768,16]{1,0:T(8,128)S(1)} %down.9.refs_3_), custom_call_target="tpu_custom_call" | custom-call | tf_op jit(solution)/shard_map/down/pallas_call | solution.py:196
  40.0 0.0 collective-permute-done.1.refs_0_
  40.0 1.0 %down.11 = f32[4,2,2,768]{3,2,1,0:T(2,128)S(1)} custom-call(bf16[16,2048]{1,0:T(8,128)(2,1)S(1)} %collective-permute-done.1.refs_0_, bf16[1,768,16384]{2,1,0:T(8,128)(2,1)S(1)} %copy-done, f32[768,16]{1,0:T(8,128)S(1)} %down.10.refs_2_), custom_call_target="tpu_custom_call" | custom-call | tf_op jit(solution)/shard_map/down/pallas_call | solution.py:196
  41.0 8.2 %all_to_all.11.blocks_ref = f32[4,2,2,768]{3,2,1,0:T(2,128)S(1)} all-to-all(f32[4,2,2,768]{3,2,1,0:T(2,128)S(1)} %down.11), channel_id=1, replica_groups={{0,2,4,6},{1,3,5,7},{8,10,12,14},{9,11,13,15},{16,18,20,22},{17,19,21,2..., dimensions={0} | all-to-all | bytes 98304 | tf_op jit(solution)/shard_map/all_to_all | solution.py:212
  49.2 1.2 %collective-permute-start.7 = (f32[2,2,768]{2,1,0:T(2,128)S(1)}, f32[2,2,768]{2,1,0:T(2,128)S(1)}, u32[]{:S(2)}, u32[]{:S(2)}) collective-permute-start(f32[2,2,768]{2,1,0:T(2,128)S(1)} %get-tuple-element.17), channel_id=1, source_target_pairs={{0,1},{1,0},{2,3},{3,2},{4,5},{5,4},{6,7},{7,6},{8,9},{9,8},{10,11... | collective-permute-start | bytes 36872 | tf_op jit(solution)/shard_map/ppermute | solution.py:171
  50.4 0.9 %collective-permute-start.9 = (f32[2,2,768]{2,1,0:T(2,128)S(1)}, f32[2,2,768]{2,1,0:T(2,128)S(1)}, u32[]{:S(2)}, u32[]{:S(2)}) collective-permute-start(f32[2,2,768]{2,1,0:T(2,128)S(1)} %get-tuple-element.19), channel_id=1, source_target_pairs={{0,9},{1,8},{2,11},{3,10},{4,13},{5,12},{6,15},{7,14},{8,1},{9,0},... | collective-permute-start | bytes 36872 | tf_op jit(solution)/shard_map/ppermute | solution.py:216
  51.3 1.6 %collective-permute-done.7.own_x_ref = f32[2,2,768]{2,1,0:T(2,128)S(1)} collective-permute-done((f32[2,2,768]{2,1,0:T(2,128)S(1)}, f32[2,2,768]{2,1,0:T(2,128)S(1)}, u32[]{:S(2)}, u32[]{:S(2)}) %collective-permute-start.7) | collective-permute-done | bytes 12320 | tf_op jit(solution)/shard_map/ppermute | solution.py:171
  52.9 0.0 collective-permute-done.8.other_ref
  52.9 0.6 %collective-permute-done.9.other_x_ref = f32[2,2,768]{2,1,0:T(2,128)S(1)} collective-permute-done((f32[2,2,768]{2,1,0:T(2,128)S(1)}, f32[2,2,768]{2,1,0:T(2,128)S(1)}, u32[]{:S(2)}, u32[]{:S(2)}) %collective-permute-start.9) | collective-permute-done | bytes 12320 | tf_op jit(solution)/shard_map/ppermute | solution.py:216
  53.5 0.7 %combine.1 = bf16[4,3072]{1,0:T(4,128)(2,1)} custom-call(f32[2,2,768]{2,1,0:T(2,128)S(1)} %get-tuple-element.16.own_ref, f32[2,2,768]{2,1,0:T(2,128)S(1)} %collective-permute-done.7.own_x_ref, f32[2,2,768]{2,1,0:T(2,128)S(1)} %collective-permute-done.8.other_ref, f32[2,2,768]{2,1,0:T(2,128)S(1)} %collective-permute-done.9.other_x_ref, ...), custom_call_target="tpu_custom_call" | custom-call | tf_op jit(solution)/shard_map/combine/pallas_call | solution.py:217
  (8 shorter events, 0.0 us)
Async XLA Ops:
  0.0 17.5 %copy-start.1 = (bf16[1,6144,2048]{2,1,0:T(8,128)(2,1)S(1)}, bf16[1,6144,2048]{2,1,0:T(8,128)(2,1)}, u32[]{:S(2)}) copy-start(bf16[1,6144,2048]{2,1,0:T(8,128)(2,1)} %w_ref.2) | copy-start | bytes 75497472
  1.0 19.8 %copy-start.2 = (bf16[1,6144,2048]{2,1,0:T(8,128)(2,1)S(1)}, bf16[1,6144,2048]{2,1,0:T(8,128)(2,1)}, u32[]{:S(2)}) copy-start(bf16[1,6144,2048]{2,1,0:T(8,128)(2,1)} %w_ref.3) | copy-start | bytes 75497472
  20.9 8.3 %copy-start = (bf16[1,768,16384]{2,1,0:T(8,128)(2,1)S(1)}, bf16[1,768,16384]{2,1,0:T(8,128)(2,1)}, u32[]{:S(2)}) copy-start(bf16[1,768,16384]{2,1,0:T(8,128)(2,1)} %refs_1_.7) | copy-start | bytes 75497472
  24.2 5.9 %collective-permute-start.2 = (bf16[16,2048]{1,0:T(8,128)(2,1)S(1)}, bf16[16,2048]{1,0:T(8,128)(2,1)S(1)}, u32[]{:S(2)}, u32[]{:S(2)}) collective-permute-start(bf16[16,2048]{1,0:T(8,128)(2,1)S(1)} %hidden.1.refs_0_), channel_id=1, source_target_pairs={{0,1},{1,0},{2,3},{3,2},{4,5},{5,4},{6,7},{7,6},{8,9},{9,8},{10,11... | collective-permute-start | bytes 196616 | tf_op jit(solution)/shard_map/ppermute | solution.py:171
  24.8 6.8 %collective-permute-start.3 = (bf16[16,2048]{1,0:T(8,128)(2,1)S(1)}, bf16[16,2048]{1,0:T(8,128)(2,1)S(1)}, u32[]{:S(2)}, u32[]{:S(2)}) collective-permute-start(bf16[16,2048]{1,0:T(8,128)(2,1)S(1)} %hidden.1.refs_0_), channel_id=1, source_target_pairs={{0,6},{1,7},{2,4},{3,5},{4,2},{5,3},{6,0},{7,1},{8,14},{9,15},{10,... | collective-permute-start | bytes 196616 | tf_op jit(solution)/shard_map/ppermute | solution.py:171
  25.8 7.6 %collective-permute-start.5 = (bf16[16,2048]{1,0:T(8,128)(2,1)S(1)}, bf16[16,2048]{1,0:T(8,128)(2,1)S(1)}, u32[]{:S(2)}, u32[]{:S(2)}) collective-permute-start(bf16[16,2048]{1,0:T(8,128)(2,1)S(1)} %hidden.1.refs_0_), channel_id=1, source_target_pairs={{0,4},{1,5},{2,6},{3,7},{4,0},{5,1},{6,2},{7,3},{8,12},{9,13},{10,... | collective-permute-start | bytes 196616 | tf_op jit(solution)/shard_map/ppermute | solution.py:171
  27.0 7.7 %collective-permute-start = (bf16[16,2048]{1,0:T(8,128)(2,1)S(1)}, bf16[16,2048]{1,0:T(8,128)(2,1)S(1)}, u32[]{:S(2)}, u32[]{:S(2)}) collective-permute-start(bf16[16,2048]{1,0:T(8,128)(2,1)S(1)} %hidden.1.refs_0_), channel_id=1, source_target_pairs={{0,2},{1,3},{2,0},{3,1},{4,6},{5,7},{6,4},{7,5},{8,10},{9,11},{10,... | collective-permute-start | bytes 196616 | tf_op jit(solution)/shard_map/ppermute | solution.py:171
  31.6 6.6 %collective-permute-start.4 = (bf16[16,2048]{1,0:T(8,128)(2,1)S(1)}, bf16[16,2048]{1,0:T(8,128)(2,1)S(1)}, u32[]{:S(2)}, u32[]{:S(2)}) collective-permute-start(bf16[16,2048]{1,0:T(8,128)(2,1)S(1)} %collective-permute-done.3.refs_0_), channel_id=1, source_target_pairs={{0,1},{1,0},{2,3},{3,2},{4,5},{5,4},{6,7},{7,6},{8,9},{9,8},{10,11... | collective-permute-start | bytes 196616 | tf_op jit(solution)/shard_map/ppermute | solution.py:171
  33.4 4.8 %collective-permute-start.6 = (bf16[16,2048]{1,0:T(8,128)(2,1)S(1)}, bf16[16,2048]{1,0:T(8,128)(2,1)S(1)}, u32[]{:S(2)}, u32[]{:S(2)}) collective-permute-start(bf16[16,2048]{1,0:T(8,128)(2,1)S(1)} %collective-permute-done.5.refs_1_), channel_id=1, source_target_pairs={{0,1},{1,0},{2,3},{3,2},{4,5},{5,4},{6,7},{7,6},{8,9},{9,8},{10,11... | collective-permute-start | bytes 196616 | tf_op jit(solution)/shard_map/ppermute | solution.py:171
  34.6 5.4 %collective-permute-start.1 = (bf16[16,2048]{1,0:T(8,128)(2,1)S(1)}, bf16[16,2048]{1,0:T(8,128)(2,1)S(1)}, u32[]{:S(2)}, u32[]{:S(2)}) collective-permute-start(bf16[16,2048]{1,0:T(8,128)(2,1)S(1)} %collective-permute-done.refs_0_), channel_id=1, source_target_pairs={{0,1},{1,0},{2,3},{3,2},{4,5},{5,4},{6,7},{7,6},{8,9},{9,8},{10,11... | collective-permute-start | bytes 196616 | tf_op jit(solution)/shard_map/ppermute | solution.py:171
  49.2 3.7 %collective-permute-start.7 = (f32[2,2,768]{2,1,0:T(2,128)S(1)}, f32[2,2,768]{2,1,0:T(2,128)S(1)}, u32[]{:S(2)}, u32[]{:S(2)}) collective-permute-start(f32[2,2,768]{2,1,0:T(2,128)S(1)} %get-tuple-element.17), channel_id=1, source_target_pairs={{0,1},{1,0},{2,3},{3,2},{4,5},{5,4},{6,7},{7,6},{8,9},{9,8},{10,11... | collective-permute-start | bytes 36872 | tf_op jit(solution)/shard_map/ppermute | solution.py:171
  50.4 2.5 %collective-permute-start.8 = (f32[2,2,768]{2,1,0:T(2,128)S(1)}, f32[2,2,768]{2,1,0:T(2,128)S(1)}, u32[]{:S(2)}, u32[]{:S(2)}) collective-permute-start(f32[2,2,768]{2,1,0:T(2,128)S(1)} %get-tuple-element.18), channel_id=1, source_target_pairs={{0,8},{8,0},{1,9},{9,1},{2,10},{10,2},{3,11},{11,3},{4,12},{12,4},... | collective-permute-start | bytes 36872 | tf_op jit(solution)/shard_map/ppermute | solution.py:174
  50.4 3.1 %collective-permute-start.9 = (f32[2,2,768]{2,1,0:T(2,128)S(1)}, f32[2,2,768]{2,1,0:T(2,128)S(1)}, u32[]{:S(2)}, u32[]{:S(2)}) collective-permute-start(f32[2,2,768]{2,1,0:T(2,128)S(1)} %get-tuple-element.19), channel_id=1, source_target_pairs={{0,9},{1,8},{2,11},{3,10},{4,13},{5,12},{6,15},{7,14},{8,1},{9,0},... | collective-permute-start | bytes 36872 | tf_op jit(solution)/shard_map/ppermute | solution.py:216

commit v12 on v10

--- a/solution.py
+++ b/solution.py
@@ -114,9 +114,15 @@
     over_columns(hidden_ref.shape[1], body)
 
 
-def down_kernel(steps, first, last, *refs):
-    n = len(steps)
-    blocks, w_ref, rest = refs[:n], refs[n], refs[n + 1:]
+def join_kernel(first_ref, second_ref, out_ref):
+    out_ref[0] = first_ref[...]
+    out_ref[1] = second_ref[...]
+
+
+def down_kernel(held, steps, first, last, *refs):
+    blocks, w_ref, rest = refs[:held], refs[held], refs[held + 1:]
+    if held < len(steps):
+        blocks = [blocks[0].at[i] for i in range(len(steps))]
     out_ref = rest[-1]
     me = lax.axis_index("tile")
     slots, width = blocks[0].shape
@@ -184,20 +190,19 @@
         first = total is None
         out = f32(tiles, SLOTS, features) if last else f32(features, slots)
         return call(
-            functools.partial(down_kernel, steps, first, last), "down", out,
+            functools.partial(down_kernel, len(blocks), steps, first, last), "down", out,
             [VMEM] * (len(blocks) + 2 - first), 10 * MIB, 0e-6,
         )(*blocks, in_vmem(w_down), *(() if first else (total,)))
 
-    column = [swap(hidden, k) for k in (6, 4, 2)]
-    beside = swap(hidden, 1)
-    total = down(None, [0], [hidden], False)
-    total = down(total, [1], [beside], False)
-    total, column[0] = lax.optimization_barrier((total, column[0]))
-    other_column = [swap(block, 1) for block in column]
-    total = down(total, [6, 4], column[:2], False)
-    total = down(total, [2], column[2:], False)
-    total = down(total, [7, 5], other_column[:2], False)
-    result = down(total, [3], other_column[2:], True)
+    beside, near, middle, far = (swap(hidden, k) for k in (1, 2, 4, 6))
+    near_beside = swap(near, 1)
+    total = down(None, [0, 1], [hidden, beside], False)
+    total, middle, far, near_beside = lax.optimization_barrier((total, middle, far, near_beside))
+    joined = call(join_kernel, "join", bf16(2, slots, width), [VMEM] * 2, 4 * MIB)(middle, far)
+    joined_beside = swap(joined, 1)
+    total = down(total, [4, 6], [joined], False)
+    total = down(total, [2, 3], [near, near_beside], False)
+    result = down(total, [5, 7], [joined_beside], True)
     back = lax.all_to_all(result, "tile", split_axis=0, concat_axis=0, tiled=True)
     return call(combine_kernel, "combine", bf16(rows, half_width), [VMEM] * 3, 4 * MIB)(back, to_core(back), table)
 

time: 53.1 us -> 53.2 us (level)
  waiting for transfers between devices: 2.13 us -> 3.96 us
  starting transfers between devices: 8.4 us -> 6.77 us
    ppermute x7 -> x6, waiting for transfers between devices: 0.91 us -> 2.73 us  [swap(): return lax.ppermute(x, 'tile', [(t, t ^ bit) for t in range(tiles)])]
    ppermute x7 -> x6, starting transfers between devices: 8.4 us -> 6.77 us  [swap(): return lax.ppermute(x, 'tile', [(t, t ^ bit) for t in range(tiles)])]
    pallas_call x6 -> x5, Pallas kernels: 7.4 us -> 7.09 us  [the longest x4 7.08 us: down(): call(functools.partial(down_kernel, len(blocks), steps, first, last), 'do...]
  transfers between devices with their start and end apart: 8 -> 7, of which waited for: 3 -> 3; matrix products, arithmetic and copies ran while one was open for 0% -> 0% of each run, Pallas kernels for 12% -> 10%
where the time goes in v12:
time: 53.2 us; the launch traced here: 53 us
  blocking collectives  26.6 us (50%)
  Pallas kernels  15.6 us (29%)
  starting transfers between devices  6.77 us (13%)
  waiting for transfers between devices  3.96 us (7%)
    all_to_all x1, blocking collectives, local_direct(): lax.all_to_all(sends, ('expert', 'tile'), split_axis=0, concat_axis=0, ti...  16.4 us
    all_to_all x1, blocking collectives, local_direct(): lax.all_to_all(result, 'tile', split_axis=0, concat_axis=0, tiled=True)  10.2 us
    pallas_call x4, Pallas kernels, down(): call(functools.partial(down_kernel, len(blocks), steps, first, last), 'do...  7.08 us
    ppermute x6, starting transfers between devices, swap(): return lax.ppermute(x, 'tile', [(t, t ^ bit) for t in range(tiles)])  6.77 us
    pallas_call x1, Pallas kernels, local_direct(): call(hidden_kernel, 'hidden', bf16(slots, width), [VMEM] * 3, 4 * MIB, 0....  3.37 us
    pallas_call x1, Pallas kernels, local_direct(): call(gate_kernel, 'gate', f32(slots, width), [VMEM] * 2, 4 * MIB, 0.0)  3.34 us
    ppermute x6, waiting for transfers between devices, swap(): return lax.ppermute(x, 'tile', [(t, t ^ bit) for t in range(tiles)])  2.73 us
    ppermute x1, waiting for transfers between devices, to_core(): return lax.ppermute(x, 'expert', [(0, 1), (1, 0)])  1.23 us
  transfers between devices with their start and end apart: 7, of which 3 were waited for; matrix products, arithmetic and copies ran while one was open for 0% of the time, Pallas kernels for 10%

profile of v12, /device:TPU:0, one launch (start us, length us, event | category | flops | bytes accessed | tf_op | source)
XLA Modules:
  0.0 53.0 jit_solution(15861743212975272822)
XLA Ops:
  0.0 0.0 copy-start.1
  0.0 1.0 %dispatch.1 = (bf16[16,2,3072]{2,1,0:T(2,128)(2,1)S(1)}, f32[6,4,128]{2,1,0:T(4,128)S(1)}) custom-call(bf16[4,3072]{1,0:T(4,128)(2,1)} %tokens_hbm.1, s32[2,4]{1,0:T(2,128)} %bitcast.2, f32[2,4]{1,0:T(2,128)} %bitcast.3), custom_call_target="tpu_custom_call" | custom-call | flops 599999971328 | tf_op jit(solution)/shard_map/dispatch/pallas_call | solution.py:174
  1.0 0.0 copy-start.2
  1.0 16.4 %all_to_all.10.blocks_ref = bf16[16,2,3072]{2,1,0:T(2,128)(2,1)S(1)} all-to-all(bf16[16,2,3072]{2,1,0:T(2,128)(2,1)S(1)} %get-tuple-element.11), channel_id=1, replica_groups=mesh['group'=2,'expert'=2,'tile'=8] {'expert','tile'}, dimensions={0} | all-to-all | bytes 393216 | tf_op jit(solution)/shard_map/all_to_all | solution.py:184
  17.5 0.0 copy-done.1
  17.5 3.3 %gate.1.gate_ref = f32[16,2048]{1,0:T(8,128)S(1)} custom-call(bf16[32,3072]{1,0:T(8,128)(2,1)S(1)} %merge.1.rows_ref, bf16[1,6144,2048]{2,1,0:T(8,128)(2,1)S(1)} %copy-done.1), custom_call_target="tpu_custom_call" | custom-call | tf_op jit(solution)/shard_map/gate/pallas_call | solution.py:186
  20.9 0.0 copy-done.2
  20.9 0.0 copy-start
  20.9 3.4 %hidden.1.refs_0_ = bf16[16,2048]{1,0:T(8,128)(2,1)S(1)} custom-call(bf16[32,3072]{1,0:T(8,128)(2,1)S(1)} %merge.1.rows_ref, bf16[1,6144,2048]{2,1,0:T(8,128)(2,1)S(1)} %copy-done.2, f32[16,2048]{1,0:T(8,128)S(1)} %gate.1.gate_ref), custom_call_target="tpu_custom_call" | custom-call | flops 199999995904 | tf_op jit(solution)/shard_map/hidden/pallas_call | solution.py:187
  24.2 0.7 %collective-permute-start.3 = (bf16[16,2048]{1,0:T(8,128)(2,1)S(1)}, bf16[16,2048]{1,0:T(8,128)(2,1)S(1)}, u32[]{:S(2)}, u32[]{:S(2)}) collective-permute-start(bf16[16,2048]{1,0:T(8,128)(2,1)S(1)} %hidden.1.refs_0_), channel_id=1, source_target_pairs={{0,2},{1,3},{2,0},{3,1},{4,6},{5,7},{6,4},{7,5},{8,10},{9,11},{10,... | collective-permute-start | bytes 196616 | tf_op jit(solution)/shard_map/ppermute | solution.py:167
  24.9 0.6 %collective-permute-start = (bf16[16,2048]{1,0:T(8,128)(2,1)S(1)}, bf16[16,2048]{1,0:T(8,128)(2,1)S(1)}, u32[]{:S(2)}, u32[]{:S(2)}) collective-permute-start(bf16[16,2048]{1,0:T(8,128)(2,1)S(1)} %hidden.1.refs_0_), channel_id=1, source_target_pairs={{0,1},{1,0},{2,3},{3,2},{4,5},{5,4},{6,7},{7,6},{8,9},{9,8},{10,11... | collective-permute-start | bytes 196616 | tf_op jit(solution)/shard_map/ppermute | solution.py:167
  25.5 1.5 %collective-permute-start.2 = (bf16[16,2048]{1,0:T(8,128)(2,1)S(1)}, bf16[16,2048]{1,0:T(8,128)(2,1)S(1)}, u32[]{:S(2)}, u32[]{:S(2)}) collective-permute-start(bf16[16,2048]{1,0:T(8,128)(2,1)S(1)} %hidden.1.refs_0_), channel_id=1, source_target_pairs={{0,6},{1,7},{2,4},{3,5},{4,2},{5,3},{6,0},{7,1},{8,14},{9,15},{10,... | collective-permute-start | bytes 196616 | tf_op jit(solution)/shard_map/ppermute | solution.py:167
  27.0 1.3 %collective-permute-start.1 = (bf16[16,2048]{1,0:T(8,128)(2,1)S(1)}, bf16[16,2048]{1,0:T(8,128)(2,1)S(1)}, u32[]{:S(2)}, u32[]{:S(2)}) collective-permute-start(bf16[16,2048]{1,0:T(8,128)(2,1)S(1)} %hidden.1.refs_0_), channel_id=1, source_target_pairs={{0,4},{1,5},{2,6},{3,7},{4,0},{5,1},{6,2},{7,3},{8,12},{9,13},{10,... | collective-permute-start | bytes 196616 | tf_op jit(solution)/shard_map/ppermute | solution.py:167
  28.3 0.2 collective-permute-done.3.refs_0_
  28.5 1.3 %collective-permute-start.4 = (bf16[16,2048]{1,0:T(8,128)(2,1)S(1)}, bf16[16,2048]{1,0:T(8,128)(2,1)S(1)}, u32[]{:S(2)}, u32[]{:S(2)}) collective-permute-start(bf16[16,2048]{1,0:T(8,128)(2,1)S(1)} %collective-permute-done.3.refs_0_), channel_id=1, source_target_pairs={{0,1},{1,0},{2,3},{3,2},{4,5},{5,4},{6,7},{7,6},{8,9},{9,8},{10,11... | collective-permute-start | bytes 196616 | tf_op jit(solution)/shard_map/ppermute | solution.py:167
  29.8 0.0 collective-permute-done.refs_1_
  29.8 0.0 copy-done
  29.8 1.8 %down.4.refs_2_ = f32[768,16]{1,0:T(8,128)S(1)} custom-call(bf16[16,2048]{1,0:T(8,128)(2,1)S(1)} %hidden.1.refs_0_, bf16[16,2048]{1,0:T(8,128)(2,1)S(1)} %collective-permute-done.refs_1_, bf16[1,768,16384]{2,1,0:T(8,128)(2,1)S(1)} %copy-done), custom_call_target="tpu_custom_call" | custom-call | tf_op jit(solution)/shard_map/down/pallas_call | solution.py:192
  31.5 0.0 collective-permute-done.2.second_ref
  31.6 2.4 %collective-permute-done.1.first_ref = bf16[16,2048]{1,0:T(8,128)(2,1)S(1)} collective-permute-done((bf16[16,2048]{1,0:T(8,128)(2,1)S(1)}, bf16[16,2048]{1,0:T(8,128)(2,1)S(1)}, u32[]{:S(2)}, u32[]{:S(2)}) %collective-permute-start.1) | collective-permute-done | bytes 65568 | tf_op jit(solution)/shard_map/ppermute | solution.py:167
  34.0 0.0 collective-permute-done.4.refs_1_
  34.0 1.5 %collective-permute-start.5 = (bf16[2,16,2048]{2,1,0:T(8,128)(2,1)S(1)}, bf16[2,16,2048]{2,1,0:T(8,128)(2,1)S(1)}, u32[]{:S(2)}, u32[]{:S(2)}) collective-permute-start(bf16[2,16,2048]{2,1,0:T(8,128)(2,1)S(1)} %join.1.refs_0_), channel_id=1, source_target_pairs={{0,1},{1,0},{2,3},{3,2},{4,5},{5,4},{6,7},{7,6},{8,9},{9,8},{10,11... | collective-permute-start | bytes 393224 | tf_op jit(solution)/shard_map/ppermute | solution.py:167
  35.5 1.8 %down.5.refs_3_ = f32[768,16]{1,0:T(8,128)S(1)} custom-call(bf16[2,16,2048]{2,1,0:T(8,128)(2,1)S(1)} %join.1.refs_0_, bf16[1,768,16384]{2,1,0:T(8,128)(2,1)S(1)} %copy-done, f32[768,16]{1,0:T(8,128)S(1)} %down.4.refs_2_), custom_call_target="tpu_custom_call" | custom-call | tf_op jit(solution)/shard_map/down/pallas_call | solution.py:192
  37.2 1.8 %down.6.refs_2_ = f32[768,16]{1,0:T(8,128)S(1)} custom-call(bf16[16,2048]{1,0:T(8,128)(2,1)S(1)} %collective-permute-done.3.refs_0_, bf16[16,2048]{1,0:T(8,128)(2,1)S(1)} %collective-permute-done.4.refs_1_, bf16[1,768,16384]{2,1,0:T(8,128)(2,1)S(1)} %copy-done, f32[768,16]{1,0:T(8,128)S(1)} %down.5.refs_3_), custom_call_target="tpu_custom_call" | custom-call | tf_op jit(solution)/shard_map/down/pallas_call | solution.py:192
  39.0 0.0 collective-permute-done.5.refs_0_
  39.1 1.8 %down.7 = f32[8,2,768]{2,1,0:T(2,128)S(1)} custom-call(bf16[2,16,2048]{2,1,0:T(8,128)(2,1)S(1)} %collective-permute-done.5.refs_0_, bf16[1,768,16384]{2,1,0:T(8,128)(2,1)S(1)} %copy-done, f32[768,16]{1,0:T(8,128)S(1)} %down.6.refs_2_), custom_call_target="tpu_custom_call" | custom-call | tf_op jit(solution)/shard_map/down/pallas_call | solution.py:192
  40.8 10.2 %all_to_all.11.own_ref = f32[8,2,768]{2,1,0:T(2,128)S(1)} all-to-all(f32[8,2,768]{2,1,0:T(2,128)S(1)} %down.7), channel_id=1, replica_groups=mesh['group'=2,'expert'=2,'tile'=8] {'tile'}, dimensions={0} | all-to-all | bytes 98304 | tf_op jit(solution)/shard_map/all_to_all | solution.py:206
  51.0 0.0 collective-permute-start.6
  51.0 1.2 %collective-permute-done.6.other_ref = f32[8,2,768]{2,1,0:T(2,128)S(1)} collective-permute-done((f32[8,2,768]{2,1,0:T(2,128)S(1)}, f32[8,2,768]{2,1,0:T(2,128)S(1)}, u32[]{:S(2)}, u32[]{:S(2)}) %collective-permute-start.6) | collective-permute-done | bytes 49184 | tf_op jit(solution)/shard_map/ppermute | solution.py:170
  52.3 0.7 %combine.1 = bf16[4,3072]{1,0:T(4,128)(2,1)} custom-call(f32[8,2,768]{2,1,0:T(2,128)S(1)} %all_to_all.11.own_ref, f32[8,2,768]{2,1,0:T(2,128)S(1)} %collective-permute-done.6.other_ref, f32[6,4,128]{2,1,0:T(4,128)S(1)} %get-tuple-element.16.table_ref), custom_call_target="tpu_custom_call" | custom-call | tf_op jit(solution)/shard_map/combine/pallas_call | solution.py:207
  (2 shorter events, 0.0 us)
Async XLA Ops:
  0.0 17.5 %copy-start.1 = (bf16[1,6144,2048]{2,1,0:T(8,128)(2,1)S(1)}, bf16[1,6144,2048]{2,1,0:T(8,128)(2,1)}, u32[]{:S(2)}) copy-start(bf16[1,6144,2048]{2,1,0:T(8,128)(2,1)} %w_ref.2) | copy-start | bytes 75497472
  1.0 19.8 %copy-start.2 = (bf16[1,6144,2048]{2,1,0:T(8,128)(2,1)S(1)}, bf16[1,6144,2048]{2,1,0:T(8,128)(2,1)}, u32[]{:S(2)}) copy-start(bf16[1,6144,2048]{2,1,0:T(8,128)(2,1)} %w_ref.3) | copy-start | bytes 75497472
  20.9 8.9 %copy-start = (bf16[1,768,16384]{2,1,0:T(8,128)(2,1)S(1)}, bf16[1,768,16384]{2,1,0:T(8,128)(2,1)}, u32[]{:S(2)}) copy-start(bf16[1,768,16384]{2,1,0:T(8,128)(2,1)} %refs_1_.3) | copy-start | bytes 75497472
  24.2 4.3 %collective-permute-start.3 = (bf16[16,2048]{1,0:T(8,128)(2,1)S(1)}, bf16[16,2048]{1,0:T(8,128)(2,1)S(1)}, u32[]{:S(2)}, u32[]{:S(2)}) collective-permute-start(bf16[16,2048]{1,0:T(8,128)(2,1)S(1)} %hidden.1.refs_0_), channel_id=1, source_target_pairs={{0,2},{1,3},{2,0},{3,1},{4,6},{5,7},{6,4},{7,5},{8,10},{9,11},{10,... | collective-permute-start | bytes 196616 | tf_op jit(solution)/shard_map/ppermute | solution.py:167
  24.9 4.8 %collective-permute-start = (bf16[16,2048]{1,0:T(8,128)(2,1)S(1)}, bf16[16,2048]{1,0:T(8,128)(2,1)S(1)}, u32[]{:S(2)}, u32[]{:S(2)}) collective-permute-start(bf16[16,2048]{1,0:T(8,128)(2,1)S(1)} %hidden.1.refs_0_), channel_id=1, source_target_pairs={{0,1},{1,0},{2,3},{3,2},{4,5},{5,4},{6,7},{7,6},{8,9},{9,8},{10,11... | collective-permute-start | bytes 196616 | tf_op jit(solution)/shard_map/ppermute | solution.py:167
  25.5 6.1 %collective-permute-start.2 = (bf16[16,2048]{1,0:T(8,128)(2,1)S(1)}, bf16[16,2048]{1,0:T(8,128)(2,1)S(1)}, u32[]{:S(2)}, u32[]{:S(2)}) collective-permute-start(bf16[16,2048]{1,0:T(8,128)(2,1)S(1)} %hidden.1.refs_0_), channel_id=1, source_target_pairs={{0,6},{1,7},{2,4},{3,5},{4,2},{5,3},{6,0},{7,1},{8,14},{9,15},{10,... | collective-permute-start | bytes 196616 | tf_op jit(solution)/shard_map/ppermute | solution.py:167
  27.0 7.1 %collective-permute-start.1 = (bf16[16,2048]{1,0:T(8,128)(2,1)S(1)}, bf16[16,2048]{1,0:T(8,128)(2,1)S(1)}, u32[]{:S(2)}, u32[]{:S(2)}) collective-permute-start(bf16[16,2048]{1,0:T(8,128)(2,1)S(1)} %hidden.1.refs_0_), channel_id=1, source_target_pairs={{0,4},{1,5},{2,6},{3,7},{4,0},{5,1},{6,2},{7,3},{8,12},{9,13},{10,... | collective-permute-start | bytes 196616 | tf_op jit(solution)/shard_map/ppermute | solution.py:167
  28.5 5.5 %collective-permute-start.4 = (bf16[16,2048]{1,0:T(8,128)(2,1)S(1)}, bf16[16,2048]{1,0:T(8,128)(2,1)S(1)}, u32[]{:S(2)}, u32[]{:S(2)}) collective-permute-start(bf16[16,2048]{1,0:T(8,128)(2,1)S(1)} %collective-permute-done.3.refs_0_), channel_id=1, source_target_pairs={{0,1},{1,0},{2,3},{3,2},{4,5},{5,4},{6,7},{7,6},{8,9},{9,8},{10,11... | collective-permute-start | bytes 196616 | tf_op jit(solution)/shard_map/ppermute | solution.py:167
  34.0 5.0 %collective-permute-start.5 = (bf16[2,16,2048]{2,1,0:T(8,128)(2,1)S(1)}, bf16[2,16,2048]{2,1,0:T(8,128)(2,1)S(1)}, u32[]{:S(2)}, u32[]{:S(2)}) collective-permute-start(bf16[2,16,2048]{2,1,0:T(8,128)(2,1)S(1)} %join.1.refs_0_), channel_id=1, source_target_pairs={{0,1},{1,0},{2,3},{3,2},{4,5},{5,4},{6,7},{7,6},{8,9},{9,8},{10,11... | collective-permute-start | bytes 393224 | tf_op jit(solution)/shard_map/ppermute | solution.py:167
  51.0 1.2 %collective-permute-start.6 = (f32[8,2,768]{2,1,0:T(2,128)S(1)}, f32[8,2,768]{2,1,0:T(2,128)S(1)}, u32[]{:S(2)}, u32[]{:S(2)}) collective-permute-start(f32[8,2,768]{2,1,0:T(2,128)S(1)} %all_to_all.11.own_ref), channel_id=1, source_target_pairs={{0,8},{8,0},{1,9},{9,1},{2,10},{10,2},{3,11},{11,3},{4,12},{12,4},... | collective-permute-start | bytes 147464 | tf_op jit(solution)/shard_map/ppermute | solution.py:170

commit v13 on v10

--- a/solution.py
+++ b/solution.py
@@ -180,24 +180,27 @@
     gate = call(gate_kernel, "gate", f32(slots, width), [VMEM] * 2, 4 * MIB, 0e-6)(x, in_vmem(w_gate))
     hidden = call(hidden_kernel, "hidden", bf16(slots, width), [VMEM] * 3, 4 * MIB, 200e-6)(x, in_vmem(w_up), gate)
 
-    def down(total, steps, blocks, last):
+    def down(total, steps, block, last):
         first = total is None
         out = f32(tiles, SLOTS, features) if last else f32(features, slots)
         return call(
             functools.partial(down_kernel, steps, first, last), "down", out,
-            [VMEM] * (len(blocks) + 2 - first), 10 * MIB, 0e-6,
-        )(*blocks, in_vmem(w_down), *(() if first else (total,)))
-
-    column = [swap(hidden, k) for k in (6, 4, 2)]
-    beside = swap(hidden, 1)
-    total = down(None, [0], [hidden], False)
-    total = down(total, [1], [beside], False)
-    total, column[0] = lax.optimization_barrier((total, column[0]))
-    other_column = [swap(block, 1) for block in column]
-    total = down(total, [6, 4], column[:2], False)
-    total = down(total, [2], column[2:], False)
-    total = down(total, [7, 5], other_column[:2], False)
-    result = down(total, [3], other_column[2:], True)
+            [VMEM] * (len(steps) + 2 - first), 10 * MIB, 0e-6,
+        )(*(block[k] for k in steps), in_vmem(w_down), *(() if first else (total,)))
+
+    block = {0: hidden}
+    for k in (4, 2, 1):
+        block[k] = swap(hidden, k)
+    block[3] = swap(block[2], 1)
+    block[6] = swap(block[4], 2)
+    block[5] = swap(block[4], 1)
+    total = down(None, [0, 1], block, False)
+    total, block[6] = lax.optimization_barrier((total, block[6]))
+    block[7] = swap(block[6], 1)
+    total = down(total, [2, 4], block, False)
+    total = down(total, [3, 6], block, False)
+    total = down(total, [5], block, False)
+    result = down(total, [7], block, True)
     back = lax.all_to_all(result, "tile", split_axis=0, concat_axis=0, tiled=True)
     return call(combine_kernel, "combine", bf16(rows, half_width), [VMEM] * 3, 4 * MIB)(back, to_core(back), table)
 

time: 53.1 us -> 53.4 us (level)
  starting transfers between devices: 8.4 us -> 5.2 us
  waiting for transfers between devices: 2.13 us -> 5.23 us
    ppermute x7, starting transfers between devices: 8.4 us -> 5.2 us  [swap(): return lax.ppermute(x, 'tile', [(t, t ^ bit) for t in range(tiles)])]
    ppermute x7, waiting for transfers between devices: 0.91 us -> 4 us  [swap(): return lax.ppermute(x, 'tile', [(t, t ^ bit) for t in range(tiles)])]
    all_to_all x1, blocking collectives: 9.93 us -> 10.5 us  [local_direct(): lax.all_to_all(result, 'tile', split_axis=0, concat_axis=0, tiled=True)]
    pallas_call x6 -> x5, Pallas kernels: 7.4 us -> 7.24 us  [down(): call(functools.partial(down_kernel, steps, first, last), 'down', out, [VM...]
where the time goes in v13:
time: 53.4 us; the launch traced here: 53.2 us
  blocking collectives  26.9 us (50%)
  Pallas kernels  15.7 us (29%)
  waiting for transfers between devices  5.23 us (10%)
  starting transfers between devices  5.2 us (10%)
    all_to_all x1, blocking collectives, local_direct(): lax.all_to_all(sends, ('expert', 'tile'), split_axis=0, concat_axis=0, ti...  16.4 us
    all_to_all x1, blocking collectives, local_direct(): lax.all_to_all(result, 'tile', split_axis=0, concat_axis=0, tiled=True)  10.5 us
    pallas_call x5, Pallas kernels, down(): call(functools.partial(down_kernel, steps, first, last), 'down', out, [VM...  7.24 us
    ppermute x7, starting transfers between devices, swap(): return lax.ppermute(x, 'tile', [(t, t ^ bit) for t in range(tiles)])  5.2 us
    ppermute x7, waiting for transfers between devices, swap(): return lax.ppermute(x, 'tile', [(t, t ^ bit) for t in range(tiles)])  4 us
    pallas_call x1, Pallas kernels, local_direct(): call(hidden_kernel, 'hidden', bf16(slots, width), [VMEM] * 3, 4 * MIB, 0....  3.37 us
    pallas_call x1, Pallas kernels, local_direct(): call(gate_kernel, 'gate', f32(slots, width), [VMEM] * 2, 4 * MIB, 0.0)  3.34 us
    ppermute x1, waiting for transfers between devices, to_core(): return lax.ppermute(x, 'expert', [(0, 1), (1, 0)])  1.23 us
  transfers between devices with their start and end apart: 8, of which 3 were waited for; matrix products, arithmetic and copies ran while one was open for 0% of the time, Pallas kernels for 12%

profile of v13, /device:TPU:0, one launch (start us, length us, event | category | flops | bytes accessed | tf_op | source)
XLA Modules:
  0.0 53.2 jit_solution(14972268587906566993)
XLA Ops:
  0.0 0.0 copy-start.1
  0.0 1.0 %dispatch.1 = (bf16[16,2,3072]{2,1,0:T(2,128)(2,1)S(1)}, f32[6,4,128]{2,1,0:T(4,128)S(1)}) custom-call(bf16[4,3072]{1,0:T(4,128)(2,1)} %tokens_hbm.1, s32[2,4]{1,0:T(2,128)} %bitcast.2, f32[2,4]{1,0:T(2,128)} %bitcast.3), custom_call_target="tpu_custom_call" | custom-call | flops 599999971328 | tf_op jit(solution)/shard_map/dispatch/pallas_call | solution.py:168
  1.0 0.0 copy-start.2
  1.0 16.4 %all_to_all.10.blocks_ref = bf16[16,2,3072]{2,1,0:T(2,128)(2,1)S(1)} all-to-all(bf16[16,2,3072]{2,1,0:T(2,128)(2,1)S(1)} %get-tuple-element.9), channel_id=1, replica_groups=mesh['group'=2,'expert'=2,'tile'=8] {'expert','tile'}, dimensions={0} | all-to-all | bytes 393216 | tf_op jit(solution)/shard_map/all_to_all | solution.py:178
  17.5 0.0 copy-done.1
  17.5 3.3 %gate.1.gate_ref = f32[16,2048]{1,0:T(8,128)S(1)} custom-call(bf16[32,3072]{1,0:T(8,128)(2,1)S(1)} %merge.1.rows_ref, bf16[1,6144,2048]{2,1,0:T(8,128)(2,1)S(1)} %copy-done.1), custom_call_target="tpu_custom_call" | custom-call | tf_op jit(solution)/shard_map/gate/pallas_call | solution.py:180
  20.9 0.0 copy-done.2
  20.9 3.4 %hidden.1.refs_0_ = bf16[16,2048]{1,0:T(8,128)(2,1)S(1)} custom-call(bf16[32,3072]{1,0:T(8,128)(2,1)S(1)} %merge.1.rows_ref, bf16[1,6144,2048]{2,1,0:T(8,128)(2,1)S(1)} %copy-done.2, f32[16,2048]{1,0:T(8,128)S(1)} %gate.1.gate_ref), custom_call_target="tpu_custom_call" | custom-call | flops 199999995904 | tf_op jit(solution)/shard_map/hidden/pallas_call | solution.py:181
  24.2 0.4 collective-permute-start.1
  24.7 1.3 %collective-permute-start.5 = (bf16[16,2048]{1,0:T(8,128)(2,1)S(1)}, bf16[16,2048]{1,0:T(8,128)(2,1)S(1)}, u32[]{:S(2)}, u32[]{:S(2)}) collective-permute-start(bf16[16,2048]{1,0:T(8,128)(2,1)S(1)} %hidden.1.refs_0_), channel_id=1, source_target_pairs={{0,2},{1,3},{2,0},{3,1},{4,6},{5,7},{6,4},{7,5},{8,10},{9,11},{10,... | collective-permute-start | bytes 196616 | tf_op jit(solution)/shard_map/ppermute | solution.py:161
  26.0 0.4 collective-permute-start
  26.3 3.8 %collective-permute-done.1.refs_1_ = bf16[16,2048]{1,0:T(8,128)(2,1)S(1)} collective-permute-done((bf16[16,2048]{1,0:T(8,128)(2,1)S(1)}, bf16[16,2048]{1,0:T(8,128)(2,1)S(1)}, u32[]{:S(2)}, u32[]{:S(2)}) %collective-permute-start.1) | collective-permute-done | bytes 65568 | tf_op jit(solution)/shard_map/ppermute | solution.py:161
  30.1 0.2 collective-permute-start.2
  30.3 0.9 %collective-permute-start.4 = (bf16[16,2048]{1,0:T(8,128)(2,1)S(1)}, bf16[16,2048]{1,0:T(8,128)(2,1)S(1)}, u32[]{:S(2)}, u32[]{:S(2)}) collective-permute-start(bf16[16,2048]{1,0:T(8,128)(2,1)S(1)} %collective-permute-done.1.refs_1_), channel_id=1, source_target_pairs={{0,1},{1,0},{2,3},{3,2},{4,5},{5,4},{6,7},{7,6},{8,9},{9,8},{10,11... | collective-permute-start | bytes 196616 | tf_op jit(solution)/shard_map/ppermute | solution.py:161
  31.2 0.0 collective-permute-done.5.refs_0_
  31.2 1.2 %collective-permute-start.6 = (bf16[16,2048]{1,0:T(8,128)(2,1)S(1)}, bf16[16,2048]{1,0:T(8,128)(2,1)S(1)}, u32[]{:S(2)}, u32[]{:S(2)}) collective-permute-start(bf16[16,2048]{1,0:T(8,128)(2,1)S(1)} %collective-permute-done.5.refs_0_), channel_id=1, source_target_pairs={{0,1},{1,0},{2,3},{3,2},{4,5},{5,4},{6,7},{7,6},{8,9},{9,8},{10,11... | collective-permute-start | bytes 196616 | tf_op jit(solution)/shard_map/ppermute | solution.py:161
  32.4 0.0 collective-permute-done.refs_1_
  32.4 0.0 copy-done
  32.4 1.8 %down.5.refs_3_ = f32[768,16]{1,0:T(8,128)S(1)} custom-call(bf16[16,2048]{1,0:T(8,128)(2,1)S(1)} %hidden.1.refs_0_, bf16[16,2048]{1,0:T(8,128)(2,1)S(1)} %collective-permute-done.refs_1_, bf16[1,768,16384]{2,1,0:T(8,128)(2,1)S(1)} %copy-done), custom_call_target="tpu_custom_call" | custom-call | tf_op jit(solution)/shard_map/down/pallas_call | solution.py:186
  34.1 0.2 collective-permute-done.2.refs_1_
  34.4 0.8 %collective-permute-start.3 = (bf16[16,2048]{1,0:T(8,128)(2,1)S(1)}, bf16[16,2048]{1,0:T(8,128)(2,1)S(1)}, u32[]{:S(2)}, u32[]{:S(2)}) collective-permute-start(bf16[16,2048]{1,0:T(8,128)(2,1)S(1)} %collective-permute-done.2.refs_1_), channel_id=1, source_target_pairs={{0,1},{1,0},{2,3},{3,2},{4,5},{5,4},{6,7},{7,6},{8,9},{9,8},{10,11... | collective-permute-start | bytes 196616 | tf_op jit(solution)/shard_map/ppermute | solution.py:161
  35.2 1.8 %down.6.refs_3_ = f32[768,16]{1,0:T(8,128)S(1)} custom-call(bf16[16,2048]{1,0:T(8,128)(2,1)S(1)} %collective-permute-done.5.refs_0_, bf16[16,2048]{1,0:T(8,128)(2,1)S(1)} %collective-permute-done.1.refs_1_, bf16[1,768,16384]{2,1,0:T(8,128)(2,1)S(1)} %copy-done, f32[768,16]{1,0:T(8,128)S(1)} %down.5.refs_3_), custom_call_target="tpu_custom_call" | custom-call | tf_op jit(solution)/shard_map/down/pallas_call | solution.py:186
  37.0 0.0 collective-permute-done.6.refs_0_
  37.0 1.8 %down.7.refs_2_ = f32[768,16]{1,0:T(8,128)S(1)} custom-call(bf16[16,2048]{1,0:T(8,128)(2,1)S(1)} %collective-permute-done.6.refs_0_, bf16[16,2048]{1,0:T(8,128)(2,1)S(1)} %collective-permute-done.2.refs_1_, bf16[1,768,16384]{2,1,0:T(8,128)(2,1)S(1)} %copy-done, f32[768,16]{1,0:T(8,128)S(1)} %down.6.refs_3_), custom_call_target="tpu_custom_call" | custom-call | tf_op jit(solution)/shard_map/down/pallas_call | solution.py:186
  38.7 0.0 collective-permute-done.4.refs_0_
  38.8 1.0 %down.8.refs_2_ = f32[768,16]{1,0:T(8,128)S(1)} custom-call(bf16[16,2048]{1,0:T(8,128)(2,1)S(1)} %collective-permute-done.4.refs_0_, bf16[1,768,16384]{2,1,0:T(8,128)(2,1)S(1)} %copy-done, f32[768,16]{1,0:T(8,128)S(1)} %down.7.refs_2_), custom_call_target="tpu_custom_call" | custom-call | tf_op jit(solution)/shard_map/down/pallas_call | solution.py:186
  39.7 0.0 collective-permute-done.3.refs_0_
  39.7 1.0 %down.9 = f32[8,2,768]{2,1,0:T(2,128)S(1)} custom-call(bf16[16,2048]{1,0:T(8,128)(2,1)S(1)} %collective-permute-done.3.refs_0_, bf16[1,768,16384]{2,1,0:T(8,128)(2,1)S(1)} %copy-done, f32[768,16]{1,0:T(8,128)S(1)} %down.8.refs_2_), custom_call_target="tpu_custom_call" | custom-call | tf_op jit(solution)/shard_map/down/pallas_call | solution.py:186
  40.7 10.5 %all_to_all.11.own_ref = f32[8,2,768]{2,1,0:T(2,128)S(1)} all-to-all(f32[8,2,768]{2,1,0:T(2,128)S(1)} %down.9), channel_id=1, replica_groups=mesh['group'=2,'expert'=2,'tile'=8] {'tile'}, dimensions={0} | all-to-all | bytes 98304 | tf_op jit(solution)/shard_map/all_to_all | solution.py:204
  51.2 0.0 collective-permute-start.7
  51.2 1.2 %collective-permute-done.7.other_ref = f32[8,2,768]{2,1,0:T(2,128)S(1)} collective-permute-done((f32[8,2,768]{2,1,0:T(2,128)S(1)}, f32[8,2,768]{2,1,0:T(2,128)S(1)}, u32[]{:S(2)}, u32[]{:S(2)}) %collective-permute-start.7) | collective-permute-done | bytes 49184 | tf_op jit(solution)/shard_map/ppermute | solution.py:164
  52.4 0.7 %combine.1 = bf16[4,3072]{1,0:T(4,128)(2,1)} custom-call(f32[8,2,768]{2,1,0:T(2,128)S(1)} %all_to_all.11.own_ref, f32[8,2,768]{2,1,0:T(2,128)S(1)} %collective-permute-done.7.other_ref, f32[6,4,128]{2,1,0:T(4,128)S(1)} %get-tuple-element.12.table_ref), custom_call_target="tpu_custom_call" | custom-call | tf_op jit(solution)/shard_map/combine/pallas_call | solution.py:205
  (2 shorter events, 0.0 us)
Async XLA Ops:
  0.0 17.5 %copy-start.1 = (bf16[1,6144,2048]{2,1,0:T(8,128)(2,1)S(1)}, bf16[1,6144,2048]{2,1,0:T(8,128)(2,1)}, u32[]{:S(2)}) copy-start(bf16[1,6144,2048]{2,1,0:T(8,128)(2,1)} %w_ref.2) | copy-start | bytes 75497472
  1.0 19.8 %copy-start.2 = (bf16[1,6144,2048]{2,1,0:T(8,128)(2,1)S(1)}, bf16[1,6144,2048]{2,1,0:T(8,128)(2,1)}, u32[]{:S(2)}) copy-start(bf16[1,6144,2048]{2,1,0:T(8,128)(2,1)} %w_ref.3) | copy-start | bytes 75497472
  20.9 11.5 %copy-start = (bf16[1,768,16384]{2,1,0:T(8,128)(2,1)S(1)}, bf16[1,768,16384]{2,1,0:T(8,128)(2,1)}, u32[]{:S(2)}) copy-start(bf16[1,768,16384]{2,1,0:T(8,128)(2,1)} %refs_1_.3) | copy-start | bytes 75497472
  24.2 5.9 %collective-permute-start.1 = (bf16[16,2048]{1,0:T(8,128)(2,1)S(1)}, bf16[16,2048]{1,0:T(8,128)(2,1)S(1)}, u32[]{:S(2)}, u32[]{:S(2)}) collective-permute-start(bf16[16,2048]{1,0:T(8,128)(2,1)S(1)} %hidden.1.refs_0_), channel_id=1, source_target_pairs={{0,4},{1,5},{2,6},{3,7},{4,0},{5,1},{6,2},{7,3},{8,12},{9,13},{10,... | collective-permute-start | bytes 196616 | tf_op jit(solution)/shard_map/ppermute | solution.py:161
  24.7 6.5 %collective-permute-start.5 = (bf16[16,2048]{1,0:T(8,128)(2,1)S(1)}, bf16[16,2048]{1,0:T(8,128)(2,1)S(1)}, u32[]{:S(2)}, u32[]{:S(2)}) collective-permute-start(bf16[16,2048]{1,0:T(8,128)(2,1)S(1)} %hidden.1.refs_0_), channel_id=1, source_target_pairs={{0,2},{1,3},{2,0},{3,1},{4,6},{5,7},{6,4},{7,5},{8,10},{9,11},{10,... | collective-permute-start | bytes 196616 | tf_op jit(solution)/shard_map/ppermute | solution.py:161
  26.0 6.4 %collective-permute-start = (bf16[16,2048]{1,0:T(8,128)(2,1)S(1)}, bf16[16,2048]{1,0:T(8,128)(2,1)S(1)}, u32[]{:S(2)}, u32[]{:S(2)}) collective-permute-start(bf16[16,2048]{1,0:T(8,128)(2,1)S(1)} %hidden.1.refs_0_), channel_id=1, source_target_pairs={{0,1},{1,0},{2,3},{3,2},{4,5},{5,4},{6,7},{7,6},{8,9},{9,8},{10,11... | collective-permute-start | bytes 196616 | tf_op jit(solution)/shard_map/ppermute | solution.py:161
  30.1 4.3 %collective-permute-start.2 = (bf16[16,2048]{1,0:T(8,128)(2,1)S(1)}, bf16[16,2048]{1,0:T(8,128)(2,1)S(1)}, u32[]{:S(2)}, u32[]{:S(2)}) collective-permute-start(bf16[16,2048]{1,0:T(8,128)(2,1)S(1)} %collective-permute-done.1.refs_1_), channel_id=1, source_target_pairs={{0,2},{1,3},{2,0},{3,1},{4,6},{5,7},{6,4},{7,5},{8,10},{9,11},{10,... | collective-permute-start | bytes 196616 | tf_op jit(solution)/shard_map/ppermute | solution.py:161
  30.3 8.4 %collective-permute-start.4 = (bf16[16,2048]{1,0:T(8,128)(2,1)S(1)}, bf16[16,2048]{1,0:T(8,128)(2,1)S(1)}, u32[]{:S(2)}, u32[]{:S(2)}) collective-permute-start(bf16[16,2048]{1,0:T(8,128)(2,1)S(1)} %collective-permute-done.1.refs_1_), channel_id=1, source_target_pairs={{0,1},{1,0},{2,3},{3,2},{4,5},{5,4},{6,7},{7,6},{8,9},{9,8},{10,11... | collective-permute-start | bytes 196616 | tf_op jit(solution)/shard_map/ppermute | solution.py:161
  31.2 5.8 %collective-permute-start.6 = (bf16[16,2048]{1,0:T(8,128)(2,1)S(1)}, bf16[16,2048]{1,0:T(8,128)(2,1)S(1)}, u32[]{:S(2)}, u32[]{:S(2)}) collective-permute-start(bf16[16,2048]{1,0:T(8,128)(2,1)S(1)} %collective-permute-done.5.refs_0_), channel_id=1, source_target_pairs={{0,1},{1,0},{2,3},{3,2},{4,5},{5,4},{6,7},{7,6},{8,9},{9,8},{10,11... | collective-permute-start | bytes 196616 | tf_op jit(solution)/shard_map/ppermute | solution.py:161
  34.4 5.4 %collective-permute-start.3 = (bf16[16,2048]{1,0:T(8,128)(2,1)S(1)}, bf16[16,2048]{1,0:T(8,128)(2,1)S(1)}, u32[]{:S(2)}, u32[]{:S(2)}) collective-permute-start(bf16[16,2048]{1,0:T(8,128)(2,1)S(1)} %collective-permute-done.2.refs_1_), channel_id=1, source_target_pairs={{0,1},{1,0},{2,3},{3,2},{4,5},{5,4},{6,7},{7,6},{8,9},{9,8},{10,11... | collective-permute-start | bytes 196616 | tf_op jit(solution)/shard_map/ppermute | solution.py:161
  51.2 1.2 %collective-permute-start.7 = (f32[8,2,768]{2,1,0:T(2,128)S(1)}, f32[8,2,768]{2,1,0:T(2,128)S(1)}, u32[]{:S(2)}, u32[]{:S(2)}) collective-permute-start(f32[8,2,768]{2,1,0:T(2,128)S(1)} %all_to_all.11.own_ref), channel_id=1, source_target_pairs={{0,8},{8,0},{1,9},{9,1},{2,10},{10,2},{3,11},{11,3},{4,12},{12,4},... | collective-permute-start | bytes 147464 | tf_op jit(solution)/shard_map/ppermute | solution.py:164

commit v14 on v13

--- a/solution.py
+++ b/solution.py
@@ -192,13 +192,15 @@
     for k in (4, 2, 1):
         block[k] = swap(hidden, k)
     block[3] = swap(block[2], 1)
+    total = down(None, [0, 1], block, False)
+    total, block[4] = lax.optimization_barrier((total, block[4]))
     block[6] = swap(block[4], 2)
+    block[4], block[3] = lax.optimization_barrier((block[4], block[3]))
     block[5] = swap(block[4], 1)
-    total = down(None, [0, 1], block, False)
+    total = down(total, [2, 3], block, False)
     total, block[6] = lax.optimization_barrier((total, block[6]))
     block[7] = swap(block[6], 1)
-    total = down(total, [2, 4], block, False)
-    total = down(total, [3, 6], block, False)
+    total = down(total, [4, 6], block, False)
     total = down(total, [5], block, False)
     result = down(total, [7], block, True)
     back = lax.all_to_all(result, "tile", split_axis=0, concat_axis=0, tiled=True)

time: 53.4 us -> 52.8 us (0.989)
  blocking collectives: 26.9 us -> 25.9 us
  starting transfers between devices: 5.2 us -> 5.84 us
    all_to_all x1, blocking collectives: 10.5 us -> 9.5 us  [local_direct(): lax.all_to_all(result, 'tile', split_axis=0, concat_axis=0, tiled=True)]
    ppermute x7, starting transfers between devices: 5.2 us -> 5.84 us  [swap(): return lax.ppermute(x, 'tile', [(t, t ^ bit) for t in range(tiles)])]
where the time goes in v14:
time: 52.8 us; the launch traced here: 52.6 us
  blocking collectives  25.9 us (49%)
  Pallas kernels  15.7 us (30%)
  starting transfers between devices  5.84 us (11%)
  waiting for transfers between devices  4.93 us (9%)
    all_to_all x1, blocking collectives, local_direct(): lax.all_to_all(sends, ('expert', 'tile'), split_axis=0, concat_axis=0, ti...  16.4 us
    all_to_all x1, blocking collectives, local_direct(): lax.all_to_all(result, 'tile', split_axis=0, concat_axis=0, tiled=True)  9.5 us
    pallas_call x5, Pallas kernels, down(): call(functools.partial(down_kernel, steps, first, last), 'down', out, [VM...  7.25 us
    ppermute x7, starting transfers between devices, swap(): return lax.ppermute(x, 'tile', [(t, t ^ bit) for t in range(tiles)])  5.84 us
    ppermute x7, waiting for transfers between devices, swap(): return lax.ppermute(x, 'tile', [(t, t ^ bit) for t in range(tiles)])  3.71 us
    pallas_call x1, Pallas kernels, local_direct(): call(hidden_kernel, 'hidden', bf16(slots, width), [VMEM] * 3, 4 * MIB, 0....  3.37 us
    pallas_call x1, Pallas kernels, local_direct(): call(gate_kernel, 'gate', f32(slots, width), [VMEM] * 2, 4 * MIB, 0.0)  3.34 us
    ppermute x1, waiting for transfers between devices, to_core(): return lax.ppermute(x, 'expert', [(0, 1), (1, 0)])  1.23 us
  transfers between devices with their start and end apart: 8, of which 3 were waited for; matrix products, arithmetic and copies ran while one was open for 0% of the time, Pallas kernels for 12%

profile of v14, /device:TPU:0, one launch (start us, length us, event | category | flops | bytes accessed | tf_op | source)
XLA Modules:
  0.0 52.6 jit_solution(3242305444926757988)
XLA Ops:
  0.0 0.0 copy-start.1
  0.0 1.0 %dispatch.1 = (bf16[16,2,3072]{2,1,0:T(2,128)(2,1)S(1)}, f32[6,4,128]{2,1,0:T(4,128)S(1)}) custom-call(bf16[4,3072]{1,0:T(4,128)(2,1)} %tokens_hbm.1, s32[2,4]{1,0:T(2,128)} %bitcast.2, f32[2,4]{1,0:T(2,128)} %bitcast.3), custom_call_target="tpu_custom_call" | custom-call | flops 599999971328 | tf_op jit(solution)/shard_map/dispatch/pallas_call | solution.py:168
  1.0 0.0 copy-start.2
  1.0 16.4 %all_to_all.10.blocks_ref = bf16[16,2,3072]{2,1,0:T(2,128)(2,1)S(1)} all-to-all(bf16[16,2,3072]{2,1,0:T(2,128)(2,1)S(1)} %get-tuple-element.13), channel_id=1, replica_groups=mesh['group'=2,'expert'=2,'tile'=8] {'expert','tile'}, dimensions={0} | all-to-all | bytes 393216 | tf_op jit(solution)/shard_map/all_to_all | solution.py:178
  17.5 0.0 copy-done.1
  17.5 3.3 %gate.1.gate_ref = f32[16,2048]{1,0:T(8,128)S(1)} custom-call(bf16[32,3072]{1,0:T(8,128)(2,1)S(1)} %merge.1.rows_ref, bf16[1,6144,2048]{2,1,0:T(8,128)(2,1)S(1)} %copy-done.1), custom_call_target="tpu_custom_call" | custom-call | tf_op jit(solution)/shard_map/gate/pallas_call | solution.py:180
  20.9 0.0 copy-done.2
  20.9 3.4 %hidden.1.refs_0_ = bf16[16,2048]{1,0:T(8,128)(2,1)S(1)} custom-call(bf16[32,3072]{1,0:T(8,128)(2,1)S(1)} %merge.1.rows_ref, bf16[1,6144,2048]{2,1,0:T(8,128)(2,1)S(1)} %copy-done.2, f32[16,2048]{1,0:T(8,128)S(1)} %gate.1.gate_ref), custom_call_target="tpu_custom_call" | custom-call | flops 199999995904 | tf_op jit(solution)/shard_map/hidden/pallas_call | solution.py:181
  24.2 0.7 %collective-permute-start = (bf16[16,2048]{1,0:T(8,128)(2,1)S(1)}, bf16[16,2048]{1,0:T(8,128)(2,1)S(1)}, u32[]{:S(2)}, u32[]{:S(2)}) collective-permute-start(bf16[16,2048]{1,0:T(8,128)(2,1)S(1)} %hidden.1.refs_0_), channel_id=1, source_target_pairs={{0,2},{1,3},{2,0},{3,1},{4,6},{5,7},{6,4},{7,5},{8,10},{9,11},{10,... | collective-permute-start | bytes 196616 | tf_op jit(solution)/shard_map/ppermute | solution.py:161
  24.9 0.6 %collective-permute-start.1 = (bf16[16,2048]{1,0:T(8,128)(2,1)S(1)}, bf16[16,2048]{1,0:T(8,128)(2,1)S(1)}, u32[]{:S(2)}, u32[]{:S(2)}) collective-permute-start(bf16[16,2048]{1,0:T(8,128)(2,1)S(1)} %hidden.1.refs_0_), channel_id=1, source_target_pairs={{0,1},{1,0},{2,3},{3,2},{4,5},{5,4},{6,7},{7,6},{8,9},{9,8},{10,11... | collective-permute-start | bytes 196616 | tf_op jit(solution)/shard_map/ppermute | solution.py:161
  25.5 0.9 %collective-permute-start.2 = (bf16[16,2048]{1,0:T(8,128)(2,1)S(1)}, bf16[16,2048]{1,0:T(8,128)(2,1)S(1)}, u32[]{:S(2)}, u32[]{:S(2)}) collective-permute-start(bf16[16,2048]{1,0:T(8,128)(2,1)S(1)} %hidden.1.refs_0_), channel_id=1, source_target_pairs={{0,4},{1,5},{2,6},{3,7},{4,0},{5,1},{6,2},{7,3},{8,12},{9,13},{10,... | collective-permute-start | bytes 196616 | tf_op jit(solution)/shard_map/ppermute | solution.py:161
  26.3 2.9 %collective-permute-done.refs_0_ = bf16[16,2048]{1,0:T(8,128)(2,1)S(1)} collective-permute-done((bf16[16,2048]{1,0:T(8,128)(2,1)S(1)}, bf16[16,2048]{1,0:T(8,128)(2,1)S(1)}, u32[]{:S(2)}, u32[]{:S(2)}) %collective-permute-start) | collective-permute-done | bytes 65568 | tf_op jit(solution)/shard_map/ppermute | solution.py:161
  29.2 0.0 collective-permute-start.3
  29.2 0.0 collective-permute-done.1.refs_1_
  29.2 0.0 copy-done
  29.2 1.8 %down.5.refs_3_ = f32[768,16]{1,0:T(8,128)S(1)} custom-call(bf16[16,2048]{1,0:T(8,128)(2,1)S(1)} %hidden.1.refs_0_, bf16[16,2048]{1,0:T(8,128)(2,1)S(1)} %collective-permute-done.1.refs_1_, bf16[1,768,16384]{2,1,0:T(8,128)(2,1)S(1)} %copy-done), custom_call_target="tpu_custom_call" | custom-call | tf_op jit(solution)/shard_map/down/pallas_call | solution.py:186
  31.0 0.0 collective-permute-done.2.refs_0_
  31.0 1.6 %collective-permute-start.4 = (bf16[16,2048]{1,0:T(8,128)(2,1)S(1)}, bf16[16,2048]{1,0:T(8,128)(2,1)S(1)}, u32[]{:S(2)}, u32[]{:S(2)}) collective-permute-start(bf16[16,2048]{1,0:T(8,128)(2,1)S(1)} %collective-permute-done.2.refs_0_), channel_id=1, source_target_pairs={{0,2},{1,3},{2,0},{3,1},{4,6},{5,7},{6,4},{7,5},{8,10},{9,11},{10,... | collective-permute-start | bytes 196616 | tf_op jit(solution)/shard_map/ppermute | solution.py:161
  32.6 0.8 %collective-permute-done.3.refs_1_ = bf16[16,2048]{1,0:T(8,128)(2,1)S(1)} collective-permute-done((bf16[16,2048]{1,0:T(8,128)(2,1)S(1)}, bf16[16,2048]{1,0:T(8,128)(2,1)S(1)}, u32[]{:S(2)}, u32[]{:S(2)}) %collective-permute-start.3) | collective-permute-done | bytes 65568 | tf_op jit(solution)/shard_map/ppermute | solution.py:161
  33.5 0.3 collective-permute-start.6
  33.8 1.8 %down.6.refs_3_ = f32[768,16]{1,0:T(8,128)S(1)} custom-call(bf16[16,2048]{1,0:T(8,128)(2,1)S(1)} %collective-permute-done.refs_0_, bf16[16,2048]{1,0:T(8,128)(2,1)S(1)} %collective-permute-done.3.refs_1_, bf16[1,768,16384]{2,1,0:T(8,128)(2,1)S(1)} %copy-done, f32[768,16]{1,0:T(8,128)S(1)} %down.5.refs_3_), custom_call_target="tpu_custom_call" | custom-call | tf_op jit(solution)/shard_map/down/pallas_call | solution.py:186
  35.5 0.0 collective-permute-done.4.refs_1_
  35.6 1.8 %collective-permute-start.5 = (bf16[16,2048]{1,0:T(8,128)(2,1)S(1)}, bf16[16,2048]{1,0:T(8,128)(2,1)S(1)}, u32[]{:S(2)}, u32[]{:S(2)}) collective-permute-start(bf16[16,2048]{1,0:T(8,128)(2,1)S(1)} %collective-permute-done.4.refs_1_), channel_id=1, source_target_pairs={{0,1},{1,0},{2,3},{3,2},{4,5},{5,4},{6,7},{7,6},{8,9},{9,8},{10,11... | collective-permute-start | bytes 196616 | tf_op jit(solution)/shard_map/ppermute | solution.py:161
  37.3 1.8 %down.7.refs_2_ = f32[768,16]{1,0:T(8,128)S(1)} custom-call(bf16[16,2048]{1,0:T(8,128)(2,1)S(1)} %collective-permute-done.2.refs_0_, bf16[16,2048]{1,0:T(8,128)(2,1)S(1)} %collective-permute-done.4.refs_1_, bf16[1,768,16384]{2,1,0:T(8,128)(2,1)S(1)} %copy-done, f32[768,16]{1,0:T(8,128)S(1)} %down.6.refs_3_), custom_call_target="tpu_custom_call" | custom-call | tf_op jit(solution)/shard_map/down/pallas_call | solution.py:186
  39.1 0.0 collective-permute-done.6.refs_0_
  39.1 1.0 %down.8.refs_2_ = f32[768,16]{1,0:T(8,128)S(1)} custom-call(bf16[16,2048]{1,0:T(8,128)(2,1)S(1)} %collective-permute-done.6.refs_0_, bf16[1,768,16384]{2,1,0:T(8,128)(2,1)S(1)} %copy-done, f32[768,16]{1,0:T(8,128)S(1)} %down.7.refs_2_), custom_call_target="tpu_custom_call" | custom-call | tf_op jit(solution)/shard_map/down/pallas_call | solution.py:186
  40.1 0.0 collective-permute-done.5.refs_0_
  40.1 1.0 %down.9 = f32[8,2,768]{2,1,0:T(2,128)S(1)} custom-call(bf16[16,2048]{1,0:T(8,128)(2,1)S(1)} %collective-permute-done.5.refs_0_, bf16[1,768,16384]{2,1,0:T(8,128)(2,1)S(1)} %copy-done, f32[768,16]{1,0:T(8,128)S(1)} %down.8.refs_2_), custom_call_target="tpu_custom_call" | custom-call | tf_op jit(solution)/shard_map/down/pallas_call | solution.py:186
  41.1 9.5 %all_to_all.11.own_ref = f32[8,2,768]{2,1,0:T(2,128)S(1)} all-to-all(f32[8,2,768]{2,1,0:T(2,128)S(1)} %down.9), channel_id=1, replica_groups=mesh['group'=2,'expert'=2,'tile'=8] {'tile'}, dimensions={0} | all-to-all | bytes 98304 | tf_op jit(solution)/shard_map/all_to_all | solution.py:206
  50.6 0.0 collective-permute-start.7
  50.6 1.2 %collective-permute-done.7.other_ref = f32[8,2,768]{2,1,0:T(2,128)S(1)} collective-permute-done((f32[8,2,768]{2,1,0:T(2,128)S(1)}, f32[8,2,768]{2,1,0:T(2,128)S(1)}, u32[]{:S(2)}, u32[]{:S(2)}) %collective-permute-start.7) | collective-permute-done | bytes 49184 | tf_op jit(solution)/shard_map/ppermute | solution.py:164
  51.8 0.7 %combine.1 = bf16[4,3072]{1,0:T(4,128)(2,1)} custom-call(f32[8,2,768]{2,1,0:T(2,128)S(1)} %all_to_all.11.own_ref, f32[8,2,768]{2,1,0:T(2,128)S(1)} %collective-permute-done.7.other_ref, f32[6,4,128]{2,1,0:T(4,128)S(1)} %get-tuple-element.20.table_ref), custom_call_target="tpu_custom_call" | custom-call | tf_op jit(solution)/shard_map/combine/pallas_call | solution.py:207
  (2 shorter events, 0.0 us)
Async XLA Ops:
  0.0 17.5 %copy-start.1 = (bf16[1,6144,2048]{2,1,0:T(8,128)(2,1)S(1)}, bf16[1,6144,2048]{2,1,0:T(8,128)(2,1)}, u32[]{:S(2)}) copy-start(bf16[1,6144,2048]{2,1,0:T(8,128)(2,1)} %w_ref.2) | copy-start | bytes 75497472
  1.0 19.8 %copy-start.2 = (bf16[1,6144,2048]{2,1,0:T(8,128)(2,1)S(1)}, bf16[1,6144,2048]{2,1,0:T(8,128)(2,1)}, u32[]{:S(2)}) copy-start(bf16[1,6144,2048]{2,1,0:T(8,128)(2,1)} %w_ref.3) | copy-start | bytes 75497472
  20.9 8.4 %copy-start = (bf16[1,768,16384]{2,1,0:T(8,128)(2,1)S(1)}, bf16[1,768,16384]{2,1,0:T(8,128)(2,1)}, u32[]{:S(2)}) copy-start(bf16[1,768,16384]{2,1,0:T(8,128)(2,1)} %refs_1_.3) | copy-start | bytes 75497472
  24.2 5.0 %collective-permute-start = (bf16[16,2048]{1,0:T(8,128)(2,1)S(1)}, bf16[16,2048]{1,0:T(8,128)(2,1)S(1)}, u32[]{:S(2)}, u32[]{:S(2)}) collective-permute-start(bf16[16,2048]{1,0:T(8,128)(2,1)S(1)} %hidden.1.refs_0_), channel_id=1, source_target_pairs={{0,2},{1,3},{2,0},{3,1},{4,6},{5,7},{6,4},{7,5},{8,10},{9,11},{10,... | collective-permute-start | bytes 196616 | tf_op jit(solution)/shard_map/ppermute | solution.py:161
  24.9 4.3 %collective-permute-start.1 = (bf16[16,2048]{1,0:T(8,128)(2,1)S(1)}, bf16[16,2048]{1,0:T(8,128)(2,1)S(1)}, u32[]{:S(2)}, u32[]{:S(2)}) collective-permute-start(bf16[16,2048]{1,0:T(8,128)(2,1)S(1)} %hidden.1.refs_0_), channel_id=1, source_target_pairs={{0,1},{1,0},{2,3},{3,2},{4,5},{5,4},{6,7},{7,6},{8,9},{9,8},{10,11... | collective-permute-start | bytes 196616 | tf_op jit(solution)/shard_map/ppermute | solution.py:161
  25.5 5.5 %collective-permute-start.2 = (bf16[16,2048]{1,0:T(8,128)(2,1)S(1)}, bf16[16,2048]{1,0:T(8,128)(2,1)S(1)}, u32[]{:S(2)}, u32[]{:S(2)}) collective-permute-start(bf16[16,2048]{1,0:T(8,128)(2,1)S(1)} %hidden.1.refs_0_), channel_id=1, source_target_pairs={{0,4},{1,5},{2,6},{3,7},{4,0},{5,1},{6,2},{7,3},{8,12},{9,13},{10,... | collective-permute-start | bytes 196616 | tf_op jit(solution)/shard_map/ppermute | solution.py:161
  29.2 4.3 %collective-permute-start.3 = (bf16[16,2048]{1,0:T(8,128)(2,1)S(1)}, bf16[16,2048]{1,0:T(8,128)(2,1)S(1)}, u32[]{:S(2)}, u32[]{:S(2)}) collective-permute-start(bf16[16,2048]{1,0:T(8,128)(2,1)S(1)} %collective-permute-done.refs_0_), channel_id=1, source_target_pairs={{0,1},{1,0},{2,3},{3,2},{4,5},{5,4},{6,7},{7,6},{8,9},{9,8},{10,11... | collective-permute-start | bytes 196616 | tf_op jit(solution)/shard_map/ppermute | solution.py:161
  31.0 4.5 %collective-permute-start.4 = (bf16[16,2048]{1,0:T(8,128)(2,1)S(1)}, bf16[16,2048]{1,0:T(8,128)(2,1)S(1)}, u32[]{:S(2)}, u32[]{:S(2)}) collective-permute-start(bf16[16,2048]{1,0:T(8,128)(2,1)S(1)} %collective-permute-done.2.refs_0_), channel_id=1, source_target_pairs={{0,2},{1,3},{2,0},{3,1},{4,6},{5,7},{6,4},{7,5},{8,10},{9,11},{10,... | collective-permute-start | bytes 196616 | tf_op jit(solution)/shard_map/ppermute | solution.py:161
  33.5 5.6 %collective-permute-start.6 = (bf16[16,2048]{1,0:T(8,128)(2,1)S(1)}, bf16[16,2048]{1,0:T(8,128)(2,1)S(1)}, u32[]{:S(2)}, u32[]{:S(2)}) collective-permute-start(bf16[16,2048]{1,0:T(8,128)(2,1)S(1)} %collective-permute-done.2.refs_0_), channel_id=1, source_target_pairs={{0,1},{1,0},{2,3},{3,2},{4,5},{5,4},{6,7},{7,6},{8,9},{9,8},{10,11... | collective-permute-start | bytes 196616 | tf_op jit(solution)/shard_map/ppermute | solution.py:161
  35.6 4.5 %collective-permute-start.5 = (bf16[16,2048]{1,0:T(8,128)(2,1)S(1)}, bf16[16,2048]{1,0:T(8,128)(2,1)S(1)}, u32[]{:S(2)}, u32[]{:S(2)}) collective-permute-start(bf16[16,2048]{1,0:T(8,128)(2,1)S(1)} %collective-permute-done.4.refs_1_), channel_id=1, source_target_pairs={{0,1},{1,0},{2,3},{3,2},{4,5},{5,4},{6,7},{7,6},{8,9},{9,8},{10,11... | collective-permute-start | bytes 196616 | tf_op jit(solution)/shard_map/ppermute | solution.py:161
  50.6 1.2 %collective-permute-start.7 = (f32[8,2,768]{2,1,0:T(2,128)S(1)}, f32[8,2,768]{2,1,0:T(2,128)S(1)}, u32[]{:S(2)}, u32[]{:S(2)}) collective-permute-start(f32[8,2,768]{2,1,0:T(2,128)S(1)} %all_to_all.11.own_ref), channel_id=1, source_target_pairs={{0,8},{8,0},{1,9},{9,1},{2,10},{10,2},{3,11},{11,3},{4,12},{12,4},... | collective-permute-start | bytes 147464 | tf_op jit(solution)/shard_map/ppermute | solution.py:164

commit v15 on v14

--- a/solution.py
+++ b/solution.py
@@ -44,7 +44,7 @@
     return found
 
 
-def dispatch_kernel(tokens_hbm, routes_hbm, gates_hbm, sends_ref, table_ref, tokens_ref, routes_ref, gates_ref, sems):
+def dispatch_kernel(tokens_hbm, routes_hbm, gates_hbm, own_ref, other_ref, table_ref, tokens_ref, routes_ref, gates_ref, sems):
     copies = [
         pltpu.make_async_copy(routes_hbm, routes_ref, sems.at[0]),
         pltpu.make_async_copy(gates_hbm, gates_ref, sems.at[1]),
@@ -56,7 +56,8 @@
         copy.wait()
     tokens = tokens_ref[...].astype(jnp.float32)
     rows = tokens.shape[0]
-    tiles = sends_ref.shape[0] // 2
+    mine = lax.axis_index("expert")
+    blocks = []
     for e in range(2):
         found = slot_rows(routes_ref, e, rows)
         base = e * (1 + SLOTS)
@@ -73,13 +74,27 @@
                 row = row + here * tokens[r:r + 1, :]
                 table_ref[base + 1 + c, r:r + 1, :] = jnp.full(line, here, jnp.float32)
             slots.append(row)
-        block = jnp.concatenate(slots, axis=0).astype(jnp.bfloat16)
-        for t in range(tiles):
-            sends_ref[e * tiles + t] = block
-
-
-def merge_kernel(blocks_ref, rows_ref):
-    rows_ref[...] = blocks_ref[...].reshape(rows_ref.shape)
+        blocks.append(jnp.concatenate(slots, axis=0).astype(jnp.bfloat16))
+    own_ref[...] = jnp.where(mine == 0, blocks[0], blocks[1])
+    other_ref[...] = jnp.where(mine == 0, blocks[1], blocks[0])
+
+
+def pack_kernel(own_ref, got_ref, sends_ref):
+    mine = lax.axis_index("expert")
+    own, got = own_ref[...].astype(jnp.float32), got_ref[...].astype(jnp.float32)
+    block = jnp.concatenate([jnp.where(mine == 0, own, got), jnp.where(mine == 0, got, own)], axis=0)
+    for t in range(sends_ref.shape[0]):
+        sends_ref[t] = block.astype(jnp.bfloat16)
+
+
+def merge_kernel(blocks_ref, rows_ref, first_ref, second_ref):
+    for t in range(blocks_ref.shape[0]):
+        rows = blocks_ref[t].astype(jnp.float32)
+        first_ref[t] = rows[:SLOTS]
+        second_ref[t] = rows[SLOTS:]
+    slots, half = rows_ref.shape[0] // 2, rows_ref.shape[1]
+    rows_ref[:slots, :] = first_ref[...].reshape(slots, half).astype(jnp.bfloat16)
+    rows_ref[slots:, :] = second_ref[...].reshape(slots, half).astype(jnp.bfloat16)
 
 
 def project(rows_ref, w_ref, columns):
@@ -165,9 +180,9 @@
 
     f32 = lambda *shape: jax.ShapeDtypeStruct(shape, jnp.float32)
     bf16 = lambda *shape: jax.ShapeDtypeStruct(shape, jnp.bfloat16)
-    sends, table = call(
+    own, other, table = call(
         dispatch_kernel, "dispatch",
-        (bf16(2 * tiles, SLOTS, half_width), f32(2 * (1 + SLOTS), rows, 128)), [ANY] * 3, 4 * MIB, 600e-6,
+        (bf16(SLOTS, half_width), bf16(SLOTS, half_width), f32(2 * (1 + SLOTS), rows, 128)), [ANY] * 3, 4 * MIB, 600e-6,
         [
             pltpu.VMEM((rows, half_width), jnp.bfloat16),
             pltpu.SMEM((2, rows), jnp.int32),
@@ -175,8 +190,12 @@
             pltpu.SemaphoreType.DMA((3,)),
         ],
     )(in_hbm(tokens), in_hbm(routes), in_hbm(gates))
-    blocks = lax.all_to_all(sends, ("expert", "tile"), split_axis=0, concat_axis=0, tiled=True)
-    x = call(merge_kernel, "merge", bf16(2 * slots, half_width), [VMEM], 4 * MIB, 0e-6)(blocks)
+    sends = call(pack_kernel, "pack", bf16(tiles, 2 * SLOTS, half_width), [VMEM] * 2, 4 * MIB, 0e-6)(own, to_core(other))
+    blocks = lax.all_to_all(sends, "tile", split_axis=0, concat_axis=0, tiled=True)
+    x = call(
+        merge_kernel, "merge", bf16(2 * slots, half_width), [VMEM], 4 * MIB, 0e-6,
+        [pltpu.VMEM((tiles, SLOTS, half_width), jnp.float32)] * 2,
+    )(blocks)
     gate = call(gate_kernel, "gate", f32(slots, width), [VMEM] * 2, 4 * MIB, 0e-6)(x, in_vmem(w_gate))
     hidden = call(hidden_kernel, "hidden", bf16(slots, width), [VMEM] * 3, 4 * MIB, 200e-6)(x, in_vmem(w_up), gate)
 

time: 52.8 us -> 53.8 us (1.019)
  starting transfers between devices: 5.84 us -> 7.27 us
  blocking collectives: 25.9 us -> 25.2 us
    all_to_all x1, blocking collectives: 16.4 us -> 15.5 us  [local_direct(): lax.all_to_all(sends, 'tile', split_axis=0, concat_axis=0, tiled=True)]
    ppermute x7, starting transfers between devices: 5.84 us -> 6.75 us  [swap(): return lax.ppermute(x, 'tile', [(t, t ^ bit) for t in range(tiles)])]
    ppermute x1 -> x2, waiting for transfers between devices: 1.23 us -> 2.06 us  [to_core(): return lax.ppermute(x, 'expert', [(0, 1), (1, 0)])]
    ppermute x7, waiting for transfers between devices: 3.71 us -> 3.13 us  [swap(): return lax.ppermute(x, 'tile', [(t, t ^ bit) for t in range(tiles)])]
  transfers between devices with their start and end apart: 8 -> 9, of which waited for: 3 -> 5; matrix products, arithmetic and copies ran while one was open for 0% -> 0% of each run, Pallas kernels for 12% -> 12%
where the time goes in v15:
time: 53.8 us; the launch traced here: 53.6 us
  blocking collectives  25.2 us (47%)
  Pallas kernels  15.8 us (29%)
  starting transfers between devices  7.27 us (14%)
  waiting for transfers between devices  5.19 us (10%)
    all_to_all x1, blocking collectives, local_direct(): lax.all_to_all(sends, 'tile', split_axis=0, concat_axis=0, tiled=True)  15.5 us
    all_to_all x1, blocking collectives, local_direct(): lax.all_to_all(result, 'tile', split_axis=0, concat_axis=0, tiled=True)  9.72 us
    pallas_call x5, Pallas kernels, down(): call(functools.partial(down_kernel, steps, first, last), 'down', out, [VM...  7.24 us
    ppermute x7, starting transfers between devices, swap(): return lax.ppermute(x, 'tile', [(t, t ^ bit) for t in range(tiles)])  6.75 us
    pallas_call x1, Pallas kernels, local_direct(): call(hidden_kernel, 'hidden', bf16(slots, width), [VMEM] * 3, 4 * MIB, 0....  3.37 us
    pallas_call x1, Pallas kernels, local_direct(): call(gate_kernel, 'gate', f32(slots, width), [VMEM] * 2, 4 * MIB, 0.0)  3.34 us
    ppermute x7, waiting for transfers between devices, swap(): return lax.ppermute(x, 'tile', [(t, t ^ bit) for t in range(tiles)])  3.13 us
    ppermute x2, waiting for transfers between devices, to_core(): return lax.ppermute(x, 'expert', [(0, 1), (1, 0)])  2.06 us
  transfers between devices with their start and end apart: 9, of which 5 were waited for; matrix products, arithmetic and copies ran while one was open for 0% of the time, Pallas kernels for 12%

profile of v15, /device:TPU:0, one launch (start us, length us, event | category | flops | bytes accessed | tf_op | source)
XLA Modules:
  0.0 53.6 jit_solution(18079946896904017115)
XLA Ops:
  0.0 1.0 %dispatch.1 = (bf16[2,3072]{1,0:T(2,128)(2,1)S(1)}, bf16[2,3072]{1,0:T(2,128)(2,1)S(1)}, f32[6,4,128]{2,1,0:T(4,128)S(1)}) custom-call(bf16[4,3072]{1,0:T(4,128)(2,1)} %tokens_hbm.1, s32[2,4]{1,0:T(2,128)} %bitcast.2, f32[2,4]{1,0:T(2,128)} %bitcast.3), custom_call_target="tpu_custom_call" | custom-call | flops 599999971328 | tf_op jit(solution)/shard_map/dispatch/pallas_call | solution.py:183
  1.0 0.0 copy-start.2
  1.1 0.5 collective-permute-start
  1.6 0.8 %collective-permute-done.got_ref = bf16[2,3072]{1,0:T(2,128)(2,1)S(1)} collective-permute-done((bf16[2,3072]{1,0:T(2,128)(2,1)S(1)}, bf16[2,3072]{1,0:T(2,128)(2,1)S(1)}, u32[]{:S(2)}, u32[]{:S(2)}) %collective-permute-start) | collective-permute-done | bytes 12320 | tf_op jit(solution)/shard_map/ppermute | solution.py:179
  2.4 15.5 %all_to_all.10.blocks_ref = bf16[8,4,3072]{2,1,0:T(4,128)(2,1)S(1)} all-to-all(bf16[8,4,3072]{2,1,0:T(4,128)(2,1)S(1)} %pack.1), channel_id=1, replica_groups=mesh['group'=2,'expert'=2,'tile'=8] {'tile'}, dimensions={0} | all-to-all | bytes 393216 | tf_op jit(solution)/shard_map/all_to_all | solution.py:194
  17.9 0.1 merge.1.rows_ref
  18.0 0.0 copy-done.1
  18.0 3.3 %gate.1.gate_ref = f32[16,2048]{1,0:T(8,128)S(1)} custom-call(bf16[32,3072]{1,0:T(8,128)(2,1)S(1)} %merge.1.rows_ref, bf16[1,6144,2048]{2,1,0:T(8,128)(2,1)S(1)} %copy-done.1), custom_call_target="tpu_custom_call" | custom-call | tf_op jit(solution)/shard_map/gate/pallas_call | solution.py:199
  21.4 3.4 %hidden.1.refs_0_ = bf16[16,2048]{1,0:T(8,128)(2,1)S(1)} custom-call(bf16[32,3072]{1,0:T(8,128)(2,1)S(1)} %merge.1.rows_ref, bf16[1,6144,2048]{2,1,0:T(8,128)(2,1)S(1)} %copy-done.2, f32[16,2048]{1,0:T(8,128)S(1)} %gate.1.gate_ref), custom_call_target="tpu_custom_call" | custom-call | flops 199999995904 | tf_op jit(solution)/shard_map/hidden/pallas_call | solution.py:200
  24.7 0.2 collective-permute-start.1
  24.9 1.2 %collective-permute-start.2 = (bf16[16,2048]{1,0:T(8,128)(2,1)S(1)}, bf16[16,2048]{1,0:T(8,128)(2,1)S(1)}, u32[]{:S(2)}, u32[]{:S(2)}) collective-permute-start(bf16[16,2048]{1,0:T(8,128)(2,1)S(1)} %hidden.1.refs_0_), channel_id=1, source_target_pairs={{0,1},{1,0},{2,3},{3,2},{4,5},{5,4},{6,7},{7,6},{8,9},{9,8},{10,11... | collective-permute-start | bytes 196616 | tf_op jit(solution)/shard_map/ppermute | solution.py:176
  26.1 1.6 %collective-permute-start.3 = (bf16[16,2048]{1,0:T(8,128)(2,1)S(1)}, bf16[16,2048]{1,0:T(8,128)(2,1)S(1)}, u32[]{:S(2)}, u32[]{:S(2)}) collective-permute-start(bf16[16,2048]{1,0:T(8,128)(2,1)S(1)} %hidden.1.refs_0_), channel_id=1, source_target_pairs={{0,4},{1,5},{2,6},{3,7},{4,0},{5,1},{6,2},{7,3},{8,12},{9,13},{10,... | collective-permute-start | bytes 196616 | tf_op jit(solution)/shard_map/ppermute | solution.py:176
  27.7 1.7 %collective-permute-done.1.refs_0_ = bf16[16,2048]{1,0:T(8,128)(2,1)S(1)} collective-permute-done((bf16[16,2048]{1,0:T(8,128)(2,1)S(1)}, bf16[16,2048]{1,0:T(8,128)(2,1)S(1)}, u32[]{:S(2)}, u32[]{:S(2)}) %collective-permute-start.1) | collective-permute-done | bytes 65568 | tf_op jit(solution)/shard_map/ppermute | solution.py:176
  29.5 0.6 %collective-permute-start.4 = (bf16[16,2048]{1,0:T(8,128)(2,1)S(1)}, bf16[16,2048]{1,0:T(8,128)(2,1)S(1)}, u32[]{:S(2)}, u32[]{:S(2)}) collective-permute-start(bf16[16,2048]{1,0:T(8,128)(2,1)S(1)} %collective-permute-done.1.refs_0_), channel_id=1, source_target_pairs={{0,1},{1,0},{2,3},{3,2},{4,5},{5,4},{6,7},{7,6},{8,9},{9,8},{10,11... | collective-permute-start | bytes 196616 | tf_op jit(solution)/shard_map/ppermute | solution.py:176
  30.0 0.0 collective-permute-done.2.refs_1_
  30.1 1.8 %down.5.refs_3_ = f32[768,16]{1,0:T(8,128)S(1)} custom-call(bf16[16,2048]{1,0:T(8,128)(2,1)S(1)} %hidden.1.refs_0_, bf16[16,2048]{1,0:T(8,128)(2,1)S(1)} %collective-permute-done.2.refs_1_, bf16[1,768,16384]{2,1,0:T(8,128)(2,1)S(1)} %copy-done), custom_call_target="tpu_custom_call" | custom-call | tf_op jit(solution)/shard_map/down/pallas_call | solution.py:205
  31.8 0.0 collective-permute-done.3.refs_0_
  31.8 1.1 %collective-permute-start.5 = (bf16[16,2048]{1,0:T(8,128)(2,1)S(1)}, bf16[16,2048]{1,0:T(8,128)(2,1)S(1)}, u32[]{:S(2)}, u32[]{:S(2)}) collective-permute-start(bf16[16,2048]{1,0:T(8,128)(2,1)S(1)} %collective-permute-done.3.refs_0_), channel_id=1, source_target_pairs={{0,2},{1,3},{2,0},{3,1},{4,6},{5,7},{6,4},{7,5},{8,10},{9,11},{10,... | collective-permute-start | bytes 196616 | tf_op jit(solution)/shard_map/ppermute | solution.py:176
  32.9 1.1 %collective-permute-done.4.refs_1_ = bf16[16,2048]{1,0:T(8,128)(2,1)S(1)} collective-permute-done((bf16[16,2048]{1,0:T(8,128)(2,1)S(1)}, bf16[16,2048]{1,0:T(8,128)(2,1)S(1)}, u32[]{:S(2)}, u32[]{:S(2)}) %collective-permute-start.4) | collective-permute-done | bytes 65568 | tf_op jit(solution)/shard_map/ppermute | solution.py:176
  34.0 0.8 %collective-permute-start.7 = (bf16[16,2048]{1,0:T(8,128)(2,1)S(1)}, bf16[16,2048]{1,0:T(8,128)(2,1)S(1)}, u32[]{:S(2)}, u32[]{:S(2)}) collective-permute-start(bf16[16,2048]{1,0:T(8,128)(2,1)S(1)} %collective-permute-done.3.refs_0_), channel_id=1, source_target_pairs={{0,1},{1,0},{2,3},{3,2},{4,5},{5,4},{6,7},{7,6},{8,9},{9,8},{10,11... | collective-permute-start | bytes 196616 | tf_op jit(solution)/shard_map/ppermute | solution.py:176
  34.8 1.8 %down.6.refs_3_ = f32[768,16]{1,0:T(8,128)S(1)} custom-call(bf16[16,2048]{1,0:T(8,128)(2,1)S(1)} %collective-permute-done.1.refs_0_, bf16[16,2048]{1,0:T(8,128)(2,1)S(1)} %collective-permute-done.4.refs_1_, bf16[1,768,16384]{2,1,0:T(8,128)(2,1)S(1)} %copy-done, f32[768,16]{1,0:T(8,128)S(1)} %down.5.refs_3_), custom_call_target="tpu_custom_call" | custom-call | tf_op jit(solution)/shard_map/down/pallas_call | solution.py:205
  36.6 0.0 collective-permute-done.5.refs_1_
  36.6 1.3 %collective-permute-start.6 = (bf16[16,2048]{1,0:T(8,128)(2,1)S(1)}, bf16[16,2048]{1,0:T(8,128)(2,1)S(1)}, u32[]{:S(2)}, u32[]{:S(2)}) collective-permute-start(bf16[16,2048]{1,0:T(8,128)(2,1)S(1)} %collective-permute-done.5.refs_1_), channel_id=1, source_target_pairs={{0,1},{1,0},{2,3},{3,2},{4,5},{5,4},{6,7},{7,6},{8,9},{9,8},{10,11... | collective-permute-start | bytes 196616 | tf_op jit(solution)/shard_map/ppermute | solution.py:176
  37.9 1.8 %down.7.refs_2_ = f32[768,16]{1,0:T(8,128)S(1)} custom-call(bf16[16,2048]{1,0:T(8,128)(2,1)S(1)} %collective-permute-done.3.refs_0_, bf16[16,2048]{1,0:T(8,128)(2,1)S(1)} %collective-permute-done.5.refs_1_, bf16[1,768,16384]{2,1,0:T(8,128)(2,1)S(1)} %copy-done, f32[768,16]{1,0:T(8,128)S(1)} %down.6.refs_3_), custom_call_target="tpu_custom_call" | custom-call | tf_op jit(solution)/shard_map/down/pallas_call | solution.py:205
  39.7 0.0 collective-permute-done.7.refs_0_
  39.7 1.0 %down.8.refs_2_ = f32[768,16]{1,0:T(8,128)S(1)} custom-call(bf16[16,2048]{1,0:T(8,128)(2,1)S(1)} %collective-permute-done.7.refs_0_, bf16[1,768,16384]{2,1,0:T(8,128)(2,1)S(1)} %copy-done, f32[768,16]{1,0:T(8,128)S(1)} %down.7.refs_2_), custom_call_target="tpu_custom_call" | custom-call | tf_op jit(solution)/shard_map/down/pallas_call | solution.py:205
  40.7 0.3 collective-permute-done.6.refs_0_
  40.9 1.0 %down.9 = f32[8,2,768]{2,1,0:T(2,128)S(1)} custom-call(bf16[16,2048]{1,0:T(8,128)(2,1)S(1)} %collective-permute-done.6.refs_0_, bf16[1,768,16384]{2,1,0:T(8,128)(2,1)S(1)} %copy-done, f32[768,16]{1,0:T(8,128)S(1)} %down.8.refs_2_), custom_call_target="tpu_custom_call" | custom-call | tf_op jit(solution)/shard_map/down/pallas_call | solution.py:205
  41.9 9.7 %all_to_all.11.own_ref = f32[8,2,768]{2,1,0:T(2,128)S(1)} all-to-all(f32[8,2,768]{2,1,0:T(2,128)S(1)} %down.9), channel_id=1, replica_groups=mesh['group'=2,'expert'=2,'tile'=8] {'tile'}, dimensions={0} | all-to-all | bytes 98304 | tf_op jit(solution)/shard_map/all_to_all | solution.py:225
  51.6 0.0 collective-permute-start.8
  51.6 1.2 %collective-permute-done.8.other_ref = f32[8,2,768]{2,1,0:T(2,128)S(1)} collective-permute-done((f32[8,2,768]{2,1,0:T(2,128)S(1)}, f32[8,2,768]{2,1,0:T(2,128)S(1)}, u32[]{:S(2)}, u32[]{:S(2)}) %collective-permute-start.8) | collective-permute-done | bytes 49184 | tf_op jit(solution)/shard_map/ppermute | solution.py:179
  52.9 0.7 %combine.1 = bf16[4,3072]{1,0:T(4,128)(2,1)} custom-call(f32[8,2,768]{2,1,0:T(2,128)S(1)} %all_to_all.11.own_ref, f32[8,2,768]{2,1,0:T(2,128)S(1)} %collective-permute-done.8.other_ref, f32[6,4,128]{2,1,0:T(4,128)S(1)} %get-tuple-element.22.table_ref), custom_call_target="tpu_custom_call" | custom-call | tf_op jit(solution)/shard_map/combine/pallas_call | solution.py:226
  (5 shorter events, 0.0 us)
Async XLA Ops:
  0.0 18.0 %copy-start.1 = (bf16[1,6144,2048]{2,1,0:T(8,128)(2,1)S(1)}, bf16[1,6144,2048]{2,1,0:T(8,128)(2,1)}, u32[]{:S(2)}) copy-start(bf16[1,6144,2048]{2,1,0:T(8,128)(2,1)} %w_ref.2) | copy-start | bytes 75497472
  1.0 20.3 %copy-start.2 = (bf16[1,6144,2048]{2,1,0:T(8,128)(2,1)S(1)}, bf16[1,6144,2048]{2,1,0:T(8,128)(2,1)}, u32[]{:S(2)}) copy-start(bf16[1,6144,2048]{2,1,0:T(8,128)(2,1)} %w_ref.3) | copy-start | bytes 75497472
  1.1 1.4 %collective-permute-start = (bf16[2,3072]{1,0:T(2,128)(2,1)S(1)}, bf16[2,3072]{1,0:T(2,128)(2,1)S(1)}, u32[]{:S(2)}, u32[]{:S(2)}) collective-permute-start(bf16[2,3072]{1,0:T(2,128)(2,1)S(1)} %get-tuple-element.15), channel_id=1, source_target_pairs={{0,8},{8,0},{1,9},{9,1},{2,10},{10,2},{3,11},{11,3},{4,12},{12,4},... | collective-permute-start | bytes 36872 | tf_op jit(solution)/shard_map/ppermute | solution.py:179
  21.4 8.7 %copy-start = (bf16[1,768,16384]{2,1,0:T(8,128)(2,1)S(1)}, bf16[1,768,16384]{2,1,0:T(8,128)(2,1)}, u32[]{:S(2)}) copy-start(bf16[1,768,16384]{2,1,0:T(8,128)(2,1)} %refs_1_.3) | copy-start | bytes 75497472
  24.7 4.7 %collective-permute-start.1 = (bf16[16,2048]{1,0:T(8,128)(2,1)S(1)}, bf16[16,2048]{1,0:T(8,128)(2,1)S(1)}, u32[]{:S(2)}, u32[]{:S(2)}) collective-permute-start(bf16[16,2048]{1,0:T(8,128)(2,1)S(1)} %hidden.1.refs_0_), channel_id=1, source_target_pairs={{0,2},{1,3},{2,0},{3,1},{4,6},{5,7},{6,4},{7,5},{8,10},{9,11},{10,... | collective-permute-start | bytes 196616 | tf_op jit(solution)/shard_map/ppermute | solution.py:176
  24.9 5.1 %collective-permute-start.2 = (bf16[16,2048]{1,0:T(8,128)(2,1)S(1)}, bf16[16,2048]{1,0:T(8,128)(2,1)S(1)}, u32[]{:S(2)}, u32[]{:S(2)}) collective-permute-start(bf16[16,2048]{1,0:T(8,128)(2,1)S(1)} %hidden.1.refs_0_), channel_id=1, source_target_pairs={{0,1},{1,0},{2,3},{3,2},{4,5},{5,4},{6,7},{7,6},{8,9},{9,8},{10,11... | collective-permute-start | bytes 196616 | tf_op jit(solution)/shard_map/ppermute | solution.py:176
  26.1 5.7 %collective-permute-start.3 = (bf16[16,2048]{1,0:T(8,128)(2,1)S(1)}, bf16[16,2048]{1,0:T(8,128)(2,1)S(1)}, u32[]{:S(2)}, u32[]{:S(2)}) collective-permute-start(bf16[16,2048]{1,0:T(8,128)(2,1)S(1)} %hidden.1.refs_0_), channel_id=1, source_target_pairs={{0,4},{1,5},{2,6},{3,7},{4,0},{5,1},{6,2},{7,3},{8,12},{9,13},{10,... | collective-permute-start | bytes 196616 | tf_op jit(solution)/shard_map/ppermute | solution.py:176
  29.5 4.6 %collective-permute-start.4 = (bf16[16,2048]{1,0:T(8,128)(2,1)S(1)}, bf16[16,2048]{1,0:T(8,128)(2,1)S(1)}, u32[]{:S(2)}, u32[]{:S(2)}) collective-permute-start(bf16[16,2048]{1,0:T(8,128)(2,1)S(1)} %collective-permute-done.1.refs_0_), channel_id=1, source_target_pairs={{0,1},{1,0},{2,3},{3,2},{4,5},{5,4},{6,7},{7,6},{8,9},{9,8},{10,11... | collective-permute-start | bytes 196616 | tf_op jit(solution)/shard_map/ppermute | solution.py:176
  31.8 4.7 %collective-permute-start.5 = (bf16[16,2048]{1,0:T(8,128)(2,1)S(1)}, bf16[16,2048]{1,0:T(8,128)(2,1)S(1)}, u32[]{:S(2)}, u32[]{:S(2)}) collective-permute-start(bf16[16,2048]{1,0:T(8,128)(2,1)S(1)} %collective-permute-done.3.refs_0_), channel_id=1, source_target_pairs={{0,2},{1,3},{2,0},{3,1},{4,6},{5,7},{6,4},{7,5},{8,10},{9,11},{10,... | collective-permute-start | bytes 196616 | tf_op jit(solution)/shard_map/ppermute | solution.py:176
  34.0 5.6 %collective-permute-start.7 = (bf16[16,2048]{1,0:T(8,128)(2,1)S(1)}, bf16[16,2048]{1,0:T(8,128)(2,1)S(1)}, u32[]{:S(2)}, u32[]{:S(2)}) collective-permute-start(bf16[16,2048]{1,0:T(8,128)(2,1)S(1)} %collective-permute-done.3.refs_0_), channel_id=1, source_target_pairs={{0,1},{1,0},{2,3},{3,2},{4,5},{5,4},{6,7},{7,6},{8,9},{9,8},{10,11... | collective-permute-start | bytes 196616 | tf_op jit(solution)/shard_map/ppermute | solution.py:176
  36.6 4.3 %collective-permute-start.6 = (bf16[16,2048]{1,0:T(8,128)(2,1)S(1)}, bf16[16,2048]{1,0:T(8,128)(2,1)S(1)}, u32[]{:S(2)}, u32[]{:S(2)}) collective-permute-start(bf16[16,2048]{1,0:T(8,128)(2,1)S(1)} %collective-permute-done.5.refs_1_), channel_id=1, source_target_pairs={{0,1},{1,0},{2,3},{3,2},{4,5},{5,4},{6,7},{7,6},{8,9},{9,8},{10,11... | collective-permute-start | bytes 196616 | tf_op jit(solution)/shard_map/ppermute | solution.py:176
  51.6 1.2 %collective-permute-start.8 = (f32[8,2,768]{2,1,0:T(2,128)S(1)}, f32[8,2,768]{2,1,0:T(2,128)S(1)}, u32[]{:S(2)}, u32[]{:S(2)}) collective-permute-start(f32[8,2,768]{2,1,0:T(2,128)S(1)} %all_to_all.11.own_ref), channel_id=1, source_target_pairs={{0,8},{8,0},{1,9},{9,1},{2,10},{10,2},{3,11},{11,3},{4,12},{12,4},... | collective-permute-start | bytes 147464 | tf_op jit(solution)/shard_map/ppermute | solution.py:179

commit v16 on v14

--- a/solution.py
+++ b/solution.py
@@ -185,24 +185,21 @@
         out = f32(tiles, SLOTS, features) if last else f32(features, slots)
         return call(
             functools.partial(down_kernel, steps, first, last), "down", out,
-            [VMEM] * (len(steps) + 2 - first), 10 * MIB, 0e-6,
+            [VMEM] * (len(steps) + 2 - first), 10 * MIB, 2e-6,
         )(*(block[k] for k in steps), in_vmem(w_down), *(() if first else (total,)))
 
     block = {0: hidden}
-    for k in (4, 2, 1):
+    for k in (2, 1, 6, 4):
         block[k] = swap(hidden, k)
     block[3] = swap(block[2], 1)
     total = down(None, [0, 1], block, False)
+    total, block[6], block[3] = lax.optimization_barrier((total, block[6], block[3]))
+    block[7] = swap(block[6], 1)
+    total = down(total, [2, 3], block, False)
     total, block[4] = lax.optimization_barrier((total, block[4]))
-    block[6] = swap(block[4], 2)
-    block[4], block[3] = lax.optimization_barrier((block[4], block[3]))
     block[5] = swap(block[4], 1)
-    total = down(total, [2, 3], block, False)
-    total, block[6] = lax.optimization_barrier((total, block[6]))
-    block[7] = swap(block[6], 1)
-    total = down(total, [4, 6], block, False)
-    total = down(total, [5], block, False)
-    result = down(total, [7], block, True)
+    total = down(total, [6, 7], block, False)
+    result = down(total, [4, 5], block, True)
     back = lax.all_to_all(result, "tile", split_axis=0, concat_axis=0, tiled=True)
     return call(combine_kernel, "combine", bf16(rows, half_width), [VMEM] * 3, 4 * MIB)(back, to_core(back), table)
 

time: 52.8 us -> 54.8 us (1.038)
  starting transfers between devices: 5.84 us -> 8.5 us
  waiting for transfers between devices: 4.93 us -> 4.2 us
    ppermute x7, starting transfers between devices: 5.84 us -> 8.5 us  [swap(): return lax.ppermute(x, 'tile', [(t, t ^ bit) for t in range(tiles)])]
    ppermute x7, waiting for transfers between devices: 3.71 us -> 2.97 us  [swap(): return lax.ppermute(x, 'tile', [(t, t ^ bit) for t in range(tiles)])]
    pallas_call x5 -> x4, Pallas kernels: 7.25 us -> 7.08 us  [down(): call(functools.partial(down_kernel, steps, first, last), 'down', out, [VM...]
  transfers between devices with their start and end apart: 8 -> 8, of which waited for: 3 -> 4; matrix products, arithmetic and copies ran while one was open for 0% -> 0% of each run, Pallas kernels for 12% -> 10%
where the time goes in v16:
time: 54.8 us; the launch traced here: 54.6 us
  blocking collectives  26.2 us (48%)
  Pallas kernels  15.6 us (28%)
  starting transfers between devices  8.5 us (16%)
  waiting for transfers between devices  4.2 us (8%)
    all_to_all x1, blocking collectives, local_direct(): lax.all_to_all(sends, ('expert', 'tile'), split_axis=0, concat_axis=0, ti...  16.4 us
    all_to_all x1, blocking collectives, local_direct(): lax.all_to_all(result, 'tile', split_axis=0, concat_axis=0, tiled=True)  9.77 us
    ppermute x7, starting transfers between devices, swap(): return lax.ppermute(x, 'tile', [(t, t ^ bit) for t in range(tiles)])  8.5 us
    pallas_call x4, Pallas kernels, down(): call(functools.partial(down_kernel, steps, first, last), 'down', out, [VM...  7.08 us
    pallas_call x1, Pallas kernels, local_direct(): call(hidden_kernel, 'hidden', bf16(slots, width), [VMEM] * 3, 4 * MIB, 0....  3.37 us
    pallas_call x1, Pallas kernels, local_direct(): call(gate_kernel, 'gate', f32(slots, width), [VMEM] * 2, 4 * MIB, 0.0)  3.34 us
    ppermute x7, waiting for transfers between devices, swap(): return lax.ppermute(x, 'tile', [(t, t ^ bit) for t in range(tiles)])  2.97 us
    ppermute x1, waiting for transfers between devices, to_core(): return lax.ppermute(x, 'expert', [(0, 1), (1, 0)])  1.23 us
  transfers between devices with their start and end apart: 8, of which 4 were waited for; matrix products, arithmetic and copies ran while one was open for 0% of the time, Pallas kernels for 10%

profile of v16, /device:TPU:0, one launch (start us, length us, event | category | flops | bytes accessed | tf_op | source)
XLA Modules:
  0.0 54.6 jit_solution(17942992413793136858)
XLA Ops:
  0.0 0.0 copy-start.1
  0.0 1.0 %dispatch.1 = (bf16[16,2,3072]{2,1,0:T(2,128)(2,1)S(1)}, f32[6,4,128]{2,1,0:T(4,128)S(1)}) custom-call(bf16[4,3072]{1,0:T(4,128)(2,1)} %tokens_hbm.1, s32[2,4]{1,0:T(2,128)} %bitcast.2, f32[2,4]{1,0:T(2,128)} %bitcast.3), custom_call_target="tpu_custom_call" | custom-call | flops 599999971328 | tf_op jit(solution)/shard_map/dispatch/pallas_call | solution.py:168
  1.0 0.0 copy-start.2
  1.0 16.4 %all_to_all.10.blocks_ref = bf16[16,2,3072]{2,1,0:T(2,128)(2,1)S(1)} all-to-all(bf16[16,2,3072]{2,1,0:T(2,128)(2,1)S(1)} %get-tuple-element.12), channel_id=1, replica_groups=mesh['group'=2,'expert'=2,'tile'=8] {'expert','tile'}, dimensions={0} | all-to-all | bytes 393216 | tf_op jit(solution)/shard_map/all_to_all | solution.py:178
  17.5 0.0 copy-done.1
  17.5 3.3 %gate.1.gate_ref = f32[16,2048]{1,0:T(8,128)S(1)} custom-call(bf16[32,3072]{1,0:T(8,128)(2,1)S(1)} %merge.1.rows_ref, bf16[1,6144,2048]{2,1,0:T(8,128)(2,1)S(1)} %copy-done.1), custom_call_target="tpu_custom_call" | custom-call | tf_op jit(solution)/shard_map/gate/pallas_call | solution.py:180
  20.9 0.0 copy-done.2
  20.9 0.0 copy-start
  20.9 3.4 %hidden.1.refs_0_ = bf16[16,2048]{1,0:T(8,128)(2,1)S(1)} custom-call(bf16[32,3072]{1,0:T(8,128)(2,1)S(1)} %merge.1.rows_ref, bf16[1,6144,2048]{2,1,0:T(8,128)(2,1)S(1)} %copy-done.2, f32[16,2048]{1,0:T(8,128)S(1)} %gate.1.gate_ref), custom_call_target="tpu_custom_call" | custom-call | flops 199999995904 | tf_op jit(solution)/shard_map/hidden/pallas_call | solution.py:181
  24.2 0.7 %collective-permute-start = (bf16[16,2048]{1,0:T(8,128)(2,1)S(1)}, bf16[16,2048]{1,0:T(8,128)(2,1)S(1)}, u32[]{:S(2)}, u32[]{:S(2)}) collective-permute-start(bf16[16,2048]{1,0:T(8,128)(2,1)S(1)} %hidden.1.refs_0_), channel_id=1, source_target_pairs={{0,2},{1,3},{2,0},{3,1},{4,6},{5,7},{6,4},{7,5},{8,10},{9,11},{10,... | collective-permute-start | bytes 196616 | tf_op jit(solution)/shard_map/ppermute | solution.py:161
  24.9 0.6 %collective-permute-start.1 = (bf16[16,2048]{1,0:T(8,128)(2,1)S(1)}, bf16[16,2048]{1,0:T(8,128)(2,1)S(1)}, u32[]{:S(2)}, u32[]{:S(2)}) collective-permute-start(bf16[16,2048]{1,0:T(8,128)(2,1)S(1)} %hidden.1.refs_0_), channel_id=1, source_target_pairs={{0,1},{1,0},{2,3},{3,2},{4,5},{5,4},{6,7},{7,6},{8,9},{9,8},{10,11... | collective-permute-start | bytes 196616 | tf_op jit(solution)/shard_map/ppermute | solution.py:161
  25.5 0.9 %collective-permute-start.4 = (bf16[16,2048]{1,0:T(8,128)(2,1)S(1)}, bf16[16,2048]{1,0:T(8,128)(2,1)S(1)}, u32[]{:S(2)}, u32[]{:S(2)}) collective-permute-start(bf16[16,2048]{1,0:T(8,128)(2,1)S(1)} %hidden.1.refs_0_), channel_id=1, source_target_pairs={{0,4},{1,5},{2,6},{3,7},{4,0},{5,1},{6,2},{7,3},{8,12},{9,13},{10,... | collective-permute-start | bytes 196616 | tf_op jit(solution)/shard_map/ppermute | solution.py:161
  26.3 2.8 %collective-permute-start.2 = (bf16[16,2048]{1,0:T(8,128)(2,1)S(1)}, bf16[16,2048]{1,0:T(8,128)(2,1)S(1)}, u32[]{:S(2)}, u32[]{:S(2)}) collective-permute-start(bf16[16,2048]{1,0:T(8,128)(2,1)S(1)} %hidden.1.refs_0_), channel_id=1, source_target_pairs={{0,6},{1,7},{2,4},{3,5},{4,2},{5,3},{6,0},{7,1},{8,14},{9,15},{10,... | collective-permute-start | bytes 196616 | tf_op jit(solution)/shard_map/ppermute | solution.py:161
  29.2 0.0 collective-permute-done.refs_0_
  29.2 1.4 %collective-permute-start.3 = (bf16[16,2048]{1,0:T(8,128)(2,1)S(1)}, bf16[16,2048]{1,0:T(8,128)(2,1)S(1)}, u32[]{:S(2)}, u32[]{:S(2)}) collective-permute-start(bf16[16,2048]{1,0:T(8,128)(2,1)S(1)} %collective-permute-done.refs_0_), channel_id=1, source_target_pairs={{0,1},{1,0},{2,3},{3,2},{4,5},{5,4},{6,7},{7,6},{8,9},{9,8},{10,11... | collective-permute-start | bytes 196616 | tf_op jit(solution)/shard_map/ppermute | solution.py:161
  30.7 0.0 collective-permute-done.1.refs_1_
  30.7 0.0 copy-done
  30.7 1.8 %down.4.refs_3_ = f32[768,16]{1,0:T(8,128)S(1)} custom-call(bf16[16,2048]{1,0:T(8,128)(2,1)S(1)} %hidden.1.refs_0_, bf16[16,2048]{1,0:T(8,128)(2,1)S(1)} %collective-permute-done.1.refs_1_, bf16[1,768,16384]{2,1,0:T(8,128)(2,1)S(1)} %copy-done), custom_call_target="tpu_custom_call" | custom-call | flops 2000000000 | tf_op jit(solution)/shard_map/down/pallas_call | solution.py:186
  32.4 0.0 collective-permute-done.2.refs_0_
  32.4 1.0 %collective-permute-done.3.refs_1_ = bf16[16,2048]{1,0:T(8,128)(2,1)S(1)} collective-permute-done((bf16[16,2048]{1,0:T(8,128)(2,1)S(1)}, bf16[16,2048]{1,0:T(8,128)(2,1)S(1)}, u32[]{:S(2)}, u32[]{:S(2)}) %collective-permute-start.3) | collective-permute-done | bytes 65568 | tf_op jit(solution)/shard_map/ppermute | solution.py:161
  33.5 1.4 %collective-permute-start.6 = (bf16[16,2048]{1,0:T(8,128)(2,1)S(1)}, bf16[16,2048]{1,0:T(8,128)(2,1)S(1)}, u32[]{:S(2)}, u32[]{:S(2)}) collective-permute-start(bf16[16,2048]{1,0:T(8,128)(2,1)S(1)} %collective-permute-done.2.refs_0_), channel_id=1, source_target_pairs={{0,1},{1,0},{2,3},{3,2},{4,5},{5,4},{6,7},{7,6},{8,9},{9,8},{10,11... | collective-permute-start | bytes 196616 | tf_op jit(solution)/shard_map/ppermute | solution.py:161
  34.9 1.8 %down.5.refs_3_ = f32[768,16]{1,0:T(8,128)S(1)} custom-call(bf16[16,2048]{1,0:T(8,128)(2,1)S(1)} %collective-permute-done.refs_0_, bf16[16,2048]{1,0:T(8,128)(2,1)S(1)} %collective-permute-done.3.refs_1_, bf16[1,768,16384]{2,1,0:T(8,128)(2,1)S(1)} %copy-done, f32[768,16]{1,0:T(8,128)S(1)} %down.4.refs_3_), custom_call_target="tpu_custom_call" | custom-call | flops 2000000000 | tf_op jit(solution)/shard_map/down/pallas_call | solution.py:186
  36.7 0.0 collective-permute-done.4.refs_0_
  36.7 0.6 %collective-permute-start.5 = (bf16[16,2048]{1,0:T(8,128)(2,1)S(1)}, bf16[16,2048]{1,0:T(8,128)(2,1)S(1)}, u32[]{:S(2)}, u32[]{:S(2)}) collective-permute-start(bf16[16,2048]{1,0:T(8,128)(2,1)S(1)} %collective-permute-done.4.refs_0_), channel_id=1, source_target_pairs={{0,1},{1,0},{2,3},{3,2},{4,5},{5,4},{6,7},{7,6},{8,9},{9,8},{10,11... | collective-permute-start | bytes 196616 | tf_op jit(solution)/shard_map/ppermute | solution.py:161
  37.3 0.8 %collective-permute-done.6.refs_1_ = bf16[16,2048]{1,0:T(8,128)(2,1)S(1)} collective-permute-done((bf16[16,2048]{1,0:T(8,128)(2,1)S(1)}, bf16[16,2048]{1,0:T(8,128)(2,1)S(1)}, u32[]{:S(2)}, u32[]{:S(2)}) %collective-permute-start.6) | collective-permute-done | bytes 65568 | tf_op jit(solution)/shard_map/ppermute | solution.py:161
  38.1 1.8 %down.6.refs_3_ = f32[768,16]{1,0:T(8,128)S(1)} custom-call(bf16[16,2048]{1,0:T(8,128)(2,1)S(1)} %collective-permute-done.2.refs_0_, bf16[16,2048]{1,0:T(8,128)(2,1)S(1)} %collective-permute-done.6.refs_1_, bf16[1,768,16384]{2,1,0:T(8,128)(2,1)S(1)} %copy-done, f32[768,16]{1,0:T(8,128)S(1)} %down.5.refs_3_), custom_call_target="tpu_custom_call" | custom-call | flops 2000000000 | tf_op jit(solution)/shard_map/down/pallas_call | solution.py:186
  39.9 1.1 %collective-permute-done.5.refs_1_ = bf16[16,2048]{1,0:T(8,128)(2,1)S(1)} collective-permute-done((bf16[16,2048]{1,0:T(8,128)(2,1)S(1)}, bf16[16,2048]{1,0:T(8,128)(2,1)S(1)}, u32[]{:S(2)}, u32[]{:S(2)}) %collective-permute-start.5) | collective-permute-done | bytes 65568 | tf_op jit(solution)/shard_map/ppermute | solution.py:161
  41.0 1.8 %down.7 = f32[8,2,768]{2,1,0:T(2,128)S(1)} custom-call(bf16[16,2048]{1,0:T(8,128)(2,1)S(1)} %collective-permute-done.4.refs_0_, bf16[16,2048]{1,0:T(8,128)(2,1)S(1)} %collective-permute-done.5.refs_1_, bf16[1,768,16384]{2,1,0:T(8,128)(2,1)S(1)} %copy-done, f32[768,16]{1,0:T(8,128)S(1)} %down.6.refs_3_), custom_call_target="tpu_custom_call" | custom-call | flops 2000000000 | tf_op jit(solution)/shard_map/down/pallas_call | solution.py:186
  42.8 9.8 %all_to_all.11.own_ref = f32[8,2,768]{2,1,0:T(2,128)S(1)} all-to-all(f32[8,2,768]{2,1,0:T(2,128)S(1)} %down.7), channel_id=1, replica_groups=mesh['group'=2,'expert'=2,'tile'=8] {'tile'}, dimensions={0} | all-to-all | bytes 98304 | tf_op jit(solution)/shard_map/all_to_all | solution.py:203
  52.6 0.0 collective-permute-start.7
  52.6 1.2 %collective-permute-done.7.other_ref = f32[8,2,768]{2,1,0:T(2,128)S(1)} collective-permute-done((f32[8,2,768]{2,1,0:T(2,128)S(1)}, f32[8,2,768]{2,1,0:T(2,128)S(1)}, u32[]{:S(2)}, u32[]{:S(2)}) %collective-permute-start.7) | collective-permute-done | bytes 49184 | tf_op jit(solution)/shard_map/ppermute | solution.py:164
  53.8 0.7 %combine.1 = bf16[4,3072]{1,0:T(4,128)(2,1)} custom-call(f32[8,2,768]{2,1,0:T(2,128)S(1)} %all_to_all.11.own_ref, f32[8,2,768]{2,1,0:T(2,128)S(1)} %collective-permute-done.7.other_ref, f32[6,4,128]{2,1,0:T(4,128)S(1)} %get-tuple-element.18.table_ref), custom_call_target="tpu_custom_call" | custom-call | tf_op jit(solution)/shard_map/combine/pallas_call | solution.py:204
  (1 shorter events, 0.0 us)
Async XLA Ops:
  0.0 17.5 %copy-start.1 = (bf16[1,6144,2048]{2,1,0:T(8,128)(2,1)S(1)}, bf16[1,6144,2048]{2,1,0:T(8,128)(2,1)}, u32[]{:S(2)}) copy-start(bf16[1,6144,2048]{2,1,0:T(8,128)(2,1)} %w_ref.2) | copy-start | bytes 75497472
  1.0 19.8 %copy-start.2 = (bf16[1,6144,2048]{2,1,0:T(8,128)(2,1)S(1)}, bf16[1,6144,2048]{2,1,0:T(8,128)(2,1)}, u32[]{:S(2)}) copy-start(bf16[1,6144,2048]{2,1,0:T(8,128)(2,1)} %w_ref.3) | copy-start | bytes 75497472
  20.9 9.8 %copy-start = (bf16[1,768,16384]{2,1,0:T(8,128)(2,1)S(1)}, bf16[1,768,16384]{2,1,0:T(8,128)(2,1)}, u32[]{:S(2)}) copy-start(bf16[1,768,16384]{2,1,0:T(8,128)(2,1)} %refs_2_.7) | copy-start | bytes 75497472
  24.2 5.0 %collective-permute-start = (bf16[16,2048]{1,0:T(8,128)(2,1)S(1)}, bf16[16,2048]{1,0:T(8,128)(2,1)S(1)}, u32[]{:S(2)}, u32[]{:S(2)}) collective-permute-start(bf16[16,2048]{1,0:T(8,128)(2,1)S(1)} %hidden.1.refs_0_), channel_id=1, source_target_pairs={{0,2},{1,3},{2,0},{3,1},{4,6},{5,7},{6,4},{7,5},{8,10},{9,11},{10,... | collective-permute-start | bytes 196616 | tf_op jit(solution)/shard_map/ppermute | solution.py:161
  24.9 5.7 %collective-permute-start.1 = (bf16[16,2048]{1,0:T(8,128)(2,1)S(1)}, bf16[16,2048]{1,0:T(8,128)(2,1)S(1)}, u32[]{:S(2)}, u32[]{:S(2)}) collective-permute-start(bf16[16,2048]{1,0:T(8,128)(2,1)S(1)} %hidden.1.refs_0_), channel_id=1, source_target_pairs={{0,1},{1,0},{2,3},{3,2},{4,5},{5,4},{6,7},{7,6},{8,9},{9,8},{10,11... | collective-permute-start | bytes 196616 | tf_op jit(solution)/shard_map/ppermute | solution.py:161
  25.5 11.2 %collective-permute-start.4 = (bf16[16,2048]{1,0:T(8,128)(2,1)S(1)}, bf16[16,2048]{1,0:T(8,128)(2,1)S(1)}, u32[]{:S(2)}, u32[]{:S(2)}) collective-permute-start(bf16[16,2048]{1,0:T(8,128)(2,1)S(1)} %hidden.1.refs_0_), channel_id=1, source_target_pairs={{0,4},{1,5},{2,6},{3,7},{4,0},{5,1},{6,2},{7,3},{8,12},{9,13},{10,... | collective-permute-start | bytes 196616 | tf_op jit(solution)/shard_map/ppermute | solution.py:161
  26.3 6.1 %collective-permute-start.2 = (bf16[16,2048]{1,0:T(8,128)(2,1)S(1)}, bf16[16,2048]{1,0:T(8,128)(2,1)S(1)}, u32[]{:S(2)}, u32[]{:S(2)}) collective-permute-start(bf16[16,2048]{1,0:T(8,128)(2,1)S(1)} %hidden.1.refs_0_), channel_id=1, source_target_pairs={{0,6},{1,7},{2,4},{3,5},{4,2},{5,3},{6,0},{7,1},{8,14},{9,15},{10,... | collective-permute-start | bytes 196616 | tf_op jit(solution)/shard_map/ppermute | solution.py:161
  29.2 4.3 %collective-permute-start.3 = (bf16[16,2048]{1,0:T(8,128)(2,1)S(1)}, bf16[16,2048]{1,0:T(8,128)(2,1)S(1)}, u32[]{:S(2)}, u32[]{:S(2)}) collective-permute-start(bf16[16,2048]{1,0:T(8,128)(2,1)S(1)} %collective-permute-done.refs_0_), channel_id=1, source_target_pairs={{0,1},{1,0},{2,3},{3,2},{4,5},{5,4},{6,7},{7,6},{8,9},{9,8},{10,11... | collective-permute-start | bytes 196616 | tf_op jit(solution)/shard_map/ppermute | solution.py:161
  33.5 4.7 %collective-permute-start.6 = (bf16[16,2048]{1,0:T(8,128)(2,1)S(1)}, bf16[16,2048]{1,0:T(8,128)(2,1)S(1)}, u32[]{:S(2)}, u32[]{:S(2)}) collective-permute-start(bf16[16,2048]{1,0:T(8,128)(2,1)S(1)} %collective-permute-done.2.refs_0_), channel_id=1, source_target_pairs={{0,1},{1,0},{2,3},{3,2},{4,5},{5,4},{6,7},{7,6},{8,9},{9,8},{10,11... | collective-permute-start | bytes 196616 | tf_op jit(solution)/shard_map/ppermute | solution.py:161
  36.7 4.3 %collective-permute-start.5 = (bf16[16,2048]{1,0:T(8,128)(2,1)S(1)}, bf16[16,2048]{1,0:T(8,128)(2,1)S(1)}, u32[]{:S(2)}, u32[]{:S(2)}) collective-permute-start(bf16[16,2048]{1,0:T(8,128)(2,1)S(1)} %collective-permute-done.4.refs_0_), channel_id=1, source_target_pairs={{0,1},{1,0},{2,3},{3,2},{4,5},{5,4},{6,7},{7,6},{8,9},{9,8},{10,11... | collective-permute-start | bytes 196616 | tf_op jit(solution)/shard_map/ppermute | solution.py:161
  52.6 1.2 %collective-permute-start.7 = (f32[8,2,768]{2,1,0:T(2,128)S(1)}, f32[8,2,768]{2,1,0:T(2,128)S(1)}, u32[]{:S(2)}, u32[]{:S(2)}) collective-permute-start(f32[8,2,768]{2,1,0:T(2,128)S(1)} %all_to_all.11.own_ref), channel_id=1, source_target_pairs={{0,8},{8,0},{1,9},{9,1},{2,10},{10,2},{3,11},{11,3},{4,12},{12,4},... | collective-permute-start | bytes 147464 | tf_op jit(solution)/shard_map/ppermute | solution.py:164

commit v17 on v10

--- a/solution.py
+++ b/solution.py
@@ -114,9 +114,13 @@
     over_columns(hidden_ref.shape[1], body)
 
 
+def join_kernel(first_ref, second_ref, out_ref):
+    out_ref[0] = first_ref[...]
+    out_ref[1] = second_ref[...]
+
+
 def down_kernel(steps, first, last, *refs):
-    n = len(steps)
-    blocks, w_ref, rest = refs[:n], refs[n], refs[n + 1:]
+    blocks, w_ref, rest = [refs[0].at[i] for i in range(len(steps))], refs[1], refs[2:]
     out_ref = rest[-1]
     me = lax.axis_index("tile")
     slots, width = blocks[0].shape
@@ -185,19 +189,24 @@
         out = f32(tiles, SLOTS, features) if last else f32(features, slots)
         return call(
             functools.partial(down_kernel, steps, first, last), "down", out,
-            [VMEM] * (len(blocks) + 2 - first), 10 * MIB, 0e-6,
-        )(*blocks, in_vmem(w_down), *(() if first else (total,)))
-
-    column = [swap(hidden, k) for k in (6, 4, 2)]
-    beside = swap(hidden, 1)
-    total = down(None, [0], [hidden], False)
-    total = down(total, [1], [beside], False)
-    total, column[0] = lax.optimization_barrier((total, column[0]))
-    other_column = [swap(block, 1) for block in column]
-    total = down(total, [6, 4], column[:2], False)
-    total = down(total, [2], column[2:], False)
-    total = down(total, [7, 5], other_column[:2], False)
-    result = down(total, [3], other_column[2:], True)
+            [VMEM] * (3 - first), 10 * MIB, 2e-6,
+        )(blocks, in_vmem(w_down), *(() if first else (total,)))
+
+    def join(first, second):
+        return call(join_kernel, "join", bf16(2, slots, width), [VMEM] * 2, 4 * MIB)(first, second)
+
+    four = swap(hidden, 4)
+    pair = join(hidden, swap(hidden, 1))
+    near = swap(pair, 2)
+    four, _ = lax.optimization_barrier((four, pair))
+    five = swap(four, 1)
+    total = down(None, [0, 1], pair, False)
+    total, five = lax.optimization_barrier((total, five))
+    middle = join(four, five)
+    far = swap(middle, 2)
+    total = down(total, [2, 3], near, False)
+    total = down(total, [4, 5], middle, False)
+    result = down(total, [6, 7], far, True)
     back = lax.all_to_all(result, "tile", split_axis=0, concat_axis=0, tiled=True)
     return call(combine_kernel, "combine", bf16(rows, half_width), [VMEM] * 3, 4 * MIB)(back, to_core(back), table)
 

time: 53.1 us -> 54.3 us (1.023)
  waiting for transfers between devices: 2.13 us -> 8.25 us
  starting transfers between devices: 8.4 us -> 3.49 us
    ppermute x7 -> x5, waiting for transfers between devices: 0.91 us -> 7.03 us  [swap(): return lax.ppermute(x, 'tile', [(t, t ^ bit) for t in range(tiles)])]
    ppermute x7 -> x5, starting transfers between devices: 8.4 us -> 3.49 us  [swap(): return lax.ppermute(x, 'tile', [(t, t ^ bit) for t in range(tiles)])]
    pallas_call x6 -> x4, Pallas kernels: 7.4 us -> 7.08 us  [down(): call(functools.partial(down_kernel, steps, first, last), 'down', out, [VM...]
  transfers between devices with their start and end apart: 8 -> 6, of which waited for: 3 -> 5; matrix products, arithmetic and copies ran while one was open for 0% -> 0% of each run, Pallas kernels for 12% -> 10%
where the time goes in v17:
time: 54.3 us; the launch traced here: 54.1 us
  blocking collectives  26.7 us (49%)
  Pallas kernels  15.6 us (29%)
  waiting for transfers between devices  8.25 us (15%)
  starting transfers between devices  3.49 us (6%)
    all_to_all x1, blocking collectives, local_direct(): lax.all_to_all(sends, ('expert', 'tile'), split_axis=0, concat_axis=0, ti...  16.4 us
    all_to_all x1, blocking collectives, local_direct(): lax.all_to_all(result, 'tile', split_axis=0, concat_axis=0, tiled=True)  10.2 us
    pallas_call x4, Pallas kernels, down(): call(functools.partial(down_kernel, steps, first, last), 'down', out, [VM...  7.08 us
    ppermute x5, waiting for transfers between devices, swap(): return lax.ppermute(x, 'tile', [(t, t ^ bit) for t in range(tiles)])  7.03 us
    ppermute x5, starting transfers between devices, swap(): return lax.ppermute(x, 'tile', [(t, t ^ bit) for t in range(tiles)])  3.49 us
    pallas_call x1, Pallas kernels, local_direct(): call(hidden_kernel, 'hidden', bf16(slots, width), [VMEM] * 3, 4 * MIB, 0....  3.37 us
    pallas_call x1, Pallas kernels, local_direct(): call(gate_kernel, 'gate', f32(slots, width), [VMEM] * 2, 4 * MIB, 0.0)  3.34 us
    ppermute x1, waiting for transfers between devices, to_core(): return lax.ppermute(x, 'expert', [(0, 1), (1, 0)])  1.23 us
  transfers between devices with their start and end apart: 6, of which 5 were waited for; matrix products, arithmetic and copies ran while one was open for 0% of the time, Pallas kernels for 10%

profile of v17, /device:TPU:0, one launch (start us, length us, event | category | flops | bytes accessed | tf_op | source)
XLA Modules:
  0.0 54.1 jit_solution(17842705863012776181)
XLA Ops:
  0.0 0.0 copy-start.1
  0.0 1.0 %dispatch.1 = (bf16[16,2,3072]{2,1,0:T(2,128)(2,1)S(1)}, f32[6,4,128]{2,1,0:T(4,128)S(1)}) custom-call(bf16[4,3072]{1,0:T(4,128)(2,1)} %tokens_hbm.1, s32[2,4]{1,0:T(2,128)} %bitcast.2, f32[2,4]{1,0:T(2,128)} %bitcast.3), custom_call_target="tpu_custom_call" | custom-call | flops 599999971328 | tf_op jit(solution)/shard_map/dispatch/pallas_call | solution.py:172
  1.0 0.0 copy-start.2
  1.0 16.4 %all_to_all.10.blocks_ref = bf16[16,2,3072]{2,1,0:T(2,128)(2,1)S(1)} all-to-all(bf16[16,2,3072]{2,1,0:T(2,128)(2,1)S(1)} %get-tuple-element.10), channel_id=1, replica_groups=mesh['group'=2,'expert'=2,'tile'=8] {'expert','tile'}, dimensions={0} | all-to-all | bytes 393216 | tf_op jit(solution)/shard_map/all_to_all | solution.py:182
  17.5 0.0 copy-done.1
  17.5 3.3 %gate.1.gate_ref = f32[16,2048]{1,0:T(8,128)S(1)} custom-call(bf16[32,3072]{1,0:T(8,128)(2,1)S(1)} %merge.1.rows_ref, bf16[1,6144,2048]{2,1,0:T(8,128)(2,1)S(1)} %copy-done.1), custom_call_target="tpu_custom_call" | custom-call | tf_op jit(solution)/shard_map/gate/pallas_call | solution.py:184
  20.9 0.0 copy-done.2
  20.9 0.0 copy-start
  20.9 3.4 %hidden.1.first_ref = bf16[16,2048]{1,0:T(8,128)(2,1)S(1)} custom-call(bf16[32,3072]{1,0:T(8,128)(2,1)S(1)} %merge.1.rows_ref, bf16[1,6144,2048]{2,1,0:T(8,128)(2,1)S(1)} %copy-done.2, f32[16,2048]{1,0:T(8,128)S(1)} %gate.1.gate_ref), custom_call_target="tpu_custom_call" | custom-call | flops 199999995904 | tf_op jit(solution)/shard_map/hidden/pallas_call | solution.py:185
  24.2 0.6 %collective-permute-start.1 = (bf16[16,2048]{1,0:T(8,128)(2,1)S(1)}, bf16[16,2048]{1,0:T(8,128)(2,1)S(1)}, u32[]{:S(2)}, u32[]{:S(2)}) collective-permute-start(bf16[16,2048]{1,0:T(8,128)(2,1)S(1)} %hidden.1.first_ref), channel_id=1, source_target_pairs={{0,1},{1,0},{2,3},{3,2},{4,5},{5,4},{6,7},{7,6},{8,9},{9,8},{10,11... | collective-permute-start | bytes 196616 | tf_op jit(solution)/shard_map/ppermute | solution.py:165
  24.8 0.7 %collective-permute-start = (bf16[16,2048]{1,0:T(8,128)(2,1)S(1)}, bf16[16,2048]{1,0:T(8,128)(2,1)S(1)}, u32[]{:S(2)}, u32[]{:S(2)}) collective-permute-start(bf16[16,2048]{1,0:T(8,128)(2,1)S(1)} %hidden.1.first_ref), channel_id=1, source_target_pairs={{0,4},{1,5},{2,6},{3,7},{4,0},{5,1},{6,2},{7,3},{8,12},{9,13},{10,... | collective-permute-start | bytes 196616 | tf_op jit(solution)/shard_map/ppermute | solution.py:165
  25.5 3.0 %collective-permute-done.1.second_ref = bf16[16,2048]{1,0:T(8,128)(2,1)S(1)} collective-permute-done((bf16[16,2048]{1,0:T(8,128)(2,1)S(1)}, bf16[16,2048]{1,0:T(8,128)(2,1)S(1)}, u32[]{:S(2)}, u32[]{:S(2)}) %collective-permute-start.1) | collective-permute-done | bytes 65568 | tf_op jit(solution)/shard_map/ppermute | solution.py:165
  28.5 0.8 %collective-permute-start.4 = (bf16[2,16,2048]{2,1,0:T(8,128)(2,1)S(1)}, bf16[2,16,2048]{2,1,0:T(8,128)(2,1)S(1)}, u32[]{:S(2)}, u32[]{:S(2)}) collective-permute-start(bf16[2,16,2048]{2,1,0:T(8,128)(2,1)S(1)} %join.2.refs_0_), channel_id=1, source_target_pairs={{0,2},{1,3},{2,0},{3,1},{4,6},{5,7},{6,4},{7,5},{8,10},{9,11},{10,... | collective-permute-start | bytes 393224 | tf_op jit(solution)/shard_map/ppermute | solution.py:165
  29.3 1.5 %collective-permute-done.first_ref = bf16[16,2048]{1,0:T(8,128)(2,1)S(1)} collective-permute-done((bf16[16,2048]{1,0:T(8,128)(2,1)S(1)}, bf16[16,2048]{1,0:T(8,128)(2,1)S(1)}, u32[]{:S(2)}, u32[]{:S(2)}) %collective-permute-start) | collective-permute-done | bytes 65568 | tf_op jit(solution)/shard_map/ppermute | solution.py:165
  30.8 1.2 %collective-permute-start.2 = (bf16[16,2048]{1,0:T(8,128)(2,1)S(1)}, bf16[16,2048]{1,0:T(8,128)(2,1)S(1)}, u32[]{:S(2)}, u32[]{:S(2)}) collective-permute-start(bf16[16,2048]{1,0:T(8,128)(2,1)S(1)} %collective-permute-done.first_ref), channel_id=1, source_target_pairs={{0,1},{1,0},{2,3},{3,2},{4,5},{5,4},{6,7},{7,6},{8,9},{9,8},{10,11... | collective-permute-start | bytes 196616 | tf_op jit(solution)/shard_map/ppermute | solution.py:165
  32.0 0.0 copy-done
  32.0 1.8 %down.4.refs_2_ = f32[768,16]{1,0:T(8,128)S(1)} custom-call(bf16[2,16,2048]{2,1,0:T(8,128)(2,1)S(1)} %join.2.refs_0_, bf16[1,768,16384]{2,1,0:T(8,128)(2,1)S(1)} %copy-done), custom_call_target="tpu_custom_call" | custom-call | flops 2000000000 | tf_op jit(solution)/shard_map/down/pallas_call | solution.py:190
  33.8 1.3 %collective-permute-done.2.second_ref = bf16[16,2048]{1,0:T(8,128)(2,1)S(1)} collective-permute-done((bf16[16,2048]{1,0:T(8,128)(2,1)S(1)}, bf16[16,2048]{1,0:T(8,128)(2,1)S(1)}, u32[]{:S(2)}, u32[]{:S(2)}) %collective-permute-start.2) | collective-permute-done | bytes 65568 | tf_op jit(solution)/shard_map/ppermute | solution.py:165
  35.0 0.2 collective-permute-start.3
  35.3 0.0 collective-permute-done.4.refs_0_
  35.3 1.8 %down.5.refs_2_ = f32[768,16]{1,0:T(8,128)S(1)} custom-call(bf16[2,16,2048]{2,1,0:T(8,128)(2,1)S(1)} %collective-permute-done.4.refs_0_, bf16[1,768,16384]{2,1,0:T(8,128)(2,1)S(1)} %copy-done, f32[768,16]{1,0:T(8,128)S(1)} %down.4.refs_2_), custom_call_target="tpu_custom_call" | custom-call | flops 2000000000 | tf_op jit(solution)/shard_map/down/pallas_call | solution.py:190
  37.1 1.8 %down.6.refs_2_ = f32[768,16]{1,0:T(8,128)S(1)} custom-call(bf16[2,16,2048]{2,1,0:T(8,128)(2,1)S(1)} %join.3.refs_0_, bf16[1,768,16384]{2,1,0:T(8,128)(2,1)S(1)} %copy-done, f32[768,16]{1,0:T(8,128)S(1)} %down.5.refs_2_), custom_call_target="tpu_custom_call" | custom-call | flops 2000000000 | tf_op jit(solution)/shard_map/down/pallas_call | solution.py:190
  38.8 1.2 %collective-permute-done.3.refs_0_ = bf16[2,16,2048]{2,1,0:T(8,128)(2,1)S(1)} collective-permute-done((bf16[2,16,2048]{2,1,0:T(8,128)(2,1)S(1)}, bf16[2,16,2048]{2,1,0:T(8,128)(2,1)S(1)}, u32[]{:S(2)}, u32[]{:S(2)}) %collective-permute-start.3) | collective-permute-done | bytes 131104 | tf_op jit(solution)/shard_map/ppermute | solution.py:165
  40.1 1.8 %down.7 = f32[8,2,768]{2,1,0:T(2,128)S(1)} custom-call(bf16[2,16,2048]{2,1,0:T(8,128)(2,1)S(1)} %collective-permute-done.3.refs_0_, bf16[1,768,16384]{2,1,0:T(8,128)(2,1)S(1)} %copy-done, f32[768,16]{1,0:T(8,128)S(1)} %down.6.refs_2_), custom_call_target="tpu_custom_call" | custom-call | flops 2000000000 | tf_op jit(solution)/shard_map/down/pallas_call | solution.py:190
  41.9 10.2 %all_to_all.11.own_ref = f32[8,2,768]{2,1,0:T(2,128)S(1)} all-to-all(f32[8,2,768]{2,1,0:T(2,128)S(1)} %down.7), channel_id=1, replica_groups=mesh['group'=2,'expert'=2,'tile'=8] {'tile'}, dimensions={0} | all-to-all | bytes 98304 | tf_op jit(solution)/shard_map/all_to_all | solution.py:210
  52.1 0.0 collective-permute-start.5
  52.1 1.2 %collective-permute-done.5.other_ref = f32[8,2,768]{2,1,0:T(2,128)S(1)} collective-permute-done((f32[8,2,768]{2,1,0:T(2,128)S(1)}, f32[8,2,768]{2,1,0:T(2,128)S(1)}, u32[]{:S(2)}, u32[]{:S(2)}) %collective-permute-start.5) | collective-permute-done | bytes 49184 | tf_op jit(solution)/shard_map/ppermute | solution.py:168
  53.3 0.7 %combine.1 = bf16[4,3072]{1,0:T(4,128)(2,1)} custom-call(f32[8,2,768]{2,1,0:T(2,128)S(1)} %all_to_all.11.own_ref, f32[8,2,768]{2,1,0:T(2,128)S(1)} %collective-permute-done.5.other_ref, f32[6,4,128]{2,1,0:T(4,128)S(1)} %get-tuple-element.14.table_ref), custom_call_target="tpu_custom_call" | custom-call | tf_op jit(solution)/shard_map/combine/pallas_call | solution.py:211
  (3 shorter events, 0.0 us)
Async XLA Ops:
  0.0 17.5 %copy-start.1 = (bf16[1,6144,2048]{2,1,0:T(8,128)(2,1)S(1)}, bf16[1,6144,2048]{2,1,0:T(8,128)(2,1)}, u32[]{:S(2)}) copy-start(bf16[1,6144,2048]{2,1,0:T(8,128)(2,1)} %w_ref.2) | copy-start | bytes 75497472
  1.0 19.8 %copy-start.2 = (bf16[1,6144,2048]{2,1,0:T(8,128)(2,1)S(1)}, bf16[1,6144,2048]{2,1,0:T(8,128)(2,1)}, u32[]{:S(2)}) copy-start(bf16[1,6144,2048]{2,1,0:T(8,128)(2,1)} %w_ref.3) | copy-start | bytes 75497472
  20.9 11.1 %copy-start = (bf16[1,768,16384]{2,1,0:T(8,128)(2,1)S(1)}, bf16[1,768,16384]{2,1,0:T(8,128)(2,1)}, u32[]{:S(2)}) copy-start(bf16[1,768,16384]{2,1,0:T(8,128)(2,1)} %refs_1_.7) | copy-start | bytes 75497472
  24.2 4.3 %collective-permute-start.1 = (bf16[16,2048]{1,0:T(8,128)(2,1)S(1)}, bf16[16,2048]{1,0:T(8,128)(2,1)S(1)}, u32[]{:S(2)}, u32[]{:S(2)}) collective-permute-start(bf16[16,2048]{1,0:T(8,128)(2,1)S(1)} %hidden.1.first_ref), channel_id=1, source_target_pairs={{0,1},{1,0},{2,3},{3,2},{4,5},{5,4},{6,7},{7,6},{8,9},{9,8},{10,11... | collective-permute-start | bytes 196616 | tf_op jit(solution)/shard_map/ppermute | solution.py:165
  24.8 6.0 %collective-permute-start = (bf16[16,2048]{1,0:T(8,128)(2,1)S(1)}, bf16[16,2048]{1,0:T(8,128)(2,1)S(1)}, u32[]{:S(2)}, u32[]{:S(2)}) collective-permute-start(bf16[16,2048]{1,0:T(8,128)(2,1)S(1)} %hidden.1.first_ref), channel_id=1, source_target_pairs={{0,4},{1,5},{2,6},{3,7},{4,0},{5,1},{6,2},{7,3},{8,12},{9,13},{10,... | collective-permute-start | bytes 196616 | tf_op jit(solution)/shard_map/ppermute | solution.py:165
  28.5 6.8 %collective-permute-start.4 = (bf16[2,16,2048]{2,1,0:T(8,128)(2,1)S(1)}, bf16[2,16,2048]{2,1,0:T(8,128)(2,1)S(1)}, u32[]{:S(2)}, u32[]{:S(2)}) collective-permute-start(bf16[2,16,2048]{2,1,0:T(8,128)(2,1)S(1)} %join.2.refs_0_), channel_id=1, source_target_pairs={{0,2},{1,3},{2,0},{3,1},{4,6},{5,7},{6,4},{7,5},{8,10},{9,11},{10,... | collective-permute-start | bytes 393224 | tf_op jit(solution)/shard_map/ppermute | solution.py:165
  30.8 4.3 %collective-permute-start.2 = (bf16[16,2048]{1,0:T(8,128)(2,1)S(1)}, bf16[16,2048]{1,0:T(8,128)(2,1)S(1)}, u32[]{:S(2)}, u32[]{:S(2)}) collective-permute-start(bf16[16,2048]{1,0:T(8,128)(2,1)S(1)} %collective-permute-done.first_ref), channel_id=1, source_target_pairs={{0,1},{1,0},{2,3},{3,2},{4,5},{5,4},{6,7},{7,6},{8,9},{9,8},{10,11... | collective-permute-start | bytes 196616 | tf_op jit(solution)/shard_map/ppermute | solution.py:165
  35.0 5.0 %collective-permute-start.3 = (bf16[2,16,2048]{2,1,0:T(8,128)(2,1)S(1)}, bf16[2,16,2048]{2,1,0:T(8,128)(2,1)S(1)}, u32[]{:S(2)}, u32[]{:S(2)}) collective-permute-start(bf16[2,16,2048]{2,1,0:T(8,128)(2,1)S(1)} %join.3.refs_0_), channel_id=1, source_target_pairs={{0,2},{1,3},{2,0},{3,1},{4,6},{5,7},{6,4},{7,5},{8,10},{9,11},{10,... | collective-permute-start | bytes 393224 | tf_op jit(solution)/shard_map/ppermute | solution.py:165
  52.1 1.2 %collective-permute-start.5 = (f32[8,2,768]{2,1,0:T(2,128)S(1)}, f32[8,2,768]{2,1,0:T(2,128)S(1)}, u32[]{:S(2)}, u32[]{:S(2)}) collective-permute-start(f32[8,2,768]{2,1,0:T(2,128)S(1)} %all_to_all.11.own_ref), channel_id=1, source_target_pairs={{0,8},{8,0},{1,9},{9,1},{2,10},{10,2},{3,11},{11,3},{4,12},{12,4},... | collective-permute-start | bytes 147464 | tf_op jit(solution)/shard_map/ppermute | solution.py:168

commit v18 on v14

--- a/solution.py
+++ b/solution.py
@@ -89,13 +89,13 @@
 
 
 def over_columns(width, body):
-    tile = 256
+    tile = 512
 
     def step(i, carry):
         body(pl.ds(pl.multiple_of(i * tile, tile), tile))
         return carry
 
-    lax.fori_loop(0, width // tile, step, 0, unroll=8)
+    lax.fori_loop(0, width // tile, step, 0, unroll=4)
 
 
 def gate_kernel(rows_ref, w_ref, out_ref):

time: 52.8 us -> 52.8 us (level)
  no operation moved by 1% of the time
where the time goes in v18:
time: 52.8 us; the launch traced here: 52.6 us
  blocking collectives  25.9 us (49%)
  Pallas kernels  15.7 us (30%)
  starting transfers between devices  5.84 us (11%)
  waiting for transfers between devices  4.93 us (9%)
    all_to_all x1, blocking collectives, local_direct(): lax.all_to_all(sends, ('expert', 'tile'), split_axis=0, concat_axis=0, ti...  16.4 us
    all_to_all x1, blocking collectives, local_direct(): lax.all_to_all(result, 'tile', split_axis=0, concat_axis=0, tiled=True)  9.5 us
    pallas_call x5, Pallas kernels, down(): call(functools.partial(down_kernel, steps, first, last), 'down', out, [VM...  7.25 us
    ppermute x7, starting transfers between devices, swap(): return lax.ppermute(x, 'tile', [(t, t ^ bit) for t in range(tiles)])  5.84 us
    ppermute x7, waiting for transfers between devices, swap(): return lax.ppermute(x, 'tile', [(t, t ^ bit) for t in range(tiles)])  3.71 us
    pallas_call x1, Pallas kernels, local_direct(): call(hidden_kernel, 'hidden', bf16(slots, width), [VMEM] * 3, 4 * MIB, 0....  3.37 us
    pallas_call x1, Pallas kernels, local_direct(): call(gate_kernel, 'gate', f32(slots, width), [VMEM] * 2, 4 * MIB, 0.0)  3.34 us
    ppermute x1, waiting for transfers between devices, to_core(): return lax.ppermute(x, 'expert', [(0, 1), (1, 0)])  1.23 us
  transfers between devices with their start and end apart: 8, of which 3 were waited for; matrix products, arithmetic and copies ran while one was open for 0% of the time, Pallas kernels for 12%

profile of v18, /device:TPU:0, one launch (start us, length us, event | category | flops | bytes accessed | tf_op | source)
XLA Modules:
  0.0 52.6 jit_solution(3242305444926757988)
XLA Ops:
  0.0 0.0 copy-start.1
  0.0 1.0 %dispatch.1 = (bf16[16,2,3072]{2,1,0:T(2,128)(2,1)S(1)}, f32[6,4,128]{2,1,0:T(4,128)S(1)}) custom-call(bf16[4,3072]{1,0:T(4,128)(2,1)} %tokens_hbm.1, s32[2,4]{1,0:T(2,128)} %bitcast.2, f32[2,4]{1,0:T(2,128)} %bitcast.3), custom_call_target="tpu_custom_call" | custom-call | flops 599999971328 | tf_op jit(solution)/shard_map/dispatch/pallas_call | solution.py:168
  1.0 0.0 copy-start.2
  1.0 16.4 %all_to_all.10.blocks_ref = bf16[16,2,3072]{2,1,0:T(2,128)(2,1)S(1)} all-to-all(bf16[16,2,3072]{2,1,0:T(2,128)(2,1)S(1)} %get-tuple-element.13), channel_id=1, replica_groups=mesh['group'=2,'expert'=2,'tile'=8] {'expert','tile'}, dimensions={0} | all-to-all | bytes 393216 | tf_op jit(solution)/shard_map/all_to_all | solution.py:178
  17.5 0.0 copy-done.1
  17.5 3.3 %gate.1.gate_ref = f32[16,2048]{1,0:T(8,128)S(1)} custom-call(bf16[32,3072]{1,0:T(8,128)(2,1)S(1)} %merge.1.rows_ref, bf16[1,6144,2048]{2,1,0:T(8,128)(2,1)S(1)} %copy-done.1), custom_call_target="tpu_custom_call" | custom-call | tf_op jit(solution)/shard_map/gate/pallas_call | solution.py:180
  20.9 0.0 copy-done.2
  20.9 3.4 %hidden.1.refs_0_ = bf16[16,2048]{1,0:T(8,128)(2,1)S(1)} custom-call(bf16[32,3072]{1,0:T(8,128)(2,1)S(1)} %merge.1.rows_ref, bf16[1,6144,2048]{2,1,0:T(8,128)(2,1)S(1)} %copy-done.2, f32[16,2048]{1,0:T(8,128)S(1)} %gate.1.gate_ref), custom_call_target="tpu_custom_call" | custom-call | flops 199999995904 | tf_op jit(solution)/shard_map/hidden/pallas_call | solution.py:181
  24.2 0.7 %collective-permute-start = (bf16[16,2048]{1,0:T(8,128)(2,1)S(1)}, bf16[16,2048]{1,0:T(8,128)(2,1)S(1)}, u32[]{:S(2)}, u32[]{:S(2)}) collective-permute-start(bf16[16,2048]{1,0:T(8,128)(2,1)S(1)} %hidden.1.refs_0_), channel_id=1, source_target_pairs={{0,2},{1,3},{2,0},{3,1},{4,6},{5,7},{6,4},{7,5},{8,10},{9,11},{10,... | collective-permute-start | bytes 196616 | tf_op jit(solution)/shard_map/ppermute | solution.py:161
  24.9 0.6 %collective-permute-start.1 = (bf16[16,2048]{1,0:T(8,128)(2,1)S(1)}, bf16[16,2048]{1,0:T(8,128)(2,1)S(1)}, u32[]{:S(2)}, u32[]{:S(2)}) collective-permute-start(bf16[16,2048]{1,0:T(8,128)(2,1)S(1)} %hidden.1.refs_0_), channel_id=1, source_target_pairs={{0,1},{1,0},{2,3},{3,2},{4,5},{5,4},{6,7},{7,6},{8,9},{9,8},{10,11... | collective-permute-start | bytes 196616 | tf_op jit(solution)/shard_map/ppermute | solution.py:161
  25.5 0.9 %collective-permute-start.2 = (bf16[16,2048]{1,0:T(8,128)(2,1)S(1)}, bf16[16,2048]{1,0:T(8,128)(2,1)S(1)}, u32[]{:S(2)}, u32[]{:S(2)}) collective-permute-start(bf16[16,2048]{1,0:T(8,128)(2,1)S(1)} %hidden.1.refs_0_), channel_id=1, source_target_pairs={{0,4},{1,5},{2,6},{3,7},{4,0},{5,1},{6,2},{7,3},{8,12},{9,13},{10,... | collective-permute-start | bytes 196616 | tf_op jit(solution)/shard_map/ppermute | solution.py:161
  26.3 2.9 %collective-permute-done.refs_0_ = bf16[16,2048]{1,0:T(8,128)(2,1)S(1)} collective-permute-done((bf16[16,2048]{1,0:T(8,128)(2,1)S(1)}, bf16[16,2048]{1,0:T(8,128)(2,1)S(1)}, u32[]{:S(2)}, u32[]{:S(2)}) %collective-permute-start) | collective-permute-done | bytes 65568 | tf_op jit(solution)/shard_map/ppermute | solution.py:161
  29.2 0.0 collective-permute-start.3
  29.2 0.0 collective-permute-done.1.refs_1_
  29.2 0.0 copy-done
  29.2 1.8 %down.5.refs_3_ = f32[768,16]{1,0:T(8,128)S(1)} custom-call(bf16[16,2048]{1,0:T(8,128)(2,1)S(1)} %hidden.1.refs_0_, bf16[16,2048]{1,0:T(8,128)(2,1)S(1)} %collective-permute-done.1.refs_1_, bf16[1,768,16384]{2,1,0:T(8,128)(2,1)S(1)} %copy-done), custom_call_target="tpu_custom_call" | custom-call | tf_op jit(solution)/shard_map/down/pallas_call | solution.py:186
  31.0 0.0 collective-permute-done.2.refs_0_
  31.0 1.6 %collective-permute-start.4 = (bf16[16,2048]{1,0:T(8,128)(2,1)S(1)}, bf16[16,2048]{1,0:T(8,128)(2,1)S(1)}, u32[]{:S(2)}, u32[]{:S(2)}) collective-permute-start(bf16[16,2048]{1,0:T(8,128)(2,1)S(1)} %collective-permute-done.2.refs_0_), channel_id=1, source_target_pairs={{0,2},{1,3},{2,0},{3,1},{4,6},{5,7},{6,4},{7,5},{8,10},{9,11},{10,... | collective-permute-start | bytes 196616 | tf_op jit(solution)/shard_map/ppermute | solution.py:161
  32.6 0.8 %collective-permute-done.3.refs_1_ = bf16[16,2048]{1,0:T(8,128)(2,1)S(1)} collective-permute-done((bf16[16,2048]{1,0:T(8,128)(2,1)S(1)}, bf16[16,2048]{1,0:T(8,128)(2,1)S(1)}, u32[]{:S(2)}, u32[]{:S(2)}) %collective-permute-start.3) | collective-permute-done | bytes 65568 | tf_op jit(solution)/shard_map/ppermute | solution.py:161
  33.5 0.3 collective-permute-start.6
  33.8 1.8 %down.6.refs_3_ = f32[768,16]{1,0:T(8,128)S(1)} custom-call(bf16[16,2048]{1,0:T(8,128)(2,1)S(1)} %collective-permute-done.refs_0_, bf16[16,2048]{1,0:T(8,128)(2,1)S(1)} %collective-permute-done.3.refs_1_, bf16[1,768,16384]{2,1,0:T(8,128)(2,1)S(1)} %copy-done, f32[768,16]{1,0:T(8,128)S(1)} %down.5.refs_3_), custom_call_target="tpu_custom_call" | custom-call | tf_op jit(solution)/shard_map/down/pallas_call | solution.py:186
  35.5 0.0 collective-permute-done.4.refs_1_
  35.6 1.8 %collective-permute-start.5 = (bf16[16,2048]{1,0:T(8,128)(2,1)S(1)}, bf16[16,2048]{1,0:T(8,128)(2,1)S(1)}, u32[]{:S(2)}, u32[]{:S(2)}) collective-permute-start(bf16[16,2048]{1,0:T(8,128)(2,1)S(1)} %collective-permute-done.4.refs_1_), channel_id=1, source_target_pairs={{0,1},{1,0},{2,3},{3,2},{4,5},{5,4},{6,7},{7,6},{8,9},{9,8},{10,11... | collective-permute-start | bytes 196616 | tf_op jit(solution)/shard_map/ppermute | solution.py:161
  37.3 1.8 %down.7.refs_2_ = f32[768,16]{1,0:T(8,128)S(1)} custom-call(bf16[16,2048]{1,0:T(8,128)(2,1)S(1)} %collective-permute-done.2.refs_0_, bf16[16,2048]{1,0:T(8,128)(2,1)S(1)} %collective-permute-done.4.refs_1_, bf16[1,768,16384]{2,1,0:T(8,128)(2,1)S(1)} %copy-done, f32[768,16]{1,0:T(8,128)S(1)} %down.6.refs_3_), custom_call_target="tpu_custom_call" | custom-call | tf_op jit(solution)/shard_map/down/pallas_call | solution.py:186
  39.1 0.0 collective-permute-done.6.refs_0_
  39.1 1.0 %down.8.refs_2_ = f32[768,16]{1,0:T(8,128)S(1)} custom-call(bf16[16,2048]{1,0:T(8,128)(2,1)S(1)} %collective-permute-done.6.refs_0_, bf16[1,768,16384]{2,1,0:T(8,128)(2,1)S(1)} %copy-done, f32[768,16]{1,0:T(8,128)S(1)} %down.7.refs_2_), custom_call_target="tpu_custom_call" | custom-call | tf_op jit(solution)/shard_map/down/pallas_call | solution.py:186
  40.1 0.0 collective-permute-done.5.refs_0_
  40.1 1.0 %down.9 = f32[8,2,768]{2,1,0:T(2,128)S(1)} custom-call(bf16[16,2048]{1,0:T(8,128)(2,1)S(1)} %collective-permute-done.5.refs_0_, bf16[1,768,16384]{2,1,0:T(8,128)(2,1)S(1)} %copy-done, f32[768,16]{1,0:T(8,128)S(1)} %down.8.refs_2_), custom_call_target="tpu_custom_call" | custom-call | tf_op jit(solution)/shard_map/down/pallas_call | solution.py:186
  41.1 9.5 %all_to_all.11.own_ref = f32[8,2,768]{2,1,0:T(2,128)S(1)} all-to-all(f32[8,2,768]{2,1,0:T(2,128)S(1)} %down.9), channel_id=1, replica_groups=mesh['group'=2,'expert'=2,'tile'=8] {'tile'}, dimensions={0} | all-to-all | bytes 98304 | tf_op jit(solution)/shard_map/all_to_all | solution.py:206
  50.6 0.0 collective-permute-start.7
  50.6 1.2 %collective-permute-done.7.other_ref = f32[8,2,768]{2,1,0:T(2,128)S(1)} collective-permute-done((f32[8,2,768]{2,1,0:T(2,128)S(1)}, f32[8,2,768]{2,1,0:T(2,128)S(1)}, u32[]{:S(2)}, u32[]{:S(2)}) %collective-permute-start.7) | collective-permute-done | bytes 49184 | tf_op jit(solution)/shard_map/ppermute | solution.py:164
  51.8 0.7 %combine.1 = bf16[4,3072]{1,0:T(4,128)(2,1)} custom-call(f32[8,2,768]{2,1,0:T(2,128)S(1)} %all_to_all.11.own_ref, f32[8,2,768]{2,1,0:T(2,128)S(1)} %collective-permute-done.7.other_ref, f32[6,4,128]{2,1,0:T(4,128)S(1)} %get-tuple-element.20.table_ref), custom_call_target="tpu_custom_call" | custom-call | tf_op jit(solution)/shard_map/combine/pallas_call | solution.py:207
  (2 shorter events, 0.0 us)
Async XLA Ops:
  0.0 17.5 %copy-start.1 = (bf16[1,6144,2048]{2,1,0:T(8,128)(2,1)S(1)}, bf16[1,6144,2048]{2,1,0:T(8,128)(2,1)}, u32[]{:S(2)}) copy-start(bf16[1,6144,2048]{2,1,0:T(8,128)(2,1)} %w_ref.2) | copy-start | bytes 75497472
  1.0 19.8 %copy-start.2 = (bf16[1,6144,2048]{2,1,0:T(8,128)(2,1)S(1)}, bf16[1,6144,2048]{2,1,0:T(8,128)(2,1)}, u32[]{:S(2)}) copy-start(bf16[1,6144,2048]{2,1,0:T(8,128)(2,1)} %w_ref.3) | copy-start | bytes 75497472
  20.9 8.4 %copy-start = (bf16[1,768,16384]{2,1,0:T(8,128)(2,1)S(1)}, bf16[1,768,16384]{2,1,0:T(8,128)(2,1)}, u32[]{:S(2)}) copy-start(bf16[1,768,16384]{2,1,0:T(8,128)(2,1)} %refs_1_.3) | copy-start | bytes 75497472
  24.2 5.0 %collective-permute-start = (bf16[16,2048]{1,0:T(8,128)(2,1)S(1)}, bf16[16,2048]{1,0:T(8,128)(2,1)S(1)}, u32[]{:S(2)}, u32[]{:S(2)}) collective-permute-start(bf16[16,2048]{1,0:T(8,128)(2,1)S(1)} %hidden.1.refs_0_), channel_id=1, source_target_pairs={{0,2},{1,3},{2,0},{3,1},{4,6},{5,7},{6,4},{7,5},{8,10},{9,11},{10,... | collective-permute-start | bytes 196616 | tf_op jit(solution)/shard_map/ppermute | solution.py:161
  24.9 4.3 %collective-permute-start.1 = (bf16[16,2048]{1,0:T(8,128)(2,1)S(1)}, bf16[16,2048]{1,0:T(8,128)(2,1)S(1)}, u32[]{:S(2)}, u32[]{:S(2)}) collective-permute-start(bf16[16,2048]{1,0:T(8,128)(2,1)S(1)} %hidden.1.refs_0_), channel_id=1, source_target_pairs={{0,1},{1,0},{2,3},{3,2},{4,5},{5,4},{6,7},{7,6},{8,9},{9,8},{10,11... | collective-permute-start | bytes 196616 | tf_op jit(solution)/shard_map/ppermute | solution.py:161
  25.5 5.5 %collective-permute-start.2 = (bf16[16,2048]{1,0:T(8,128)(2,1)S(1)}, bf16[16,2048]{1,0:T(8,128)(2,1)S(1)}, u32[]{:S(2)}, u32[]{:S(2)}) collective-permute-start(bf16[16,2048]{1,0:T(8,128)(2,1)S(1)} %hidden.1.refs_0_), channel_id=1, source_target_pairs={{0,4},{1,5},{2,6},{3,7},{4,0},{5,1},{6,2},{7,3},{8,12},{9,13},{10,... | collective-permute-start | bytes 196616 | tf_op jit(solution)/shard_map/ppermute | solution.py:161
  29.2 4.3 %collective-permute-start.3 = (bf16[16,2048]{1,0:T(8,128)(2,1)S(1)}, bf16[16,2048]{1,0:T(8,128)(2,1)S(1)}, u32[]{:S(2)}, u32[]{:S(2)}) collective-permute-start(bf16[16,2048]{1,0:T(8,128)(2,1)S(1)} %collective-permute-done.refs_0_), channel_id=1, source_target_pairs={{0,1},{1,0},{2,3},{3,2},{4,5},{5,4},{6,7},{7,6},{8,9},{9,8},{10,11... | collective-permute-start | bytes 196616 | tf_op jit(solution)/shard_map/ppermute | solution.py:161
  31.0 4.5 %collective-permute-start.4 = (bf16[16,2048]{1,0:T(8,128)(2,1)S(1)}, bf16[16,2048]{1,0:T(8,128)(2,1)S(1)}, u32[]{:S(2)}, u32[]{:S(2)}) collective-permute-start(bf16[16,2048]{1,0:T(8,128)(2,1)S(1)} %collective-permute-done.2.refs_0_), channel_id=1, source_target_pairs={{0,2},{1,3},{2,0},{3,1},{4,6},{5,7},{6,4},{7,5},{8,10},{9,11},{10,... | collective-permute-start | bytes 196616 | tf_op jit(solution)/shard_map/ppermute | solution.py:161
  33.5 5.6 %collective-permute-start.6 = (bf16[16,2048]{1,0:T(8,128)(2,1)S(1)}, bf16[16,2048]{1,0:T(8,128)(2,1)S(1)}, u32[]{:S(2)}, u32[]{:S(2)}) collective-permute-start(bf16[16,2048]{1,0:T(8,128)(2,1)S(1)} %collective-permute-done.2.refs_0_), channel_id=1, source_target_pairs={{0,1},{1,0},{2,3},{3,2},{4,5},{5,4},{6,7},{7,6},{8,9},{9,8},{10,11... | collective-permute-start | bytes 196616 | tf_op jit(solution)/shard_map/ppermute | solution.py:161
  35.6 4.5 %collective-permute-start.5 = (bf16[16,2048]{1,0:T(8,128)(2,1)S(1)}, bf16[16,2048]{1,0:T(8,128)(2,1)S(1)}, u32[]{:S(2)}, u32[]{:S(2)}) collective-permute-start(bf16[16,2048]{1,0:T(8,128)(2,1)S(1)} %collective-permute-done.4.refs_1_), channel_id=1, source_target_pairs={{0,1},{1,0},{2,3},{3,2},{4,5},{5,4},{6,7},{7,6},{8,9},{9,8},{10,11... | collective-permute-start | bytes 196616 | tf_op jit(solution)/shard_map/ppermute | solution.py:161
  50.6 1.2 %collective-permute-start.7 = (f32[8,2,768]{2,1,0:T(2,128)S(1)}, f32[8,2,768]{2,1,0:T(2,128)S(1)}, u32[]{:S(2)}, u32[]{:S(2)}) collective-permute-start(f32[8,2,768]{2,1,0:T(2,128)S(1)} %all_to_all.11.own_ref), channel_id=1, source_target_pairs={{0,8},{8,0},{1,9},{9,1},{2,10},{10,2},{3,11},{11,3},{4,12},{12,4},... | collective-permute-start | bytes 147464 | tf_op jit(solution)/shard_map/ppermute | solution.py:164

commit v19 on v18

--- a/solution.py
+++ b/solution.py
@@ -189,18 +189,16 @@
         )(*(block[k] for k in steps), in_vmem(w_down), *(() if first else (total,)))
 
     block = {0: hidden}
-    for k in (4, 2, 1):
+    for k in (2, 1, 4, 6):
         block[k] = swap(hidden, k)
     block[3] = swap(block[2], 1)
     total = down(None, [0, 1], block, False)
     total, block[4] = lax.optimization_barrier((total, block[4]))
-    block[6] = swap(block[4], 2)
-    block[4], block[3] = lax.optimization_barrier((block[4], block[3]))
     block[5] = swap(block[4], 1)
-    total = down(total, [2, 3], block, False)
-    total, block[6] = lax.optimization_barrier((total, block[6]))
+    total = down(total, [2, 4], block, False)
+    total, block[6], block[3] = lax.optimization_barrier((total, block[6], block[3]))
     block[7] = swap(block[6], 1)
-    total = down(total, [4, 6], block, False)
+    total = down(total, [3, 6], block, False)
     total = down(total, [5], block, False)
     result = down(total, [7], block, True)
     back = lax.all_to_all(result, "tile", split_axis=0, concat_axis=0, tiled=True)

time: 52.8 us -> 53 us (level)
  starting transfers between devices: 5.84 us -> 8.5 us
  waiting for transfers between devices: 4.93 us -> 2.82 us
    ppermute x7, starting transfers between devices: 5.84 us -> 8.5 us  [swap(): return lax.ppermute(x, 'tile', [(t, t ^ bit) for t in range(tiles)])]
    ppermute x7, waiting for transfers between devices: 3.71 us -> 1.6 us  [swap(): return lax.ppermute(x, 'tile', [(t, t ^ bit) for t in range(tiles)])]
where the time goes in v19:
time: 53 us; the launch traced here: 52.8 us
  blocking collectives  25.6 us (48%)
  Pallas kernels  15.7 us (30%)
  starting transfers between devices  8.5 us (16%)
  waiting for transfers between devices  2.82 us (5%)
    all_to_all x1, blocking collectives, local_direct(): lax.all_to_all(sends, ('expert', 'tile'), split_axis=0, concat_axis=0, ti...  16.4 us
    all_to_all x1, blocking collectives, local_direct(): lax.all_to_all(result, 'tile', split_axis=0, concat_axis=0, tiled=True)  9.17 us
    ppermute x7, starting transfers between devices, swap(): return lax.ppermute(x, 'tile', [(t, t ^ bit) for t in range(tiles)])  8.5 us
    pallas_call x5, Pallas kernels, down(): call(functools.partial(down_kernel, steps, first, last), 'down', out, [VM...  7.24 us
    pallas_call x1, Pallas kernels, local_direct(): call(hidden_kernel, 'hidden', bf16(slots, width), [VMEM] * 3, 4 * MIB, 0....  3.37 us
    pallas_call x1, Pallas kernels, local_direct(): call(gate_kernel, 'gate', f32(slots, width), [VMEM] * 2, 4 * MIB, 0.0)  3.34 us
    ppermute x7, waiting for transfers between devices, swap(): return lax.ppermute(x, 'tile', [(t, t ^ bit) for t in range(tiles)])  1.6 us
    ppermute x1, waiting for transfers between devices, to_core(): return lax.ppermute(x, 'expert', [(0, 1), (1, 0)])  1.23 us
  transfers between devices with their start and end apart: 8, of which 3 were waited for; matrix products, arithmetic and copies ran while one was open for 0% of the time, Pallas kernels for 12%

profile of v19, /device:TPU:0, one launch (start us, length us, event | category | flops | bytes accessed | tf_op | source)
XLA Modules:
  0.0 52.8 jit_solution(3731457330949117655)
XLA Ops:
  0.0 0.0 copy-start.1
  0.0 1.0 %dispatch.1 = (bf16[16,2,3072]{2,1,0:T(2,128)(2,1)S(1)}, f32[6,4,128]{2,1,0:T(4,128)S(1)}) custom-call(bf16[4,3072]{1,0:T(4,128)(2,1)} %tokens_hbm.1, s32[2,4]{1,0:T(2,128)} %bitcast.2, f32[2,4]{1,0:T(2,128)} %bitcast.3), custom_call_target="tpu_custom_call" | custom-call | flops 599999971328 | tf_op jit(solution)/shard_map/dispatch/pallas_call | solution.py:168
  1.0 0.0 copy-start.2
  1.0 16.4 %all_to_all.10.blocks_ref = bf16[16,2,3072]{2,1,0:T(2,128)(2,1)S(1)} all-to-all(bf16[16,2,3072]{2,1,0:T(2,128)(2,1)S(1)} %get-tuple-element.12), channel_id=1, replica_groups=mesh['group'=2,'expert'=2,'tile'=8] {'expert','tile'}, dimensions={0} | all-to-all | bytes 393216 | tf_op jit(solution)/shard_map/all_to_all | solution.py:178
  17.5 0.0 copy-done.1
  17.5 3.3 %gate.1.gate_ref = f32[16,2048]{1,0:T(8,128)S(1)} custom-call(bf16[32,3072]{1,0:T(8,128)(2,1)S(1)} %merge.1.rows_ref, bf16[1,6144,2048]{2,1,0:T(8,128)(2,1)S(1)} %copy-done.1), custom_call_target="tpu_custom_call" | custom-call | tf_op jit(solution)/shard_map/gate/pallas_call | solution.py:180
  20.9 0.0 copy-done.2
  20.9 3.4 %hidden.1.refs_0_ = bf16[16,2048]{1,0:T(8,128)(2,1)S(1)} custom-call(bf16[32,3072]{1,0:T(8,128)(2,1)S(1)} %merge.1.rows_ref, bf16[1,6144,2048]{2,1,0:T(8,128)(2,1)S(1)} %copy-done.2, f32[16,2048]{1,0:T(8,128)S(1)} %gate.1.gate_ref), custom_call_target="tpu_custom_call" | custom-call | flops 199999995904 | tf_op jit(solution)/shard_map/hidden/pallas_call | solution.py:181
  24.2 0.7 %collective-permute-start = (bf16[16,2048]{1,0:T(8,128)(2,1)S(1)}, bf16[16,2048]{1,0:T(8,128)(2,1)S(1)}, u32[]{:S(2)}, u32[]{:S(2)}) collective-permute-start(bf16[16,2048]{1,0:T(8,128)(2,1)S(1)} %hidden.1.refs_0_), channel_id=1, source_target_pairs={{0,2},{1,3},{2,0},{3,1},{4,6},{5,7},{6,4},{7,5},{8,10},{9,11},{10,... | collective-permute-start | bytes 196616 | tf_op jit(solution)/shard_map/ppermute | solution.py:161
  24.9 0.6 %collective-permute-start.1 = (bf16[16,2048]{1,0:T(8,128)(2,1)S(1)}, bf16[16,2048]{1,0:T(8,128)(2,1)S(1)}, u32[]{:S(2)}, u32[]{:S(2)}) collective-permute-start(bf16[16,2048]{1,0:T(8,128)(2,1)S(1)} %hidden.1.refs_0_), channel_id=1, source_target_pairs={{0,1},{1,0},{2,3},{3,2},{4,5},{5,4},{6,7},{7,6},{8,9},{9,8},{10,11... | collective-permute-start | bytes 196616 | tf_op jit(solution)/shard_map/ppermute | solution.py:161
  25.5 0.9 %collective-permute-start.2 = (bf16[16,2048]{1,0:T(8,128)(2,1)S(1)}, bf16[16,2048]{1,0:T(8,128)(2,1)S(1)}, u32[]{:S(2)}, u32[]{:S(2)}) collective-permute-start(bf16[16,2048]{1,0:T(8,128)(2,1)S(1)} %hidden.1.refs_0_), channel_id=1, source_target_pairs={{0,4},{1,5},{2,6},{3,7},{4,0},{5,1},{6,2},{7,3},{8,12},{9,13},{10,... | collective-permute-start | bytes 196616 | tf_op jit(solution)/shard_map/ppermute | solution.py:161
  26.3 2.8 %collective-permute-start.3 = (bf16[16,2048]{1,0:T(8,128)(2,1)S(1)}, bf16[16,2048]{1,0:T(8,128)(2,1)S(1)}, u32[]{:S(2)}, u32[]{:S(2)}) collective-permute-start(bf16[16,2048]{1,0:T(8,128)(2,1)S(1)} %hidden.1.refs_0_), channel_id=1, source_target_pairs={{0,6},{1,7},{2,4},{3,5},{4,2},{5,3},{6,0},{7,1},{8,14},{9,15},{10,... | collective-permute-start | bytes 196616 | tf_op jit(solution)/shard_map/ppermute | solution.py:161
  29.2 0.0 collective-permute-done.refs_0_
  29.2 1.4 %collective-permute-start.4 = (bf16[16,2048]{1,0:T(8,128)(2,1)S(1)}, bf16[16,2048]{1,0:T(8,128)(2,1)S(1)}, u32[]{:S(2)}, u32[]{:S(2)}) collective-permute-start(bf16[16,2048]{1,0:T(8,128)(2,1)S(1)} %collective-permute-done.refs_0_), channel_id=1, source_target_pairs={{0,1},{1,0},{2,3},{3,2},{4,5},{5,4},{6,7},{7,6},{8,9},{9,8},{10,11... | collective-permute-start | bytes 196616 | tf_op jit(solution)/shard_map/ppermute | solution.py:161
  30.7 0.0 collective-permute-done.1.refs_1_
  30.7 0.0 copy-done
  30.7 1.8 %down.5.refs_3_ = f32[768,16]{1,0:T(8,128)S(1)} custom-call(bf16[16,2048]{1,0:T(8,128)(2,1)S(1)} %hidden.1.refs_0_, bf16[16,2048]{1,0:T(8,128)(2,1)S(1)} %collective-permute-done.1.refs_1_, bf16[1,768,16384]{2,1,0:T(8,128)(2,1)S(1)} %copy-done), custom_call_target="tpu_custom_call" | custom-call | tf_op jit(solution)/shard_map/down/pallas_call | solution.py:186
  32.4 0.6 %collective-permute-done.2.refs_1_ = bf16[16,2048]{1,0:T(8,128)(2,1)S(1)} collective-permute-done((bf16[16,2048]{1,0:T(8,128)(2,1)S(1)}, bf16[16,2048]{1,0:T(8,128)(2,1)S(1)}, u32[]{:S(2)}, u32[]{:S(2)}) %collective-permute-start.2) | collective-permute-done | bytes 65568 | tf_op jit(solution)/shard_map/ppermute | solution.py:161
  33.1 1.4 %collective-permute-start.6 = (bf16[16,2048]{1,0:T(8,128)(2,1)S(1)}, bf16[16,2048]{1,0:T(8,128)(2,1)S(1)}, u32[]{:S(2)}, u32[]{:S(2)}) collective-permute-start(bf16[16,2048]{1,0:T(8,128)(2,1)S(1)} %collective-permute-done.2.refs_1_), channel_id=1, source_target_pairs={{0,1},{1,0},{2,3},{3,2},{4,5},{5,4},{6,7},{7,6},{8,9},{9,8},{10,11... | collective-permute-start | bytes 196616 | tf_op jit(solution)/shard_map/ppermute | solution.py:161
  34.5 1.8 %down.6.refs_3_ = f32[768,16]{1,0:T(8,128)S(1)} custom-call(bf16[16,2048]{1,0:T(8,128)(2,1)S(1)} %collective-permute-done.refs_0_, bf16[16,2048]{1,0:T(8,128)(2,1)S(1)} %collective-permute-done.2.refs_1_, bf16[1,768,16384]{2,1,0:T(8,128)(2,1)S(1)} %copy-done, f32[768,16]{1,0:T(8,128)S(1)} %down.5.refs_3_), custom_call_target="tpu_custom_call" | custom-call | tf_op jit(solution)/shard_map/down/pallas_call | solution.py:186
  36.3 0.0 collective-permute-done.3.refs_1_
  36.3 0.0 collective-permute-done.4.refs_0_
  36.3 0.6 %collective-permute-start.5 = (bf16[16,2048]{1,0:T(8,128)(2,1)S(1)}, bf16[16,2048]{1,0:T(8,128)(2,1)S(1)}, u32[]{:S(2)}, u32[]{:S(2)}) collective-permute-start(bf16[16,2048]{1,0:T(8,128)(2,1)S(1)} %collective-permute-done.3.refs_1_), channel_id=1, source_target_pairs={{0,1},{1,0},{2,3},{3,2},{4,5},{5,4},{6,7},{7,6},{8,9},{9,8},{10,11... | collective-permute-start | bytes 196616 | tf_op jit(solution)/shard_map/ppermute | solution.py:161
  36.9 1.8 %down.7.refs_2_ = f32[768,16]{1,0:T(8,128)S(1)} custom-call(bf16[16,2048]{1,0:T(8,128)(2,1)S(1)} %collective-permute-done.4.refs_0_, bf16[16,2048]{1,0:T(8,128)(2,1)S(1)} %collective-permute-done.3.refs_1_, bf16[1,768,16384]{2,1,0:T(8,128)(2,1)S(1)} %copy-done, f32[768,16]{1,0:T(8,128)S(1)} %down.6.refs_3_), custom_call_target="tpu_custom_call" | custom-call | tf_op jit(solution)/shard_map/down/pallas_call | solution.py:186
  38.7 0.0 collective-permute-done.6.refs_0_
  38.7 1.0 %down.8.refs_2_ = f32[768,16]{1,0:T(8,128)S(1)} custom-call(bf16[16,2048]{1,0:T(8,128)(2,1)S(1)} %collective-permute-done.6.refs_0_, bf16[1,768,16384]{2,1,0:T(8,128)(2,1)S(1)} %copy-done, f32[768,16]{1,0:T(8,128)S(1)} %down.7.refs_2_), custom_call_target="tpu_custom_call" | custom-call | tf_op jit(solution)/shard_map/down/pallas_call | solution.py:186
  39.7 0.9 %collective-permute-done.5.refs_0_ = bf16[16,2048]{1,0:T(8,128)(2,1)S(1)} collective-permute-done((bf16[16,2048]{1,0:T(8,128)(2,1)S(1)}, bf16[16,2048]{1,0:T(8,128)(2,1)S(1)}, u32[]{:S(2)}, u32[]{:S(2)}) %collective-permute-start.5) | collective-permute-done | bytes 65568 | tf_op jit(solution)/shard_map/ppermute | solution.py:161
  40.6 1.0 %down.9 = f32[8,2,768]{2,1,0:T(2,128)S(1)} custom-call(bf16[16,2048]{1,0:T(8,128)(2,1)S(1)} %collective-permute-done.5.refs_0_, bf16[1,768,16384]{2,1,0:T(8,128)(2,1)S(1)} %copy-done, f32[768,16]{1,0:T(8,128)S(1)} %down.8.refs_2_), custom_call_target="tpu_custom_call" | custom-call | tf_op jit(solution)/shard_map/down/pallas_call | solution.py:186
  41.6 9.2 %all_to_all.11.own_ref = f32[8,2,768]{2,1,0:T(2,128)S(1)} all-to-all(f32[8,2,768]{2,1,0:T(2,128)S(1)} %down.9), channel_id=1, replica_groups=mesh['group'=2,'expert'=2,'tile'=8] {'tile'}, dimensions={0} | all-to-all | bytes 98304 | tf_op jit(solution)/shard_map/all_to_all | solution.py:204
  50.8 0.0 collective-permute-start.7
  50.8 1.2 %collective-permute-done.7.other_ref = f32[8,2,768]{2,1,0:T(2,128)S(1)} collective-permute-done((f32[8,2,768]{2,1,0:T(2,128)S(1)}, f32[8,2,768]{2,1,0:T(2,128)S(1)}, u32[]{:S(2)}, u32[]{:S(2)}) %collective-permute-start.7) | collective-permute-done | bytes 49184 | tf_op jit(solution)/shard_map/ppermute | solution.py:164
  52.0 0.7 %combine.1 = bf16[4,3072]{1,0:T(4,128)(2,1)} custom-call(f32[8,2,768]{2,1,0:T(2,128)S(1)} %all_to_all.11.own_ref, f32[8,2,768]{2,1,0:T(2,128)S(1)} %collective-permute-done.7.other_ref, f32[6,4,128]{2,1,0:T(4,128)S(1)} %get-tuple-element.18.table_ref), custom_call_target="tpu_custom_call" | custom-call | tf_op jit(solution)/shard_map/combine/pallas_call | solution.py:205
  (2 shorter events, 0.0 us)
Async XLA Ops:
  0.0 17.5 %copy-start.1 = (bf16[1,6144,2048]{2,1,0:T(8,128)(2,1)S(1)}, bf16[1,6144,2048]{2,1,0:T(8,128)(2,1)}, u32[]{:S(2)}) copy-start(bf16[1,6144,2048]{2,1,0:T(8,128)(2,1)} %w_ref.2) | copy-start | bytes 75497472
  1.0 19.8 %copy-start.2 = (bf16[1,6144,2048]{2,1,0:T(8,128)(2,1)S(1)}, bf16[1,6144,2048]{2,1,0:T(8,128)(2,1)}, u32[]{:S(2)}) copy-start(bf16[1,6144,2048]{2,1,0:T(8,128)(2,1)} %w_ref.3) | copy-start | bytes 75497472
  20.9 9.8 %copy-start = (bf16[1,768,16384]{2,1,0:T(8,128)(2,1)S(1)}, bf16[1,768,16384]{2,1,0:T(8,128)(2,1)}, u32[]{:S(2)}) copy-start(bf16[1,768,16384]{2,1,0:T(8,128)(2,1)} %refs_1_.3) | copy-start | bytes 75497472
  24.2 5.0 %collective-permute-start = (bf16[16,2048]{1,0:T(8,128)(2,1)S(1)}, bf16[16,2048]{1,0:T(8,128)(2,1)S(1)}, u32[]{:S(2)}, u32[]{:S(2)}) collective-permute-start(bf16[16,2048]{1,0:T(8,128)(2,1)S(1)} %hidden.1.refs_0_), channel_id=1, source_target_pairs={{0,2},{1,3},{2,0},{3,1},{4,6},{5,7},{6,4},{7,5},{8,10},{9,11},{10,... | collective-permute-start | bytes 196616 | tf_op jit(solution)/shard_map/ppermute | solution.py:161
  24.9 5.7 %collective-permute-start.1 = (bf16[16,2048]{1,0:T(8,128)(2,1)S(1)}, bf16[16,2048]{1,0:T(8,128)(2,1)S(1)}, u32[]{:S(2)}, u32[]{:S(2)}) collective-permute-start(bf16[16,2048]{1,0:T(8,128)(2,1)S(1)} %hidden.1.refs_0_), channel_id=1, source_target_pairs={{0,1},{1,0},{2,3},{3,2},{4,5},{5,4},{6,7},{7,6},{8,9},{9,8},{10,11... | collective-permute-start | bytes 196616 | tf_op jit(solution)/shard_map/ppermute | solution.py:161
  25.5 7.6 %collective-permute-start.2 = (bf16[16,2048]{1,0:T(8,128)(2,1)S(1)}, bf16[16,2048]{1,0:T(8,128)(2,1)S(1)}, u32[]{:S(2)}, u32[]{:S(2)}) collective-permute-start(bf16[16,2048]{1,0:T(8,128)(2,1)S(1)} %hidden.1.refs_0_), channel_id=1, source_target_pairs={{0,4},{1,5},{2,6},{3,7},{4,0},{5,1},{6,2},{7,3},{8,12},{9,13},{10,... | collective-permute-start | bytes 196616 | tf_op jit(solution)/shard_map/ppermute | solution.py:161
  26.3 9.9 %collective-permute-start.3 = (bf16[16,2048]{1,0:T(8,128)(2,1)S(1)}, bf16[16,2048]{1,0:T(8,128)(2,1)S(1)}, u32[]{:S(2)}, u32[]{:S(2)}) collective-permute-start(bf16[16,2048]{1,0:T(8,128)(2,1)S(1)} %hidden.1.refs_0_), channel_id=1, source_target_pairs={{0,6},{1,7},{2,4},{3,5},{4,2},{5,3},{6,0},{7,1},{8,14},{9,15},{10,... | collective-permute-start | bytes 196616 | tf_op jit(solution)/shard_map/ppermute | solution.py:161
  29.2 7.1 %collective-permute-start.4 = (bf16[16,2048]{1,0:T(8,128)(2,1)S(1)}, bf16[16,2048]{1,0:T(8,128)(2,1)S(1)}, u32[]{:S(2)}, u32[]{:S(2)}) collective-permute-start(bf16[16,2048]{1,0:T(8,128)(2,1)S(1)} %collective-permute-done.refs_0_), channel_id=1, source_target_pairs={{0,1},{1,0},{2,3},{3,2},{4,5},{5,4},{6,7},{7,6},{8,9},{9,8},{10,11... | collective-permute-start | bytes 196616 | tf_op jit(solution)/shard_map/ppermute | solution.py:161
  33.1 5.7 %collective-permute-start.6 = (bf16[16,2048]{1,0:T(8,128)(2,1)S(1)}, bf16[16,2048]{1,0:T(8,128)(2,1)S(1)}, u32[]{:S(2)}, u32[]{:S(2)}) collective-permute-start(bf16[16,2048]{1,0:T(8,128)(2,1)S(1)} %collective-permute-done.2.refs_1_), channel_id=1, source_target_pairs={{0,1},{1,0},{2,3},{3,2},{4,5},{5,4},{6,7},{7,6},{8,9},{9,8},{10,11... | collective-permute-start | bytes 196616 | tf_op jit(solution)/shard_map/ppermute | solution.py:161
  36.3 4.3 %collective-permute-start.5 = (bf16[16,2048]{1,0:T(8,128)(2,1)S(1)}, bf16[16,2048]{1,0:T(8,128)(2,1)S(1)}, u32[]{:S(2)}, u32[]{:S(2)}) collective-permute-start(bf16[16,2048]{1,0:T(8,128)(2,1)S(1)} %collective-permute-done.3.refs_1_), channel_id=1, source_target_pairs={{0,1},{1,0},{2,3},{3,2},{4,5},{5,4},{6,7},{7,6},{8,9},{9,8},{10,11... | collective-permute-start | bytes 196616 | tf_op jit(solution)/shard_map/ppermute | solution.py:161
  50.8 1.2 %collective-permute-start.7 = (f32[8,2,768]{2,1,0:T(2,128)S(1)}, f32[8,2,768]{2,1,0:T(2,128)S(1)}, u32[]{:S(2)}, u32[]{:S(2)}) collective-permute-start(f32[8,2,768]{2,1,0:T(2,128)S(1)} %all_to_all.11.own_ref), channel_id=1, source_target_pairs={{0,8},{8,0},{1,9},{9,1},{2,10},{10,2},{3,11},{11,3},{4,12},{12,4},... | collective-permute-start | bytes 147464 | tf_op jit(solution)/shard_map/ppermute | solution.py:164

commit v20 on v18

--- a/solution.py
+++ b/solution.py
@@ -130,20 +130,22 @@
         out_ref[...] = total
     else:
         total = total.T
-        for t in range(out_ref.shape[0]):
-            out_ref[t] = total[t * SLOTS:(t + 1) * SLOTS, :]
-
-
-def combine_kernel(own_ref, other_ref, table_ref, out_ref):
+        tiles = out_ref.shape[0] // 2
+        for t in range(tiles):
+            for e in range(2):
+                out_ref[e * tiles + t] = total[t * SLOTS:(t + 1) * SLOTS, :]
+
+
+def combine_kernel(back_ref, table_ref, out_ref):
     mine = lax.axis_index("expert")
-    halves, features = own_ref.shape[0] // 2, own_ref.shape[2]
+    tiles, features = back_ref.shape[0] // 2, back_ref.shape[2]
+    halves = tiles // 2
     weight = [table_ref[e * (1 + SLOTS)][:, :1] for e in range(2)]
     inside = [[table_ref[e * (1 + SLOTS) + 1 + c][:, :1] for c in range(SLOTS)] for e in range(2)]
     for i in range(halves):
-        own, other = own_ref[mine * halves + i], other_ref[mine * halves + i]
         mixed = jnp.zeros((out_ref.shape[0], features), jnp.float32)
         for e in range(2):
-            both = jnp.where(mine == e, own, other)
+            both = back_ref[e * tiles + mine * halves + i]
             for c in range(SLOTS):
                 value = (weight[e] * both[c:c + 1]).astype(jnp.bfloat16).astype(jnp.float32)
                 mixed = mixed + jnp.where(inside[e][c] != 0.0, value, 0.0)
@@ -159,9 +161,6 @@
 
     def swap(x, bit):
         return lax.ppermute(x, "tile", [(t, t ^ bit) for t in range(tiles)])
-
-    def to_core(x):
-        return lax.ppermute(x, "expert", [(0, 1), (1, 0)])
 
     f32 = lambda *shape: jax.ShapeDtypeStruct(shape, jnp.float32)
     bf16 = lambda *shape: jax.ShapeDtypeStruct(shape, jnp.bfloat16)
@@ -182,7 +181,7 @@
 
     def down(total, steps, block, last):
         first = total is None
-        out = f32(tiles, SLOTS, features) if last else f32(features, slots)
+        out = f32(2 * tiles, SLOTS, features) if last else f32(features, slots)
         return call(
             functools.partial(down_kernel, steps, first, last), "down", out,
             [VMEM] * (len(steps) + 2 - first), 10 * MIB, 0e-6,
@@ -203,8 +202,8 @@
     total = down(total, [4, 6], block, False)
     total = down(total, [5], block, False)
     result = down(total, [7], block, True)
-    back = lax.all_to_all(result, "tile", split_axis=0, concat_axis=0, tiled=True)
-    return call(combine_kernel, "combine", bf16(rows, half_width), [VMEM] * 3, 4 * MIB)(back, to_core(back), table)
+    back = lax.all_to_all(result, ("expert", "tile"), split_axis=0, concat_axis=0, tiled=True)
+    return call(combine_kernel, "combine", bf16(rows, half_width), [VMEM] * 2, 4 * MIB)(back, table)
 
 
 def local_gathered(tokens, routes, gates, w_gate, w_up, w_down):

time: 52.8 us -> 52.1 us (0.987)
  waiting for transfers between devices: 4.93 us -> 3.71 us
    ppermute x1 -> x0, waiting for transfers between devices: 1.23 us -> none  [to_core(): return lax.ppermute(x, 'expert', [(0, 1), (1, 0)])]
  transfers between devices with their start and end apart: 8 -> 7, of which waited for: 3 -> 2; matrix products, arithmetic and copies ran while one was open for 0% -> 0% of each run, Pallas kernels for 12% -> 12%
where the time goes in v20:
time: 52.1 us; the launch traced here: 51.9 us
  blocking collectives  26.4 us (51%)
  Pallas kernels  15.7 us (30%)
  starting transfers between devices  5.84 us (11%)
  waiting for transfers between devices  3.71 us (7%)
    all_to_all x1, blocking collectives, local_direct(): lax.all_to_all(sends, ('expert', 'tile'), split_axis=0, concat_axis=0, ti...  16.4 us
    all_to_all x1, blocking collectives, local_direct(): lax.all_to_all(result, ('expert', 'tile'), split_axis=0, concat_axis=0, t...  10 us
    pallas_call x5, Pallas kernels, down(): call(functools.partial(down_kernel, steps, first, last), 'down', out, [VM...  7.25 us
    ppermute x7, starting transfers between devices, swap(): return lax.ppermute(x, 'tile', [(t, t ^ bit) for t in range(tiles)])  5.84 us
    ppermute x7, waiting for transfers between devices, swap(): return lax.ppermute(x, 'tile', [(t, t ^ bit) for t in range(tiles)])  3.71 us
    pallas_call x1, Pallas kernels, local_direct(): call(hidden_kernel, 'hidden', bf16(slots, width), [VMEM] * 3, 4 * MIB, 0....  3.37 us
    pallas_call x1, Pallas kernels, local_direct(): call(gate_kernel, 'gate', f32(slots, width), [VMEM] * 2, 4 * MIB, 0.0)  3.34 us
  transfers between devices with their start and end apart: 7, of which 2 were waited for; matrix products, arithmetic and copies ran while one was open for 0% of the time, Pallas kernels for 12%

profile of v20, /device:TPU:0, one launch (start us, length us, event | category | flops | bytes accessed | tf_op | source)
XLA Modules:
  0.0 51.9 jit_solution(12827154857629284431)
XLA Ops:
  0.0 0.0 copy-start.1
  0.0 1.0 %dispatch.1 = (bf16[16,2,3072]{2,1,0:T(2,128)(2,1)S(1)}, f32[6,4,128]{2,1,0:T(4,128)S(1)}) custom-call(bf16[4,3072]{1,0:T(4,128)(2,1)} %tokens_hbm.1, s32[2,4]{1,0:T(2,128)} %bitcast.2, f32[2,4]{1,0:T(2,128)} %bitcast.3), custom_call_target="tpu_custom_call" | custom-call | flops 599999971328 | tf_op jit(solution)/shard_map/dispatch/pallas_call | solution.py:167
  1.0 0.0 copy-start.2
  1.0 16.4 %all_to_all.10.blocks_ref = bf16[16,2,3072]{2,1,0:T(2,128)(2,1)S(1)} all-to-all(bf16[16,2,3072]{2,1,0:T(2,128)(2,1)S(1)} %get-tuple-element.13), channel_id=1, replica_groups=mesh['group'=2,'expert'=2,'tile'=8] {'expert','tile'}, dimensions={0} | all-to-all | bytes 393216 | tf_op jit(solution)/shard_map/all_to_all | solution.py:177
  17.5 0.0 copy-done.1
  17.5 3.3 %gate.1.gate_ref = f32[16,2048]{1,0:T(8,128)S(1)} custom-call(bf16[32,3072]{1,0:T(8,128)(2,1)S(1)} %merge.1.rows_ref, bf16[1,6144,2048]{2,1,0:T(8,128)(2,1)S(1)} %copy-done.1), custom_call_target="tpu_custom_call" | custom-call | tf_op jit(solution)/shard_map/gate/pallas_call | solution.py:179
  20.9 0.0 copy-done.2
  20.9 0.0 copy-start
  20.9 3.4 %hidden.1.refs_0_ = bf16[16,2048]{1,0:T(8,128)(2,1)S(1)} custom-call(bf16[32,3072]{1,0:T(8,128)(2,1)S(1)} %merge.1.rows_ref, bf16[1,6144,2048]{2,1,0:T(8,128)(2,1)S(1)} %copy-done.2, f32[16,2048]{1,0:T(8,128)S(1)} %gate.1.gate_ref), custom_call_target="tpu_custom_call" | custom-call | flops 199999995904 | tf_op jit(solution)/shard_map/hidden/pallas_call | solution.py:180
  24.2 0.7 %collective-permute-start = (bf16[16,2048]{1,0:T(8,128)(2,1)S(1)}, bf16[16,2048]{1,0:T(8,128)(2,1)S(1)}, u32[]{:S(2)}, u32[]{:S(2)}) collective-permute-start(bf16[16,2048]{1,0:T(8,128)(2,1)S(1)} %hidden.1.refs_0_), channel_id=1, source_target_pairs={{0,2},{1,3},{2,0},{3,1},{4,6},{5,7},{6,4},{7,5},{8,10},{9,11},{10,... | collective-permute-start | bytes 196616 | tf_op jit(solution)/shard_map/ppermute | solution.py:163
  24.9 0.6 %collective-permute-start.1 = (bf16[16,2048]{1,0:T(8,128)(2,1)S(1)}, bf16[16,2048]{1,0:T(8,128)(2,1)S(1)}, u32[]{:S(2)}, u32[]{:S(2)}) collective-permute-start(bf16[16,2048]{1,0:T(8,128)(2,1)S(1)} %hidden.1.refs_0_), channel_id=1, source_target_pairs={{0,1},{1,0},{2,3},{3,2},{4,5},{5,4},{6,7},{7,6},{8,9},{9,8},{10,11... | collective-permute-start | bytes 196616 | tf_op jit(solution)/shard_map/ppermute | solution.py:163
  25.5 0.9 %collective-permute-start.2 = (bf16[16,2048]{1,0:T(8,128)(2,1)S(1)}, bf16[16,2048]{1,0:T(8,128)(2,1)S(1)}, u32[]{:S(2)}, u32[]{:S(2)}) collective-permute-start(bf16[16,2048]{1,0:T(8,128)(2,1)S(1)} %hidden.1.refs_0_), channel_id=1, source_target_pairs={{0,4},{1,5},{2,6},{3,7},{4,0},{5,1},{6,2},{7,3},{8,12},{9,13},{10,... | collective-permute-start | bytes 196616 | tf_op jit(solution)/shard_map/ppermute | solution.py:163
  26.3 2.9 %collective-permute-done.refs_0_ = bf16[16,2048]{1,0:T(8,128)(2,1)S(1)} collective-permute-done((bf16[16,2048]{1,0:T(8,128)(2,1)S(1)}, bf16[16,2048]{1,0:T(8,128)(2,1)S(1)}, u32[]{:S(2)}, u32[]{:S(2)}) %collective-permute-start) | collective-permute-done | bytes 65568 | tf_op jit(solution)/shard_map/ppermute | solution.py:163
  29.2 0.0 collective-permute-start.3
  29.2 0.0 collective-permute-done.1.refs_1_
  29.2 0.0 copy-done
  29.2 1.8 %down.5.refs_3_ = f32[768,16]{1,0:T(8,128)S(1)} custom-call(bf16[16,2048]{1,0:T(8,128)(2,1)S(1)} %hidden.1.refs_0_, bf16[16,2048]{1,0:T(8,128)(2,1)S(1)} %collective-permute-done.1.refs_1_, bf16[1,768,16384]{2,1,0:T(8,128)(2,1)S(1)} %copy-done), custom_call_target="tpu_custom_call" | custom-call | tf_op jit(solution)/shard_map/down/pallas_call | solution.py:185
  31.0 0.0 collective-permute-done.2.refs_0_
  31.0 1.6 %collective-permute-start.4 = (bf16[16,2048]{1,0:T(8,128)(2,1)S(1)}, bf16[16,2048]{1,0:T(8,128)(2,1)S(1)}, u32[]{:S(2)}, u32[]{:S(2)}) collective-permute-start(bf16[16,2048]{1,0:T(8,128)(2,1)S(1)} %collective-permute-done.2.refs_0_), channel_id=1, source_target_pairs={{0,2},{1,3},{2,0},{3,1},{4,6},{5,7},{6,4},{7,5},{8,10},{9,11},{10,... | collective-permute-start | bytes 196616 | tf_op jit(solution)/shard_map/ppermute | solution.py:163
  32.6 0.8 %collective-permute-done.3.refs_1_ = bf16[16,2048]{1,0:T(8,128)(2,1)S(1)} collective-permute-done((bf16[16,2048]{1,0:T(8,128)(2,1)S(1)}, bf16[16,2048]{1,0:T(8,128)(2,1)S(1)}, u32[]{:S(2)}, u32[]{:S(2)}) %collective-permute-start.3) | collective-permute-done | bytes 65568 | tf_op jit(solution)/shard_map/ppermute | solution.py:163
  33.5 0.3 collective-permute-start.6
  33.8 1.8 %down.6.refs_3_ = f32[768,16]{1,0:T(8,128)S(1)} custom-call(bf16[16,2048]{1,0:T(8,128)(2,1)S(1)} %collective-permute-done.refs_0_, bf16[16,2048]{1,0:T(8,128)(2,1)S(1)} %collective-permute-done.3.refs_1_, bf16[1,768,16384]{2,1,0:T(8,128)(2,1)S(1)} %copy-done, f32[768,16]{1,0:T(8,128)S(1)} %down.5.refs_3_), custom_call_target="tpu_custom_call" | custom-call | tf_op jit(solution)/shard_map/down/pallas_call | solution.py:185
  35.5 0.0 collective-permute-done.4.refs_1_
  35.6 1.8 %collective-permute-start.5 = (bf16[16,2048]{1,0:T(8,128)(2,1)S(1)}, bf16[16,2048]{1,0:T(8,128)(2,1)S(1)}, u32[]{:S(2)}, u32[]{:S(2)}) collective-permute-start(bf16[16,2048]{1,0:T(8,128)(2,1)S(1)} %collective-permute-done.4.refs_1_), channel_id=1, source_target_pairs={{0,1},{1,0},{2,3},{3,2},{4,5},{5,4},{6,7},{7,6},{8,9},{9,8},{10,11... | collective-permute-start | bytes 196616 | tf_op jit(solution)/shard_map/ppermute | solution.py:163
  37.3 1.8 %down.7.refs_2_ = f32[768,16]{1,0:T(8,128)S(1)} custom-call(bf16[16,2048]{1,0:T(8,128)(2,1)S(1)} %collective-permute-done.2.refs_0_, bf16[16,2048]{1,0:T(8,128)(2,1)S(1)} %collective-permute-done.4.refs_1_, bf16[1,768,16384]{2,1,0:T(8,128)(2,1)S(1)} %copy-done, f32[768,16]{1,0:T(8,128)S(1)} %down.6.refs_3_), custom_call_target="tpu_custom_call" | custom-call | tf_op jit(solution)/shard_map/down/pallas_call | solution.py:185
  39.1 0.0 collective-permute-done.6.refs_0_
  39.1 1.0 %down.8.refs_2_ = f32[768,16]{1,0:T(8,128)S(1)} custom-call(bf16[16,2048]{1,0:T(8,128)(2,1)S(1)} %collective-permute-done.6.refs_0_, bf16[1,768,16384]{2,1,0:T(8,128)(2,1)S(1)} %copy-done, f32[768,16]{1,0:T(8,128)S(1)} %down.7.refs_2_), custom_call_target="tpu_custom_call" | custom-call | tf_op jit(solution)/shard_map/down/pallas_call | solution.py:185
  40.1 0.0 collective-permute-done.5.refs_0_
  40.1 1.0 %down.9 = f32[16,2,768]{2,1,0:T(2,128)S(1)} custom-call(bf16[16,2048]{1,0:T(8,128)(2,1)S(1)} %collective-permute-done.5.refs_0_, bf16[1,768,16384]{2,1,0:T(8,128)(2,1)S(1)} %copy-done, f32[768,16]{1,0:T(8,128)S(1)} %down.8.refs_2_), custom_call_target="tpu_custom_call" | custom-call | tf_op jit(solution)/shard_map/down/pallas_call | solution.py:185
  41.1 10.0 %all_to_all.11.back_ref = f32[16,2,768]{2,1,0:T(2,128)S(1)} all-to-all(f32[16,2,768]{2,1,0:T(2,128)S(1)} %down.9), channel_id=1, replica_groups=mesh['group'=2,'expert'=2,'tile'=8] {'expert','tile'}, dimensions={0} | all-to-all | bytes 196608 | tf_op jit(solution)/shard_map/all_to_all | solution.py:205
  51.1 0.7 %combine.1 = bf16[4,3072]{1,0:T(4,128)(2,1)} custom-call(f32[16,2,768]{2,1,0:T(2,128)S(1)} %all_to_all.11.back_ref, f32[6,4,128]{2,1,0:T(4,128)S(1)} %get-tuple-element.20.table_ref), custom_call_target="tpu_custom_call" | custom-call | tf_op jit(solution)/shard_map/combine/pallas_call | solution.py:206
  (1 shorter events, 0.0 us)
Async XLA Ops:
  0.0 17.5 %copy-start.1 = (bf16[1,6144,2048]{2,1,0:T(8,128)(2,1)S(1)}, bf16[1,6144,2048]{2,1,0:T(8,128)(2,1)}, u32[]{:S(2)}) copy-start(bf16[1,6144,2048]{2,1,0:T(8,128)(2,1)} %w_ref.2) | copy-start | bytes 75497472
  1.0 19.8 %copy-start.2 = (bf16[1,6144,2048]{2,1,0:T(8,128)(2,1)S(1)}, bf16[1,6144,2048]{2,1,0:T(8,128)(2,1)}, u32[]{:S(2)}) copy-start(bf16[1,6144,2048]{2,1,0:T(8,128)(2,1)} %w_ref.3) | copy-start | bytes 75497472
  20.9 8.4 %copy-start = (bf16[1,768,16384]{2,1,0:T(8,128)(2,1)S(1)}, bf16[1,768,16384]{2,1,0:T(8,128)(2,1)}, u32[]{:S(2)}) copy-start(bf16[1,768,16384]{2,1,0:T(8,128)(2,1)} %refs_1_.3) | copy-start | bytes 75497472
  24.2 5.0 %collective-permute-start = (bf16[16,2048]{1,0:T(8,128)(2,1)S(1)}, bf16[16,2048]{1,0:T(8,128)(2,1)S(1)}, u32[]{:S(2)}, u32[]{:S(2)}) collective-permute-start(bf16[16,2048]{1,0:T(8,128)(2,1)S(1)} %hidden.1.refs_0_), channel_id=1, source_target_pairs={{0,2},{1,3},{2,0},{3,1},{4,6},{5,7},{6,4},{7,5},{8,10},{9,11},{10,... | collective-permute-start | bytes 196616 | tf_op jit(solution)/shard_map/ppermute | solution.py:163
  24.9 4.3 %collective-permute-start.1 = (bf16[16,2048]{1,0:T(8,128)(2,1)S(1)}, bf16[16,2048]{1,0:T(8,128)(2,1)S(1)}, u32[]{:S(2)}, u32[]{:S(2)}) collective-permute-start(bf16[16,2048]{1,0:T(8,128)(2,1)S(1)} %hidden.1.refs_0_), channel_id=1, source_target_pairs={{0,1},{1,0},{2,3},{3,2},{4,5},{5,4},{6,7},{7,6},{8,9},{9,8},{10,11... | collective-permute-start | bytes 196616 | tf_op jit(solution)/shard_map/ppermute | solution.py:163
  25.5 5.5 %collective-permute-start.2 = (bf16[16,2048]{1,0:T(8,128)(2,1)S(1)}, bf16[16,2048]{1,0:T(8,128)(2,1)S(1)}, u32[]{:S(2)}, u32[]{:S(2)}) collective-permute-start(bf16[16,2048]{1,0:T(8,128)(2,1)S(1)} %hidden.1.refs_0_), channel_id=1, source_target_pairs={{0,4},{1,5},{2,6},{3,7},{4,0},{5,1},{6,2},{7,3},{8,12},{9,13},{10,... | collective-permute-start | bytes 196616 | tf_op jit(solution)/shard_map/ppermute | solution.py:163
  29.2 4.3 %collective-permute-start.3 = (bf16[16,2048]{1,0:T(8,128)(2,1)S(1)}, bf16[16,2048]{1,0:T(8,128)(2,1)S(1)}, u32[]{:S(2)}, u32[]{:S(2)}) collective-permute-start(bf16[16,2048]{1,0:T(8,128)(2,1)S(1)} %collective-permute-done.refs_0_), channel_id=1, source_target_pairs={{0,1},{1,0},{2,3},{3,2},{4,5},{5,4},{6,7},{7,6},{8,9},{9,8},{10,11... | collective-permute-start | bytes 196616 | tf_op jit(solution)/shard_map/ppermute | solution.py:163
  31.0 4.5 %collective-permute-start.4 = (bf16[16,2048]{1,0:T(8,128)(2,1)S(1)}, bf16[16,2048]{1,0:T(8,128)(2,1)S(1)}, u32[]{:S(2)}, u32[]{:S(2)}) collective-permute-start(bf16[16,2048]{1,0:T(8,128)(2,1)S(1)} %collective-permute-done.2.refs_0_), channel_id=1, source_target_pairs={{0,2},{1,3},{2,0},{3,1},{4,6},{5,7},{6,4},{7,5},{8,10},{9,11},{10,... | collective-permute-start | bytes 196616 | tf_op jit(solution)/shard_map/ppermute | solution.py:163
  33.5 5.6 %collective-permute-start.6 = (bf16[16,2048]{1,0:T(8,128)(2,1)S(1)}, bf16[16,2048]{1,0:T(8,128)(2,1)S(1)}, u32[]{:S(2)}, u32[]{:S(2)}) collective-permute-start(bf16[16,2048]{1,0:T(8,128)(2,1)S(1)} %collective-permute-done.2.refs_0_), channel_id=1, source_target_pairs={{0,1},{1,0},{2,3},{3,2},{4,5},{5,4},{6,7},{7,6},{8,9},{9,8},{10,11... | collective-permute-start | bytes 196616 | tf_op jit(solution)/shard_map/ppermute | solution.py:163
  35.6 4.5 %collective-permute-start.5 = (bf16[16,2048]{1,0:T(8,128)(2,1)S(1)}, bf16[16,2048]{1,0:T(8,128)(2,1)S(1)}, u32[]{:S(2)}, u32[]{:S(2)}) collective-permute-start(bf16[16,2048]{1,0:T(8,128)(2,1)S(1)} %collective-permute-done.4.refs_1_), channel_id=1, source_target_pairs={{0,1},{1,0},{2,3},{3,2},{4,5},{5,4},{6,7},{7,6},{8,9},{9,8},{10,11... | collective-permute-start | bytes 196616 | tf_op jit(solution)/shard_map/ppermute | solution.py:163

commit v21 on v20

--- a/solution.py
+++ b/solution.py
@@ -188,18 +188,16 @@
         )(*(block[k] for k in steps), in_vmem(w_down), *(() if first else (total,)))
 
     block = {0: hidden}
-    for k in (4, 2, 1):
+    for k in (2, 1, 4, 6):
         block[k] = swap(hidden, k)
     block[3] = swap(block[2], 1)
     total = down(None, [0, 1], block, False)
     total, block[4] = lax.optimization_barrier((total, block[4]))
-    block[6] = swap(block[4], 2)
-    block[4], block[3] = lax.optimization_barrier((block[4], block[3]))
     block[5] = swap(block[4], 1)
-    total = down(total, [2, 3], block, False)
-    total, block[6] = lax.optimization_barrier((total, block[6]))
+    total = down(total, [2, 4], block, False)
+    total, block[6], block[3] = lax.optimization_barrier((total, block[6], block[3]))
     block[7] = swap(block[6], 1)
-    total = down(total, [4, 6], block, False)
+    total = down(total, [3, 6], block, False)
     total = down(total, [5], block, False)
     result = down(total, [7], block, True)
     back = lax.all_to_all(result, ("expert", "tile"), split_axis=0, concat_axis=0, tiled=True)

time: 52.1 us -> 52.3 us (level)
  starting transfers between devices: 5.84 us -> 8.5 us
  waiting for transfers between devices: 3.71 us -> 1.6 us
    ppermute x7, starting transfers between devices: 5.84 us -> 8.5 us  [swap(): return lax.ppermute(x, 'tile', [(t, t ^ bit) for t in range(tiles)])]
    ppermute x7, waiting for transfers between devices: 3.71 us -> 1.6 us  [swap(): return lax.ppermute(x, 'tile', [(t, t ^ bit) for t in range(tiles)])]
where the time goes in v21:
time: 52.3 us; the launch traced here: 52.1 us
  blocking collectives  26.2 us (50%)
  Pallas kernels  15.7 us (30%)
  starting transfers between devices  8.5 us (16%)
  waiting for transfers between devices  1.6 us (3%)
    all_to_all x1, blocking collectives, local_direct(): lax.all_to_all(sends, ('expert', 'tile'), split_axis=0, concat_axis=0, ti...  16.4 us
    all_to_all x1, blocking collectives, local_direct(): lax.all_to_all(result, ('expert', 'tile'), split_axis=0, concat_axis=0, t...  9.76 us
    ppermute x7, starting transfers between devices, swap(): return lax.ppermute(x, 'tile', [(t, t ^ bit) for t in range(tiles)])  8.5 us
    pallas_call x5, Pallas kernels, down(): call(functools.partial(down_kernel, steps, first, last), 'down', out, [VM...  7.24 us
    pallas_call x1, Pallas kernels, local_direct(): call(hidden_kernel, 'hidden', bf16(slots, width), [VMEM] * 3, 4 * MIB, 0....  3.37 us
    pallas_call x1, Pallas kernels, local_direct(): call(gate_kernel, 'gate', f32(slots, width), [VMEM] * 2, 4 * MIB, 0.0)  3.34 us
    ppermute x7, waiting for transfers between devices, swap(): return lax.ppermute(x, 'tile', [(t, t ^ bit) for t in range(tiles)])  1.6 us
  transfers between devices with their start and end apart: 7, of which 2 were waited for; matrix products, arithmetic and copies ran while one was open for 0% of the time, Pallas kernels for 12%

profile of v21, /device:TPU:0, one launch (start us, length us, event | category | flops | bytes accessed | tf_op | source)
XLA Modules:
  0.0 52.1 jit_solution(8876659124909958877)
XLA Ops:
  0.0 0.0 copy-start.1
  0.0 1.0 %dispatch.1 = (bf16[16,2,3072]{2,1,0:T(2,128)(2,1)S(1)}, f32[6,4,128]{2,1,0:T(4,128)S(1)}) custom-call(bf16[4,3072]{1,0:T(4,128)(2,1)} %tokens_hbm.1, s32[2,4]{1,0:T(2,128)} %bitcast.2, f32[2,4]{1,0:T(2,128)} %bitcast.3), custom_call_target="tpu_custom_call" | custom-call | flops 599999971328 | tf_op jit(solution)/shard_map/dispatch/pallas_call | solution.py:167
  1.0 0.0 copy-start.2
  1.0 16.4 %all_to_all.10.blocks_ref = bf16[16,2,3072]{2,1,0:T(2,128)(2,1)S(1)} all-to-all(bf16[16,2,3072]{2,1,0:T(2,128)(2,1)S(1)} %get-tuple-element.12), channel_id=1, replica_groups=mesh['group'=2,'expert'=2,'tile'=8] {'expert','tile'}, dimensions={0} | all-to-all | bytes 393216 | tf_op jit(solution)/shard_map/all_to_all | solution.py:177
  17.5 0.0 copy-done.1
  17.5 3.3 %gate.1.gate_ref = f32[16,2048]{1,0:T(8,128)S(1)} custom-call(bf16[32,3072]{1,0:T(8,128)(2,1)S(1)} %merge.1.rows_ref, bf16[1,6144,2048]{2,1,0:T(8,128)(2,1)S(1)} %copy-done.1), custom_call_target="tpu_custom_call" | custom-call | tf_op jit(solution)/shard_map/gate/pallas_call | solution.py:179
  20.9 0.0 copy-done.2
  20.9 0.0 copy-start
  20.9 3.4 %hidden.1.refs_0_ = bf16[16,2048]{1,0:T(8,128)(2,1)S(1)} custom-call(bf16[32,3072]{1,0:T(8,128)(2,1)S(1)} %merge.1.rows_ref, bf16[1,6144,2048]{2,1,0:T(8,128)(2,1)S(1)} %copy-done.2, f32[16,2048]{1,0:T(8,128)S(1)} %gate.1.gate_ref), custom_call_target="tpu_custom_call" | custom-call | flops 199999995904 | tf_op jit(solution)/shard_map/hidden/pallas_call | solution.py:180
  24.2 0.7 %collective-permute-start = (bf16[16,2048]{1,0:T(8,128)(2,1)S(1)}, bf16[16,2048]{1,0:T(8,128)(2,1)S(1)}, u32[]{:S(2)}, u32[]{:S(2)}) collective-permute-start(bf16[16,2048]{1,0:T(8,128)(2,1)S(1)} %hidden.1.refs_0_), channel_id=1, source_target_pairs={{0,2},{1,3},{2,0},{3,1},{4,6},{5,7},{6,4},{7,5},{8,10},{9,11},{10,... | collective-permute-start | bytes 196616 | tf_op jit(solution)/shard_map/ppermute | solution.py:163
  24.9 0.6 %collective-permute-start.1 = (bf16[16,2048]{1,0:T(8,128)(2,1)S(1)}, bf16[16,2048]{1,0:T(8,128)(2,1)S(1)}, u32[]{:S(2)}, u32[]{:S(2)}) collective-permute-start(bf16[16,2048]{1,0:T(8,128)(2,1)S(1)} %hidden.1.refs_0_), channel_id=1, source_target_pairs={{0,1},{1,0},{2,3},{3,2},{4,5},{5,4},{6,7},{7,6},{8,9},{9,8},{10,11... | collective-permute-start | bytes 196616 | tf_op jit(solution)/shard_map/ppermute | solution.py:163
  25.5 0.9 %collective-permute-start.2 = (bf16[16,2048]{1,0:T(8,128)(2,1)S(1)}, bf16[16,2048]{1,0:T(8,128)(2,1)S(1)}, u32[]{:S(2)}, u32[]{:S(2)}) collective-permute-start(bf16[16,2048]{1,0:T(8,128)(2,1)S(1)} %hidden.1.refs_0_), channel_id=1, source_target_pairs={{0,4},{1,5},{2,6},{3,7},{4,0},{5,1},{6,2},{7,3},{8,12},{9,13},{10,... | collective-permute-start | bytes 196616 | tf_op jit(solution)/shard_map/ppermute | solution.py:163
  26.3 2.8 %collective-permute-start.3 = (bf16[16,2048]{1,0:T(8,128)(2,1)S(1)}, bf16[16,2048]{1,0:T(8,128)(2,1)S(1)}, u32[]{:S(2)}, u32[]{:S(2)}) collective-permute-start(bf16[16,2048]{1,0:T(8,128)(2,1)S(1)} %hidden.1.refs_0_), channel_id=1, source_target_pairs={{0,6},{1,7},{2,4},{3,5},{4,2},{5,3},{6,0},{7,1},{8,14},{9,15},{10,... | collective-permute-start | bytes 196616 | tf_op jit(solution)/shard_map/ppermute | solution.py:163
  29.2 0.0 collective-permute-done.refs_0_
  29.2 1.4 %collective-permute-start.4 = (bf16[16,2048]{1,0:T(8,128)(2,1)S(1)}, bf16[16,2048]{1,0:T(8,128)(2,1)S(1)}, u32[]{:S(2)}, u32[]{:S(2)}) collective-permute-start(bf16[16,2048]{1,0:T(8,128)(2,1)S(1)} %collective-permute-done.refs_0_), channel_id=1, source_target_pairs={{0,1},{1,0},{2,3},{3,2},{4,5},{5,4},{6,7},{7,6},{8,9},{9,8},{10,11... | collective-permute-start | bytes 196616 | tf_op jit(solution)/shard_map/ppermute | solution.py:163
  30.7 0.0 collective-permute-done.1.refs_1_
  30.7 0.0 copy-done
  30.7 1.8 %down.5.refs_3_ = f32[768,16]{1,0:T(8,128)S(1)} custom-call(bf16[16,2048]{1,0:T(8,128)(2,1)S(1)} %hidden.1.refs_0_, bf16[16,2048]{1,0:T(8,128)(2,1)S(1)} %collective-permute-done.1.refs_1_, bf16[1,768,16384]{2,1,0:T(8,128)(2,1)S(1)} %copy-done), custom_call_target="tpu_custom_call" | custom-call | tf_op jit(solution)/shard_map/down/pallas_call | solution.py:185
  32.4 0.6 %collective-permute-done.2.refs_1_ = bf16[16,2048]{1,0:T(8,128)(2,1)S(1)} collective-permute-done((bf16[16,2048]{1,0:T(8,128)(2,1)S(1)}, bf16[16,2048]{1,0:T(8,128)(2,1)S(1)}, u32[]{:S(2)}, u32[]{:S(2)}) %collective-permute-start.2) | collective-permute-done | bytes 65568 | tf_op jit(solution)/shard_map/ppermute | solution.py:163
  33.1 1.4 %collective-permute-start.6 = (bf16[16,2048]{1,0:T(8,128)(2,1)S(1)}, bf16[16,2048]{1,0:T(8,128)(2,1)S(1)}, u32[]{:S(2)}, u32[]{:S(2)}) collective-permute-start(bf16[16,2048]{1,0:T(8,128)(2,1)S(1)} %collective-permute-done.2.refs_1_), channel_id=1, source_target_pairs={{0,1},{1,0},{2,3},{3,2},{4,5},{5,4},{6,7},{7,6},{8,9},{9,8},{10,11... | collective-permute-start | bytes 196616 | tf_op jit(solution)/shard_map/ppermute | solution.py:163
  34.5 1.8 %down.6.refs_3_ = f32[768,16]{1,0:T(8,128)S(1)} custom-call(bf16[16,2048]{1,0:T(8,128)(2,1)S(1)} %collective-permute-done.refs_0_, bf16[16,2048]{1,0:T(8,128)(2,1)S(1)} %collective-permute-done.2.refs_1_, bf16[1,768,16384]{2,1,0:T(8,128)(2,1)S(1)} %copy-done, f32[768,16]{1,0:T(8,128)S(1)} %down.5.refs_3_), custom_call_target="tpu_custom_call" | custom-call | tf_op jit(solution)/shard_map/down/pallas_call | solution.py:185
  36.3 0.0 collective-permute-done.3.refs_1_
  36.3 0.0 collective-permute-done.4.refs_0_
  36.3 0.6 %collective-permute-start.5 = (bf16[16,2048]{1,0:T(8,128)(2,1)S(1)}, bf16[16,2048]{1,0:T(8,128)(2,1)S(1)}, u32[]{:S(2)}, u32[]{:S(2)}) collective-permute-start(bf16[16,2048]{1,0:T(8,128)(2,1)S(1)} %collective-permute-done.3.refs_1_), channel_id=1, source_target_pairs={{0,1},{1,0},{2,3},{3,2},{4,5},{5,4},{6,7},{7,6},{8,9},{9,8},{10,11... | collective-permute-start | bytes 196616 | tf_op jit(solution)/shard_map/ppermute | solution.py:163
  36.9 1.8 %down.7.refs_2_ = f32[768,16]{1,0:T(8,128)S(1)} custom-call(bf16[16,2048]{1,0:T(8,128)(2,1)S(1)} %collective-permute-done.4.refs_0_, bf16[16,2048]{1,0:T(8,128)(2,1)S(1)} %collective-permute-done.3.refs_1_, bf16[1,768,16384]{2,1,0:T(8,128)(2,1)S(1)} %copy-done, f32[768,16]{1,0:T(8,128)S(1)} %down.6.refs_3_), custom_call_target="tpu_custom_call" | custom-call | tf_op jit(solution)/shard_map/down/pallas_call | solution.py:185
  38.7 0.0 collective-permute-done.6.refs_0_
  38.7 1.0 %down.8.refs_2_ = f32[768,16]{1,0:T(8,128)S(1)} custom-call(bf16[16,2048]{1,0:T(8,128)(2,1)S(1)} %collective-permute-done.6.refs_0_, bf16[1,768,16384]{2,1,0:T(8,128)(2,1)S(1)} %copy-done, f32[768,16]{1,0:T(8,128)S(1)} %down.7.refs_2_), custom_call_target="tpu_custom_call" | custom-call | tf_op jit(solution)/shard_map/down/pallas_call | solution.py:185
  39.7 0.9 %collective-permute-done.5.refs_0_ = bf16[16,2048]{1,0:T(8,128)(2,1)S(1)} collective-permute-done((bf16[16,2048]{1,0:T(8,128)(2,1)S(1)}, bf16[16,2048]{1,0:T(8,128)(2,1)S(1)}, u32[]{:S(2)}, u32[]{:S(2)}) %collective-permute-start.5) | collective-permute-done | bytes 65568 | tf_op jit(solution)/shard_map/ppermute | solution.py:163
  40.6 1.0 %down.9 = f32[16,2,768]{2,1,0:T(2,128)S(1)} custom-call(bf16[16,2048]{1,0:T(8,128)(2,1)S(1)} %collective-permute-done.5.refs_0_, bf16[1,768,16384]{2,1,0:T(8,128)(2,1)S(1)} %copy-done, f32[768,16]{1,0:T(8,128)S(1)} %down.8.refs_2_), custom_call_target="tpu_custom_call" | custom-call | tf_op jit(solution)/shard_map/down/pallas_call | solution.py:185
  41.6 9.8 %all_to_all.11.back_ref = f32[16,2,768]{2,1,0:T(2,128)S(1)} all-to-all(f32[16,2,768]{2,1,0:T(2,128)S(1)} %down.9), channel_id=1, replica_groups=mesh['group'=2,'expert'=2,'tile'=8] {'expert','tile'}, dimensions={0} | all-to-all | bytes 196608 | tf_op jit(solution)/shard_map/all_to_all | solution.py:203
  51.4 0.7 %combine.1 = bf16[4,3072]{1,0:T(4,128)(2,1)} custom-call(f32[16,2,768]{2,1,0:T(2,128)S(1)} %all_to_all.11.back_ref, f32[6,4,128]{2,1,0:T(4,128)S(1)} %get-tuple-element.18.table_ref), custom_call_target="tpu_custom_call" | custom-call | tf_op jit(solution)/shard_map/combine/pallas_call | solution.py:204
  (1 shorter events, 0.0 us)
Async XLA Ops:
  0.0 17.5 %copy-start.1 = (bf16[1,6144,2048]{2,1,0:T(8,128)(2,1)S(1)}, bf16[1,6144,2048]{2,1,0:T(8,128)(2,1)}, u32[]{:S(2)}) copy-start(bf16[1,6144,2048]{2,1,0:T(8,128)(2,1)} %w_ref.2) | copy-start | bytes 75497472
  1.0 19.8 %copy-start.2 = (bf16[1,6144,2048]{2,1,0:T(8,128)(2,1)S(1)}, bf16[1,6144,2048]{2,1,0:T(8,128)(2,1)}, u32[]{:S(2)}) copy-start(bf16[1,6144,2048]{2,1,0:T(8,128)(2,1)} %w_ref.3) | copy-start | bytes 75497472
  20.9 9.8 %copy-start = (bf16[1,768,16384]{2,1,0:T(8,128)(2,1)S(1)}, bf16[1,768,16384]{2,1,0:T(8,128)(2,1)}, u32[]{:S(2)}) copy-start(bf16[1,768,16384]{2,1,0:T(8,128)(2,1)} %refs_1_.3) | copy-start | bytes 75497472
  24.2 5.0 %collective-permute-start = (bf16[16,2048]{1,0:T(8,128)(2,1)S(1)}, bf16[16,2048]{1,0:T(8,128)(2,1)S(1)}, u32[]{:S(2)}, u32[]{:S(2)}) collective-permute-start(bf16[16,2048]{1,0:T(8,128)(2,1)S(1)} %hidden.1.refs_0_), channel_id=1, source_target_pairs={{0,2},{1,3},{2,0},{3,1},{4,6},{5,7},{6,4},{7,5},{8,10},{9,11},{10,... | collective-permute-start | bytes 196616 | tf_op jit(solution)/shard_map/ppermute | solution.py:163
  24.9 5.7 %collective-permute-start.1 = (bf16[16,2048]{1,0:T(8,128)(2,1)S(1)}, bf16[16,2048]{1,0:T(8,128)(2,1)S(1)}, u32[]{:S(2)}, u32[]{:S(2)}) collective-permute-start(bf16[16,2048]{1,0:T(8,128)(2,1)S(1)} %hidden.1.refs_0_), channel_id=1, source_target_pairs={{0,1},{1,0},{2,3},{3,2},{4,5},{5,4},{6,7},{7,6},{8,9},{9,8},{10,11... | collective-permute-start | bytes 196616 | tf_op jit(solution)/shard_map/ppermute | solution.py:163
  25.5 7.6 %collective-permute-start.2 = (bf16[16,2048]{1,0:T(8,128)(2,1)S(1)}, bf16[16,2048]{1,0:T(8,128)(2,1)S(1)}, u32[]{:S(2)}, u32[]{:S(2)}) collective-permute-start(bf16[16,2048]{1,0:T(8,128)(2,1)S(1)} %hidden.1.refs_0_), channel_id=1, source_target_pairs={{0,4},{1,5},{2,6},{3,7},{4,0},{5,1},{6,2},{7,3},{8,12},{9,13},{10,... | collective-permute-start | bytes 196616 | tf_op jit(solution)/shard_map/ppermute | solution.py:163
  26.3 9.9 %collective-permute-start.3 = (bf16[16,2048]{1,0:T(8,128)(2,1)S(1)}, bf16[16,2048]{1,0:T(8,128)(2,1)S(1)}, u32[]{:S(2)}, u32[]{:S(2)}) collective-permute-start(bf16[16,2048]{1,0:T(8,128)(2,1)S(1)} %hidden.1.refs_0_), channel_id=1, source_target_pairs={{0,6},{1,7},{2,4},{3,5},{4,2},{5,3},{6,0},{7,1},{8,14},{9,15},{10,... | collective-permute-start | bytes 196616 | tf_op jit(solution)/shard_map/ppermute | solution.py:163
  29.2 7.1 %collective-permute-start.4 = (bf16[16,2048]{1,0:T(8,128)(2,1)S(1)}, bf16[16,2048]{1,0:T(8,128)(2,1)S(1)}, u32[]{:S(2)}, u32[]{:S(2)}) collective-permute-start(bf16[16,2048]{1,0:T(8,128)(2,1)S(1)} %collective-permute-done.refs_0_), channel_id=1, source_target_pairs={{0,1},{1,0},{2,3},{3,2},{4,5},{5,4},{6,7},{7,6},{8,9},{9,8},{10,11... | collective-permute-start | bytes 196616 | tf_op jit(solution)/shard_map/ppermute | solution.py:163
  33.1 5.7 %collective-permute-start.6 = (bf16[16,2048]{1,0:T(8,128)(2,1)S(1)}, bf16[16,2048]{1,0:T(8,128)(2,1)S(1)}, u32[]{:S(2)}, u32[]{:S(2)}) collective-permute-start(bf16[16,2048]{1,0:T(8,128)(2,1)S(1)} %collective-permute-done.2.refs_1_), channel_id=1, source_target_pairs={{0,1},{1,0},{2,3},{3,2},{4,5},{5,4},{6,7},{7,6},{8,9},{9,8},{10,11... | collective-permute-start | bytes 196616 | tf_op jit(solution)/shard_map/ppermute | solution.py:163
  36.3 4.3 %collective-permute-start.5 = (bf16[16,2048]{1,0:T(8,128)(2,1)S(1)}, bf16[16,2048]{1,0:T(8,128)(2,1)S(1)}, u32[]{:S(2)}, u32[]{:S(2)}) collective-permute-start(bf16[16,2048]{1,0:T(8,128)(2,1)S(1)} %collective-permute-done.3.refs_1_), channel_id=1, source_target_pairs={{0,1},{1,0},{2,3},{3,2},{4,5},{5,4},{6,7},{7,6},{8,9},{9,8},{10,11... | collective-permute-start | bytes 196616 | tf_op jit(solution)/shard_map/ppermute | solution.py:163
